TPU v7x, 256 devices: a whole 4x4x8 slice. The times are simulated.
256 devices in a mesh: leaf: 64 (over y, x, z_hi), probe: 4 (over z_lo, core).
Axes of the slice: x: 4, y: 4, z: 8 (z_hi: 4, z_lo: 2; z = z_hi * 2 + z_lo), core: 2. Of those that a mesh axis runs over, the one named last changes fastest.
Arguments:
- leaf_blocks: float32 [65536, 1024], P('leaf'), may hold values from -0.1875 to 0.1875
- block_mask: int32 [64, 8, 8], P('leaf'), may hold values 0 or 1
- row_factor_stack: float32 [6, 65536, 128], P(None, 'leaf'), may hold values from -0.5 to 0.5
- column_factor_stack: float32 [6, 65536, 128], P(None, 'leaf'), may hold values from -0.0234375 to 0.0234375
- probes: float32 [65536, 1024], P('leaf', 'probe'), may hold values from -6 to 6
Outputs:
- applied: float32 [65536, 1024], P('leaf', 'probe')
- probe_gram: float32 [1024, 1024], P('leaf', 'probe')
All inputs are finite; a program needn't handle non-finite values. No bound on the sum of `block_mask` on one device may be relied on, other than what follows from the above.
Results may differ from a plain program's by a relative error of at most 0.0001.
Values sent between devices are 32-bit elements; how exact they have to be, the bound alone decides.
No kernel may reach another device: no remote copies, remote signals or barrier semaphores. Data moves between devices by JAX's collectives and lax.ppermute only.
A program may use at most 64 MiB of HBM per device.

v0:
```python
import jax
import jax.numpy as jnp
from jax import lax
from jax.sharding import PartitionSpec as P


def partner(value, axis, distance):
    mask = 2**distance
    pairs = [(source, source ^ mask) for source in range(lax.axis_size(axis))]
    return lax.ppermute(value, axis, pairs)


def local(leaf_blocks, block_mask, row_factor_stack, column_factor_stack, probes):
    leaf_points = leaf_blocks.shape[1]
    mask_side = block_mask.shape[1]
    block_span_width = leaf_points // mask_side
    depth = row_factor_stack.shape[0]
    weights = block_mask[0].astype(jnp.float32)
    masked = (
        leaf_blocks.reshape(mask_side, block_span_width, mask_side, block_span_width)
        * weights[:, None, :, None]
    ).reshape(leaf_points, leaf_points)
    applied = jnp.dot(
        masked, probes, precision=lax.Precision.HIGHEST, preferred_element_type=jnp.float32
    )
    probe_projected = jnp.einsum(
        "tec,eg->tcg", column_factor_stack, probes, precision=lax.Precision.HIGHEST
    )
    sibling_nodes = []
    for level_bit in range(depth):
        own_total = probe_projected[level_bit]
        for lowest_level_flag in range(level_bit):
            own_total = own_total + partner(own_total, "leaf", lowest_level_flag)
        sibling_nodes.append(partner(own_total, "leaf", level_bit))
    applied = applied + jnp.einsum(
        "tvi,tic->vc", row_factor_stack, jnp.stack(sibling_nodes), precision=lax.Precision.HIGHEST
    )
    total_points = leaf_points * lax.axis_size("leaf")
    gathered = lax.all_gather(applied, "probe", axis=1, tiled=True)
    probe_gram = (
        lax.psum_scatter(
            jnp.dot(
                gathered.T,
                applied,
                precision=lax.Precision.HIGHEST,
                preferred_element_type=jnp.float32,
            ),
            "leaf",
            scatter_dimension=0,
            tiled=True,
        )
        / total_points
    )
    return (applied, probe_gram)


def solution(mesh):
    return jax.shard_map(
        local,
        mesh=mesh,
        in_specs=(
            P("leaf", None),
            P("leaf", None, None),
            P(None, "leaf", None),
            P(None, "leaf", None),
            P("leaf", "probe"),
        ),
        out_specs=(P("leaf", "probe"), P("leaf", "probe")),
        check_vma=False,
    )
```

profile of v0, /device:TPU:32, one launch (start us, length us, event | category | flops | bytes accessed | tf_op | source)
XLA Modules:
  0.0 564.1 jit_solution(11488975324971652614)
XLA Ops:
  7.2 0.0 all-gather.2.cloned.1.call-start
  7.3 7.4 %fusion.3 = f32[6,128,256]{2,1,0:T(8,128)S(1)} fusion(f32[6,1024,128]{2,1,0:T(8,128)} %param.8, f32[1024,256]{1,0:T(8,128)} %param.9), kind=kOutput, calls=%fused_computation.5 | convolution fusion | flops 2415919104 | bytes 4980736 | tf_op jit(solution)/shard_map/tec,eg->tcg/dot_general | solution.py:26
  14.6 0.1 slice_bitcast_fusion
  14.7 3.4 collective-permute-start.15
  18.1 0.1 collective-permute-start.10
  18.2 2.8 collective-permute-start.6
  21.0 0.1 collective-permute-start.3
  21.1 2.8 collective-permute-start.1
  23.9 0.3 mul.11
  24.3 3.6 fusion
  27.9 8.0 %collective-permute-done.15 = f32[128,256]{1,0:T(8,128)S(1)} collective-permute-done((f32[128,256]{1,0:T(8,128)S(1)}, f32[128,256]{1,0:T(8,128)S(1)}, u32[]{:S(2)}, u32[]{:S(2)}) %collective-permute-start.15) | collective-permute-done | bytes 131104 | tf_op jit(solution)/shard_map/ppermute | solution.py:10
  35.9 3.4 collective-permute-start
  39.3 0.8 collective-permute-done.10
  40.1 2.8 collective-permute-done.6
  42.9 2.8 collective-permute-done.3
  45.8 2.8 collective-permute-done.1
  48.6 0.1 fusion.9
  48.7 5.5 collective-permute-start.2
  54.2 0.5 collective-permute-start.16
  54.7 5.4 collective-permute-start.11
  60.1 0.5 collective-permute-start.7
  60.6 5.4 collective-permute-start.4
  66.0 0.2 collective-permute-done.16
  66.3 1.6 collective-permute-start.17
  67.8 2.8 collective-permute-done.11
  70.6 1.5 collective-permute-start.12
  72.1 1.4 collective-permute-done.7
  73.6 1.5 collective-permute-start.8
  75.1 2.2 collective-permute-done.4
  77.3 1.4 collective-permute-start.5
  78.8 3.0 collective-permute-start.18
  81.8 0.7 collective-permute-start.13
  82.5 3.0 collective-permute-start.9
  85.5 3.3 collective-permute-done.18
  88.8 1.5 collective-permute-start.19
  90.4 1.0 collective-permute-done.13
  91.4 1.5 collective-permute-start.14
  92.9 1.0 collective-permute-done.19
  93.9 3.3 collective-permute-start.20
  97.3 3.3 collective-permute-done.20
  100.7 3.6 fusion.2
  104.3 0.0 all-gather.2.cloned.1.call-update
  104.3 0.3 reduce-scatter.2.cloned.1.call-start
  104.6 56.6 %all-gather.2.cloned.1.call-done = f32[1024,1024]{1,0:T(8,128)} async-done(((f32[1024,256]{1,0:T(8,128)}), f32[1024,1024]{1,0:T(8,128)}) %all-gather.2.cloned.1.call-update) | async-done | bytes 4194320 | tf_op jit(solution)/shard_map/all_gather | solution.py:39
  161.2 10.2 %fusion.10 = f32[1024,256]{1,0:T(8,128)} fusion(f32[1024,1024]{1,0:T(8,128)} %all-gather.2.cloned.1.call-done, f32[1024,256]{1,0:T(8,128)} %fusion.2), kind=kOutput, calls=%fused_computation.26 | convolution fusion | flops 3221225472 | bytes 6291456 | tf_op jit(solution)/shard_map/dot_general | solution.py:42
  171.4 0.0 reduce-scatter.2.cloned.1.call-update
  171.4 384.5 %reduce-scatter.2.cloned.1.call-done = f32[16,256]{1,0:T(8,128)} async-done(((f32[1024,256]{1,0:T(8,128)}), f32[16,256]{1,0:T(8,128)}) %reduce-scatter.2.cloned.1.call-update) | async-done | bytes 16400 | tf_op jit(solution)/shard_map/reduce_scatter | solution.py:41
  556.0 1.3 broadcast_multiply_fusion
  (33 shorter events, 0.3 us)
Async XLA Ops:
  7.2 93.5 %copy-start = (f32[6,1024,128]{2,1,0:T(8,128)S(1)}, f32[6,1024,128]{2,1,0:T(8,128)}, u32[]{:S(2)}) copy-start(f32[6,1024,128]{2,1,0:T(8,128)} %param.7) | copy-start | bytes 9437188
  7.2 16.8 %copy-start.3 = (s32[1,8,8]{2,1,0:T(8,128)S(1)}, s32[1,8,8]{2,1,0:T(8,128)}, u32[]{:S(2)}) copy-start(s32[1,8,8]{2,1,0:T(8,128)} %param.6) | copy-start | bytes 772
  7.2 154.1 %all-gather.2.cloned.1.call-start = ((), (), s32[]{:S(2)}) async-start(), calls=%async_computation.1 | async-start | bytes 5242880 | tf_op jit(solution)/shard_map/all_gather | solution.py:39
  7.2 17.0 %copy-start.1 = (f32[1024,256]{1,0:T(8,128)S(1)}, f32[1024,256]{1,0:T(8,128)}, u32[]{:S(2)}) copy-start(f32[1024,256]{1,0:T(8,128)} %param.9) | copy-start | bytes 3145732
  7.2 17.0 %copy-start.2 = (f32[1024,1024]{1,0:T(8,128)S(1)}, f32[1024,1024]{1,0:T(8,128)}, u32[]{:S(2)}) copy-start(f32[1024,1024]{1,0:T(8,128)} %param.5) | copy-start | bytes 12582916
  14.7 21.2 %collective-permute-start.15 = (f32[128,256]{1,0:T(8,128)S(1)}, f32[128,256]{1,0:T(8,128)S(1)}, u32[]{:S(2)}, u32[]{:S(2)}) collective-permute-start(f32[128,256]{1,0:T(8,128)S(1)} %get-tuple-element.7), channel_id=1, source_target_pairs={{0,4},{4,0},{8,12},{12,8},{16,20},{20,16},{24,28},{28,24},{32,36},... | collective-permute-start | bytes 393224 | tf_op jit(solution)/shard_map/ppermute | solution.py:10
  18.1 22.1 %collective-permute-start.10 = (f32[128,256]{1,0:T(8,128)S(1)}, f32[128,256]{1,0:T(8,128)S(1)}, u32[]{:S(2)}, u32[]{:S(2)}) collective-permute-start(f32[128,256]{1,0:T(8,128)S(1)} %get-tuple-element.8), channel_id=1, source_target_pairs={{0,4},{4,0},{8,12},{12,8},{16,20},{20,16},{24,28},{28,24},{32,36},... | collective-permute-start | bytes 393224 | tf_op jit(solution)/shard_map/ppermute | solution.py:10
  18.2 24.8 %collective-permute-start.6 = (f32[128,256]{1,0:T(8,128)S(1)}, f32[128,256]{1,0:T(8,128)S(1)}, u32[]{:S(2)}, u32[]{:S(2)}) collective-permute-start(f32[128,256]{1,0:T(8,128)S(1)} %get-tuple-element.9), channel_id=1, source_target_pairs={{0,4},{4,0},{8,12},{12,8},{16,20},{20,16},{24,28},{28,24},{32,36},... | collective-permute-start | bytes 393224 | tf_op jit(solution)/shard_map/ppermute | solution.py:10
  21.0 24.8 %collective-permute-start.3 = (f32[128,256]{1,0:T(8,128)S(1)}, f32[128,256]{1,0:T(8,128)S(1)}, u32[]{:S(2)}, u32[]{:S(2)}) collective-permute-start(f32[128,256]{1,0:T(8,128)S(1)} %get-tuple-element.10), channel_id=1, source_target_pairs={{0,4},{4,0},{8,12},{12,8},{16,20},{20,16},{24,28},{28,24},{32,36},... | collective-permute-start | bytes 393224 | tf_op jit(solution)/shard_map/ppermute | solution.py:10
  21.1 27.5 %collective-permute-start.1 = (f32[128,256]{1,0:T(8,128)S(1)}, f32[128,256]{1,0:T(8,128)S(1)}, u32[]{:S(2)}, u32[]{:S(2)}) collective-permute-start(f32[128,256]{1,0:T(8,128)S(1)} %get-tuple-element.11), channel_id=1, source_target_pairs={{0,4},{4,0},{8,12},{12,8},{16,20},{20,16},{24,28},{28,24},{32,36},... | collective-permute-start | bytes 393224 | tf_op jit(solution)/shard_map/ppermute | solution.py:10
  35.9 24.7 %collective-permute-start = (f32[128,256]{1,0:T(8,128)S(1)}, f32[128,256]{1,0:T(8,128)S(1)}, u32[]{:S(2)}, u32[]{:S(2)}) collective-permute-start(f32[128,256]{1,0:T(8,128)S(1)} %get-tuple-element.12), channel_id=1, source_target_pairs={{0,4},{4,0},{8,12},{12,8},{16,20},{20,16},{24,28},{28,24},{32,36},... | collective-permute-start | bytes 393224 | tf_op jit(solution)/shard_map/ppermute | solution.py:10
  48.7 30.1 %collective-permute-start.2 = (f32[128,256]{1,0:T(8,128)S(1)}, f32[128,256]{1,0:T(8,128)S(1)}, u32[]{:S(2)}, u32[]{:S(2)}) collective-permute-start(f32[128,256]{1,0:T(8,128)S(1)} %get-tuple-element.6), channel_id=1, source_target_pairs={{0,8},{4,12},{8,0},{12,4},{16,24},{20,28},{24,16},{28,20},{32,40},... | collective-permute-start | bytes 393224 | tf_op jit(solution)/shard_map/ppermute | solution.py:10
  54.2 12.1 %collective-permute-start.16 = (f32[128,256]{1,0:T(8,128)S(1)}, f32[128,256]{1,0:T(8,128)S(1)}, u32[]{:S(2)}, u32[]{:S(2)}) collective-permute-start(f32[128,256]{1,0:T(8,128)S(1)} %get-tuple-element.2), channel_id=1, source_target_pairs={{0,8},{4,12},{8,0},{12,4},{16,24},{20,28},{24,16},{28,20},{32,40},... | collective-permute-start | bytes 393224 | tf_op jit(solution)/shard_map/ppermute | solution.py:10
  54.7 16.0 %collective-permute-start.11 = (f32[128,256]{1,0:T(8,128)S(1)}, f32[128,256]{1,0:T(8,128)S(1)}, u32[]{:S(2)}, u32[]{:S(2)}) collective-permute-start(f32[128,256]{1,0:T(8,128)S(1)} %get-tuple-element.3), channel_id=1, source_target_pairs={{0,8},{4,12},{8,0},{12,4},{16,24},{20,28},{24,16},{28,20},{32,40},... | collective-permute-start | bytes 393224 | tf_op jit(solution)/shard_map/ppermute | solution.py:10
  60.1 13.5 %collective-permute-start.7 = (f32[128,256]{1,0:T(8,128)S(1)}, f32[128,256]{1,0:T(8,128)S(1)}, u32[]{:S(2)}, u32[]{:S(2)}) collective-permute-start(f32[128,256]{1,0:T(8,128)S(1)} %get-tuple-element.4), channel_id=1, source_target_pairs={{0,8},{4,12},{8,0},{12,4},{16,24},{20,28},{24,16},{28,20},{32,40},... | collective-permute-start | bytes 393224 | tf_op jit(solution)/shard_map/ppermute | solution.py:10
  60.6 16.7 %collective-permute-start.4 = (f32[128,256]{1,0:T(8,128)S(1)}, f32[128,256]{1,0:T(8,128)S(1)}, u32[]{:S(2)}, u32[]{:S(2)}) collective-permute-start(f32[128,256]{1,0:T(8,128)S(1)} %get-tuple-element.5), channel_id=1, source_target_pairs={{0,8},{4,12},{8,0},{12,4},{16,24},{20,28},{24,16},{28,20},{32,40},... | collective-permute-start | bytes 393224 | tf_op jit(solution)/shard_map/ppermute | solution.py:10
  66.3 12.5 %collective-permute-start.17 = (f32[128,256]{1,0:T(8,128)S(1)}, f32[128,256]{1,0:T(8,128)S(1)}, u32[]{:S(2)}, u32[]{:S(2)}) collective-permute-start(f32[128,256]{1,0:T(8,128)S(1)} %add.61), channel_id=1, source_target_pairs={{0,16},{4,20},{8,24},{12,28},{16,0},{20,4},{24,8},{28,12},{32,48},... | collective-permute-start | bytes 393224 | tf_op jit(solution)/shard_map/ppermute | solution.py:10
  70.6 11.1 %collective-permute-start.12 = (f32[128,256]{1,0:T(8,128)S(1)}, f32[128,256]{1,0:T(8,128)S(1)}, u32[]{:S(2)}, u32[]{:S(2)}) collective-permute-start(f32[128,256]{1,0:T(8,128)S(1)} %add.57), channel_id=1, source_target_pairs={{0,16},{4,20},{8,24},{12,28},{16,0},{20,4},{24,8},{28,12},{32,48},... | collective-permute-start | bytes 393224 | tf_op jit(solution)/shard_map/ppermute | solution.py:10
  73.6 8.9 %collective-permute-start.8 = (f32[128,256]{1,0:T(8,128)S(1)}, f32[128,256]{1,0:T(8,128)S(1)}, u32[]{:S(2)}, u32[]{:S(2)}) collective-permute-start(f32[128,256]{1,0:T(8,128)S(1)} %add.54), channel_id=1, source_target_pairs={{0,16},{4,20},{8,24},{12,28},{16,0},{20,4},{24,8},{28,12},{32,48},... | collective-permute-start | bytes 393224 | tf_op jit(solution)/shard_map/ppermute | solution.py:10
  77.3 8.2 %collective-permute-start.5 = (f32[128,256]{1,0:T(8,128)S(1)}, f32[128,256]{1,0:T(8,128)S(1)}, u32[]{:S(2)}, u32[]{:S(2)}) collective-permute-start(f32[128,256]{1,0:T(8,128)S(1)} %add.52), channel_id=1, source_target_pairs={{0,16},{4,20},{8,24},{12,28},{16,0},{20,4},{24,8},{28,12},{32,48},... | collective-permute-start | bytes 393224 | tf_op jit(solution)/shard_map/ppermute | solution.py:10
  78.8 10.0 %collective-permute-start.18 = (f32[128,256]{1,0:T(8,128)S(1)}, f32[128,256]{1,0:T(8,128)S(1)}, u32[]{:S(2)}, u32[]{:S(2)}) collective-permute-start(f32[128,256]{1,0:T(8,128)S(1)} %add.62), channel_id=1, source_target_pairs={{0,32},{4,36},{8,40},{12,44},{16,48},{20,52},{24,56},{28,60},{32,0... | collective-permute-start | bytes 393224 | tf_op jit(solution)/shard_map/ppermute | solution.py:10
  81.8 9.6 %collective-permute-start.13 = (f32[128,256]{1,0:T(8,128)S(1)}, f32[128,256]{1,0:T(8,128)S(1)}, u32[]{:S(2)}, u32[]{:S(2)}) collective-permute-start(f32[128,256]{1,0:T(8,128)S(1)} %add.58), channel_id=1, source_target_pairs={{0,32},{4,36},{8,40},{12,44},{16,48},{20,52},{24,56},{28,60},{32,0... | collective-permute-start | bytes 393224 | tf_op jit(solution)/shard_map/ppermute | solution.py:10
  82.5 10.4 %collective-permute-start.9 = (f32[128,256]{1,0:T(8,128)S(1)}, f32[128,256]{1,0:T(8,128)S(1)}, u32[]{:S(2)}, u32[]{:S(2)}) collective-permute-start(f32[128,256]{1,0:T(8,128)S(1)} %add.55), channel_id=1, source_target_pairs={{0,32},{4,36},{8,40},{12,44},{16,48},{20,52},{24,56},{28,60},{32,0... | collective-permute-start | bytes 393224 | tf_op jit(solution)/shard_map/ppermute | solution.py:10
  88.8 5.1 collective-permute-start.19
  91.4 5.9 %collective-permute-start.14 = (f32[128,256]{1,0:T(8,128)S(1)}, f32[128,256]{1,0:T(8,128)S(1)}, u32[]{:S(2)}, u32[]{:S(2)}) collective-permute-start(f32[128,256]{1,0:T(8,128)S(1)} %add.59), channel_id=1, source_target_pairs={{0,64},{4,68},{8,72},{12,76},{16,80},{20,84},{24,88},{28,92},{32,9... | collective-permute-start | bytes 393224 | tf_op jit(solution)/shard_map/ppermute | solution.py:10
  93.9 6.7 %collective-permute-start.20 = (f32[128,256]{1,0:T(8,128)S(1)}, f32[128,256]{1,0:T(8,128)S(1)}, u32[]{:S(2)}, u32[]{:S(2)}) collective-permute-start(f32[128,256]{1,0:T(8,128)S(1)} %add.64), channel_id=1, source_target_pairs={{0,128},{4,132},{8,136},{12,140},{16,144},{20,148},{24,152},{28,15... | collective-permute-start | bytes 393224 | tf_op jit(solution)/shard_map/ppermute | solution.py:10
  104.3 451.6 %reduce-scatter.2.cloned.1.call-start = ((), (), s32[]{:S(2)}) async-start(), calls=%async_computation.2 | async-start | bytes 1064960 | tf_op jit(solution)/shard_map/reduce_scatter | solution.py:41
Sparse Core Ops, SparseCore 0:
  104.4 56.7 all-gather.1
  171.5 384.3 reduce-scatter.1
where the time goes:
time: 564 us
  waiting for transfers between devices  474 us (84%)
  starting transfers between devices  49.3 us (9%)
  matrix products  24.8 us (4%)
  between operations  14.2 us (3%)
    reduce_scatter x1, waiting for transfers between devices, local(): lax.psum_scatter(jnp.dot(gathered.T, applied, precision=lax.Precision.HIG...  385 us
    all_gather x1, waiting for transfers between devices, local(): gathered = lax.all_gather(applied, 'probe', axis=1, tiled=True)  56.6 us
    ppermute x21, starting transfers between devices, partner(): return lax.ppermute(value, axis, pairs)  49 us
    ppermute x21, waiting for transfers between devices, partner(): return lax.ppermute(value, axis, pairs)  32.6 us
  transfers between devices with their start and end apart: 23, of which 15 were waited for; matrix products, arithmetic and copies ran while one was open for 1% of the time, Pallas kernels for 0%

commit v1 on v0

v1 whole, which is shorter than its diff:
```python
import jax
import jax.numpy as jnp
from jax import lax
from jax.sharding import PartitionSpec as P

HIGH = lax.Precision.HIGH


def swap(value, axis, mask):
    pairs = [(source, source ^ mask) for source in range(lax.axis_size(axis))]
    return lax.ppermute(value, axis, pairs)


def halves(value, axis, bit):
    size = value.shape[axis] // 2
    keep = lax.dynamic_slice_in_dim(value, bit * size, size, axis)
    give = lax.dynamic_slice_in_dim(value, (1 - bit) * size, size, axis)
    return keep, give


def join(own, other, axis, bit):
    first = jnp.where(bit == 0, own, other)
    second = jnp.where(bit == 0, other, own)
    return jnp.concatenate([first, second], axis)


def project(columns, probes):
    return jnp.einsum("tec,eg->tcg", columns, probes, precision=HIGH)


def expand(rows, nodes):
    return jnp.einsum("tvi,tic->vc", rows, nodes, precision=HIGH)


def local(leaf_blocks, block_mask, row_factor_stack, column_factor_stack, probes):
    leaf_points = leaf_blocks.shape[1]
    side = block_mask.shape[1]
    span = leaf_points // side
    leaf = lax.axis_index("leaf")
    probe = lax.axis_index("probe")
    bit = [(leaf >> k) & 1 for k in range(6)]

    high = project(column_factor_stack[3:6], probes)
    keep, give = halves(high, 1, bit[2])
    high = keep + swap(give, "leaf", 4)
    keep, give = halves(high[1:], 1, bit[3])
    sent = jnp.concatenate([high[0], give.reshape(64, -1)])
    got = swap(sent, "leaf", 8)
    three = got[:64]
    upper = keep.reshape(64, -1) + got[64:]
    got = swap(upper, "leaf", 16)
    four = got[:32]
    five = upper[32:] + got[32:]
    five = swap(five, "leaf", 32)
    part = jnp.concatenate([three, four, five])
    low = project(column_factor_stack[:3], probes)
    got = swap(jnp.stack([low[0], low[2]]), "leaf", 1)
    zero = got[0]
    two = low[2] + got[1]
    two = two + swap(two, "leaf", 2)
    two = swap(two, "leaf", 4)
    part = part + swap(part, "leaf", 1)
    part = part + swap(part, "leaf", 2)
    upper = part[64:].reshape(2, 32, -1)
    upper = join(upper, swap(upper, "leaf", 8), 1, bit[3])
    high = jnp.concatenate([part[None, :64], upper])
    high = join(high, swap(high, "leaf", 4), 1, bit[2])
    one = low[1] + swap(low[1], "leaf", 1)
    one = swap(one, "leaf", 2)

    weights = block_mask[0].astype(jnp.float32)
    masked = (
        leaf_blocks.reshape(side, span, side, span) * weights[:, None, :, None]
    ).reshape(leaf_points, leaf_points)
    near = jnp.dot(masked, probes, precision=HIGH, preferred_element_type=jnp.float32)
    nodes = jnp.concatenate([jnp.stack([zero, one, two]), high])
    applied = near + expand(row_factor_stack, nodes)

    def gram(other):
        return lax.dot_general(
            other, applied, (((0,), (0,)), ((), ())), precision=HIGH,
            preferred_element_type=jnp.float32,
        )

    def scatter_x(block):
        keep, give = halves(block, 0, bit[3])
        block = keep + swap(give, "leaf", 8)
        keep, give = halves(block, 0, bit[2])
        return keep + swap(give, "leaf", 4)

    beside = swap(applied, "probe", 1)
    width = applied.shape[1] // 2
    far = [swap(applied[:, h * width:(h + 1) * width], "probe", 2) for h in range(2)]
    blocks = scatter_x(gram(applied)), scatter_x(gram(beside))
    across = [swap(half, "probe", 1) for half in far]
    far = jnp.concatenate(far, 1)
    across = jnp.concatenate(across, 1)
    blocks += scatter_x(gram(far)), scatter_x(gram(across))
    total = jnp.stack(blocks).reshape(2, 2, 64, -1)
    keep, give = halves(total, 0, bit[5] ^ (probe >> 1))
    total = (keep + swap(give, "leaf", 32))[0]
    keep, give = halves(total, 0, bit[4] ^ (probe & 1))
    total = (keep + swap(give, "leaf", 16))[0]
    keep, give = halves(total, 0, bit[1])
    total = keep + swap(give, "leaf", 2)
    keep, give = halves(total, 0, bit[0])
    total = keep + swap(give, "leaf", 1)
    total_points = leaf_points * lax.axis_size("leaf")
    return applied, total / total_points


def solution(mesh):
    return jax.shard_map(
        local,
        mesh=mesh,
        in_specs=(
            P("leaf", None),
            P("leaf", None, None),
            P(None, "leaf", None),
            P(None, "leaf", None),
            P("leaf", "probe"),
        ),
        out_specs=(P("leaf", "probe"), P("leaf", "probe")),
        check_vma=False,
    )
```

time: 564 us -> 169 us (0.30)
  waiting for transfers between devices: 474 us -> 60.6 us
  between operations: 14.2 us -> 1.04 us
  other arithmetic: 1.59 us -> 13.7 us
  local copies, waits for them, and re-layouts: 0.5 us -> 11.6 us
  starting transfers between devices: 49.3 us -> 59.2 us
    reduce_scatter x1 -> x0, waiting for transfers between devices: 385 us -> none  [local(): lax.psum_scatter(jnp.dot(gathered.T, applied, precision=lax.Precision.HIG...]
    all_gather x1 -> x0, waiting for transfers between devices: 56.6 us -> none  [local(): gathered = lax.all_gather(applied, 'probe', axis=1, tiled=True)]
    ppermute x21 -> x30, waiting for transfers between devices: 32.6 us -> 60.6 us  [swap(): return lax.ppermute(value, axis, pairs)]
    ppermute x21 -> x30, starting transfers between devices: 49 us -> 59.2 us  [swap(): return lax.ppermute(value, axis, pairs)]
    dot_general x4 -> x8, matrix products: 24.8 us -> 19.6 us  [the longest x4 6.8 us: gram(): lax.dot_general(other, applied, (((0,), (0,)), ((), ())), precision=HIGH,...]
  transfers between devices with their start and end apart: 23 -> 30, of which waited for: 15 -> 21; matrix products, arithmetic and copies ran while one was open for 1% -> 19% of each run, Pallas kernels for 0% -> 0%
where the time goes in v1:
time: 169 us; the launch traced here: 166 us
  waiting for transfers between devices  60.6 us (36%)
  starting transfers between devices  59.2 us (35%)
  matrix products  19.6 us (12%)
  other arithmetic  13.7 us (8%)
  local copies, waits for them, and re-layouts  11.6 us (7%)
    ppermute x30, waiting for transfers between devices, swap(): return lax.ppermute(value, axis, pairs)  60.6 us
    ppermute x30, starting transfers between devices, swap(): return lax.ppermute(value, axis, pairs)  59.2 us
    dot_general x4, matrix products, gram(): lax.dot_general(other, applied, (((0,), (0,)), ((), ())), precision=HIGH,...  6.8 us
    dot_general x2, matrix products, project(): return jnp.einsum('tec,eg->tcg', columns, probes, precision=HIGH)  6.4 us
  transfers between devices with their start and end apart: 30, of which 21 were waited for; matrix products, arithmetic and copies ran while one was open for 19% of the time, Pallas kernels for 0%

profile of v1, /device:TPU:32, one launch (start us, length us, event | category | flops | bytes accessed | tf_op | source)
XLA Modules:
  0.0 165.7 jit_solution(8638336733737655293)
XLA Ops:
  0.7 3.3 %fusion.11 = f32[3,128,256]{2,1,0:T(8,128)S(1)} fusion(f32[6,1024,128]{2,1,0:T(8,128)} %param.8, f32[1024,256]{1,0:T(8,128)} %param.9), kind=kOutput, calls=%fused_computation.13 | convolution fusion | flops 603979776 | bytes 4587520 | tf_op jit(solution)/shard_map/tec,eg->tcg/dot_general | solution.py:28
  4.7 1.5 collective-permute-start.5
  6.2 3.1 %fusion.13 = f32[3,128,256]{2,1,0:T(8,128)S(1)} fusion(f32[6,1024,128]{2,1,0:T(8,128)} %param.8, f32[1024,256]{1,0:T(8,128)} %param.9), kind=kOutput, calls=%fused_computation.15 | convolution fusion | flops 603979776 | bytes 4587520 | tf_op jit(solution)/shard_map/tec,eg->tcg/dot_general | solution.py:28
  9.3 2.3 %collective-permute-done.5 = f32[3,64,256]{2,1,0:T(8,128)} collective-permute-done((f32[3,64,256]{2,1,0:T(8,128)}, f32[3,64,256]{2,1,0:T(8,128)}, u32[]{:S(2)}, u32[]{:S(2)}) %collective-permute-start.5) | collective-permute-done | bytes 196640 | tf_op jit(solution)/shard_map/ppermute | solution.py:11
  12.7 3.1 %collective-permute-start.6 = (f32[128,256]{1,0:T(8,128)S(1)}, f32[128,256]{1,0:T(8,128)S(1)}, u32[]{:S(2)}, u32[]{:S(2)}) collective-permute-start(f32[128,256]{1,0:T(8,128)S(1)} %pad_maximum_fusion.2), channel_id=1, source_target_pairs={{0,32},{4,36},{8,40},{12,44},{16,48},{20,52},{24,56},{28,60},{32,0... | collective-permute-start | bytes 393224 | tf_op jit(solution)/shard_map/ppermute | solution.py:11
  15.8 3.4 %collective-permute-done.6 = f32[128,256]{1,0:T(8,128)S(1)} collective-permute-done((f32[128,256]{1,0:T(8,128)S(1)}, f32[128,256]{1,0:T(8,128)S(1)}, u32[]{:S(2)}, u32[]{:S(2)}) %collective-permute-start.6) | collective-permute-done | bytes 131104 | tf_op jit(solution)/shard_map/ppermute | solution.py:11
  19.9 1.6 collective-permute-start.7
  22.2 3.3 %collective-permute-start = (f32[2,128,256]{2,1,0:T(8,128)}, f32[2,128,256]{2,1,0:T(8,128)}, u32[]{:S(2)}, u32[]{:S(2)}) collective-permute-start(f32[2,128,256]{2,1,0:T(8,128)} %pad_maximum_fusion), channel_id=1, source_target_pairs={{0,4},{4,0},{8,12},{12,8},{16,20},{20,16},{24,28},{28,24},{32,36},... | collective-permute-start | bytes 786440 | tf_op jit(solution)/shard_map/ppermute | solution.py:11
  26.1 2.9 %collective-permute-start.8 = (f32[32,256]{1,0:T(8,128)}, f32[32,256]{1,0:T(8,128)}, u32[]{:S(2)}, u32[]{:S(2)}) collective-permute-start(f32[32,256]{1,0:T(8,128)} %get-tuple-element.20), channel_id=1, source_target_pairs={{0,128},{4,132},{8,136},{12,140},{16,144},{20,148},{24,152},{28,15... | collective-permute-start | bytes 98312 | tf_op jit(solution)/shard_map/ppermute | solution.py:11
  29.0 2.8 %collective-permute-done.8 = f32[32,256]{1,0:T(8,128)} collective-permute-done((f32[32,256]{1,0:T(8,128)}, f32[32,256]{1,0:T(8,128)}, u32[]{:S(2)}, u32[]{:S(2)}) %collective-permute-start.8) | collective-permute-done | bytes 32800 | tf_op jit(solution)/shard_map/ppermute | solution.py:11
  32.7 2.1 %collective-permute-start.9 = (f32[128,256]{1,0:T(8,128)S(1)}, f32[128,256]{1,0:T(8,128)S(1)}, u32[]{:S(2)}, u32[]{:S(2)}) collective-permute-start(f32[128,256]{1,0:T(8,128)S(1)} %pad_maximum_fusion.3), channel_id=1, source_target_pairs={{0,4},{4,0},{8,12},{12,8},{16,20},{20,16},{24,28},{28,24},{32,36},... | collective-permute-start | bytes 393224 | tf_op jit(solution)/shard_map/ppermute | solution.py:11
  34.7 3.0 %collective-permute-done = f32[2,128,256]{2,1,0:T(8,128)} collective-permute-done((f32[2,128,256]{2,1,0:T(8,128)}, f32[2,128,256]{2,1,0:T(8,128)}, u32[]{:S(2)}, u32[]{:S(2)}) %collective-permute-start) | collective-permute-done | bytes 262176 | tf_op jit(solution)/shard_map/ppermute | solution.py:11
  37.8 1.7 %slice_bitcast_fusion = (f32[128,256]{1,0:T(8,128)}, f32[128,256]{1,0:T(8,128)S(1)}, f32[1,128,256]{2,1,0:T(8,128)}) fusion(f32[3,128,256]{2,1,0:T(8,128)S(1)} %fusion.13, f32[2,128,256]{2,1,0:T(8,128)} %collective-permute-done), kind=kLoop, calls=%fused_computation.34 | loop fusion | flops 32768 | bytes 917504 | tf_op jit(solution)/shard_map/squeeze | solution.py:68
  39.5 3.3 %collective-permute-start.3 = (f32[128,256]{1,0:T(8,128)S(1)}, f32[128,256]{1,0:T(8,128)S(1)}, u32[]{:S(2)}, u32[]{:S(2)}) collective-permute-start(f32[128,256]{1,0:T(8,128)S(1)} %get-tuple-element.9), channel_id=1, source_target_pairs={{0,8},{4,12},{8,0},{12,4},{16,24},{20,28},{24,16},{28,20},{32,40},... | collective-permute-start | bytes 393224 | tf_op jit(solution)/shard_map/ppermute | solution.py:11
  43.7 3.4 %collective-permute-start.10 = (f32[128,256]{1,0:T(8,128)S(1)}, f32[128,256]{1,0:T(8,128)S(1)}, u32[]{:S(2)}, u32[]{:S(2)}) collective-permute-start(f32[128,256]{1,0:T(8,128)S(1)} %fusion.29), channel_id=1, source_target_pairs={{0,8},{4,12},{8,0},{12,4},{16,24},{20,28},{24,16},{28,20},{32,40},... | collective-permute-start | bytes 393224 | tf_op jit(solution)/shard_map/ppermute | solution.py:11
  47.1 3.4 %collective-permute-start.1 = (f32[128,256]{1,0:T(8,128)}, f32[128,256]{1,0:T(8,128)}, u32[]{:S(2)}, u32[]{:S(2)}) collective-permute-start(f32[128,256]{1,0:T(8,128)} %get-tuple-element.8), channel_id=1, source_target_pairs={{0,4},{4,0},{8,12},{12,8},{16,20},{20,16},{24,28},{28,24},{32,36},... | collective-permute-start | bytes 393224 | tf_op jit(solution)/shard_map/ppermute | solution.py:11
  51.2 1.5 collective-permute-start.4
  52.7 1.5 collective-permute-done.10
  54.8 1.7 %copy.10 = f32[2,32,256]{1,2,0:T(8,128)} copy(f32[2,32,256]{2,1,0:T(8,128)} %bitcast.64) | data formatting | bytes 131072 | tf_op jit(solution)/shard_map/reshape | solution.py:64
  56.5 3.0 %collective-permute-start.11 = (f32[2,32,256]{1,2,0:T(8,128)}, f32[2,32,256]{1,2,0:T(8,128)}, u32[]{:S(2)}, u32[]{:S(2)}) collective-permute-start(f32[2,32,256]{1,2,0:T(8,128)} %copy.10), channel_id=1, source_target_pairs={{0,32},{4,36},{8,40},{12,44},{16,48},{20,52},{24,56},{28,60},{32,0... | collective-permute-start | bytes 196616 | tf_op jit(solution)/shard_map/ppermute | solution.py:11
  60.4 1.6 fusion.28
  61.9 2.3 %collective-permute-start.2 = (f32[128,256]{1,0:T(8,128)}, f32[128,256]{1,0:T(8,128)}, u32[]{:S(2)}, u32[]{:S(2)}) collective-permute-start(f32[128,256]{1,0:T(8,128)} %fusion.28), channel_id=1, source_target_pairs={{0,8},{4,12},{8,0},{12,4},{16,24},{20,28},{24,16},{28,20},{32,40},... | collective-permute-start | bytes 393224 | tf_op jit(solution)/shard_map/ppermute | solution.py:11
  67.6 1.5 collective-permute-start.12
  69.4 3.4 %fusion = f32[1024,256]{1,0:T(8,128)} fusion(f32[1024,256]{1,0:T(8,128)S(1)} %copy-done.3, f32[1024,1024]{1,0:T(8,128)S(1)} %copy-done.4, f32[128,8,8,128]{3,2,1,0:T(8,128)S(1)} %bitcast.61), kind=kOutput, calls=%fused_computation.1 | convolution fusion | flops 1611661312 | bytes 10485760 | tf_op jit(solution)/shard_map/dot_general | solution.py:75
  72.8 1.7 copy.13
  74.5 1.6 copy.15
  76.1 1.7 %copy.14 = f32[1,128,256]{1,2,0:T(8,128)} copy(f32[1,128,256]{2,1,0:T(8,128)} %bitcast.3) | data formatting | bytes 262144 | tf_op jit(solution)/shard_map/stack | solution.py:76
  79.7 3.0 %fusion.2 = f32[1024,256]{1,0:T(8,128)S(1)} fusion(f32[1024,256]{1,0:T(8,128)} %fusion, f32[6,1024,128]{2,1,0:T(8,128)S(1)} %copy-done, f32[3,64,256]{1,2,0:T(8,128)S(1)} %get-tuple-element.5, f32[3,64,256]{1,2,0:T(8,128)S(1)} %get-tuple-element.4, f32[1,128,256]{1,2,0:T(8,128)} %copy.15, f32[1,128,256]{1,2,0:T(8,128)} %copy.14, f32[1,128,256]{1,2,0:T(8,128)} %copy.13), kind=kOutput, calls=%fused_computation.4 | convolution fusion | flops 1209008128 | bytes 6029312 | tf_op jit(solution)/shard_map/tvi,tic->vc/dot_general | solution.py:32
  84.7 4.0 %collective-permute-start.19 = (f32[1024,128]{1,0:T(8,128)}, f32[1024,128]{1,0:T(8,128)}, u32[]{:S(2)}, u32[]{:S(2)}) collective-permute-start(f32[1024,128]{1,0:T(8,128)} %get-tuple-element.3), channel_id=1, source_target_pairs={{0,2},{1,3},{2,0},{3,1},{4,6},{5,7},{6,4},{7,5},{8,10},{9,11},{10,... | collective-permute-start | bytes 1572872 | tf_op jit(solution)/shard_map/ppermute | solution.py:11
  88.7 2.6 %fusion.34 = f32[256,256]{1,0:T(8,128)S(1)} fusion(f32[1024,256]{1,0:T(8,128)} %copy-done.1), kind=kOutput, calls=%fused_computation.80 | convolution fusion | flops 402653184 | bytes 1310720 | tf_op jit(solution)/shard_map/dot_general | solution.py:80
  91.4 2.7 %collective-permute-start.13 = (f32[128,256]{1,0:T(8,128)S(1)}, f32[128,256]{1,0:T(8,128)S(1)}, u32[]{:S(2)}, u32[]{:S(2)}) collective-permute-start(f32[128,256]{1,0:T(8,128)S(1)} %constant_dynamic-slice_fusion.9), channel_id=1, source_target_pairs={{0,32},{4,36},{8,40},{12,44},{16,48},{20,52},{24,56},{28,60},{32,0... | collective-permute-start | bytes 393224 | tf_op jit(solution)/shard_map/ppermute | solution.py:11
  94.1 7.8 %collective-permute-done.19 = f32[1024,128]{1,0:T(8,128)} collective-permute-done((f32[1024,128]{1,0:T(8,128)}, f32[1024,128]{1,0:T(8,128)}, u32[]{:S(2)}, u32[]{:S(2)}) %collective-permute-start.19) | collective-permute-done | bytes 524320 | tf_op jit(solution)/shard_map/ppermute | solution.py:11
  101.9 8.2 %collective-permute-done.18 = f32[1024,128]{1,0:T(8,128)} collective-permute-done((f32[1024,128]{1,0:T(8,128)}, f32[1024,128]{1,0:T(8,128)}, u32[]{:S(2)}, u32[]{:S(2)}) %collective-permute-start.18) | collective-permute-done | bytes 524320 | tf_op jit(solution)/shard_map/ppermute | solution.py:11
  110.1 2.2 %fusion.3 = f32[256,256]{1,0:T(8,128)S(1)} fusion(f32[1024,256]{1,0:T(8,128)S(1)} %copy-done.2, f32[1024,128]{1,0:T(8,128)} %collective-permute-done.19, f32[1024,128]{1,0:T(8,128)} %collective-permute-done.18), kind=kOutput, calls=%fused_computation.5 | convolution fusion | flops 402915328 | bytes 2359296 | tf_op jit(solution)/shard_map/dot_general | solution.py:80
  112.3 2.8 %collective-permute-start.20 = (f32[128,256]{1,0:T(8,128)S(1)}, f32[128,256]{1,0:T(8,128)S(1)}, u32[]{:S(2)}, u32[]{:S(2)}) collective-permute-start(f32[128,256]{1,0:T(8,128)S(1)} %constant_dynamic-slice_fusion.5), channel_id=1, source_target_pairs={{0,32},{4,36},{8,40},{12,44},{16,48},{20,52},{24,56},{28,60},{32,0... | collective-permute-start | bytes 393224 | tf_op jit(solution)/shard_map/ppermute | solution.py:11
  116.0 2.9 %collective-permute-done.20 = f32[128,256]{1,0:T(8,128)S(1)} collective-permute-done((f32[128,256]{1,0:T(8,128)S(1)}, f32[128,256]{1,0:T(8,128)S(1)}, u32[]{:S(2)}, u32[]{:S(2)}) %collective-permute-start.20) | collective-permute-done | bytes 131104 | tf_op jit(solution)/shard_map/ppermute | solution.py:11
  120.1 3.4 %collective-permute-done.21 = f32[64,256]{1,0:T(8,128)S(1)} collective-permute-done((f32[64,256]{1,0:T(8,128)S(1)}, f32[64,256]{1,0:T(8,128)S(1)}, u32[]{:S(2)}, u32[]{:S(2)}) %collective-permute-start.21) | collective-permute-done | bytes 65568 | tf_op jit(solution)/shard_map/ppermute | solution.py:11
  124.5 2.8 %collective-permute-start.24 = (f32[128,256]{1,0:T(8,128)S(1)}, f32[128,256]{1,0:T(8,128)S(1)}, u32[]{:S(2)}, u32[]{:S(2)}) collective-permute-start(f32[128,256]{1,0:T(8,128)S(1)} %constant_dynamic-slice_fusion.3), channel_id=1, source_target_pairs={{0,32},{4,36},{8,40},{12,44},{16,48},{20,52},{24,56},{28,60},{32,0... | collective-permute-start | bytes 393224 | tf_op jit(solution)/shard_map/ppermute | solution.py:11
  129.3 2.4 %collective-permute-done.24 = f32[128,256]{1,0:T(8,128)S(1)} collective-permute-done((f32[128,256]{1,0:T(8,128)S(1)}, f32[128,256]{1,0:T(8,128)S(1)}, u32[]{:S(2)}, u32[]{:S(2)}) %collective-permute-start.24) | collective-permute-done | bytes 131104 | tf_op jit(solution)/shard_map/ppermute | solution.py:11
  132.5 3.1 %collective-permute-done.16 = f32[128,256]{1,0:T(8,128)S(1)} collective-permute-done((f32[128,256]{1,0:T(8,128)S(1)}, f32[128,256]{1,0:T(8,128)S(1)}, u32[]{:S(2)}, u32[]{:S(2)}) %collective-permute-start.16) | collective-permute-done | bytes 131104 | tf_op jit(solution)/shard_map/ppermute | solution.py:11
  136.1 3.9 %collective-permute-done.17 = f32[64,256]{1,0:T(8,128)S(1)} collective-permute-done((f32[64,256]{1,0:T(8,128)S(1)}, f32[64,256]{1,0:T(8,128)S(1)}, u32[]{:S(2)}, u32[]{:S(2)}) %collective-permute-start.17) | collective-permute-done | bytes 65568 | tf_op jit(solution)/shard_map/ppermute | solution.py:11
  140.0 4.0 %collective-permute-start.26 = (f32[1,2,64,256]{3,2,1,0:T(8,128)S(1)}, f32[1,2,64,256]{3,2,1,0:T(8,128)}, u32[]{:S(2)}, u32[]{:S(2)}) collective-permute-start(f32[1,2,64,256]{3,2,1,0:T(8,128)S(1)} %constant_dynamic-slice_fusion.1), channel_id=1, source_target_pairs={{0,128},{4,132},{8,136},{12,140},{16,144},{20,148},{24,152},{28,15... | collective-permute-start | bytes 393224 | tf_op jit(solution)/shard_map/ppermute | solution.py:11
  144.0 3.1 %collective-permute-done.26 = f32[1,2,64,256]{3,2,1,0:T(8,128)} collective-permute-done((f32[1,2,64,256]{3,2,1,0:T(8,128)S(1)}, f32[1,2,64,256]{3,2,1,0:T(8,128)}, u32[]{:S(2)}, u32[]{:S(2)}) %collective-permute-start.26) | collective-permute-done | bytes 131104 | tf_op jit(solution)/shard_map/ppermute | solution.py:11
  148.3 4.1 %collective-permute-done.27 = f32[1,64,256]{2,1,0:T(8,128)S(1)} collective-permute-done((f32[1,64,256]{2,1,0:T(8,128)S(1)}, f32[1,64,256]{2,1,0:T(8,128)S(1)}, u32[]{:S(2)}, u32[]{:S(2)}) %collective-permute-start.27) | collective-permute-done | bytes 65568 | tf_op jit(solution)/shard_map/ppermute | solution.py:11
  152.4 3.6 %collective-permute-start.28 = (f32[32,256]{1,0:T(8,128)S(1)}, f32[32,256]{1,0:T(8,128)S(1)}, u32[]{:S(2)}, u32[]{:S(2)}) collective-permute-start(f32[32,256]{1,0:T(8,128)S(1)} %dynamic-slice_bitcast_fusion.1), channel_id=1, source_target_pairs={{0,8},{4,12},{8,0},{12,4},{16,24},{20,28},{24,16},{28,20},{32,40},... | collective-permute-start | bytes 98312 | tf_op jit(solution)/shard_map/ppermute | solution.py:11
  156.1 4.3 %collective-permute-done.28 = f32[32,256]{1,0:T(8,128)S(1)} collective-permute-done((f32[32,256]{1,0:T(8,128)S(1)}, f32[32,256]{1,0:T(8,128)S(1)}, u32[]{:S(2)}, u32[]{:S(2)}) %collective-permute-start.28) | collective-permute-done | bytes 32800 | tf_op jit(solution)/shard_map/ppermute | solution.py:11
  160.4 2.5 %collective-permute-start.29 = (f32[16,256]{1,0:T(8,128)S(1)}, f32[16,256]{1,0:T(8,128)S(1)}, u32[]{:S(2)}, u32[]{:S(2)}) collective-permute-start(f32[16,256]{1,0:T(8,128)S(1)} %constant_dynamic-slice_fusion), channel_id=1, source_target_pairs={{0,4},{4,0},{8,12},{12,8},{16,20},{20,16},{24,28},{28,24},{32,36},... | collective-permute-start | bytes 49160 | tf_op jit(solution)/shard_map/ppermute | solution.py:11
  162.9 2.2 %collective-permute-done.29 = f32[16,256]{1,0:T(8,128)S(1)} collective-permute-done((f32[16,256]{1,0:T(8,128)S(1)}, f32[16,256]{1,0:T(8,128)S(1)}, u32[]{:S(2)}, u32[]{:S(2)}) %collective-permute-start.29) | collective-permute-done | bytes 16416 | tf_op jit(solution)/shard_map/ppermute | solution.py:11
  (91 shorter events, 23.5 us)
Async XLA Ops:
  0.6 79.0 %copy-start = (f32[6,1024,128]{2,1,0:T(8,128)S(1)}, f32[6,1024,128]{2,1,0:T(8,128)}, u32[]{:S(2)}) copy-start(f32[6,1024,128]{2,1,0:T(8,128)} %param.7) | copy-start | bytes 9437188
  3.9 2.3 %copy-start.6 = (f32[3,128,256]{2,1,0:T(8,128)}, f32[3,128,256]{2,1,0:T(8,128)S(1)}, u32[]{:S(2)}) copy-start(f32[3,128,256]{2,1,0:T(8,128)S(1)} %fusion.11) | copy-start | bytes 1179652
  4.7 7.0 %collective-permute-start.5 = (f32[3,64,256]{2,1,0:T(8,128)}, f32[3,64,256]{2,1,0:T(8,128)}, u32[]{:S(2)}, u32[]{:S(2)}) collective-permute-start(f32[3,64,256]{2,1,0:T(8,128)} %constant_dynamic-slice_fusion.12), channel_id=1, source_target_pairs={{0,16},{4,20},{8,24},{12,28},{16,0},{20,4},{24,8},{28,12},{32,48},... | collective-permute-start | bytes 589832 | tf_op jit(solution)/shard_map/ppermute | solution.py:11
  6.2 5.5 %copy-start.7 = (f32[3,128,256]{2,1,0:T(8,128)S(1)}, f32[3,128,256]{2,1,0:T(8,128)}, u32[]{:S(2)}) copy-start(f32[3,128,256]{2,1,0:T(8,128)} %copy-done.6) | copy-start | bytes 1179652
  9.3 37.8 %copy-start.8 = (s32[1,8,8]{2,1,0:T(8,128)S(1)}, s32[1,8,8]{2,1,0:T(8,128)}, u32[]{:S(2)}) copy-start(s32[1,8,8]{2,1,0:T(8,128)} %param.6) | copy-start | bytes 772
  12.7 6.6 %collective-permute-start.6 = (f32[128,256]{1,0:T(8,128)S(1)}, f32[128,256]{1,0:T(8,128)S(1)}, u32[]{:S(2)}, u32[]{:S(2)}) collective-permute-start(f32[128,256]{1,0:T(8,128)S(1)} %pad_maximum_fusion.2), channel_id=1, source_target_pairs={{0,32},{4,36},{8,40},{12,44},{16,48},{20,52},{24,56},{28,60},{32,0... | collective-permute-start | bytes 393224 | tf_op jit(solution)/shard_map/ppermute | solution.py:11
  19.9 5.6 %collective-permute-start.7 = (f32[64,256]{1,0:T(8,128)S(1)}, f32[64,256]{1,0:T(8,128)S(1)}, u32[]{:S(2)}, u32[]{:S(2)}) collective-permute-start(f32[64,256]{1,0:T(8,128)S(1)} %get-tuple-element.16), channel_id=1, source_target_pairs={{0,64},{4,68},{8,72},{12,76},{16,80},{20,84},{24,88},{28,92},{32,9... | collective-permute-start | bytes 196616 | tf_op jit(solution)/shard_map/ppermute | solution.py:11
  22.2 15.6 %collective-permute-start = (f32[2,128,256]{2,1,0:T(8,128)}, f32[2,128,256]{2,1,0:T(8,128)}, u32[]{:S(2)}, u32[]{:S(2)}) collective-permute-start(f32[2,128,256]{2,1,0:T(8,128)} %pad_maximum_fusion), channel_id=1, source_target_pairs={{0,4},{4,0},{8,12},{12,8},{16,20},{20,16},{24,28},{28,24},{32,36},... | collective-permute-start | bytes 786440 | tf_op jit(solution)/shard_map/ppermute | solution.py:11
  26.1 5.7 %collective-permute-start.8 = (f32[32,256]{1,0:T(8,128)}, f32[32,256]{1,0:T(8,128)}, u32[]{:S(2)}, u32[]{:S(2)}) collective-permute-start(f32[32,256]{1,0:T(8,128)} %get-tuple-element.20), channel_id=1, source_target_pairs={{0,128},{4,132},{8,136},{12,140},{16,144},{20,148},{24,152},{28,15... | collective-permute-start | bytes 98312 | tf_op jit(solution)/shard_map/ppermute | solution.py:11
  32.7 10.1 %collective-permute-start.9 = (f32[128,256]{1,0:T(8,128)S(1)}, f32[128,256]{1,0:T(8,128)S(1)}, u32[]{:S(2)}, u32[]{:S(2)}) collective-permute-start(f32[128,256]{1,0:T(8,128)S(1)} %pad_maximum_fusion.3), channel_id=1, source_target_pairs={{0,4},{4,0},{8,12},{12,8},{16,20},{20,16},{24,28},{28,24},{32,36},... | collective-permute-start | bytes 393224 | tf_op jit(solution)/shard_map/ppermute | solution.py:11
  39.5 11.1 %collective-permute-start.3 = (f32[128,256]{1,0:T(8,128)S(1)}, f32[128,256]{1,0:T(8,128)S(1)}, u32[]{:S(2)}, u32[]{:S(2)}) collective-permute-start(f32[128,256]{1,0:T(8,128)S(1)} %get-tuple-element.9), channel_id=1, source_target_pairs={{0,8},{4,12},{8,0},{12,4},{16,24},{20,28},{24,16},{28,20},{32,40},... | collective-permute-start | bytes 393224 | tf_op jit(solution)/shard_map/ppermute | solution.py:11
  43.7 10.5 %collective-permute-start.10 = (f32[128,256]{1,0:T(8,128)S(1)}, f32[128,256]{1,0:T(8,128)S(1)}, u32[]{:S(2)}, u32[]{:S(2)}) collective-permute-start(f32[128,256]{1,0:T(8,128)S(1)} %fusion.29), channel_id=1, source_target_pairs={{0,8},{4,12},{8,0},{12,4},{16,24},{20,28},{24,16},{28,20},{32,40},... | collective-permute-start | bytes 393224 | tf_op jit(solution)/shard_map/ppermute | solution.py:11
  47.1 13.2 %collective-permute-start.1 = (f32[128,256]{1,0:T(8,128)}, f32[128,256]{1,0:T(8,128)}, u32[]{:S(2)}, u32[]{:S(2)}) collective-permute-start(f32[128,256]{1,0:T(8,128)} %get-tuple-element.8), channel_id=1, source_target_pairs={{0,4},{4,0},{8,12},{12,8},{16,20},{20,16},{24,28},{28,24},{32,36},... | collective-permute-start | bytes 393224 | tf_op jit(solution)/shard_map/ppermute | solution.py:11
  51.2 23.3 %collective-permute-start.4 = (f32[128,256]{1,0:T(8,128)}, f32[128,256]{1,0:T(8,128)}, u32[]{:S(2)}, u32[]{:S(2)}) collective-permute-start(f32[128,256]{1,0:T(8,128)} %add.127), channel_id=1, source_target_pairs={{0,16},{4,20},{8,24},{12,28},{16,0},{20,4},{24,8},{28,12},{32,48},... | collective-permute-start | bytes 393224 | tf_op jit(solution)/shard_map/ppermute | solution.py:11
  56.5 9.0 %collective-permute-start.11 = (f32[2,32,256]{1,2,0:T(8,128)}, f32[2,32,256]{1,2,0:T(8,128)}, u32[]{:S(2)}, u32[]{:S(2)}) collective-permute-start(f32[2,32,256]{1,2,0:T(8,128)} %copy.10), channel_id=1, source_target_pairs={{0,32},{4,36},{8,40},{12,44},{16,48},{20,52},{24,56},{28,60},{32,0... | collective-permute-start | bytes 196616 | tf_op jit(solution)/shard_map/ppermute | solution.py:11
  61.9 14.2 %collective-permute-start.2 = (f32[128,256]{1,0:T(8,128)}, f32[128,256]{1,0:T(8,128)}, u32[]{:S(2)}, u32[]{:S(2)}) collective-permute-start(f32[128,256]{1,0:T(8,128)} %fusion.28), channel_id=1, source_target_pairs={{0,8},{4,12},{8,0},{12,4},{16,24},{20,28},{24,16},{28,20},{32,40},... | collective-permute-start | bytes 393224 | tf_op jit(solution)/shard_map/ppermute | solution.py:11
  65.2 4.2 %copy-start.3 = (f32[1024,256]{1,0:T(8,128)S(1)}, f32[1024,256]{1,0:T(8,128)}, u32[]{:S(2)}) copy-start(f32[1024,256]{1,0:T(8,128)} %param.9) | copy-start | bytes 3145732
  65.2 4.2 %copy-start.4 = (f32[1024,1024]{1,0:T(8,128)S(1)}, f32[1024,1024]{1,0:T(8,128)}, u32[]{:S(2)}) copy-start(f32[1024,1024]{1,0:T(8,128)} %param.5) | copy-start | bytes 12582916
  66.7 0.9 copy-start.5
  67.6 10.9 %collective-permute-start.12 = (f32[3,64,256]{1,2,0:T(8,128)}, f32[3,64,256]{1,2,0:T(8,128)}, u32[]{:S(2)}, u32[]{:S(2)}) collective-permute-start(f32[3,64,256]{1,2,0:T(8,128)} %maximum_maximum_fusion), channel_id=1, source_target_pairs={{0,16},{4,20},{8,24},{12,28},{16,0},{20,4},{24,8},{28,12},{32,48},... | collective-permute-start | bytes 589832 | tf_op jit(solution)/shard_map/ppermute | solution.py:11
  82.6 1.0 copy-start.1
  84.7 17.2 %collective-permute-start.19 = (f32[1024,128]{1,0:T(8,128)}, f32[1024,128]{1,0:T(8,128)}, u32[]{:S(2)}, u32[]{:S(2)}) collective-permute-start(f32[1024,128]{1,0:T(8,128)} %get-tuple-element.3), channel_id=1, source_target_pairs={{0,2},{1,3},{2,0},{3,1},{4,6},{5,7},{6,4},{7,5},{8,10},{9,11},{10,... | collective-permute-start | bytes 1572872 | tf_op jit(solution)/shard_map/ppermute | solution.py:11
  88.7 21.4 %collective-permute-start.18 = (f32[1024,128]{1,0:T(8,128)}, f32[1024,128]{1,0:T(8,128)}, u32[]{:S(2)}, u32[]{:S(2)}) collective-permute-start(f32[1024,128]{1,0:T(8,128)} %get-tuple-element.2), channel_id=1, source_target_pairs={{0,2},{1,3},{2,0},{3,1},{4,6},{5,7},{6,4},{7,5},{8,10},{9,11},{10,... | collective-permute-start | bytes 1572872 | tf_op jit(solution)/shard_map/ppermute | solution.py:11
  88.7 21.3 %copy-start.2 = (f32[1024,256]{1,0:T(8,128)S(1)}, f32[1024,256]{1,0:T(8,128)}, u32[]{:S(2)}) copy-start(f32[1024,256]{1,0:T(8,128)} %copy-done.1) | copy-start | bytes 3145732
  88.7 38.6 %collective-permute-start.15 = (f32[1024,256]{1,0:T(8,128)}, f32[1024,256]{1,0:T(8,128)S(1)}, u32[]{:S(2)}, u32[]{:S(2)}) collective-permute-start(f32[1024,256]{1,0:T(8,128)} %copy-done.1), channel_id=1, source_target_pairs={{0,1},{1,0},{2,3},{3,2},{4,5},{5,4},{6,7},{7,6},{8,9},{9,8},{10,11... | collective-permute-start | bytes 3145736 | tf_op jit(solution)/shard_map/ppermute | solution.py:11
  91.4 23.7 %collective-permute-start.13 = (f32[128,256]{1,0:T(8,128)S(1)}, f32[128,256]{1,0:T(8,128)S(1)}, u32[]{:S(2)}, u32[]{:S(2)}) collective-permute-start(f32[128,256]{1,0:T(8,128)S(1)} %constant_dynamic-slice_fusion.9), channel_id=1, source_target_pairs={{0,32},{4,36},{8,40},{12,44},{16,48},{20,52},{24,56},{28,60},{32,0... | collective-permute-start | bytes 393224 | tf_op jit(solution)/shard_map/ppermute | solution.py:11
  112.3 6.6 %collective-permute-start.20 = (f32[128,256]{1,0:T(8,128)S(1)}, f32[128,256]{1,0:T(8,128)S(1)}, u32[]{:S(2)}, u32[]{:S(2)}) collective-permute-start(f32[128,256]{1,0:T(8,128)S(1)} %constant_dynamic-slice_fusion.5), channel_id=1, source_target_pairs={{0,32},{4,36},{8,40},{12,44},{16,48},{20,52},{24,56},{28,60},{32,0... | collective-permute-start | bytes 393224 | tf_op jit(solution)/shard_map/ppermute | solution.py:11
  115.2 4.9 %collective-permute-start.14 = (f32[64,256]{1,0:T(8,128)S(1)}, f32[64,256]{1,0:T(8,128)S(1)}, u32[]{:S(2)}, u32[]{:S(2)}) collective-permute-start(f32[64,256]{1,0:T(8,128)S(1)} %constant_dynamic-slice_fusion.8), channel_id=1, source_target_pairs={{0,16},{4,20},{8,24},{12,28},{16,0},{20,4},{24,8},{28,12},{32,48},... | collective-permute-start | bytes 196616 | tf_op jit(solution)/shard_map/ppermute | solution.py:11
  115.5 8.0 %collective-permute-start.23 = (f32[1024,128]{1,0:T(8,128)}, f32[1024,128]{1,0:T(8,128)S(1)}, u32[]{:S(2)}, u32[]{:S(2)}) collective-permute-start(f32[1024,128]{1,0:T(8,128)} %collective-permute-done.19), channel_id=1, source_target_pairs={{0,1},{1,0},{2,3},{3,2},{4,5},{5,4},{6,7},{7,6},{8,9},{9,8},{10,11... | collective-permute-start | bytes 1572872 | tf_op jit(solution)/shard_map/ppermute | solution.py:11
  115.5 8.0 %collective-permute-start.22 = (f32[1024,128]{1,0:T(8,128)}, f32[1024,128]{1,0:T(8,128)S(1)}, u32[]{:S(2)}, u32[]{:S(2)}) collective-permute-start(f32[1024,128]{1,0:T(8,128)} %collective-permute-done.18), channel_id=1, source_target_pairs={{0,1},{1,0},{2,3},{3,2},{4,5},{5,4},{6,7},{7,6},{8,9},{9,8},{10,11... | collective-permute-start | bytes 1572872 | tf_op jit(solution)/shard_map/ppermute | solution.py:11
  118.9 4.6 %collective-permute-start.21 = (f32[64,256]{1,0:T(8,128)S(1)}, f32[64,256]{1,0:T(8,128)S(1)}, u32[]{:S(2)}, u32[]{:S(2)}) collective-permute-start(f32[64,256]{1,0:T(8,128)S(1)} %constant_dynamic-slice_fusion.4), channel_id=1, source_target_pairs={{0,16},{4,20},{8,24},{12,28},{16,0},{20,4},{24,8},{28,12},{32,48},... | collective-permute-start | bytes 196616 | tf_op jit(solution)/shard_map/ppermute | solution.py:11
  124.5 7.1 %collective-permute-start.24 = (f32[128,256]{1,0:T(8,128)S(1)}, f32[128,256]{1,0:T(8,128)S(1)}, u32[]{:S(2)}, u32[]{:S(2)}) collective-permute-start(f32[128,256]{1,0:T(8,128)S(1)} %constant_dynamic-slice_fusion.3), channel_id=1, source_target_pairs={{0,32},{4,36},{8,40},{12,44},{16,48},{20,52},{24,56},{28,60},{32,0... | collective-permute-start | bytes 393224 | tf_op jit(solution)/shard_map/ppermute | solution.py:11
  128.4 7.2 %collective-permute-start.16 = (f32[128,256]{1,0:T(8,128)S(1)}, f32[128,256]{1,0:T(8,128)S(1)}, u32[]{:S(2)}, u32[]{:S(2)}) collective-permute-start(f32[128,256]{1,0:T(8,128)S(1)} %constant_dynamic-slice_fusion.7), channel_id=1, source_target_pairs={{0,32},{4,36},{8,40},{12,44},{16,48},{20,52},{24,56},{28,60},{32,0... | collective-permute-start | bytes 393224 | tf_op jit(solution)/shard_map/ppermute | solution.py:11
  131.7 4.4 %collective-permute-start.25 = (f32[64,256]{1,0:T(8,128)S(1)}, f32[64,256]{1,0:T(8,128)S(1)}, u32[]{:S(2)}, u32[]{:S(2)}) collective-permute-start(f32[64,256]{1,0:T(8,128)S(1)} %constant_dynamic-slice_fusion.2), channel_id=1, source_target_pairs={{0,16},{4,20},{8,24},{12,28},{16,0},{20,4},{24,8},{28,12},{32,48},... | collective-permute-start | bytes 196616 | tf_op jit(solution)/shard_map/ppermute | solution.py:11
  135.6 4.4 %collective-permute-start.17 = (f32[64,256]{1,0:T(8,128)S(1)}, f32[64,256]{1,0:T(8,128)S(1)}, u32[]{:S(2)}, u32[]{:S(2)}) collective-permute-start(f32[64,256]{1,0:T(8,128)S(1)} %constant_dynamic-slice_fusion.6), channel_id=1, source_target_pairs={{0,16},{4,20},{8,24},{12,28},{16,0},{20,4},{24,8},{28,12},{32,48},... | collective-permute-start | bytes 196616 | tf_op jit(solution)/shard_map/ppermute | solution.py:11
  140.0 7.1 %collective-permute-start.26 = (f32[1,2,64,256]{3,2,1,0:T(8,128)S(1)}, f32[1,2,64,256]{3,2,1,0:T(8,128)}, u32[]{:S(2)}, u32[]{:S(2)}) collective-permute-start(f32[1,2,64,256]{3,2,1,0:T(8,128)S(1)} %constant_dynamic-slice_fusion.1), channel_id=1, source_target_pairs={{0,128},{4,132},{8,136},{12,140},{16,144},{20,148},{24,152},{28,15... | collective-permute-start | bytes 393224 | tf_op jit(solution)/shard_map/ppermute | solution.py:11
  148.0 4.4 %collective-permute-start.27 = (f32[1,64,256]{2,1,0:T(8,128)S(1)}, f32[1,64,256]{2,1,0:T(8,128)S(1)}, u32[]{:S(2)}, u32[]{:S(2)}) collective-permute-start(f32[1,64,256]{2,1,0:T(8,128)S(1)} %dynamic-slice_bitcast_fusion), channel_id=1, source_target_pairs={{0,64},{4,68},{8,72},{12,76},{16,80},{20,84},{24,88},{28,92},{32,9... | collective-permute-start | bytes 196616 | tf_op jit(solution)/shard_map/ppermute | solution.py:11
  152.4 7.9 %collective-permute-start.28 = (f32[32,256]{1,0:T(8,128)S(1)}, f32[32,256]{1,0:T(8,128)S(1)}, u32[]{:S(2)}, u32[]{:S(2)}) collective-permute-start(f32[32,256]{1,0:T(8,128)S(1)} %dynamic-slice_bitcast_fusion.1), channel_id=1, source_target_pairs={{0,8},{4,12},{8,0},{12,4},{16,24},{20,28},{24,16},{28,20},{32,40},... | collective-permute-start | bytes 98312 | tf_op jit(solution)/shard_map/ppermute | solution.py:11
  160.4 4.7 %collective-permute-start.29 = (f32[16,256]{1,0:T(8,128)S(1)}, f32[16,256]{1,0:T(8,128)S(1)}, u32[]{:S(2)}, u32[]{:S(2)}) collective-permute-start(f32[16,256]{1,0:T(8,128)S(1)} %constant_dynamic-slice_fusion), channel_id=1, source_target_pairs={{0,4},{4,0},{8,12},{12,8},{16,20},{20,16},{24,28},{28,24},{32,36},... | collective-permute-start | bytes 49160 | tf_op jit(solution)/shard_map/ppermute | solution.py:11

commit v2 on v0

v2 whole, which is shorter than its diff:
```python
import functools

import jax
import jax.numpy as jnp
from jax import lax
from jax.experimental import pallas as pl
from jax.experimental.pallas import tpu as pltpu
from jax.sharding import PartitionSpec as P

HIGH = lax.Precision.HIGH
F32 = jnp.float32
LIMIT = 40 * 2**20


def swap(value, axis, mask):
    pairs = [(source, source ^ mask) for source in range(lax.axis_size(axis))]
    return lax.ppermute(value, axis, pairs)


def split(value):
    top = value.astype(jnp.bfloat16)
    return top, (value - top.astype(F32)).astype(jnp.bfloat16)


def dot3(left, right, dims):
    dot = functools.partial(
        lax.dot_general, dimension_numbers=(dims, ((), ())), preferred_element_type=F32
    )
    return dot(left[0], right[0]) + (dot(left[0], right[1]) + dot(left[1], right[0]))


ROWS = ((0,), (0,))
MATMUL = ((1,), (0,))


def whole(shape):
    return pl.BlockSpec(shape, lambda *_: (0,) * len(shape))


def shapes(*dims):
    return [jax.ShapeDtypeStruct(d, F32) for d in dims]


def call(body, outs, specs, operands, scratch=(), flops=0, grid=(1,), out_specs=None):
    moved = sum(o.size * 4 for o in operands) + sum(o.size * 4 for o in outs)
    return pl.pallas_call(
        body,
        out_shape=outs,
        grid=grid,
        in_specs=specs,
        out_specs=[whole(o.shape) for o in outs] if out_specs is None else out_specs,
        scratch_shapes=list(scratch),
        compiler_params=pltpu.CompilerParams(vmem_limit_bytes=LIMIT),
        cost_estimate=pl.CostEstimate(flops=flops, bytes_accessed=moved, transcendentals=0),
    )(*operands)


def place():
    leaf = lax.axis_index("leaf")
    return leaf >> 4, (leaf >> 2) & 3, leaf & 3


def project_high(columns, probes):
    def body(c_ref, p_ref, keep, one, two, three, total):
        _, x, _ = place()
        right = split(p_ref[...])
        for level in range(3):
            total[level] = dot3(split(c_ref[level]), right, ROWS)
        for part, out in ((1, one), (2, two), (3, three)):
            base = 0 if part == 1 else 64
            if part > 1:
                half = ((x ^ part) & 1) * 64
                out[:64] = total[0, pl.ds(pl.multiple_of(half, 64), 64)]
            row = pl.multiple_of((x ^ part) * 32, 32)
            out[base:base + 32] = total[1, pl.ds(row, 32)]
            out[base + 32:base + 64] = total[2, pl.ds(row, 32)]
        row = pl.multiple_of(x * 32, 32)
        keep[:32] = total[1, pl.ds(row, 32)]
        keep[32:] = total[2, pl.ds(row, 32)]

    _, points, rank = columns.shape
    wide = probes.shape[1]
    return call(
        body,
        shapes((64, wide), (64, wide), (128, wide), (128, wide)),
        [pl.BlockSpec((3, points, rank), lambda _: (1, 0, 0)), whole(probes.shape)],
        [columns, probes],
        [pltpu.VMEM((3, rank, wide), F32)],
        flops=18 * points * rank * wide,
    )


def project_low(columns, probes):
    def body(c_ref, p_ref, pair, one):
        right = split(p_ref[...])
        pair[0] = dot3(split(c_ref[0]), right, ROWS)
        pair[1] = dot3(split(c_ref[2]), right, ROWS)
        one[...] = dot3(split(c_ref[1]), right, ROWS)

    _, points, rank = columns.shape
    wide = probes.shape[1]
    return call(
        body,
        shapes((2, rank, wide), (rank, wide)),
        [pl.BlockSpec((3, points, rank), lambda _: (0, 0, 0)), whole(probes.shape)],
        [columns, probes],
        flops=18 * points * rank * wide,
    )


def expand(near, rows, zero, one, two, part, part1, part2, part3):
    def body(n_ref, u_ref, z_ref, o_ref, t_ref, q0, q1, q2, q3, out, total, high, low):
        _, x, _ = place()

        @pl.when(pl.program_id(0) == 0)
        def _():
            total[0:128] = z_ref[...]
            total[128:256] = o_ref[...]
            total[256:384] = t_ref[...]
            for k, ref in ((0, q0), (1, q1)):
                total[pl.ds(pl.multiple_of(384 + ((x ^ k) & 1) * 64, 64), 64)] = ref[:64]
            for k, ref in ((0, q0), (1, q1), (2, q2), (3, q3)):
                base = 64 if k < 2 else 0
                row = pl.multiple_of((x ^ k) * 32, 32)
                total[pl.ds(512 + row, 32)] = ref[base:base + 32]
                total[pl.ds(640 + row, 32)] = ref[base + 32:base + 64]
            high[...], low[...] = split(total[...])

        left = jnp.concatenate([u_ref[t] for t in range(6)], axis=1)
        out[...] = n_ref[...] + dot3(split(left), (high[...], low[...]), MATMUL)

    levels, points, rank = rows.shape
    wide = near.shape[1]
    tile = 256
    nodes = [zero, one, two, part, part1, part2, part3]
    return call(
        body,
        shapes(near.shape),
        [
            pl.BlockSpec((tile, wide), lambda i: (i, 0)),
            pl.BlockSpec((levels, tile, rank), lambda i: (0, i, 0)),
        ] + [whole(n.shape) for n in nodes],
        [near, rows] + nodes,
        [
            pltpu.VMEM((levels * rank, wide), F32),
            pltpu.VMEM((levels * rank, wide), jnp.bfloat16),
            pltpu.VMEM((levels * rank, wide), jnp.bfloat16),
        ],
        flops=6 * levels * rank * points * wide,
        grid=(points // tile,),
        out_specs=[pl.BlockSpec((tile, wide), lambda i: (i, 0))],
    )[0]


def gram(others, applied):
    wide = applied.shape[1]
    given = [applied] if others[0] is applied else [applied, others[0]]
    given = given + [others[1]]

    def body(*refs):
        (a_ref, first), second = (refs[0], refs[len(given) - 2]), refs[len(given) - 1]
        outs, total = refs[len(given):-1], refs[-1]
        _, x, _ = place()
        right = split(a_ref[...])
        left = right if first is a_ref else split(first[...])
        total[0] = dot3(left, right, ROWS)
        total[1] = dot3(split(second[...]), right, ROWS)
        for k, out in enumerate(outs):
            row = pl.multiple_of((x ^ k) * (wide // 4), wide // 4)
            out[...] = total[:, pl.ds(row, wide // 4)]

    return call(
        body,
        shapes(*[(2, wide // 4, wide)] * 4),
        [whole(g.shape) for g in given],
        given,
        [pltpu.VMEM((2, wide, wide), F32)],
        flops=12 * wide * wide * applied.shape[0],
    )


def cut_y(near, far):
    _, rows, wide = near[0].shape

    def body(*refs):
        ins, outs, total = refs[:8], refs[8:12], refs[12]
        y, _, _ = place()
        probe = lax.axis_index("probe")
        total[:2] = (ins[0][...] + ins[1][...]) + (ins[2][...] + ins[3][...])
        total[2:] = (ins[4][...] + ins[5][...]) + (ins[6][...] + ins[7][...])
        for k, out in enumerate(outs):
            out[...] = total[probe ^ y ^ k]

    ins = [*near, *far]
    return call(
        body,
        shapes(*[(rows, wide)] * 4),
        [whole(i.shape) for i in ins],
        ins,
        [pltpu.VMEM((4, rows, wide), F32)],
    )


def cut_z(ins):
    rows, wide = ins[0].shape

    def body(*refs):
        ins, outs, total = refs[:4], refs[4:8], refs[8]
        _, _, z = place()
        total[...] = (ins[0][...] + ins[1][...]) + (ins[2][...] + ins[3][...])
        for k, out in enumerate(outs):
            out[...] = total[pl.ds(pl.multiple_of((z ^ k) * (rows // 4), rows // 4), rows // 4)]

    return call(
        body,
        shapes(*[(rows // 4, wide)] * 4),
        [whole(i.shape) for i in ins],
        list(ins),
        [pltpu.VMEM((rows, wide), F32)],
    )


def around(parts, scale):
    return [parts[0]] + [swap(parts[k], "leaf", k * scale) for k in (1, 2, 3)]


def local(leaf_blocks, block_mask, row_factor_stack, column_factor_stack, probes):
    leaf_points = leaf_blocks.shape[1]
    side = block_mask.shape[1]
    span = leaf_points // side

    keep, *sent = project_high(column_factor_stack, probes)
    _, one, two, three = around([keep, *sent], 4)
    pair, low1 = project_low(column_factor_stack, probes)
    got = swap(pair, "leaf", 1)
    node0, node2 = got[0], pair[1] + got[1]
    part3 = two[:64] + three[:64]
    upper = keep + one + two[64:] + three[64:]
    part4 = swap(upper[:32], "leaf", 16)
    five = upper[32:]
    part5 = swap(five, "leaf", 32) + swap(five, "leaf", 48)
    part = jnp.concatenate([part3, part4, part5])
    node2 = node2 + swap(node2, "leaf", 2)
    node2 = swap(node2, "leaf", 4)
    part = part + swap(part, "leaf", 1)
    part = part + swap(part, "leaf", 2)
    gathered = [swap(part, "leaf", 4), swap(part[64:], "leaf", 8), swap(part[64:], "leaf", 12)]
    node1 = low1 + swap(low1, "leaf", 1)
    node1 = swap(node1, "leaf", 2)

    weights = block_mask[0].astype(F32)
    masked = (
        leaf_blocks.reshape(side, span, side, span) * weights[:, None, :, None]
    ).reshape(leaf_points, leaf_points)
    near = jnp.dot(masked, probes, precision=HIGH, preferred_element_type=F32)
    applied = expand(near, row_factor_stack, node0, node1, node2, part, *gathered)

    far = swap(applied, "probe", 2)
    beside = swap(applied, "probe", 1)
    first = around(gram([applied, beside], applied), 4)
    far, *first = lax.optimization_barrier((far, *first))
    across = swap(far, "probe", 1)
    second = around(gram([far, across], applied), 4)
    blocks = around(cut_y(first, second), 16)
    blocks = around(cut_z(blocks), 1)
    total = (blocks[0] + blocks[1]) + (blocks[2] + blocks[3])
    return applied, total / (leaf_points * lax.axis_size("leaf"))


def solution(mesh):
    return jax.shard_map(
        local,
        mesh=mesh,
        in_specs=(
            P("leaf", None),
            P("leaf", None, None),
            P(None, "leaf", None),
            P(None, "leaf", None),
            P("leaf", "probe"),
        ),
        out_specs=(P("leaf", "probe"), P("leaf", "probe")),
        check_vma=False,
    )
```

time: 564 us -> 133 us (0.24)
  waiting for transfers between devices: 474 us -> 48.1 us
  matrix products: 24.8 us -> 2.41 us
  starting transfers between devices: 49.3 us -> 67.7 us
  between operations: 14.2 us -> 0.83 us
  Pallas kernels: 0 us -> 7.29 us
    reduce_scatter x1 -> x0, waiting for transfers between devices: 385 us -> none  [local(): lax.psum_scatter(jnp.dot(gathered.T, applied, precision=lax.Precision.HIG...]
    all_gather x1 -> x0, waiting for transfers between devices: 56.6 us -> none  [local(): gathered = lax.all_gather(applied, 'probe', axis=1, tiled=True)]
    dot_general x4 -> x1, matrix products: 24.8 us -> 2.41 us  [local(): near = jnp.dot(masked, probes, precision=HIGH, preferred_element_type=F32)]
    ppermute x21 -> x31, starting transfers between devices: 49 us -> 67.7 us  [swap(): return lax.ppermute(value, axis, pairs)]
    ppermute x21 -> x31, waiting for transfers between devices: 32.6 us -> 48.1 us  [swap(): return lax.ppermute(value, axis, pairs)]
    pallas_call x0 -> x7, Pallas kernels: none -> 7.29 us  [call(): pl.pallas_call(body, out_shape=outs, grid=grid, in_specs=specs, out_specs...]
  transfers between devices with their start and end apart: 23 -> 31, of which waited for: 15 -> 17; matrix products, arithmetic and copies ran while one was open for 1% -> 2% of each run, Pallas kernels for 0% -> 1%
where the time goes in v2:
time: 133 us
  starting transfers between devices  67.7 us (51%)
  waiting for transfers between devices  48.1 us (36%)
  Pallas kernels  7.29 us (5%)
  local copies, waits for them, and re-layouts  5.95 us (4%)
  matrix products  2.41 us (2%)
    ppermute x31, starting transfers between devices, swap(): return lax.ppermute(value, axis, pairs)  67.7 us
    ppermute x31, waiting for transfers between devices, swap(): return lax.ppermute(value, axis, pairs)  48.1 us
    pallas_call x7, Pallas kernels, call(): pl.pallas_call(body, out_shape=outs, grid=grid, in_specs=specs, out_specs...  7.29 us
    unnamed x14, local copies, waits for them, and re-layouts  5.6 us
  transfers between devices with their start and end apart: 31, of which 17 were waited for; matrix products, arithmetic and copies ran while one was open for 2% of the time, Pallas kernels for 1%

profile of v2, /device:TPU:32, one launch (start us, length us, event | category | flops | bytes accessed | tf_op | source)
XLA Modules:
  0.0 133.0 jit_solution(10712617874938882323)
XLA Ops:
  0.6 1.9 %copy-done = f32[6,1024,128]{2,1,0:T(8,128)S(1)} copy-done((f32[6,1024,128]{2,1,0:T(8,128)S(1)}, f32[6,1024,128]{2,1,0:T(8,128)}, u32[]{:S(2)}) %copy-start) | copy-done | bytes 3145752
  2.5 1.2 copy-done.1
  3.7 0.9 shard_map.69
  4.6 2.8 %collective-permute-start.6 = (f32[128,256]{1,0:T(8,128)S(1)}, f32[128,256]{1,0:T(8,128)S(1)}, u32[]{:S(2)}, u32[]{:S(2)}) collective-permute-start(f32[128,256]{1,0:T(8,128)S(1)} %get-tuple-element.32), channel_id=1, source_target_pairs={{0,48},{4,52},{8,56},{12,60},{16,32},{20,36},{24,40},{28,44},{32,1... | collective-permute-start | bytes 393224 | tf_op jit(solution)/shard_map/ppermute | solution.py:17
  7.5 0.8 collective-permute-start.5
  8.8 0.8 shard_map.68
  9.7 3.4 %collective-permute-start = (f32[2,128,256]{2,1,0:T(8,128)S(1)}, f32[2,128,256]{2,1,0:T(8,128)S(1)}, u32[]{:S(2)}, u32[]{:S(2)}) collective-permute-start(f32[2,128,256]{2,1,0:T(8,128)S(1)} %get-tuple-element.29), channel_id=1, source_target_pairs={{0,4},{4,0},{8,12},{12,8},{16,20},{20,16},{24,28},{28,24},{32,36},... | collective-permute-start | bytes 786440 | tf_op jit(solution)/shard_map/ppermute | solution.py:17
  13.2 1.4 %collective-permute-done.5 = f32[128,256]{1,0:T(8,128)S(1)} collective-permute-done((f32[128,256]{1,0:T(8,128)S(1)}, f32[128,256]{1,0:T(8,128)S(1)}, u32[]{:S(2)}, u32[]{:S(2)}) %collective-permute-start.5) | collective-permute-done | bytes 131104 | tf_op jit(solution)/shard_map/ppermute | solution.py:17
  14.7 3.3 %collective-permute-start.9 = (f32[32,256]{1,0:T(8,128)S(1)}, f32[32,256]{1,0:T(8,128)S(1)}, u32[]{:S(2)}, u32[]{:S(2)}) collective-permute-start(f32[32,256]{1,0:T(8,128)S(1)} %get-tuple-element.61), channel_id=1, source_target_pairs={{0,128},{4,132},{8,136},{12,140},{16,144},{20,148},{24,152},{28,15... | collective-permute-start | bytes 98312 | tf_op jit(solution)/shard_map/ppermute | solution.py:17
  18.0 1.1 collective-permute-start.10
  19.0 3.3 %collective-permute-start.1 = (f32[128,256]{1,0:T(8,128)S(1)}, f32[128,256]{1,0:T(8,128)S(1)}, u32[]{:S(2)}, u32[]{:S(2)}) collective-permute-start(f32[128,256]{1,0:T(8,128)S(1)} %get-tuple-element.30), channel_id=1, source_target_pairs={{0,4},{4,0},{8,12},{12,8},{16,20},{20,16},{24,28},{28,24},{32,36},... | collective-permute-start | bytes 393224 | tf_op jit(solution)/shard_map/ppermute | solution.py:17
  22.3 0.8 collective-permute-done.10
  23.1 3.4 %collective-permute-start.11 = (f32[128,256]{1,0:T(8,128)S(1)}, f32[128,256]{1,0:T(8,128)S(1)}, u32[]{:S(2)}, u32[]{:S(2)}) collective-permute-start(f32[128,256]{1,0:T(8,128)S(1)} %pad_maximum_fusion), channel_id=1, source_target_pairs={{0,4},{4,0},{8,12},{12,8},{16,20},{20,16},{24,28},{28,24},{32,36},... | collective-permute-start | bytes 393224 | tf_op jit(solution)/shard_map/ppermute | solution.py:17
  26.5 0.8 collective-permute-done
  27.4 5.5 %collective-permute-start.3 = (f32[128,256]{1,0:T(8,128)S(1)}, f32[128,256]{1,0:T(8,128)S(1)}, u32[]{:S(2)}, u32[]{:S(2)}) collective-permute-start(f32[128,256]{1,0:T(8,128)S(1)} %get-tuple-element.58), channel_id=1, source_target_pairs={{0,8},{4,12},{8,0},{12,4},{16,24},{20,28},{24,16},{28,20},{32,40},... | collective-permute-start | bytes 393224 | tf_op jit(solution)/shard_map/ppermute | solution.py:17
  32.8 4.3 %collective-permute-done.11 = f32[128,256]{1,0:T(8,128)S(1)} collective-permute-done((f32[128,256]{1,0:T(8,128)S(1)}, f32[128,256]{1,0:T(8,128)S(1)}, u32[]{:S(2)}, u32[]{:S(2)}) %collective-permute-start.11) | collective-permute-done | bytes 131104 | tf_op jit(solution)/shard_map/ppermute | solution.py:17
  37.1 7.7 %collective-permute-start.12 = (f32[128,256]{1,0:T(8,128)S(1)}, f32[128,256]{1,0:T(8,128)S(1)}, u32[]{:S(2)}, u32[]{:S(2)}) collective-permute-start(f32[128,256]{1,0:T(8,128)S(1)} %fusion.3), channel_id=1, source_target_pairs={{0,8},{4,12},{8,0},{12,4},{16,24},{20,28},{24,16},{28,20},{32,40},... | collective-permute-start | bytes 393224 | tf_op jit(solution)/shard_map/ppermute | solution.py:17
  45.0 1.4 %collective-permute-start.4 = (f32[128,256]{1,0:T(8,128)S(1)}, f32[128,256]{1,0:T(8,128)S(1)}, u32[]{:S(2)}, u32[]{:S(2)}) collective-permute-start(f32[128,256]{1,0:T(8,128)S(1)} %add.45), channel_id=1, source_target_pairs={{0,16},{4,20},{8,24},{12,28},{16,0},{20,4},{24,8},{28,12},{32,48},... | collective-permute-start | bytes 393224 | tf_op jit(solution)/shard_map/ppermute | solution.py:17
  46.4 3.2 %collective-permute-done.12 = f32[128,256]{1,0:T(8,128)S(1)} collective-permute-done((f32[128,256]{1,0:T(8,128)S(1)}, f32[128,256]{1,0:T(8,128)S(1)}, u32[]{:S(2)}, u32[]{:S(2)}) %collective-permute-start.12) | collective-permute-done | bytes 131104 | tf_op jit(solution)/shard_map/ppermute | solution.py:17
  49.6 3.1 %collective-permute-start.13 = (f32[128,256]{1,0:T(8,128)S(1)}, f32[128,256]{1,0:T(8,128)S(1)}, u32[]{:S(2)}, u32[]{:S(2)}) collective-permute-start(f32[128,256]{1,0:T(8,128)S(1)} %add.52.q0), channel_id=1, source_target_pairs={{0,16},{4,20},{8,24},{12,28},{16,0},{20,4},{24,8},{28,12},{32,48},... | collective-permute-start | bytes 393224 | tf_op jit(solution)/shard_map/ppermute | solution.py:17
  52.8 2.0 %collective-permute-start.14 = (f32[64,256]{1,0:T(8,128)S(1)}, f32[64,256]{1,0:T(8,128)S(1)}, u32[]{:S(2)}, u32[]{:S(2)}) collective-permute-start(f32[64,256]{1,0:T(8,128)S(1)} %slice.49), channel_id=1, source_target_pairs={{0,32},{4,36},{8,40},{12,44},{16,48},{20,52},{24,56},{28,60},{32,0... | collective-permute-start | bytes 196616 | tf_op jit(solution)/shard_map/ppermute | solution.py:17
  54.8 0.8 collective-permute-start.15
  55.9 2.4 %fusion.n_ref = f32[1024,256]{1,0:T(8,128)S(1)} fusion(f32[1024,256]{1,0:T(8,128)S(1)} %copy-done.1, f32[1024,1024]{1,0:T(8,128)S(1)} %copy-done.5, f32[128,8,8,128]{3,2,1,0:T(8,128)S(1)} %bitcast.12), kind=kOutput, calls=%fused_computation.1 | convolution fusion | flops 1611661312 | bytes 10485760 | tf_op jit(solution)/shard_map/dot_general | solution.py:255
  58.8 1.5 %collective-permute-done.15.q3 = f32[64,256]{1,0:T(8,128)S(1)} collective-permute-done((f32[64,256]{1,0:T(8,128)S(1)}, f32[64,256]{1,0:T(8,128)S(1)}, u32[]{:S(2)}, u32[]{:S(2)}) %collective-permute-start.15) | collective-permute-done | bytes 65568 | tf_op jit(solution)/shard_map/ppermute | solution.py:17
  60.3 3.3 %shard_map.70.refs_0_ = f32[1024,256]{1,0:T(8,128)} custom-call(f32[1024,256]{1,0:T(8,128)S(1)} %fusion.n_ref, f32[6,1024,128]{2,1,0:T(8,128)S(1)} %copy-done.4, f32[128,256]{1,0:T(8,128)S(1)} %get-tuple-element.59.z_ref, f32[128,256]{1,0:T(8,128)S(1)} %collective-permute-done.2.o_ref, f32[128,256]{1,0:T(8,128)S(1)} %collective-permute-done.4.t_ref, ...), custom_call_target="tpu_custom_call" | custom-call | flops 1207959552 | bytes 6029312 | tf_op jit(solution)/shard_map/pallas_call | solution.py:46
  63.6 3.9 %collective-permute-start.16 = (f32[1024,256]{1,0:T(8,128)}, f32[1024,256]{1,0:T(8,128)S(1)}, u32[]{:S(2)}, u32[]{:S(2)}) collective-permute-start(f32[1024,256]{1,0:T(8,128)} %shard_map.70.refs_0_), channel_id=1, source_target_pairs={{0,2},{1,3},{2,0},{3,1},{4,6},{5,7},{6,4},{7,5},{8,10},{9,11},{10,... | collective-permute-start | bytes 3145736 | tf_op jit(solution)/shard_map/ppermute | solution.py:17
  67.5 1.3 copy-done.2
  68.8 1.1 shard_map.71
  69.9 2.0 %collective-permute-start.19 = (f32[2,64,256]{2,1,0:T(8,128)S(1)}, f32[2,64,256]{2,1,0:T(8,128)S(1)}, u32[]{:S(2)}, u32[]{:S(2)}) collective-permute-start(f32[2,64,256]{2,1,0:T(8,128)S(1)} %get-tuple-element.37), channel_id=1, source_target_pairs={{0,32},{4,36},{8,40},{12,44},{16,48},{20,52},{24,56},{28,60},{32,0... | collective-permute-start | bytes 393224 | tf_op jit(solution)/shard_map/ppermute | solution.py:17
  72.0 2.6 %collective-permute-start.20 = (f32[2,64,256]{2,1,0:T(8,128)S(1)}, f32[2,64,256]{2,1,0:T(8,128)S(1)}, u32[]{:S(2)}, u32[]{:S(2)}) collective-permute-start(f32[2,64,256]{2,1,0:T(8,128)S(1)} %get-tuple-element.38), channel_id=1, source_target_pairs={{0,48},{4,52},{8,56},{12,60},{16,32},{20,36},{24,40},{28,44},{32,1... | collective-permute-start | bytes 393224 | tf_op jit(solution)/shard_map/ppermute | solution.py:17
  74.6 16.9 %collective-permute-done.16.refs_1_ = f32[1024,256]{1,0:T(8,128)S(1)} collective-permute-done((f32[1024,256]{1,0:T(8,128)}, f32[1024,256]{1,0:T(8,128)S(1)}, u32[]{:S(2)}, u32[]{:S(2)}) %collective-permute-start.16) | collective-permute-done | bytes 1048608 | tf_op jit(solution)/shard_map/ppermute | solution.py:17
  91.7 2.6 %collective-permute-done.21.refs_2_ = f32[1024,256]{1,0:T(8,128)S(1)} collective-permute-done((f32[1024,256]{1,0:T(8,128)S(1)}, f32[1024,256]{1,0:T(8,128)S(1)}, u32[]{:S(2)}, u32[]{:S(2)}) %collective-permute-start.21) | collective-permute-done | bytes 1048608 | tf_op jit(solution)/shard_map/ppermute | solution.py:17
  94.3 1.2 copy-done.3
  95.5 1.1 shard_map.72
  96.7 2.0 %collective-permute-start.23 = (f32[2,64,256]{2,1,0:T(8,128)S(1)}, f32[2,64,256]{2,1,0:T(8,128)S(1)}, u32[]{:S(2)}, u32[]{:S(2)}) collective-permute-start(f32[2,64,256]{2,1,0:T(8,128)S(1)} %get-tuple-element.46), channel_id=1, source_target_pairs={{0,32},{4,36},{8,40},{12,44},{16,48},{20,52},{24,56},{28,60},{32,0... | collective-permute-start | bytes 393224 | tf_op jit(solution)/shard_map/ppermute | solution.py:17
  98.8 2.6 %collective-permute-start.24 = (f32[2,64,256]{2,1,0:T(8,128)S(1)}, f32[2,64,256]{2,1,0:T(8,128)S(1)}, u32[]{:S(2)}, u32[]{:S(2)}) collective-permute-start(f32[2,64,256]{2,1,0:T(8,128)S(1)} %get-tuple-element.47), channel_id=1, source_target_pairs={{0,48},{4,52},{8,56},{12,60},{16,32},{20,36},{24,40},{28,44},{32,1... | collective-permute-start | bytes 393224 | tf_op jit(solution)/shard_map/ppermute | solution.py:17
  101.4 1.6 %collective-permute-done.22.refs_5_ = f32[2,64,256]{2,1,0:T(8,128)S(1)} collective-permute-done((f32[2,64,256]{2,1,0:T(8,128)S(1)}, f32[2,64,256]{2,1,0:T(8,128)S(1)}, u32[]{:S(2)}, u32[]{:S(2)}) %collective-permute-start.22) | collective-permute-done | bytes 131104 | tf_op jit(solution)/shard_map/ppermute | solution.py:17
  103.0 2.1 %collective-permute-done.23.refs_6_ = f32[2,64,256]{2,1,0:T(8,128)S(1)} collective-permute-done((f32[2,64,256]{2,1,0:T(8,128)S(1)}, f32[2,64,256]{2,1,0:T(8,128)S(1)}, u32[]{:S(2)}, u32[]{:S(2)}) %collective-permute-start.23) | collective-permute-done | bytes 131104 | tf_op jit(solution)/shard_map/ppermute | solution.py:17
  105.2 2.2 %collective-permute-done.24.refs_7_ = f32[2,64,256]{2,1,0:T(8,128)S(1)} collective-permute-done((f32[2,64,256]{2,1,0:T(8,128)S(1)}, f32[2,64,256]{2,1,0:T(8,128)S(1)}, u32[]{:S(2)}, u32[]{:S(2)}) %collective-permute-start.24) | collective-permute-done | bytes 131104 | tf_op jit(solution)/shard_map/ppermute | solution.py:17
  107.5 1.7 %collective-permute-start.25 = (f32[64,256]{1,0:T(8,128)S(1)}, f32[64,256]{1,0:T(8,128)S(1)}, u32[]{:S(2)}, u32[]{:S(2)}) collective-permute-start(f32[64,256]{1,0:T(8,128)S(1)} %get-tuple-element.49), channel_id=1, source_target_pairs={{0,64},{4,68},{8,72},{12,76},{16,80},{20,84},{24,88},{28,92},{32,9... | collective-permute-start | bytes 196616 | tf_op jit(solution)/shard_map/ppermute | solution.py:17
  109.2 2.9 %collective-permute-start.26 = (f32[64,256]{1,0:T(8,128)S(1)}, f32[64,256]{1,0:T(8,128)S(1)}, u32[]{:S(2)}, u32[]{:S(2)}) collective-permute-start(f32[64,256]{1,0:T(8,128)S(1)} %get-tuple-element.50), channel_id=1, source_target_pairs={{0,128},{4,132},{8,136},{12,140},{16,144},{20,148},{24,152},{28,15... | collective-permute-start | bytes 196616 | tf_op jit(solution)/shard_map/ppermute | solution.py:17
  112.3 2.7 %collective-permute-done.26.refs_2_ = f32[64,256]{1,0:T(8,128)S(1)} collective-permute-done((f32[64,256]{1,0:T(8,128)S(1)}, f32[64,256]{1,0:T(8,128)S(1)}, u32[]{:S(2)}, u32[]{:S(2)}) %collective-permute-start.26) | collective-permute-done | bytes 65568 | tf_op jit(solution)/shard_map/ppermute | solution.py:17
  115.0 2.5 %collective-permute-done.27.refs_3_ = f32[64,256]{1,0:T(8,128)S(1)} collective-permute-done((f32[64,256]{1,0:T(8,128)S(1)}, f32[64,256]{1,0:T(8,128)S(1)}, u32[]{:S(2)}, u32[]{:S(2)}) %collective-permute-start.27) | collective-permute-done | bytes 65568 | tf_op jit(solution)/shard_map/ppermute | solution.py:17
  117.6 6.5 %collective-permute-start.29 = (f32[16,256]{1,0:T(8,128)S(1)}, f32[16,256]{1,0:T(8,128)S(1)}, u32[]{:S(2)}, u32[]{:S(2)}) collective-permute-start(f32[16,256]{1,0:T(8,128)S(1)} %get-tuple-element.54), channel_id=1, source_target_pairs={{0,8},{4,12},{8,0},{12,4},{16,24},{20,28},{24,16},{28,20},{32,40},... | collective-permute-start | bytes 49160 | tf_op jit(solution)/shard_map/ppermute | solution.py:17
  124.1 3.7 %collective-permute-start.30 = (f32[16,256]{1,0:T(8,128)S(1)}, f32[16,256]{1,0:T(8,128)S(1)}, u32[]{:S(2)}, u32[]{:S(2)}) collective-permute-start(f32[16,256]{1,0:T(8,128)S(1)} %get-tuple-element.55), channel_id=1, source_target_pairs={{0,12},{4,8},{8,4},{12,0},{16,28},{20,24},{24,20},{28,16},{32,44},... | collective-permute-start | bytes 49160 | tf_op jit(solution)/shard_map/ppermute | solution.py:17
  127.8 2.2 %collective-permute-done.30 = f32[16,256]{1,0:T(8,128)S(1)} collective-permute-done((f32[16,256]{1,0:T(8,128)S(1)}, f32[16,256]{1,0:T(8,128)S(1)}, u32[]{:S(2)}, u32[]{:S(2)}) %collective-permute-start.30) | collective-permute-done | bytes 16416 | tf_op jit(solution)/shard_map/ppermute | solution.py:17
  130.0 2.5 %collective-permute-done.28 = f32[16,256]{1,0:T(8,128)S(1)} collective-permute-done((f32[16,256]{1,0:T(8,128)S(1)}, f32[16,256]{1,0:T(8,128)S(1)}, u32[]{:S(2)}, u32[]{:S(2)}) %collective-permute-start.28) | collective-permute-done | bytes 16416 | tf_op jit(solution)/shard_map/ppermute | solution.py:17
  132.4 0.6 add_multiply_fusion
  (49 shorter events, 2.4 us)
Async XLA Ops:
  0.6 1.9 %copy-start = (f32[6,1024,128]{2,1,0:T(8,128)S(1)}, f32[6,1024,128]{2,1,0:T(8,128)}, u32[]{:S(2)}) copy-start(f32[6,1024,128]{2,1,0:T(8,128)} %c_ref.3) | copy-start | bytes 9437188
  2.5 1.2 copy-start.1
  3.7 41.1 %copy-start.6 = (s32[1,8,8]{2,1,0:T(8,128)S(1)}, s32[1,8,8]{2,1,0:T(8,128)}, u32[]{:S(2)}) copy-start(s32[1,8,8]{2,1,0:T(8,128)} %param.6) | copy-start | bytes 772
  4.6 8.6 %collective-permute-start.6 = (f32[128,256]{1,0:T(8,128)S(1)}, f32[128,256]{1,0:T(8,128)S(1)}, u32[]{:S(2)}, u32[]{:S(2)}) collective-permute-start(f32[128,256]{1,0:T(8,128)S(1)} %get-tuple-element.32), channel_id=1, source_target_pairs={{0,48},{4,52},{8,56},{12,60},{16,32},{20,36},{24,40},{28,44},{32,1... | collective-permute-start | bytes 393224 | tf_op jit(solution)/shard_map/ppermute | solution.py:17
  7.5 7.2 %collective-permute-start.5 = (f32[128,256]{1,0:T(8,128)S(1)}, f32[128,256]{1,0:T(8,128)S(1)}, u32[]{:S(2)}, u32[]{:S(2)}) collective-permute-start(f32[128,256]{1,0:T(8,128)S(1)} %get-tuple-element.31), channel_id=1, source_target_pairs={{0,32},{4,36},{8,40},{12,44},{16,48},{20,52},{24,56},{28,60},{32,0... | collective-permute-start | bytes 393224 | tf_op jit(solution)/shard_map/ppermute | solution.py:17
  8.3 4.9 %collective-permute-start.7 = (f32[64,256]{1,0:T(8,128)S(1)}, f32[64,256]{1,0:T(8,128)S(1)}, u32[]{:S(2)}, u32[]{:S(2)}) collective-permute-start(f32[64,256]{1,0:T(8,128)S(1)} %get-tuple-element.34), channel_id=1, source_target_pairs={{0,16},{4,20},{8,24},{12,28},{16,0},{20,4},{24,8},{28,12},{32,48},... | collective-permute-start | bytes 196616 | tf_op jit(solution)/shard_map/ppermute | solution.py:17
  9.7 46.2 %copy-start.5 = (f32[1024,1024]{1,0:T(8,128)S(1)}, f32[1024,1024]{1,0:T(8,128)}, u32[]{:S(2)}) copy-start(f32[1024,1024]{1,0:T(8,128)} %param.5) | copy-start | bytes 12582916
  9.7 17.7 %collective-permute-start = (f32[2,128,256]{2,1,0:T(8,128)S(1)}, f32[2,128,256]{2,1,0:T(8,128)S(1)}, u32[]{:S(2)}, u32[]{:S(2)}) collective-permute-start(f32[2,128,256]{2,1,0:T(8,128)S(1)} %get-tuple-element.29), channel_id=1, source_target_pairs={{0,4},{4,0},{8,12},{12,8},{16,20},{20,16},{24,28},{28,24},{32,36},... | collective-permute-start | bytes 786440 | tf_op jit(solution)/shard_map/ppermute | solution.py:17
  14.7 7.6 %collective-permute-start.9 = (f32[32,256]{1,0:T(8,128)S(1)}, f32[32,256]{1,0:T(8,128)S(1)}, u32[]{:S(2)}, u32[]{:S(2)}) collective-permute-start(f32[32,256]{1,0:T(8,128)S(1)} %get-tuple-element.61), channel_id=1, source_target_pairs={{0,128},{4,132},{8,136},{12,140},{16,144},{20,148},{24,152},{28,15... | collective-permute-start | bytes 98312 | tf_op jit(solution)/shard_map/ppermute | solution.py:17
  18.0 5.1 %collective-permute-start.10 = (f32[32,256]{1,0:T(8,128)S(1)}, f32[32,256]{1,0:T(8,128)S(1)}, u32[]{:S(2)}, u32[]{:S(2)}) collective-permute-start(f32[32,256]{1,0:T(8,128)S(1)} %get-tuple-element.61), channel_id=1, source_target_pairs={{0,192},{4,196},{8,200},{12,204},{16,208},{20,212},{24,216},{28,22... | collective-permute-start | bytes 98312 | tf_op jit(solution)/shard_map/ppermute | solution.py:17
  19.0 4.1 %collective-permute-start.8 = (f32[32,256]{1,0:T(8,128)S(1)}, f32[32,256]{1,0:T(8,128)S(1)}, u32[]{:S(2)}, u32[]{:S(2)}) collective-permute-start(f32[32,256]{1,0:T(8,128)S(1)} %get-tuple-element.60), channel_id=1, source_target_pairs={{0,64},{4,68},{8,72},{12,76},{16,80},{20,84},{24,88},{28,92},{32,9... | collective-permute-start | bytes 98312 | tf_op jit(solution)/shard_map/ppermute | solution.py:17
  19.0 25.8 %collective-permute-start.1 = (f32[128,256]{1,0:T(8,128)S(1)}, f32[128,256]{1,0:T(8,128)S(1)}, u32[]{:S(2)}, u32[]{:S(2)}) collective-permute-start(f32[128,256]{1,0:T(8,128)S(1)} %get-tuple-element.30), channel_id=1, source_target_pairs={{0,4},{4,0},{8,12},{12,8},{16,20},{20,16},{24,28},{28,24},{32,36},... | collective-permute-start | bytes 393224 | tf_op jit(solution)/shard_map/ppermute | solution.py:17
  23.1 14.0 %collective-permute-start.11 = (f32[128,256]{1,0:T(8,128)S(1)}, f32[128,256]{1,0:T(8,128)S(1)}, u32[]{:S(2)}, u32[]{:S(2)}) collective-permute-start(f32[128,256]{1,0:T(8,128)S(1)} %pad_maximum_fusion), channel_id=1, source_target_pairs={{0,4},{4,0},{8,12},{12,8},{16,20},{20,16},{24,28},{28,24},{32,36},... | collective-permute-start | bytes 393224 | tf_op jit(solution)/shard_map/ppermute | solution.py:17
  27.4 17.6 %collective-permute-start.3 = (f32[128,256]{1,0:T(8,128)S(1)}, f32[128,256]{1,0:T(8,128)S(1)}, u32[]{:S(2)}, u32[]{:S(2)}) collective-permute-start(f32[128,256]{1,0:T(8,128)S(1)} %get-tuple-element.58), channel_id=1, source_target_pairs={{0,8},{4,12},{8,0},{12,4},{16,24},{20,28},{24,16},{28,20},{32,40},... | collective-permute-start | bytes 393224 | tf_op jit(solution)/shard_map/ppermute | solution.py:17
  37.1 12.5 %collective-permute-start.12 = (f32[128,256]{1,0:T(8,128)S(1)}, f32[128,256]{1,0:T(8,128)S(1)}, u32[]{:S(2)}, u32[]{:S(2)}) collective-permute-start(f32[128,256]{1,0:T(8,128)S(1)} %fusion.3), channel_id=1, source_target_pairs={{0,8},{4,12},{8,0},{12,4},{16,24},{20,28},{24,16},{28,20},{32,40},... | collective-permute-start | bytes 393224 | tf_op jit(solution)/shard_map/ppermute | solution.py:17
  44.9 13.5 %collective-permute-start.2 = (f32[128,256]{1,0:T(8,128)S(1)}, f32[128,256]{1,0:T(8,128)S(1)}, u32[]{:S(2)}, u32[]{:S(2)}) collective-permute-start(f32[128,256]{1,0:T(8,128)S(1)} %add.42), channel_id=1, source_target_pairs={{0,8},{4,12},{8,0},{12,4},{16,24},{20,28},{24,16},{28,20},{32,40},... | collective-permute-start | bytes 393224 | tf_op jit(solution)/shard_map/ppermute | solution.py:17
  45.0 15.2 %collective-permute-start.4 = (f32[128,256]{1,0:T(8,128)S(1)}, f32[128,256]{1,0:T(8,128)S(1)}, u32[]{:S(2)}, u32[]{:S(2)}) collective-permute-start(f32[128,256]{1,0:T(8,128)S(1)} %add.45), channel_id=1, source_target_pairs={{0,16},{4,20},{8,24},{12,28},{16,0},{20,4},{24,8},{28,12},{32,48},... | collective-permute-start | bytes 393224 | tf_op jit(solution)/shard_map/ppermute | solution.py:17
  49.6 10.6 %collective-permute-start.13 = (f32[128,256]{1,0:T(8,128)S(1)}, f32[128,256]{1,0:T(8,128)S(1)}, u32[]{:S(2)}, u32[]{:S(2)}) collective-permute-start(f32[128,256]{1,0:T(8,128)S(1)} %add.52.q0), channel_id=1, source_target_pairs={{0,16},{4,20},{8,24},{12,28},{16,0},{20,4},{24,8},{28,12},{32,48},... | collective-permute-start | bytes 393224 | tf_op jit(solution)/shard_map/ppermute | solution.py:17
  52.8 6.0 %collective-permute-start.14 = (f32[64,256]{1,0:T(8,128)S(1)}, f32[64,256]{1,0:T(8,128)S(1)}, u32[]{:S(2)}, u32[]{:S(2)}) collective-permute-start(f32[64,256]{1,0:T(8,128)S(1)} %slice.49), channel_id=1, source_target_pairs={{0,32},{4,36},{8,40},{12,44},{16,48},{20,52},{24,56},{28,60},{32,0... | collective-permute-start | bytes 196616 | tf_op jit(solution)/shard_map/ppermute | solution.py:17
  54.8 5.5 %collective-permute-start.15 = (f32[64,256]{1,0:T(8,128)S(1)}, f32[64,256]{1,0:T(8,128)S(1)}, u32[]{:S(2)}, u32[]{:S(2)}) collective-permute-start(f32[64,256]{1,0:T(8,128)S(1)} %slice.49), channel_id=1, source_target_pairs={{0,48},{4,52},{8,56},{12,60},{16,32},{20,36},{24,40},{28,44},{32,1... | collective-permute-start | bytes 196616 | tf_op jit(solution)/shard_map/ppermute | solution.py:17
  55.9 4.3 %copy-start.4 = (f32[6,1024,128]{2,1,0:T(8,128)S(1)}, f32[6,1024,128]{2,1,0:T(8,128)}, u32[]{:S(2)}) copy-start(f32[6,1024,128]{2,1,0:T(8,128)} %u_ref.1) | copy-start | bytes 9437188
  63.6 3.9 %collective-permute-start.17 = (f32[1024,256]{1,0:T(8,128)}, f32[1024,256]{1,0:T(8,128)S(1)}, u32[]{:S(2)}, u32[]{:S(2)}) collective-permute-start(f32[1024,256]{1,0:T(8,128)} %shard_map.70.refs_0_), channel_id=1, source_target_pairs={{0,1},{1,0},{2,3},{3,2},{4,5},{5,4},{6,7},{7,6},{8,9},{9,8},{10,11... | collective-permute-start | bytes 3145736 | tf_op jit(solution)/shard_map/ppermute | solution.py:17
  63.6 27.9 %collective-permute-start.16 = (f32[1024,256]{1,0:T(8,128)}, f32[1024,256]{1,0:T(8,128)S(1)}, u32[]{:S(2)}, u32[]{:S(2)}) collective-permute-start(f32[1024,256]{1,0:T(8,128)} %shard_map.70.refs_0_), channel_id=1, source_target_pairs={{0,2},{1,3},{2,0},{3,1},{4,6},{5,7},{6,4},{7,5},{8,10},{9,11},{10,... | collective-permute-start | bytes 3145736 | tf_op jit(solution)/shard_map/ppermute | solution.py:17
  67.5 1.3 copy-start.2
  69.8 21.7 %collective-permute-start.18 = (f32[2,64,256]{2,1,0:T(8,128)S(1)}, f32[2,64,256]{2,1,0:T(8,128)S(1)}, u32[]{:S(2)}, u32[]{:S(2)}) collective-permute-start(f32[2,64,256]{2,1,0:T(8,128)S(1)} %get-tuple-element.36), channel_id=1, source_target_pairs={{0,16},{4,20},{8,24},{12,28},{16,0},{20,4},{24,8},{28,12},{32,48},... | collective-permute-start | bytes 393224 | tf_op jit(solution)/shard_map/ppermute | solution.py:17
  69.9 21.6 %collective-permute-start.19 = (f32[2,64,256]{2,1,0:T(8,128)S(1)}, f32[2,64,256]{2,1,0:T(8,128)S(1)}, u32[]{:S(2)}, u32[]{:S(2)}) collective-permute-start(f32[2,64,256]{2,1,0:T(8,128)S(1)} %get-tuple-element.37), channel_id=1, source_target_pairs={{0,32},{4,36},{8,40},{12,44},{16,48},{20,52},{24,56},{28,60},{32,0... | collective-permute-start | bytes 393224 | tf_op jit(solution)/shard_map/ppermute | solution.py:17
  72.0 19.6 %collective-permute-start.20 = (f32[2,64,256]{2,1,0:T(8,128)S(1)}, f32[2,64,256]{2,1,0:T(8,128)S(1)}, u32[]{:S(2)}, u32[]{:S(2)}) collective-permute-start(f32[2,64,256]{2,1,0:T(8,128)S(1)} %get-tuple-element.38), channel_id=1, source_target_pairs={{0,48},{4,52},{8,56},{12,60},{16,32},{20,36},{24,40},{28,44},{32,1... | collective-permute-start | bytes 393224 | tf_op jit(solution)/shard_map/ppermute | solution.py:17
  91.6 2.7 %collective-permute-start.21 = (f32[1024,256]{1,0:T(8,128)S(1)}, f32[1024,256]{1,0:T(8,128)S(1)}, u32[]{:S(2)}, u32[]{:S(2)}) collective-permute-start(f32[1024,256]{1,0:T(8,128)S(1)} %collective-permute-done.16.refs_1_), channel_id=1, source_target_pairs={{0,1},{1,0},{2,3},{3,2},{4,5},{5,4},{6,7},{7,6},{8,9},{9,8},{10,11... | collective-permute-start | bytes 3145736 | tf_op jit(solution)/shard_map/ppermute | solution.py:17
  94.3 1.2 copy-start.3
  96.6 6.4 %collective-permute-start.22 = (f32[2,64,256]{2,1,0:T(8,128)S(1)}, f32[2,64,256]{2,1,0:T(8,128)S(1)}, u32[]{:S(2)}, u32[]{:S(2)}) collective-permute-start(f32[2,64,256]{2,1,0:T(8,128)S(1)} %get-tuple-element.45), channel_id=1, source_target_pairs={{0,16},{4,20},{8,24},{12,28},{16,0},{20,4},{24,8},{28,12},{32,48},... | collective-permute-start | bytes 393224 | tf_op jit(solution)/shard_map/ppermute | solution.py:17
  96.7 8.5 %collective-permute-start.23 = (f32[2,64,256]{2,1,0:T(8,128)S(1)}, f32[2,64,256]{2,1,0:T(8,128)S(1)}, u32[]{:S(2)}, u32[]{:S(2)}) collective-permute-start(f32[2,64,256]{2,1,0:T(8,128)S(1)} %get-tuple-element.46), channel_id=1, source_target_pairs={{0,32},{4,36},{8,40},{12,44},{16,48},{20,52},{24,56},{28,60},{32,0... | collective-permute-start | bytes 393224 | tf_op jit(solution)/shard_map/ppermute | solution.py:17
  98.8 8.7 %collective-permute-start.24 = (f32[2,64,256]{2,1,0:T(8,128)S(1)}, f32[2,64,256]{2,1,0:T(8,128)S(1)}, u32[]{:S(2)}, u32[]{:S(2)}) collective-permute-start(f32[2,64,256]{2,1,0:T(8,128)S(1)} %get-tuple-element.47), channel_id=1, source_target_pairs={{0,48},{4,52},{8,56},{12,60},{16,32},{20,36},{24,40},{28,44},{32,1... | collective-permute-start | bytes 393224 | tf_op jit(solution)/shard_map/ppermute | solution.py:17
  107.5 4.8 %collective-permute-start.25 = (f32[64,256]{1,0:T(8,128)S(1)}, f32[64,256]{1,0:T(8,128)S(1)}, u32[]{:S(2)}, u32[]{:S(2)}) collective-permute-start(f32[64,256]{1,0:T(8,128)S(1)} %get-tuple-element.49), channel_id=1, source_target_pairs={{0,64},{4,68},{8,72},{12,76},{16,80},{20,84},{24,88},{28,92},{32,9... | collective-permute-start | bytes 196616 | tf_op jit(solution)/shard_map/ppermute | solution.py:17
  109.2 5.8 %collective-permute-start.26 = (f32[64,256]{1,0:T(8,128)S(1)}, f32[64,256]{1,0:T(8,128)S(1)}, u32[]{:S(2)}, u32[]{:S(2)}) collective-permute-start(f32[64,256]{1,0:T(8,128)S(1)} %get-tuple-element.50), channel_id=1, source_target_pairs={{0,128},{4,132},{8,136},{12,140},{16,144},{20,148},{24,152},{28,15... | collective-permute-start | bytes 196616 | tf_op jit(solution)/shard_map/ppermute | solution.py:17
  112.1 5.5 %collective-permute-start.27 = (f32[64,256]{1,0:T(8,128)S(1)}, f32[64,256]{1,0:T(8,128)S(1)}, u32[]{:S(2)}, u32[]{:S(2)}) collective-permute-start(f32[64,256]{1,0:T(8,128)S(1)} %get-tuple-element.51), channel_id=1, source_target_pairs={{0,192},{4,196},{8,200},{12,204},{16,208},{20,212},{24,216},{28,22... | collective-permute-start | bytes 196616 | tf_op jit(solution)/shard_map/ppermute | solution.py:17
  117.6 10.2 %collective-permute-start.29 = (f32[16,256]{1,0:T(8,128)S(1)}, f32[16,256]{1,0:T(8,128)S(1)}, u32[]{:S(2)}, u32[]{:S(2)}) collective-permute-start(f32[16,256]{1,0:T(8,128)S(1)} %get-tuple-element.54), channel_id=1, source_target_pairs={{0,8},{4,12},{8,0},{12,4},{16,24},{20,28},{24,16},{28,20},{32,40},... | collective-permute-start | bytes 49160 | tf_op jit(solution)/shard_map/ppermute | solution.py:17
  124.1 5.9 %collective-permute-start.30 = (f32[16,256]{1,0:T(8,128)S(1)}, f32[16,256]{1,0:T(8,128)S(1)}, u32[]{:S(2)}, u32[]{:S(2)}) collective-permute-start(f32[16,256]{1,0:T(8,128)S(1)} %get-tuple-element.55), channel_id=1, source_target_pairs={{0,12},{4,8},{8,4},{12,0},{16,28},{20,24},{24,20},{28,16},{32,44},... | collective-permute-start | bytes 49160 | tf_op jit(solution)/shard_map/ppermute | solution.py:17
  127.8 4.6 %collective-permute-start.28 = (f32[16,256]{1,0:T(8,128)S(1)}, f32[16,256]{1,0:T(8,128)S(1)}, u32[]{:S(2)}, u32[]{:S(2)}) collective-permute-start(f32[16,256]{1,0:T(8,128)S(1)} %get-tuple-element.53), channel_id=1, source_target_pairs={{0,4},{4,0},{8,12},{12,8},{16,20},{20,16},{24,28},{28,24},{32,36},... | collective-permute-start | bytes 49160 | tf_op jit(solution)/shard_map/ppermute | solution.py:17

commit v3 on v2

--- a/solution.py
+++ b/solution.py
@@ -10,6 +10,7 @@
 HIGH = lax.Precision.HIGH
 F32 = jnp.float32
 LIMIT = 40 * 2**20
+MOST = 52 * 2**20
 
 
 def swap(value, axis, mask):
@@ -41,7 +42,9 @@
     return [jax.ShapeDtypeStruct(d, F32) for d in dims]
 
 
-def call(body, outs, specs, operands, scratch=(), flops=0, grid=(1,), out_specs=None):
+def call(
+    body, outs, specs, operands, scratch=(), flops=0, grid=(1,), out_specs=None, limit=LIMIT
+):
     moved = sum(o.size * 4 for o in operands) + sum(o.size * 4 for o in outs)
     return pl.pallas_call(
         body,
@@ -50,7 +53,7 @@
         in_specs=specs,
         out_specs=[whole(o.shape) for o in outs] if out_specs is None else out_specs,
         scratch_shapes=list(scratch),
-        compiler_params=pltpu.CompilerParams(vmem_limit_bytes=LIMIT),
+        compiler_params=pltpu.CompilerParams(vmem_limit_bytes=limit),
         cost_estimate=pl.CostEstimate(flops=flops, bytes_accessed=moved, transcendentals=0),
     )(*operands)
 
@@ -87,69 +90,88 @@
         [columns, probes],
         [pltpu.VMEM((3, rank, wide), F32)],
         flops=18 * points * rank * wide,
+        limit=MOST,
     )
 
 
 def project_low(columns, probes):
-    def body(c_ref, p_ref, pair, one):
+    def body(c_ref, p_ref, *outs):
         right = split(p_ref[...])
-        pair[0] = dot3(split(c_ref[0]), right, ROWS)
-        pair[1] = dot3(split(c_ref[2]), right, ROWS)
-        one[...] = dot3(split(c_ref[1]), right, ROWS)
+        for level, out in enumerate(outs):
+            out[...] = dot3(split(c_ref[level]), right, ROWS)
 
     _, points, rank = columns.shape
     wide = probes.shape[1]
     return call(
         body,
-        shapes((2, rank, wide), (rank, wide)),
+        shapes(*[(rank, wide)] * 3),
         [pl.BlockSpec((3, points, rank), lambda _: (0, 0, 0)), whole(probes.shape)],
         [columns, probes],
         flops=18 * points * rank * wide,
-    )
-
-
-def expand(near, rows, zero, one, two, part, part1, part2, part3):
-    def body(n_ref, u_ref, z_ref, o_ref, t_ref, q0, q1, q2, q3, out, total, high, low):
-        _, x, _ = place()
-
-        @pl.when(pl.program_id(0) == 0)
-        def _():
-            total[0:128] = z_ref[...]
-            total[128:256] = o_ref[...]
-            total[256:384] = t_ref[...]
-            for k, ref in ((0, q0), (1, q1)):
-                total[pl.ds(pl.multiple_of(384 + ((x ^ k) & 1) * 64, 64), 64)] = ref[:64]
-            for k, ref in ((0, q0), (1, q1), (2, q2), (3, q3)):
-                base = 64 if k < 2 else 0
-                row = pl.multiple_of((x ^ k) * 32, 32)
-                total[pl.ds(512 + row, 32)] = ref[base:base + 32]
-                total[pl.ds(640 + row, 32)] = ref[base + 32:base + 64]
-            high[...], low[...] = split(total[...])
-
-        left = jnp.concatenate([u_ref[t] for t in range(6)], axis=1)
-        out[...] = n_ref[...] + dot3(split(left), (high[...], low[...]), MATMUL)
+        limit=LIMIT,
+    )
+
+
+LATE = (1, 3, 4, 5)
+
+
+def prepare(near, rows, zero, two):
+    def body(n_ref, u_ref, z_ref, t_ref, out, high, low):
+        early = jnp.concatenate([u_ref[0], u_ref[2]], axis=1)
+        nodes = jnp.concatenate([z_ref[...], t_ref[...]], axis=0)
+        out[...] = n_ref[...] + dot3(split(early), split(nodes), MATMUL)
+        high[...], low[...] = split(jnp.concatenate([u_ref[t] for t in LATE], axis=1))
 
     levels, points, rank = rows.shape
     wide = near.shape[1]
     tile = 256
-    nodes = [zero, one, two, part, part1, part2, part3]
-    return call(
-        body,
-        shapes(near.shape),
+
+    def tiled(width):
+        return pl.BlockSpec((tile, width), lambda i: (i, 0))
+
+    late = jax.ShapeDtypeStruct((points, len(LATE) * rank), jnp.bfloat16)
+    return call(
+        body,
+        shapes(near.shape) + [late, late],
         [
-            pl.BlockSpec((tile, wide), lambda i: (i, 0)),
+            tiled(wide),
             pl.BlockSpec((levels, tile, rank), lambda i: (0, i, 0)),
-        ] + [whole(n.shape) for n in nodes],
-        [near, rows] + nodes,
-        [
-            pltpu.VMEM((levels * rank, wide), F32),
-            pltpu.VMEM((levels * rank, wide), jnp.bfloat16),
-            pltpu.VMEM((levels * rank, wide), jnp.bfloat16),
+            whole(zero.shape),
+            whole(two.shape),
         ],
-        flops=6 * levels * rank * points * wide,
+        [near, rows, zero, two],
+        flops=12 * rank * points * wide,
         grid=(points // tile,),
-        out_specs=[pl.BlockSpec((tile, wide), lambda i: (i, 0))],
-    )[0]
+        out_specs=[tiled(wide), tiled(len(LATE) * rank), tiled(len(LATE) * rank)],
+    )
+
+
+def expand(base, rows_high, rows_low, one, part, part1, part2, part3):
+    def body(b_ref, h_ref, l_ref, o_ref, q0, q1, q2, q3, out, held, total):
+        _, x, _ = place()
+        total[0:128] = o_ref[...]
+        for k, ref in ((0, q0), (1, q1)):
+            total[pl.ds(pl.multiple_of(128 + ((x ^ k) & 1) * 64, 64), 64)] = ref[:64]
+        for k, ref in ((0, q0), (1, q1), (2, q2), (3, q3)):
+            base = 64 if k < 2 else 0
+            row = pl.multiple_of((x ^ k) * 32, 32)
+            total[pl.ds(256 + row, 32)] = ref[base:base + 32]
+            total[pl.ds(384 + row, 32)] = ref[base + 32:base + 64]
+        left = h_ref[...], l_ref[...]
+        held[...] = b_ref[...] + dot3(left, split(total[...]), MATMUL)
+        out[...] = held[...]
+
+    points, wide = base.shape
+    depth = rows_high.shape[1]
+    given = [base, rows_high, rows_low, one, part, part1, part2, part3]
+    return call(
+        body,
+        shapes(base.shape, base.shape),
+        [whole(g.shape) for g in given],
+        given,
+        [pltpu.VMEM((depth, wide), F32)],
+        flops=6 * depth * points * wide,
+    )
 
 
 def gram(others, applied):
@@ -229,31 +251,37 @@
     side = block_mask.shape[1]
     span = leaf_points // side
 
+    weights = block_mask[0].astype(F32)
+    masked = (
+        leaf_blocks.reshape(side, span, side, span) * weights[:, None, :, None]
+    ).reshape(leaf_points, leaf_points)
+    near = jnp.dot(masked, probes, precision=HIGH, preferred_element_type=F32)
+
     keep, *sent = project_high(column_factor_stack, probes)
     _, one, two, three = around([keep, *sent], 4)
-    pair, low1 = project_low(column_factor_stack, probes)
-    got = swap(pair, "leaf", 1)
-    node0, node2 = got[0], pair[1] + got[1]
+    low0, low1, low2 = project_low(column_factor_stack, probes)
+    two_a = swap(low2, "leaf", 3)
+    one_a = swap(low1, "leaf", 2)
+    node0 = swap(low0, "leaf", 1)
+    low2 = low2 + two_a
     part3 = two[:64] + three[:64]
     upper = keep + one + two[64:] + three[64:]
     part4 = swap(upper[:32], "leaf", 16)
     five = upper[32:]
     part5 = swap(five, "leaf", 32) + swap(five, "leaf", 48)
     part = jnp.concatenate([part3, part4, part5])
-    node2 = node2 + swap(node2, "leaf", 2)
+    node2 = low2 + swap(low2, "leaf", 2)
     node2 = swap(node2, "leaf", 4)
+    part, node0, one_a = lax.optimization_barrier((part, node0, one_a))
     part = part + swap(part, "leaf", 1)
+    part, near = lax.optimization_barrier((part, near))
     part = part + swap(part, "leaf", 2)
+    late = prepare(near, row_factor_stack, node0, node2)
+    part, low1, *late = lax.optimization_barrier((part, low1, *late))
     gathered = [swap(part, "leaf", 4), swap(part[64:], "leaf", 8), swap(part[64:], "leaf", 12)]
-    node1 = low1 + swap(low1, "leaf", 1)
-    node1 = swap(node1, "leaf", 2)
-
-    weights = block_mask[0].astype(F32)
-    masked = (
-        leaf_blocks.reshape(side, span, side, span) * weights[:, None, :, None]
-    ).reshape(leaf_points, leaf_points)
-    near = jnp.dot(masked, probes, precision=HIGH, preferred_element_type=F32)
-    applied = expand(near, row_factor_stack, node0, node1, node2, part, *gathered)
+    node1 = one_a + swap(low1, "leaf", 3)
+
+    result, applied = expand(*late, node1, part, *gathered)
 
     far = swap(applied, "probe", 2)
     beside = swap(applied, "probe", 1)
@@ -264,7 +292,7 @@
     blocks = around(cut_y(first, second), 16)
     blocks = around(cut_z(blocks), 1)
     total = (blocks[0] + blocks[1]) + (blocks[2] + blocks[3])
-    return applied, total / (leaf_points * lax.axis_size("leaf"))
+    return result, total / (leaf_points * lax.axis_size("leaf"))
 
 
 def solution(mesh):

time: 133 us -> 133 us (level)
  waiting for transfers between devices: 48.1 us -> 59.2 us
  starting transfers between devices: 67.7 us -> 58.8 us
  local copies, waits for them, and re-layouts: 5.95 us -> 1.73 us
  Pallas kernels: 7.29 us -> 9.03 us
    ppermute x31 -> x32, waiting for transfers between devices: 48.1 us -> 59.2 us  [swap(): return lax.ppermute(value, axis, pairs)]
    ppermute x31 -> x32, starting transfers between devices: 67.7 us -> 58.8 us  [swap(): return lax.ppermute(value, axis, pairs)]
    unnamed x14 -> x10, local copies, waits for them, and re-layouts: 5.6 us -> 1.39 us
    pallas_call x7 -> x8, Pallas kernels: 7.29 us -> 9.03 us  [call(): pl.pallas_call(body, out_shape=outs, grid=grid, in_specs=specs, out_specs...]
  transfers between devices with their start and end apart: 31 -> 32, of which waited for: 17 -> 16; matrix products, arithmetic and copies ran while one was open for 2% -> 2% of each run, Pallas kernels for 1% -> 3%
where the time goes in v3:
time: 133 us
  waiting for transfers between devices  59.2 us (45%)
  starting transfers between devices  58.8 us (44%)
  Pallas kernels  9.03 us (7%)
  matrix products  2.39 us (2%)
  local copies, waits for them, and re-layouts  1.73 us (1%)
    ppermute x32, waiting for transfers between devices, swap(): return lax.ppermute(value, axis, pairs)  59.2 us
    ppermute x32, starting transfers between devices, swap(): return lax.ppermute(value, axis, pairs)  58.8 us
    pallas_call x8, Pallas kernels, call(): pl.pallas_call(body, out_shape=outs, grid=grid, in_specs=specs, out_specs...  9.03 us
  transfers between devices with their start and end apart: 32, of which 16 were waited for; matrix products, arithmetic and copies ran while one was open for 2% of the time, Pallas kernels for 3%

profile of v3, /device:TPU:32, one launch (start us, length us, event | category | flops | bytes accessed | tf_op | source)
XLA Modules:
  0.0 132.8 jit_solution(1567025521438613166)
XLA Ops:
  0.7 1.4 %copy-done.1 = f32[1024,256]{1,0:T(8,128)S(1)} copy-done((f32[1024,256]{1,0:T(8,128)S(1)}, f32[1024,256]{1,0:T(8,128)}, u32[]{:S(2)}) %copy-start.1) | copy-done | bytes 1048600
  2.0 2.3 %shard_map.68 = (f32[64,256]{1,0:T(8,128)S(1)}, f32[64,256]{1,0:T(8,128)S(1)}, f32[128,256]{1,0:T(8,128)S(1)}, f32[128,256]{1,0:T(8,128)S(1)}) custom-call(f32[6,1024,128]{2,1,0:T(8,128)} %c_ref.3, f32[1024,256]{1,0:T(8,128)S(1)} %copy-done.1), custom_call_target="tpu_custom_call" | custom-call | flops 603979776 | bytes 4587520 | tf_op jit(solution)/shard_map/pallas_call | solution.py:49
  4.4 3.1 %collective-permute-start = (f32[128,256]{1,0:T(8,128)S(1)}, f32[128,256]{1,0:T(8,128)S(1)}, u32[]{:S(2)}, u32[]{:S(2)}) collective-permute-start(f32[128,256]{1,0:T(8,128)S(1)} %get-tuple-element.45), channel_id=1, source_target_pairs={{0,32},{4,36},{8,40},{12,44},{16,48},{20,52},{24,56},{28,60},{32,0... | collective-permute-start | bytes 393224 | tf_op jit(solution)/shard_map/ppermute | solution.py:18
  7.5 1.2 collective-permute-start.1
  8.6 0.8 shard_map.69
  9.5 5.5 %collective-permute-start.10 = (f32[128,256]{1,0:T(8,128)S(1)}, f32[128,256]{1,0:T(8,128)S(1)}, u32[]{:S(2)}, u32[]{:S(2)}) collective-permute-start(f32[128,256]{1,0:T(8,128)S(1)} %get-tuple-element.55), channel_id=1, source_target_pairs={{0,12},{4,8},{8,4},{12,0},{16,28},{20,24},{24,20},{28,16},{32,44},... | collective-permute-start | bytes 393224 | tf_op jit(solution)/shard_map/ppermute | solution.py:18
  15.0 3.1 %collective-permute-start.5 = (f32[32,256]{1,0:T(8,128)S(1)}, f32[32,256]{1,0:T(8,128)S(1)}, u32[]{:S(2)}, u32[]{:S(2)}) collective-permute-start(f32[32,256]{1,0:T(8,128)S(1)} %get-tuple-element.91), channel_id=1, source_target_pairs={{0,192},{4,196},{8,200},{12,204},{16,208},{20,212},{24,216},{28,22... | collective-permute-start | bytes 98312 | tf_op jit(solution)/shard_map/ppermute | solution.py:18
  18.1 2.3 %collective-permute-start.6 = (f32[128,256]{1,0:T(8,128)S(1)}, f32[128,256]{1,0:T(8,128)S(1)}, u32[]{:S(2)}, u32[]{:S(2)}) collective-permute-start(f32[128,256]{1,0:T(8,128)S(1)} %get-tuple-element.49), channel_id=1, source_target_pairs={{0,4},{4,0},{8,12},{12,8},{16,20},{20,16},{24,28},{28,24},{32,36},... | collective-permute-start | bytes 393224 | tf_op jit(solution)/shard_map/ppermute | solution.py:18
  20.4 4.5 %collective-permute-start.7 = (f32[128,256]{1,0:T(8,128)S(1)}, f32[128,256]{1,0:T(8,128)S(1)}, u32[]{:S(2)}, u32[]{:S(2)}) collective-permute-start(f32[128,256]{1,0:T(8,128)S(1)} %get-tuple-element.63), channel_id=1, source_target_pairs={{0,8},{4,12},{8,0},{12,4},{16,24},{20,28},{24,16},{28,20},{32,40},... | collective-permute-start | bytes 393224 | tf_op jit(solution)/shard_map/ppermute | solution.py:18
  24.9 0.6 collective-permute-start.4
  26.0 1.5 %collective-permute-start.11 = (f32[128,256]{1,0:T(8,128)S(1)}, f32[128,256]{1,0:T(8,128)S(1)}, u32[]{:S(2)}, u32[]{:S(2)}) collective-permute-start(f32[128,256]{1,0:T(8,128)S(1)} %add.46), channel_id=1, source_target_pairs={{0,8},{4,12},{8,0},{12,4},{16,24},{20,28},{24,16},{28,20},{32,40},... | collective-permute-start | bytes 393224 | tf_op jit(solution)/shard_map/ppermute | solution.py:18
  27.6 2.8 %collective-permute-done.4 = f32[32,256]{1,0:T(8,128)S(1)} collective-permute-done((f32[32,256]{1,0:T(8,128)S(1)}, f32[32,256]{1,0:T(8,128)S(1)}, u32[]{:S(2)}, u32[]{:S(2)}) %collective-permute-start.4) | collective-permute-done | bytes 32800 | tf_op jit(solution)/shard_map/ppermute | solution.py:18
  30.4 8.6 %collective-permute-done.6.z_ref = f32[128,256]{1,0:T(8,128)S(1)} collective-permute-done((f32[128,256]{1,0:T(8,128)S(1)}, f32[128,256]{1,0:T(8,128)S(1)}, u32[]{:S(2)}, u32[]{:S(2)}) %collective-permute-start.6) | collective-permute-done | bytes 131104 | tf_op jit(solution)/shard_map/ppermute | solution.py:18
  38.9 3.4 %collective-permute-start.8 = (f32[128,256]{1,0:T(8,128)S(1)}, f32[128,256]{1,0:T(8,128)S(1)}, u32[]{:S(2)}, u32[]{:S(2)}) collective-permute-start(f32[128,256]{1,0:T(8,128)S(1)} %pad_maximum_fusion), channel_id=1, source_target_pairs={{0,4},{4,0},{8,12},{12,8},{16,20},{20,16},{24,28},{28,24},{32,36},... | collective-permute-start | bytes 393224 | tf_op jit(solution)/shard_map/ppermute | solution.py:18
  42.3 2.2 %collective-permute-start.12 = (f32[128,256]{1,0:T(8,128)S(1)}, f32[128,256]{1,0:T(8,128)S(1)}, u32[]{:S(2)}, u32[]{:S(2)}) collective-permute-start(f32[128,256]{1,0:T(8,128)S(1)} %add.47), channel_id=1, source_target_pairs={{0,16},{4,20},{8,24},{12,28},{16,0},{20,4},{24,8},{28,12},{32,48},... | collective-permute-start | bytes 393224 | tf_op jit(solution)/shard_map/ppermute | solution.py:18
  44.9 2.4 %fusion.n_ref = f32[1024,256]{1,0:T(8,128)S(1)} fusion(f32[1024,256]{1,0:T(8,128)S(1)} %copy-done.1, f32[1024,1024]{1,0:T(8,128)S(1)} %copy-done.3, f32[128,8,8,128]{3,2,1,0:T(8,128)S(1)} %bitcast.8), kind=kOutput, calls=%fused_computation.1 | convolution fusion | flops 1611661312 | bytes 10485760 | tf_op jit(solution)/shard_map/dot_general | solution.py:258
  47.4 2.1 %collective-permute-start.9 = (f32[128,256]{1,0:T(8,128)S(1)}, f32[128,256]{1,0:T(8,128)S(1)}, u32[]{:S(2)}, u32[]{:S(2)}) collective-permute-start(f32[128,256]{1,0:T(8,128)S(1)} %add.44), channel_id=1, source_target_pairs={{0,8},{4,12},{8,0},{12,4},{16,24},{20,28},{24,16},{28,20},{32,40},... | collective-permute-start | bytes 393224 | tf_op jit(solution)/shard_map/ppermute | solution.py:18
  49.5 1.6 %shard_map.70 = (f32[1024,256]{1,0:T(8,128)S(1)}, bf16[1024,512]{1,0:T(8,128)(2,1)S(1)}, bf16[1024,512]{1,0:T(8,128)(2,1)S(1)}) custom-call(f32[1024,256]{1,0:T(8,128)S(1)} %fusion.n_ref, f32[6,1024,128]{2,1,0:T(8,128)S(1)} %copy-done.2, f32[128,256]{1,0:T(8,128)S(1)} %collective-permute-done.6.z_ref, f32[128,256]{1,0:T(8,128)S(1)} %collective-permute-done.12.t_ref), custom_call_target="tpu_custom_call" | custom-call | flops 402653184 | bytes 9699328 | tf_op jit(solution)/shard_map/pallas_call | solution.py:49
  51.1 7.6 %collective-permute-done.9 = f32[128,256]{1,0:T(8,128)S(1)} collective-permute-done((f32[128,256]{1,0:T(8,128)S(1)}, f32[128,256]{1,0:T(8,128)S(1)}, u32[]{:S(2)}, u32[]{:S(2)}) %collective-permute-start.9) | collective-permute-done | bytes 131104 | tf_op jit(solution)/shard_map/ppermute | solution.py:18
  59.0 4.6 %collective-permute-start.14 = (f32[128,256]{1,0:T(8,128)S(1)}, f32[128,256]{1,0:T(8,128)S(1)}, u32[]{:S(2)}, u32[]{:S(2)}) collective-permute-start(f32[128,256]{1,0:T(8,128)S(1)} %add.45.q0), channel_id=1, source_target_pairs={{0,16},{4,20},{8,24},{12,28},{16,0},{20,4},{24,8},{28,12},{32,48},... | collective-permute-start | bytes 393224 | tf_op jit(solution)/shard_map/ppermute | solution.py:18
  63.6 1.5 %collective-permute-start.16 = (f32[64,256]{1,0:T(8,128)S(1)}, f32[64,256]{1,0:T(8,128)S(1)}, u32[]{:S(2)}, u32[]{:S(2)}) collective-permute-start(f32[64,256]{1,0:T(8,128)S(1)} %slice.28), channel_id=1, source_target_pairs={{0,48},{4,52},{8,56},{12,60},{16,32},{20,36},{24,40},{28,44},{32,1... | collective-permute-start | bytes 196616 | tf_op jit(solution)/shard_map/ppermute | solution.py:18
  65.1 1.5 %collective-permute-start.15 = (f32[64,256]{1,0:T(8,128)S(1)}, f32[64,256]{1,0:T(8,128)S(1)}, u32[]{:S(2)}, u32[]{:S(2)}) collective-permute-start(f32[64,256]{1,0:T(8,128)S(1)} %slice.28), channel_id=1, source_target_pairs={{0,32},{4,36},{8,40},{12,44},{16,48},{20,52},{24,56},{28,60},{32,0... | collective-permute-start | bytes 196616 | tf_op jit(solution)/shard_map/ppermute | solution.py:18
  67.1 2.5 %collective-permute-done.16.q3 = f32[64,256]{1,0:T(8,128)S(1)} collective-permute-done((f32[64,256]{1,0:T(8,128)S(1)}, f32[64,256]{1,0:T(8,128)S(1)}, u32[]{:S(2)}, u32[]{:S(2)}) %collective-permute-start.16) | collective-permute-done | bytes 65568 | tf_op jit(solution)/shard_map/ppermute | solution.py:18
  69.6 1.3 collective-permute-done.15.q2
  70.9 2.0 %shard_map.71 = (f32[1024,256]{1,0:T(8,128)}, f32[1024,256]{1,0:T(8,128)S(1)}) custom-call(f32[1024,256]{1,0:T(8,128)S(1)} %get-tuple-element.59.b_ref, bf16[1024,512]{1,0:T(8,128)(2,1)S(1)} %get-tuple-element.60.h_ref, bf16[1024,512]{1,0:T(8,128)(2,1)S(1)} %get-tuple-element.61.l_ref, f32[128,256]{1,0:T(8,128)S(1)} %add.48.o_ref, f32[128,256]{1,0:T(8,128)S(1)} %add.45.q0, ...), custom_call_target="tpu_custom_call" | custom-call | flops 805306368 | bytes 7864320 | tf_op jit(solution)/shard_map/pallas_call | solution.py:49
  72.9 2.7 %collective-permute-done.18.refs_1_ = f32[1024,256]{1,0:T(8,128)S(1)} collective-permute-done((f32[1024,256]{1,0:T(8,128)S(1)}, f32[1024,256]{1,0:T(8,128)S(1)}, u32[]{:S(2)}, u32[]{:S(2)}) %collective-permute-start.18) | collective-permute-done | bytes 1048608 | tf_op jit(solution)/shard_map/ppermute | solution.py:18
  75.5 1.1 shard_map.72
  76.6 1.4 %collective-permute-start.19 = (f32[2,64,256]{2,1,0:T(8,128)S(1)}, f32[2,64,256]{2,1,0:T(8,128)S(1)}, u32[]{:S(2)}, u32[]{:S(2)}) collective-permute-start(f32[2,64,256]{2,1,0:T(8,128)S(1)} %get-tuple-element.68), channel_id=1, source_target_pairs={{0,16},{4,20},{8,24},{12,28},{16,0},{20,4},{24,8},{28,12},{32,48},... | collective-permute-start | bytes 393224 | tf_op jit(solution)/shard_map/ppermute | solution.py:18
  78.0 1.9 %collective-permute-start.20 = (f32[2,64,256]{2,1,0:T(8,128)S(1)}, f32[2,64,256]{2,1,0:T(8,128)S(1)}, u32[]{:S(2)}, u32[]{:S(2)}) collective-permute-start(f32[2,64,256]{2,1,0:T(8,128)S(1)} %get-tuple-element.69), channel_id=1, source_target_pairs={{0,32},{4,36},{8,40},{12,44},{16,48},{20,52},{24,56},{28,60},{32,0... | collective-permute-start | bytes 393224 | tf_op jit(solution)/shard_map/ppermute | solution.py:18
  79.9 1.5 %collective-permute-start.21 = (f32[2,64,256]{2,1,0:T(8,128)S(1)}, f32[2,64,256]{2,1,0:T(8,128)S(1)}, u32[]{:S(2)}, u32[]{:S(2)}) collective-permute-start(f32[2,64,256]{2,1,0:T(8,128)S(1)} %get-tuple-element.70), channel_id=1, source_target_pairs={{0,48},{4,52},{8,56},{12,60},{16,32},{20,36},{24,40},{28,44},{32,1... | collective-permute-start | bytes 393224 | tf_op jit(solution)/shard_map/ppermute | solution.py:18
  81.4 17.0 %collective-permute-done.17.refs_1_ = f32[1024,256]{1,0:T(8,128)S(1)} collective-permute-done((f32[1024,256]{1,0:T(8,128)S(1)}, f32[1024,256]{1,0:T(8,128)S(1)}, u32[]{:S(2)}, u32[]{:S(2)}) %collective-permute-start.17) | collective-permute-done | bytes 1048608 | tf_op jit(solution)/shard_map/ppermute | solution.py:18
  98.6 2.6 %collective-permute-done.22.refs_2_ = f32[1024,256]{1,0:T(8,128)S(1)} collective-permute-done((f32[1024,256]{1,0:T(8,128)S(1)}, f32[1024,256]{1,0:T(8,128)S(1)}, u32[]{:S(2)}, u32[]{:S(2)}) %collective-permute-start.22) | collective-permute-done | bytes 1048608 | tf_op jit(solution)/shard_map/ppermute | solution.py:18
  101.2 1.1 shard_map.73
  102.3 1.4 %collective-permute-start.23 = (f32[2,64,256]{2,1,0:T(8,128)S(1)}, f32[2,64,256]{2,1,0:T(8,128)S(1)}, u32[]{:S(2)}, u32[]{:S(2)}) collective-permute-start(f32[2,64,256]{2,1,0:T(8,128)S(1)} %get-tuple-element.77), channel_id=1, source_target_pairs={{0,16},{4,20},{8,24},{12,28},{16,0},{20,4},{24,8},{28,12},{32,48},... | collective-permute-start | bytes 393224 | tf_op jit(solution)/shard_map/ppermute | solution.py:18
  103.7 1.9 %collective-permute-start.24 = (f32[2,64,256]{2,1,0:T(8,128)S(1)}, f32[2,64,256]{2,1,0:T(8,128)S(1)}, u32[]{:S(2)}, u32[]{:S(2)}) collective-permute-start(f32[2,64,256]{2,1,0:T(8,128)S(1)} %get-tuple-element.78), channel_id=1, source_target_pairs={{0,32},{4,36},{8,40},{12,44},{16,48},{20,52},{24,56},{28,60},{32,0... | collective-permute-start | bytes 393224 | tf_op jit(solution)/shard_map/ppermute | solution.py:18
  105.5 1.5 %collective-permute-start.25 = (f32[2,64,256]{2,1,0:T(8,128)S(1)}, f32[2,64,256]{2,1,0:T(8,128)S(1)}, u32[]{:S(2)}, u32[]{:S(2)}) collective-permute-start(f32[2,64,256]{2,1,0:T(8,128)S(1)} %get-tuple-element.79), channel_id=1, source_target_pairs={{0,48},{4,52},{8,56},{12,60},{16,32},{20,36},{24,40},{28,44},{32,1... | collective-permute-start | bytes 393224 | tf_op jit(solution)/shard_map/ppermute | solution.py:18
  107.1 1.6 %collective-permute-done.23.refs_5_ = f32[2,64,256]{2,1,0:T(8,128)S(1)} collective-permute-done((f32[2,64,256]{2,1,0:T(8,128)S(1)}, f32[2,64,256]{2,1,0:T(8,128)S(1)}, u32[]{:S(2)}, u32[]{:S(2)}) %collective-permute-start.23) | collective-permute-done | bytes 131104 | tf_op jit(solution)/shard_map/ppermute | solution.py:18
  108.7 3.2 %collective-permute-done.24.refs_6_ = f32[2,64,256]{2,1,0:T(8,128)S(1)} collective-permute-done((f32[2,64,256]{2,1,0:T(8,128)S(1)}, f32[2,64,256]{2,1,0:T(8,128)S(1)}, u32[]{:S(2)}, u32[]{:S(2)}) %collective-permute-start.24) | collective-permute-done | bytes 131104 | tf_op jit(solution)/shard_map/ppermute | solution.py:18
  112.0 2.2 %collective-permute-done.25.refs_7_ = f32[2,64,256]{2,1,0:T(8,128)S(1)} collective-permute-done((f32[2,64,256]{2,1,0:T(8,128)S(1)}, f32[2,64,256]{2,1,0:T(8,128)S(1)}, u32[]{:S(2)}, u32[]{:S(2)}) %collective-permute-start.25) | collective-permute-done | bytes 131104 | tf_op jit(solution)/shard_map/ppermute | solution.py:18
  114.5 4.6 %collective-permute-start.28 = (f32[64,256]{1,0:T(8,128)S(1)}, f32[64,256]{1,0:T(8,128)S(1)}, u32[]{:S(2)}, u32[]{:S(2)}) collective-permute-start(f32[64,256]{1,0:T(8,128)S(1)} %get-tuple-element.83), channel_id=1, source_target_pairs={{0,192},{4,196},{8,200},{12,204},{16,208},{20,212},{24,216},{28,22... | collective-permute-start | bytes 196616 | tf_op jit(solution)/shard_map/ppermute | solution.py:18
  119.1 1.2 collective-permute-done.27.refs_2_
  120.2 1.1 collective-permute-done.28.refs_3_
  121.3 1.8 %collective-permute-start.29 = (f32[16,256]{1,0:T(8,128)S(1)}, f32[16,256]{1,0:T(8,128)S(1)}, u32[]{:S(2)}, u32[]{:S(2)}) collective-permute-start(f32[16,256]{1,0:T(8,128)S(1)} %get-tuple-element.85), channel_id=1, source_target_pairs={{0,4},{4,0},{8,12},{12,8},{16,20},{20,16},{24,28},{28,24},{32,36},... | collective-permute-start | bytes 49160 | tf_op jit(solution)/shard_map/ppermute | solution.py:18
  123.1 3.2 %collective-permute-start.30 = (f32[16,256]{1,0:T(8,128)S(1)}, f32[16,256]{1,0:T(8,128)S(1)}, u32[]{:S(2)}, u32[]{:S(2)}) collective-permute-start(f32[16,256]{1,0:T(8,128)S(1)} %get-tuple-element.86), channel_id=1, source_target_pairs={{0,8},{4,12},{8,0},{12,4},{16,24},{20,28},{24,16},{28,20},{32,40},... | collective-permute-start | bytes 49160 | tf_op jit(solution)/shard_map/ppermute | solution.py:18
  126.3 1.6 %collective-permute-start.31 = (f32[16,256]{1,0:T(8,128)S(1)}, f32[16,256]{1,0:T(8,128)S(1)}, u32[]{:S(2)}, u32[]{:S(2)}) collective-permute-start(f32[16,256]{1,0:T(8,128)S(1)} %get-tuple-element.87), channel_id=1, source_target_pairs={{0,12},{4,8},{8,4},{12,0},{16,28},{20,24},{24,20},{28,16},{32,44},... | collective-permute-start | bytes 49160 | tf_op jit(solution)/shard_map/ppermute | solution.py:18
  127.9 2.8 %collective-permute-done.30 = f32[16,256]{1,0:T(8,128)S(1)} collective-permute-done((f32[16,256]{1,0:T(8,128)S(1)}, f32[16,256]{1,0:T(8,128)S(1)}, u32[]{:S(2)}, u32[]{:S(2)}) %collective-permute-start.30) | collective-permute-done | bytes 16416 | tf_op jit(solution)/shard_map/ppermute | solution.py:18
  130.7 1.4 %collective-permute-done.31 = f32[16,256]{1,0:T(8,128)S(1)} collective-permute-done((f32[16,256]{1,0:T(8,128)S(1)}, f32[16,256]{1,0:T(8,128)S(1)}, u32[]{:S(2)}, u32[]{:S(2)}) %collective-permute-start.31) | collective-permute-done | bytes 16416 | tf_op jit(solution)/shard_map/ppermute | solution.py:18
  132.2 0.6 add_multiply_fusion
  (48 shorter events, 2.1 us)
Async XLA Ops:
  0.6 8.0 %copy-start = (f32[6,1024,128]{2,1,0:T(8,128)S(1)}, f32[6,1024,128]{2,1,0:T(8,128)}, u32[]{:S(2)}) copy-start(f32[6,1024,128]{2,1,0:T(8,128)} %c_ref.3) | copy-start | bytes 9437188
  0.6 1.4 %copy-start.1 = (f32[1024,256]{1,0:T(8,128)S(1)}, f32[1024,256]{1,0:T(8,128)}, u32[]{:S(2)}) copy-start(f32[1024,256]{1,0:T(8,128)} %p_ref.3) | copy-start | bytes 3145732
  2.0 25.5 %copy-start.4 = (s32[1,8,8]{2,1,0:T(8,128)S(1)}, s32[1,8,8]{2,1,0:T(8,128)}, u32[]{:S(2)}) copy-start(s32[1,8,8]{2,1,0:T(8,128)} %param.6) | copy-start | bytes 772
  4.4 10.6 %collective-permute-start = (f32[128,256]{1,0:T(8,128)S(1)}, f32[128,256]{1,0:T(8,128)S(1)}, u32[]{:S(2)}, u32[]{:S(2)}) collective-permute-start(f32[128,256]{1,0:T(8,128)S(1)} %get-tuple-element.45), channel_id=1, source_target_pairs={{0,32},{4,36},{8,40},{12,44},{16,48},{20,52},{24,56},{28,60},{32,0... | collective-permute-start | bytes 393224 | tf_op jit(solution)/shard_map/ppermute | solution.py:18
  7.5 7.5 %collective-permute-start.1 = (f32[128,256]{1,0:T(8,128)S(1)}, f32[128,256]{1,0:T(8,128)S(1)}, u32[]{:S(2)}, u32[]{:S(2)}) collective-permute-start(f32[128,256]{1,0:T(8,128)S(1)} %get-tuple-element.46), channel_id=1, source_target_pairs={{0,48},{4,52},{8,56},{12,60},{16,32},{20,36},{24,40},{28,44},{32,1... | collective-permute-start | bytes 393224 | tf_op jit(solution)/shard_map/ppermute | solution.py:18
  8.6 36.3 %copy-start.3 = (f32[1024,1024]{1,0:T(8,128)S(1)}, f32[1024,1024]{1,0:T(8,128)}, u32[]{:S(2)}) copy-start(f32[1024,1024]{1,0:T(8,128)} %param.5) | copy-start | bytes 12582916
  8.6 6.3 %collective-permute-start.2 = (f32[64,256]{1,0:T(8,128)S(1)}, f32[64,256]{1,0:T(8,128)S(1)}, u32[]{:S(2)}, u32[]{:S(2)}) collective-permute-start(f32[64,256]{1,0:T(8,128)S(1)} %get-tuple-element.48), channel_id=1, source_target_pairs={{0,16},{4,20},{8,24},{12,28},{16,0},{20,4},{24,8},{28,12},{32,48},... | collective-permute-start | bytes 196616 | tf_op jit(solution)/shard_map/ppermute | solution.py:18
  9.5 16.1 %collective-permute-start.10 = (f32[128,256]{1,0:T(8,128)S(1)}, f32[128,256]{1,0:T(8,128)S(1)}, u32[]{:S(2)}, u32[]{:S(2)}) collective-permute-start(f32[128,256]{1,0:T(8,128)S(1)} %get-tuple-element.55), channel_id=1, source_target_pairs={{0,12},{4,8},{8,4},{12,0},{16,28},{20,24},{24,20},{28,16},{32,44},... | collective-permute-start | bytes 393224 | tf_op jit(solution)/shard_map/ppermute | solution.py:18
  15.0 11.0 %collective-permute-start.5 = (f32[32,256]{1,0:T(8,128)S(1)}, f32[32,256]{1,0:T(8,128)S(1)}, u32[]{:S(2)}, u32[]{:S(2)}) collective-permute-start(f32[32,256]{1,0:T(8,128)S(1)} %get-tuple-element.91), channel_id=1, source_target_pairs={{0,192},{4,196},{8,200},{12,204},{16,208},{20,212},{24,216},{28,22... | collective-permute-start | bytes 98312 | tf_op jit(solution)/shard_map/ppermute | solution.py:18
  18.1 20.8 %collective-permute-start.6 = (f32[128,256]{1,0:T(8,128)S(1)}, f32[128,256]{1,0:T(8,128)S(1)}, u32[]{:S(2)}, u32[]{:S(2)}) collective-permute-start(f32[128,256]{1,0:T(8,128)S(1)} %get-tuple-element.49), channel_id=1, source_target_pairs={{0,4},{4,0},{8,12},{12,8},{16,20},{20,16},{24,28},{28,24},{32,36},... | collective-permute-start | bytes 393224 | tf_op jit(solution)/shard_map/ppermute | solution.py:18
  20.4 18.5 %collective-permute-start.7 = (f32[128,256]{1,0:T(8,128)S(1)}, f32[128,256]{1,0:T(8,128)S(1)}, u32[]{:S(2)}, u32[]{:S(2)}) collective-permute-start(f32[128,256]{1,0:T(8,128)S(1)} %get-tuple-element.63), channel_id=1, source_target_pairs={{0,8},{4,12},{8,0},{12,4},{16,24},{20,28},{24,16},{28,20},{32,40},... | collective-permute-start | bytes 393224 | tf_op jit(solution)/shard_map/ppermute | solution.py:18
  24.9 5.4 %collective-permute-start.4 = (f32[32,256]{1,0:T(8,128)S(1)}, f32[32,256]{1,0:T(8,128)S(1)}, u32[]{:S(2)}, u32[]{:S(2)}) collective-permute-start(f32[32,256]{1,0:T(8,128)S(1)} %get-tuple-element.91), channel_id=1, source_target_pairs={{0,128},{4,132},{8,136},{12,140},{16,144},{20,148},{24,152},{28,15... | collective-permute-start | bytes 98312 | tf_op jit(solution)/shard_map/ppermute | solution.py:18
  25.5 4.8 %collective-permute-start.3 = (f32[32,256]{1,0:T(8,128)S(1)}, f32[32,256]{1,0:T(8,128)S(1)}, u32[]{:S(2)}, u32[]{:S(2)}) collective-permute-start(f32[32,256]{1,0:T(8,128)S(1)} %get-tuple-element.90), channel_id=1, source_target_pairs={{0,64},{4,68},{8,72},{12,76},{16,80},{20,84},{24,88},{28,92},{32,9... | collective-permute-start | bytes 98312 | tf_op jit(solution)/shard_map/ppermute | solution.py:18
  26.0 16.3 %collective-permute-start.11 = (f32[128,256]{1,0:T(8,128)S(1)}, f32[128,256]{1,0:T(8,128)S(1)}, u32[]{:S(2)}, u32[]{:S(2)}) collective-permute-start(f32[128,256]{1,0:T(8,128)S(1)} %add.46), channel_id=1, source_target_pairs={{0,8},{4,12},{8,0},{12,4},{16,24},{20,28},{24,16},{28,20},{32,40},... | collective-permute-start | bytes 393224 | tf_op jit(solution)/shard_map/ppermute | solution.py:18
  38.9 8.4 %collective-permute-start.8 = (f32[128,256]{1,0:T(8,128)S(1)}, f32[128,256]{1,0:T(8,128)S(1)}, u32[]{:S(2)}, u32[]{:S(2)}) collective-permute-start(f32[128,256]{1,0:T(8,128)S(1)} %pad_maximum_fusion), channel_id=1, source_target_pairs={{0,4},{4,0},{8,12},{12,8},{16,20},{20,16},{24,28},{28,24},{32,36},... | collective-permute-start | bytes 393224 | tf_op jit(solution)/shard_map/ppermute | solution.py:18
  42.3 7.1 %collective-permute-start.12 = (f32[128,256]{1,0:T(8,128)S(1)}, f32[128,256]{1,0:T(8,128)S(1)}, u32[]{:S(2)}, u32[]{:S(2)}) collective-permute-start(f32[128,256]{1,0:T(8,128)S(1)} %add.47), channel_id=1, source_target_pairs={{0,16},{4,20},{8,24},{12,28},{16,0},{20,4},{24,8},{28,12},{32,48},... | collective-permute-start | bytes 393224 | tf_op jit(solution)/shard_map/ppermute | solution.py:18
  44.9 4.6 %copy-start.2 = (f32[6,1024,128]{2,1,0:T(8,128)S(1)}, f32[6,1024,128]{2,1,0:T(8,128)}, u32[]{:S(2)}) copy-start(f32[6,1024,128]{2,1,0:T(8,128)} %u_ref.1) | copy-start | bytes 9437188
  47.4 11.3 %collective-permute-start.9 = (f32[128,256]{1,0:T(8,128)S(1)}, f32[128,256]{1,0:T(8,128)S(1)}, u32[]{:S(2)}, u32[]{:S(2)}) collective-permute-start(f32[128,256]{1,0:T(8,128)S(1)} %add.44), channel_id=1, source_target_pairs={{0,8},{4,12},{8,0},{12,4},{16,24},{20,28},{24,16},{28,20},{32,40},... | collective-permute-start | bytes 393224 | tf_op jit(solution)/shard_map/ppermute | solution.py:18
  58.7 8.3 %collective-permute-start.13 = (f32[128,256]{1,0:T(8,128)S(1)}, f32[128,256]{1,0:T(8,128)S(1)}, u32[]{:S(2)}, u32[]{:S(2)}) collective-permute-start(f32[128,256]{1,0:T(8,128)S(1)} %get-tuple-element.63), channel_id=1, source_target_pairs={{0,12},{4,8},{8,4},{12,0},{16,28},{20,24},{24,20},{28,16},{32,44},... | collective-permute-start | bytes 393224 | tf_op jit(solution)/shard_map/ppermute | solution.py:18
  59.0 11.9 %collective-permute-start.14 = (f32[128,256]{1,0:T(8,128)S(1)}, f32[128,256]{1,0:T(8,128)S(1)}, u32[]{:S(2)}, u32[]{:S(2)}) collective-permute-start(f32[128,256]{1,0:T(8,128)S(1)} %add.45.q0), channel_id=1, source_target_pairs={{0,16},{4,20},{8,24},{12,28},{16,0},{20,4},{24,8},{28,12},{32,48},... | collective-permute-start | bytes 393224 | tf_op jit(solution)/shard_map/ppermute | solution.py:18
  63.6 6.0 %collective-permute-start.16 = (f32[64,256]{1,0:T(8,128)S(1)}, f32[64,256]{1,0:T(8,128)S(1)}, u32[]{:S(2)}, u32[]{:S(2)}) collective-permute-start(f32[64,256]{1,0:T(8,128)S(1)} %slice.28), channel_id=1, source_target_pairs={{0,48},{4,52},{8,56},{12,60},{16,32},{20,36},{24,40},{28,44},{32,1... | collective-permute-start | bytes 196616 | tf_op jit(solution)/shard_map/ppermute | solution.py:18
  65.1 5.8 %collective-permute-start.15 = (f32[64,256]{1,0:T(8,128)S(1)}, f32[64,256]{1,0:T(8,128)S(1)}, u32[]{:S(2)}, u32[]{:S(2)}) collective-permute-start(f32[64,256]{1,0:T(8,128)S(1)} %slice.28), channel_id=1, source_target_pairs={{0,32},{4,36},{8,40},{12,44},{16,48},{20,52},{24,56},{28,60},{32,0... | collective-permute-start | bytes 196616 | tf_op jit(solution)/shard_map/ppermute | solution.py:18
  72.9 2.7 %collective-permute-start.18 = (f32[1024,256]{1,0:T(8,128)S(1)}, f32[1024,256]{1,0:T(8,128)S(1)}, u32[]{:S(2)}, u32[]{:S(2)}) collective-permute-start(f32[1024,256]{1,0:T(8,128)S(1)} %get-tuple-element.66.refs_0_), channel_id=1, source_target_pairs={{0,1},{1,0},{2,3},{3,2},{4,5},{5,4},{6,7},{7,6},{8,9},{9,8},{10,11... | collective-permute-start | bytes 3145736 | tf_op jit(solution)/shard_map/ppermute | solution.py:18
  72.9 25.6 %collective-permute-start.17 = (f32[1024,256]{1,0:T(8,128)S(1)}, f32[1024,256]{1,0:T(8,128)S(1)}, u32[]{:S(2)}, u32[]{:S(2)}) collective-permute-start(f32[1024,256]{1,0:T(8,128)S(1)} %get-tuple-element.66.refs_0_), channel_id=1, source_target_pairs={{0,2},{1,3},{2,0},{3,1},{4,6},{5,7},{6,4},{7,5},{8,10},{9,11},{10,... | collective-permute-start | bytes 3145736 | tf_op jit(solution)/shard_map/ppermute | solution.py:18
  76.6 21.8 %collective-permute-start.19 = (f32[2,64,256]{2,1,0:T(8,128)S(1)}, f32[2,64,256]{2,1,0:T(8,128)S(1)}, u32[]{:S(2)}, u32[]{:S(2)}) collective-permute-start(f32[2,64,256]{2,1,0:T(8,128)S(1)} %get-tuple-element.68), channel_id=1, source_target_pairs={{0,16},{4,20},{8,24},{12,28},{16,0},{20,4},{24,8},{28,12},{32,48},... | collective-permute-start | bytes 393224 | tf_op jit(solution)/shard_map/ppermute | solution.py:18
  78.0 20.4 %collective-permute-start.20 = (f32[2,64,256]{2,1,0:T(8,128)S(1)}, f32[2,64,256]{2,1,0:T(8,128)S(1)}, u32[]{:S(2)}, u32[]{:S(2)}) collective-permute-start(f32[2,64,256]{2,1,0:T(8,128)S(1)} %get-tuple-element.69), channel_id=1, source_target_pairs={{0,32},{4,36},{8,40},{12,44},{16,48},{20,52},{24,56},{28,60},{32,0... | collective-permute-start | bytes 393224 | tf_op jit(solution)/shard_map/ppermute | solution.py:18
  79.9 18.6 %collective-permute-start.21 = (f32[2,64,256]{2,1,0:T(8,128)S(1)}, f32[2,64,256]{2,1,0:T(8,128)S(1)}, u32[]{:S(2)}, u32[]{:S(2)}) collective-permute-start(f32[2,64,256]{2,1,0:T(8,128)S(1)} %get-tuple-element.70), channel_id=1, source_target_pairs={{0,48},{4,52},{8,56},{12,60},{16,32},{20,36},{24,40},{28,44},{32,1... | collective-permute-start | bytes 393224 | tf_op jit(solution)/shard_map/ppermute | solution.py:18
  98.5 2.7 %collective-permute-start.22 = (f32[1024,256]{1,0:T(8,128)S(1)}, f32[1024,256]{1,0:T(8,128)S(1)}, u32[]{:S(2)}, u32[]{:S(2)}) collective-permute-start(f32[1024,256]{1,0:T(8,128)S(1)} %collective-permute-done.17.refs_1_), channel_id=1, source_target_pairs={{0,1},{1,0},{2,3},{3,2},{4,5},{5,4},{6,7},{7,6},{8,9},{9,8},{10,11... | collective-permute-start | bytes 3145736 | tf_op jit(solution)/shard_map/ppermute | solution.py:18
  102.3 6.4 %collective-permute-start.23 = (f32[2,64,256]{2,1,0:T(8,128)S(1)}, f32[2,64,256]{2,1,0:T(8,128)S(1)}, u32[]{:S(2)}, u32[]{:S(2)}) collective-permute-start(f32[2,64,256]{2,1,0:T(8,128)S(1)} %get-tuple-element.77), channel_id=1, source_target_pairs={{0,16},{4,20},{8,24},{12,28},{16,0},{20,4},{24,8},{28,12},{32,48},... | collective-permute-start | bytes 393224 | tf_op jit(solution)/shard_map/ppermute | solution.py:18
  103.7 8.3 %collective-permute-start.24 = (f32[2,64,256]{2,1,0:T(8,128)S(1)}, f32[2,64,256]{2,1,0:T(8,128)S(1)}, u32[]{:S(2)}, u32[]{:S(2)}) collective-permute-start(f32[2,64,256]{2,1,0:T(8,128)S(1)} %get-tuple-element.78), channel_id=1, source_target_pairs={{0,32},{4,36},{8,40},{12,44},{16,48},{20,52},{24,56},{28,60},{32,0... | collective-permute-start | bytes 393224 | tf_op jit(solution)/shard_map/ppermute | solution.py:18
  105.5 8.7 %collective-permute-start.25 = (f32[2,64,256]{2,1,0:T(8,128)S(1)}, f32[2,64,256]{2,1,0:T(8,128)S(1)}, u32[]{:S(2)}, u32[]{:S(2)}) collective-permute-start(f32[2,64,256]{2,1,0:T(8,128)S(1)} %get-tuple-element.79), channel_id=1, source_target_pairs={{0,48},{4,52},{8,56},{12,60},{16,32},{20,36},{24,40},{28,44},{32,1... | collective-permute-start | bytes 393224 | tf_op jit(solution)/shard_map/ppermute | solution.py:18
  114.3 4.8 %collective-permute-start.26 = (f32[64,256]{1,0:T(8,128)S(1)}, f32[64,256]{1,0:T(8,128)S(1)}, u32[]{:S(2)}, u32[]{:S(2)}) collective-permute-start(f32[64,256]{1,0:T(8,128)S(1)} %get-tuple-element.81), channel_id=1, source_target_pairs={{0,64},{4,68},{8,72},{12,76},{16,80},{20,84},{24,88},{28,92},{32,9... | collective-permute-start | bytes 196616 | tf_op jit(solution)/shard_map/ppermute | solution.py:18
  114.4 5.9 %collective-permute-start.27 = (f32[64,256]{1,0:T(8,128)S(1)}, f32[64,256]{1,0:T(8,128)S(1)}, u32[]{:S(2)}, u32[]{:S(2)}) collective-permute-start(f32[64,256]{1,0:T(8,128)S(1)} %get-tuple-element.82), channel_id=1, source_target_pairs={{0,128},{4,132},{8,136},{12,140},{16,144},{20,148},{24,152},{28,15... | collective-permute-start | bytes 196616 | tf_op jit(solution)/shard_map/ppermute | solution.py:18
  114.5 6.8 %collective-permute-start.28 = (f32[64,256]{1,0:T(8,128)S(1)}, f32[64,256]{1,0:T(8,128)S(1)}, u32[]{:S(2)}, u32[]{:S(2)}) collective-permute-start(f32[64,256]{1,0:T(8,128)S(1)} %get-tuple-element.83), channel_id=1, source_target_pairs={{0,192},{4,196},{8,200},{12,204},{16,208},{20,212},{24,216},{28,22... | collective-permute-start | bytes 196616 | tf_op jit(solution)/shard_map/ppermute | solution.py:18
  121.3 6.6 %collective-permute-start.29 = (f32[16,256]{1,0:T(8,128)S(1)}, f32[16,256]{1,0:T(8,128)S(1)}, u32[]{:S(2)}, u32[]{:S(2)}) collective-permute-start(f32[16,256]{1,0:T(8,128)S(1)} %get-tuple-element.85), channel_id=1, source_target_pairs={{0,4},{4,0},{8,12},{12,8},{16,20},{20,16},{24,28},{28,24},{32,36},... | collective-permute-start | bytes 49160 | tf_op jit(solution)/shard_map/ppermute | solution.py:18
  123.1 7.6 %collective-permute-start.30 = (f32[16,256]{1,0:T(8,128)S(1)}, f32[16,256]{1,0:T(8,128)S(1)}, u32[]{:S(2)}, u32[]{:S(2)}) collective-permute-start(f32[16,256]{1,0:T(8,128)S(1)} %get-tuple-element.86), channel_id=1, source_target_pairs={{0,8},{4,12},{8,0},{12,4},{16,24},{20,28},{24,16},{28,20},{32,40},... | collective-permute-start | bytes 49160 | tf_op jit(solution)/shard_map/ppermute | solution.py:18
  126.3 5.8 %collective-permute-start.31 = (f32[16,256]{1,0:T(8,128)S(1)}, f32[16,256]{1,0:T(8,128)S(1)}, u32[]{:S(2)}, u32[]{:S(2)}) collective-permute-start(f32[16,256]{1,0:T(8,128)S(1)} %get-tuple-element.87), channel_id=1, source_target_pairs={{0,12},{4,8},{8,4},{12,0},{16,28},{20,24},{24,20},{28,16},{32,44},... | collective-permute-start | bytes 49160 | tf_op jit(solution)/shard_map/ppermute | solution.py:18

commit v4 on v3

--- a/solution.py
+++ b/solution.py
@@ -10,7 +10,7 @@
 HIGH = lax.Precision.HIGH
 F32 = jnp.float32
 LIMIT = 40 * 2**20
-MOST = 52 * 2**20
+MOST = 53 * 2**20
 
 
 def swap(value, axis, mask):
@@ -63,53 +63,64 @@
     return leaf >> 4, (leaf >> 2) & 3, leaf & 3
 
 
-def project_high(columns, probes):
-    def body(c_ref, p_ref, keep, one, two, three, total):
-        _, x, _ = place()
-        right = split(p_ref[...])
-        for level in range(3):
-            total[level] = dot3(split(c_ref[level]), right, ROWS)
-        for part, out in ((1, one), (2, two), (3, three)):
-            base = 0 if part == 1 else 64
-            if part > 1:
-                half = ((x ^ part) & 1) * 64
-                out[:64] = total[0, pl.ds(pl.multiple_of(half, 64), 64)]
-            row = pl.multiple_of((x ^ part) * 32, 32)
-            out[base:base + 32] = total[1, pl.ds(row, 32)]
-            out[base + 32:base + 64] = total[2, pl.ds(row, 32)]
-        row = pl.multiple_of(x * 32, 32)
-        keep[:32] = total[1, pl.ds(row, 32)]
-        keep[32:] = total[2, pl.ds(row, 32)]
-
+def project(columns, probes, levels, outs, emit):
     _, points, rank = columns.shape
     wide = probes.shape[1]
-    return call(
-        body,
-        shapes((64, wide), (64, wide), (128, wide), (128, wide)),
-        [pl.BlockSpec((3, points, rank), lambda _: (1, 0, 0)), whole(probes.shape)],
+    first = levels[0]
+
+    def body(c_hbm, p_hbm, *refs):
+        *results, held, given, sems = refs
+        copies = [pltpu.make_async_copy(p_hbm, given, sems.at[0])]
+        for k, level in enumerate(levels):
+            copies.append(pltpu.make_async_copy(c_hbm.at[level], held.at[k], sems.at[k + 1]))
+        for copy in copies:
+            copy.start()
+        copies[0].wait()
+        right = split(given[...])
+        for k, level in enumerate(levels):
+            copies[k + 1].wait()
+            emit(level - first, dot3(split(held[k]), right, ROWS), *results)
+
+    return call(
+        body,
+        outs,
+        [pl.BlockSpec(memory_space=pltpu.HBM)] * 2,
         [columns, probes],
-        [pltpu.VMEM((3, rank, wide), F32)],
-        flops=18 * points * rank * wide,
+        [
+            pltpu.VMEM((len(levels), points, rank), F32),
+            pltpu.VMEM((points, wide), F32),
+            pltpu.SemaphoreType.DMA((len(levels) + 1,)),
+        ],
+        flops=6 * len(levels) * points * rank * wide,
         limit=MOST,
     )
 
 
+def project_high(columns, probes):
+    def emit(level, value, keep, one, two, three, total):
+        _, x, _ = place()
+        total[...] = value
+        if level == 0:
+            for part, out in ((2, two), (3, three)):
+                half = ((x ^ part) & 1) * 64
+                out[:64] = total[pl.ds(pl.multiple_of(half, 64), 64)]
+            return
+        low = (level - 1) * 32
+        for part, base, out in ((0, 0, keep), (1, 0, one), (2, 64, two), (3, 64, three)):
+            row = pl.multiple_of((x ^ part) * 32, 32)
+            out[base + low:base + low + 32] = total[pl.ds(row, 32)]
+
+    rank, wide = columns.shape[2], probes.shape[1]
+    outs = shapes((64, wide), (64, wide), (128, wide), (128, wide), (rank, wide))
+    return project(columns, probes, (3, 4, 5), outs, emit)[:4]
+
+
 def project_low(columns, probes):
-    def body(c_ref, p_ref, *outs):
-        right = split(p_ref[...])
-        for level, out in enumerate(outs):
-            out[...] = dot3(split(c_ref[level]), right, ROWS)
-
-    _, points, rank = columns.shape
-    wide = probes.shape[1]
-    return call(
-        body,
-        shapes(*[(rank, wide)] * 3),
-        [pl.BlockSpec((3, points, rank), lambda _: (0, 0, 0)), whole(probes.shape)],
-        [columns, probes],
-        flops=18 * points * rank * wide,
-        limit=LIMIT,
-    )
+    def emit(level, value, *outs):
+        outs[level][...] = value
+
+    outs = shapes(*[(columns.shape[2], probes.shape[1])] * 3)
+    return project(columns, probes, (0, 1, 2), outs, emit)
 
 
 LATE = (1, 3, 4, 5)
@@ -261,7 +272,6 @@
     _, one, two, three = around([keep, *sent], 4)
     low0, low1, low2 = project_low(column_factor_stack, probes)
     two_a = swap(low2, "leaf", 3)
-    one_a = swap(low1, "leaf", 2)
     node0 = swap(low0, "leaf", 1)
     low2 = low2 + two_a
     part3 = two[:64] + three[:64]
@@ -272,14 +282,14 @@
     part = jnp.concatenate([part3, part4, part5])
     node2 = low2 + swap(low2, "leaf", 2)
     node2 = swap(node2, "leaf", 4)
-    part, node0, one_a = lax.optimization_barrier((part, node0, one_a))
+    part, node0 = lax.optimization_barrier((part, node0))
     part = part + swap(part, "leaf", 1)
     part, near = lax.optimization_barrier((part, near))
     part = part + swap(part, "leaf", 2)
     late = prepare(near, row_factor_stack, node0, node2)
     part, low1, *late = lax.optimization_barrier((part, low1, *late))
     gathered = [swap(part, "leaf", 4), swap(part[64:], "leaf", 8), swap(part[64:], "leaf", 12)]
-    node1 = one_a + swap(low1, "leaf", 3)
+    node1 = swap(low1, "leaf", 2) + swap(low1, "leaf", 3)
 
     result, applied = expand(*late, node1, part, *gathered)
 

time: 133 us -> 130 us (0.977)
  waiting for transfers between devices: 59.2 us -> 53.9 us
  Pallas kernels: 9.03 us -> 12.8 us
  local copies, waits for them, and re-layouts: 1.73 us -> 0.36 us
    ppermute x32, waiting for transfers between devices: 59.2 us -> 53.9 us  [swap(): return lax.ppermute(value, axis, pairs)]
    pallas_call x8, Pallas kernels: 9.03 us -> 12.8 us  [call(): pl.pallas_call(body, out_shape=outs, grid=grid, in_specs=specs, out_specs...]
    unnamed x10 -> x8, local copies, waits for them, and re-layouts: 1.39 us -> 0.02 us
  transfers between devices with their start and end apart: 32 -> 32, of which waited for: 16 -> 16; matrix products, arithmetic and copies ran while one was open for 2% -> 2% of each run, Pallas kernels for 3% -> 5%
where the time goes in v4:
time: 130 us
  starting transfers between devices  58.9 us (45%)
  waiting for transfers between devices  53.9 us (41%)
  Pallas kernels  12.8 us (10%)
  matrix products  2.39 us (2%)
    ppermute x32, starting transfers between devices, swap(): return lax.ppermute(value, axis, pairs)  58.9 us
    ppermute x32, waiting for transfers between devices, swap(): return lax.ppermute(value, axis, pairs)  53.9 us
    pallas_call x8, Pallas kernels, call(): pl.pallas_call(body, out_shape=outs, grid=grid, in_specs=specs, out_specs...  12.8 us
  transfers between devices with their start and end apart: 32, of which 16 were waited for; matrix products, arithmetic and copies ran while one was open for 2% of the time, Pallas kernels for 5%

profile of v4, /device:TPU:32, one launch (start us, length us, event | category | flops | bytes accessed | tf_op | source)
XLA Modules:
  0.0 129.9 jit_solution(2432006218433898537)
XLA Ops:
  0.6 3.7 %shard_map.68 = (f32[64,256]{1,0:T(8,128)S(1)}, f32[64,256]{1,0:T(8,128)S(1)}, f32[128,256]{1,0:T(8,128)S(1)}, f32[128,256]{1,0:T(8,128)S(1)}, f32[128,256]{1,0:T(8,128)}) custom-call(f32[6,1024,128]{2,1,0:T(8,128)} %c_hbm.3, f32[1024,256]{1,0:T(8,128)} %p_hbm.3), custom_call_target="tpu_custom_call" | custom-call | flops 603979776 | bytes 4718592 | tf_op jit(solution)/shard_map/pallas_call | solution.py:49
  4.4 3.1 %collective-permute-start = (f32[128,256]{1,0:T(8,128)S(1)}, f32[128,256]{1,0:T(8,128)S(1)}, u32[]{:S(2)}, u32[]{:S(2)}) collective-permute-start(f32[128,256]{1,0:T(8,128)S(1)} %get-tuple-element.44), channel_id=1, source_target_pairs={{0,32},{4,36},{8,40},{12,44},{16,48},{20,52},{24,56},{28,60},{32,0... | collective-permute-start | bytes 393224 | tf_op jit(solution)/shard_map/ppermute | solution.py:18
  7.5 1.1 collective-permute-start.1
  8.6 3.2 %shard_map.69 = (f32[128,256]{1,0:T(8,128)S(1)}, f32[128,256]{1,0:T(8,128)S(1)}, f32[128,256]{1,0:T(8,128)S(1)}) custom-call(f32[6,1024,128]{2,1,0:T(8,128)} %c_hbm.3, f32[1024,256]{1,0:T(8,128)} %p_hbm.3), custom_call_target="tpu_custom_call" | custom-call | flops 603979776 | bytes 4587520 | tf_op jit(solution)/shard_map/pallas_call | solution.py:49
  11.8 3.4 %collective-permute-start.6 = (f32[128,256]{1,0:T(8,128)S(1)}, f32[128,256]{1,0:T(8,128)S(1)}, u32[]{:S(2)}, u32[]{:S(2)}) collective-permute-start(f32[128,256]{1,0:T(8,128)S(1)} %get-tuple-element.48), channel_id=1, source_target_pairs={{0,4},{4,0},{8,12},{12,8},{16,20},{20,16},{24,28},{28,24},{32,36},... | collective-permute-start | bytes 393224 | tf_op jit(solution)/shard_map/ppermute | solution.py:18
  15.2 3.6 %collective-permute-start.9 = (f32[128,256]{1,0:T(8,128)S(1)}, f32[128,256]{1,0:T(8,128)S(1)}, u32[]{:S(2)}, u32[]{:S(2)}) collective-permute-start(f32[128,256]{1,0:T(8,128)S(1)} %get-tuple-element.54), channel_id=1, source_target_pairs={{0,12},{4,8},{8,4},{12,0},{16,28},{20,24},{24,20},{28,16},{32,44},... | collective-permute-start | bytes 393224 | tf_op jit(solution)/shard_map/ppermute | solution.py:18
  18.8 3.1 %collective-permute-start.5 = (f32[32,256]{1,0:T(8,128)S(1)}, f32[32,256]{1,0:T(8,128)S(1)}, u32[]{:S(2)}, u32[]{:S(2)}) collective-permute-start(f32[32,256]{1,0:T(8,128)S(1)} %get-tuple-element.89), channel_id=1, source_target_pairs={{0,192},{4,196},{8,200},{12,204},{16,208},{20,212},{24,216},{28,22... | collective-permute-start | bytes 98312 | tf_op jit(solution)/shard_map/ppermute | solution.py:18
  21.9 0.6 collective-permute-start.4
  22.6 1.9 %collective-permute-done.9 = f32[128,256]{1,0:T(8,128)S(1)} collective-permute-done((f32[128,256]{1,0:T(8,128)S(1)}, f32[128,256]{1,0:T(8,128)S(1)}, u32[]{:S(2)}, u32[]{:S(2)}) %collective-permute-start.9) | collective-permute-done | bytes 131104 | tf_op jit(solution)/shard_map/ppermute | solution.py:18
  24.5 5.1 %collective-permute-start.10 = (f32[128,256]{1,0:T(8,128)S(1)}, f32[128,256]{1,0:T(8,128)S(1)}, u32[]{:S(2)}, u32[]{:S(2)}) collective-permute-start(f32[128,256]{1,0:T(8,128)S(1)} %add.46), channel_id=1, source_target_pairs={{0,8},{4,12},{8,0},{12,4},{16,24},{20,28},{24,16},{28,20},{32,40},... | collective-permute-start | bytes 393224 | tf_op jit(solution)/shard_map/ppermute | solution.py:18
  29.6 1.6 %collective-permute-start.3 = (f32[32,256]{1,0:T(8,128)S(1)}, f32[32,256]{1,0:T(8,128)S(1)}, u32[]{:S(2)}, u32[]{:S(2)}) collective-permute-start(f32[32,256]{1,0:T(8,128)S(1)} %get-tuple-element.88), channel_id=1, source_target_pairs={{0,64},{4,68},{8,72},{12,76},{16,80},{20,84},{24,88},{28,92},{32,9... | collective-permute-start | bytes 98312 | tf_op jit(solution)/shard_map/ppermute | solution.py:18
  31.2 2.3 %collective-permute-done.3 = f32[32,256]{1,0:T(8,128)S(1)} collective-permute-done((f32[32,256]{1,0:T(8,128)S(1)}, f32[32,256]{1,0:T(8,128)S(1)}, u32[]{:S(2)}, u32[]{:S(2)}) %collective-permute-start.3) | collective-permute-done | bytes 32800 | tf_op jit(solution)/shard_map/ppermute | solution.py:18
  33.6 2.7 %collective-permute-done.10 = f32[128,256]{1,0:T(8,128)S(1)} collective-permute-done((f32[128,256]{1,0:T(8,128)S(1)}, f32[128,256]{1,0:T(8,128)S(1)}, u32[]{:S(2)}, u32[]{:S(2)}) %collective-permute-start.10) | collective-permute-done | bytes 131104 | tf_op jit(solution)/shard_map/ppermute | solution.py:18
  36.3 1.8 %collective-permute-start.11 = (f32[128,256]{1,0:T(8,128)S(1)}, f32[128,256]{1,0:T(8,128)S(1)}, u32[]{:S(2)}, u32[]{:S(2)}) collective-permute-start(f32[128,256]{1,0:T(8,128)S(1)} %add.47), channel_id=1, source_target_pairs={{0,16},{4,20},{8,24},{12,28},{16,0},{20,4},{24,8},{28,12},{32,48},... | collective-permute-start | bytes 393224 | tf_op jit(solution)/shard_map/ppermute | solution.py:18
  38.5 2.4 %fusion.n_ref = f32[1024,256]{1,0:T(8,128)S(1)} fusion(f32[1024,256]{1,0:T(8,128)S(1)} %copy-done.1, f32[1024,1024]{1,0:T(8,128)S(1)} %copy-done.2, f32[128,8,8,128]{3,2,1,0:T(8,128)S(1)} %bitcast.8), kind=kOutput, calls=%fused_computation.1 | convolution fusion | flops 1611661312 | bytes 10485760 | tf_op jit(solution)/shard_map/dot_general | solution.py:269
  40.9 3.1 %collective-permute-start.8 = (f32[128,256]{1,0:T(8,128)S(1)}, f32[128,256]{1,0:T(8,128)S(1)}, u32[]{:S(2)}, u32[]{:S(2)}) collective-permute-start(f32[128,256]{1,0:T(8,128)S(1)} %add.44), channel_id=1, source_target_pairs={{0,8},{4,12},{8,0},{12,4},{16,24},{20,28},{24,16},{28,20},{32,40},... | collective-permute-start | bytes 393224 | tf_op jit(solution)/shard_map/ppermute | solution.py:18
  44.0 1.6 %shard_map.70 = (f32[1024,256]{1,0:T(8,128)S(1)}, bf16[1024,512]{1,0:T(8,128)(2,1)S(1)}, bf16[1024,512]{1,0:T(8,128)(2,1)S(1)}) custom-call(f32[1024,256]{1,0:T(8,128)S(1)} %fusion.n_ref, f32[6,1024,128]{2,1,0:T(8,128)S(1)} %copy-done, f32[128,256]{1,0:T(8,128)S(1)} %collective-permute-done.6.z_ref, f32[128,256]{1,0:T(8,128)S(1)} %collective-permute-done.11.t_ref), custom_call_target="tpu_custom_call" | custom-call | flops 402653184 | bytes 9699328 | tf_op jit(solution)/shard_map/pallas_call | solution.py:49
  45.7 6.0 %collective-permute-done.8 = f32[128,256]{1,0:T(8,128)S(1)} collective-permute-done((f32[128,256]{1,0:T(8,128)S(1)}, f32[128,256]{1,0:T(8,128)S(1)}, u32[]{:S(2)}, u32[]{:S(2)}) %collective-permute-start.8) | collective-permute-done | bytes 131104 | tf_op jit(solution)/shard_map/ppermute | solution.py:18
  51.6 2.4 %collective-permute-start.13 = (f32[128,256]{1,0:T(8,128)S(1)}, f32[128,256]{1,0:T(8,128)S(1)}, u32[]{:S(2)}, u32[]{:S(2)}) collective-permute-start(f32[128,256]{1,0:T(8,128)S(1)} %get-tuple-element.61), channel_id=1, source_target_pairs={{0,12},{4,8},{8,4},{12,0},{16,28},{20,24},{24,20},{28,16},{32,44},... | collective-permute-start | bytes 393224 | tf_op jit(solution)/shard_map/ppermute | solution.py:18
  54.0 4.8 %collective-permute-start.12 = (f32[128,256]{1,0:T(8,128)S(1)}, f32[128,256]{1,0:T(8,128)S(1)}, u32[]{:S(2)}, u32[]{:S(2)}) collective-permute-start(f32[128,256]{1,0:T(8,128)S(1)} %get-tuple-element.61), channel_id=1, source_target_pairs={{0,8},{4,12},{8,0},{12,4},{16,24},{20,28},{24,16},{28,20},{32,40},... | collective-permute-start | bytes 393224 | tf_op jit(solution)/shard_map/ppermute | solution.py:18
  58.8 0.8 collective-permute-start.14
  59.6 2.1 %collective-permute-start.16 = (f32[64,256]{1,0:T(8,128)S(1)}, f32[64,256]{1,0:T(8,128)S(1)}, u32[]{:S(2)}, u32[]{:S(2)}) collective-permute-start(f32[64,256]{1,0:T(8,128)S(1)} %slice.28), channel_id=1, source_target_pairs={{0,48},{4,52},{8,56},{12,60},{16,32},{20,36},{24,40},{28,44},{32,1... | collective-permute-start | bytes 196616 | tf_op jit(solution)/shard_map/ppermute | solution.py:18
  61.7 1.2 collective-permute-start.15
  63.4 2.8 %collective-permute-done.12 = f32[128,256]{1,0:T(8,128)S(1)} collective-permute-done((f32[128,256]{1,0:T(8,128)S(1)}, f32[128,256]{1,0:T(8,128)S(1)}, u32[]{:S(2)}, u32[]{:S(2)}) %collective-permute-start.12) | collective-permute-done | bytes 131104 | tf_op jit(solution)/shard_map/ppermute | solution.py:18
  66.2 1.3 collective-permute-done.15.q2
  67.5 2.0 %shard_map.71 = (f32[1024,256]{1,0:T(8,128)}, f32[1024,256]{1,0:T(8,128)S(1)}) custom-call(f32[1024,256]{1,0:T(8,128)S(1)} %get-tuple-element.58.b_ref, bf16[1024,512]{1,0:T(8,128)(2,1)S(1)} %get-tuple-element.59.h_ref, bf16[1024,512]{1,0:T(8,128)(2,1)S(1)} %get-tuple-element.60.l_ref, f32[128,256]{1,0:T(8,128)S(1)} %add.48.o_ref, f32[128,256]{1,0:T(8,128)S(1)} %add.45.q0, ...), custom_call_target="tpu_custom_call" | custom-call | flops 805306368 | bytes 7864320 | tf_op jit(solution)/shard_map/pallas_call | solution.py:49
  69.5 2.7 %collective-permute-done.18.refs_1_ = f32[1024,256]{1,0:T(8,128)S(1)} collective-permute-done((f32[1024,256]{1,0:T(8,128)S(1)}, f32[1024,256]{1,0:T(8,128)S(1)}, u32[]{:S(2)}, u32[]{:S(2)}) %collective-permute-start.18) | collective-permute-done | bytes 1048608 | tf_op jit(solution)/shard_map/ppermute | solution.py:18
  72.2 1.1 shard_map.72
  73.2 0.7 collective-permute-start.19
  73.9 2.0 %collective-permute-start.20 = (f32[2,64,256]{2,1,0:T(8,128)S(1)}, f32[2,64,256]{2,1,0:T(8,128)S(1)}, u32[]{:S(2)}, u32[]{:S(2)}) collective-permute-start(f32[2,64,256]{2,1,0:T(8,128)S(1)} %get-tuple-element.67), channel_id=1, source_target_pairs={{0,32},{4,36},{8,40},{12,44},{16,48},{20,52},{24,56},{28,60},{32,0... | collective-permute-start | bytes 393224 | tf_op jit(solution)/shard_map/ppermute | solution.py:18
  75.9 2.1 %collective-permute-start.21 = (f32[2,64,256]{2,1,0:T(8,128)S(1)}, f32[2,64,256]{2,1,0:T(8,128)S(1)}, u32[]{:S(2)}, u32[]{:S(2)}) collective-permute-start(f32[2,64,256]{2,1,0:T(8,128)S(1)} %get-tuple-element.68), channel_id=1, source_target_pairs={{0,48},{4,52},{8,56},{12,60},{16,32},{20,36},{24,40},{28,44},{32,1... | collective-permute-start | bytes 393224 | tf_op jit(solution)/shard_map/ppermute | solution.py:18
  78.0 17.0 %collective-permute-done.17.refs_1_ = f32[1024,256]{1,0:T(8,128)S(1)} collective-permute-done((f32[1024,256]{1,0:T(8,128)S(1)}, f32[1024,256]{1,0:T(8,128)S(1)}, u32[]{:S(2)}, u32[]{:S(2)}) %collective-permute-start.17) | collective-permute-done | bytes 1048608 | tf_op jit(solution)/shard_map/ppermute | solution.py:18
  95.2 2.6 %collective-permute-done.22.refs_2_ = f32[1024,256]{1,0:T(8,128)S(1)} collective-permute-done((f32[1024,256]{1,0:T(8,128)S(1)}, f32[1024,256]{1,0:T(8,128)S(1)}, u32[]{:S(2)}, u32[]{:S(2)}) %collective-permute-start.22) | collective-permute-done | bytes 1048608 | tf_op jit(solution)/shard_map/ppermute | solution.py:18
  97.8 1.1 shard_map.73
  98.9 0.7 collective-permute-start.23
  99.6 2.0 %collective-permute-start.24 = (f32[2,64,256]{2,1,0:T(8,128)S(1)}, f32[2,64,256]{2,1,0:T(8,128)S(1)}, u32[]{:S(2)}, u32[]{:S(2)}) collective-permute-start(f32[2,64,256]{2,1,0:T(8,128)S(1)} %get-tuple-element.76), channel_id=1, source_target_pairs={{0,32},{4,36},{8,40},{12,44},{16,48},{20,52},{24,56},{28,60},{32,0... | collective-permute-start | bytes 393224 | tf_op jit(solution)/shard_map/ppermute | solution.py:18
  101.6 2.1 %collective-permute-start.25 = (f32[2,64,256]{2,1,0:T(8,128)S(1)}, f32[2,64,256]{2,1,0:T(8,128)S(1)}, u32[]{:S(2)}, u32[]{:S(2)}) collective-permute-start(f32[2,64,256]{2,1,0:T(8,128)S(1)} %get-tuple-element.77), channel_id=1, source_target_pairs={{0,48},{4,52},{8,56},{12,60},{16,32},{20,36},{24,40},{28,44},{32,1... | collective-permute-start | bytes 393224 | tf_op jit(solution)/shard_map/ppermute | solution.py:18
  103.7 1.6 %collective-permute-done.23.refs_5_ = f32[2,64,256]{2,1,0:T(8,128)S(1)} collective-permute-done((f32[2,64,256]{2,1,0:T(8,128)S(1)}, f32[2,64,256]{2,1,0:T(8,128)S(1)}, u32[]{:S(2)}, u32[]{:S(2)}) %collective-permute-start.23) | collective-permute-done | bytes 131104 | tf_op jit(solution)/shard_map/ppermute | solution.py:18
  105.3 2.7 %collective-permute-done.24.refs_6_ = f32[2,64,256]{2,1,0:T(8,128)S(1)} collective-permute-done((f32[2,64,256]{2,1,0:T(8,128)S(1)}, f32[2,64,256]{2,1,0:T(8,128)S(1)}, u32[]{:S(2)}, u32[]{:S(2)}) %collective-permute-start.24) | collective-permute-done | bytes 131104 | tf_op jit(solution)/shard_map/ppermute | solution.py:18
  108.0 2.2 %collective-permute-done.25.refs_7_ = f32[2,64,256]{2,1,0:T(8,128)S(1)} collective-permute-done((f32[2,64,256]{2,1,0:T(8,128)S(1)}, f32[2,64,256]{2,1,0:T(8,128)S(1)}, u32[]{:S(2)}, u32[]{:S(2)}) %collective-permute-start.25) | collective-permute-done | bytes 131104 | tf_op jit(solution)/shard_map/ppermute | solution.py:18
  110.4 1.6 %collective-permute-start.26 = (f32[64,256]{1,0:T(8,128)S(1)}, f32[64,256]{1,0:T(8,128)S(1)}, u32[]{:S(2)}, u32[]{:S(2)}) collective-permute-start(f32[64,256]{1,0:T(8,128)S(1)} %get-tuple-element.79), channel_id=1, source_target_pairs={{0,64},{4,68},{8,72},{12,76},{16,80},{20,84},{24,88},{28,92},{32,9... | collective-permute-start | bytes 196616 | tf_op jit(solution)/shard_map/ppermute | solution.py:18
  112.0 2.9 %collective-permute-start.27 = (f32[64,256]{1,0:T(8,128)S(1)}, f32[64,256]{1,0:T(8,128)S(1)}, u32[]{:S(2)}, u32[]{:S(2)}) collective-permute-start(f32[64,256]{1,0:T(8,128)S(1)} %get-tuple-element.80), channel_id=1, source_target_pairs={{0,128},{4,132},{8,136},{12,140},{16,144},{20,148},{24,152},{28,15... | collective-permute-start | bytes 196616 | tf_op jit(solution)/shard_map/ppermute | solution.py:18
  115.1 2.7 %collective-permute-done.27.refs_2_ = f32[64,256]{1,0:T(8,128)S(1)} collective-permute-done((f32[64,256]{1,0:T(8,128)S(1)}, f32[64,256]{1,0:T(8,128)S(1)}, u32[]{:S(2)}, u32[]{:S(2)}) %collective-permute-start.27) | collective-permute-done | bytes 65568 | tf_op jit(solution)/shard_map/ppermute | solution.py:18
  117.9 2.5 %collective-permute-done.28.refs_3_ = f32[64,256]{1,0:T(8,128)S(1)} collective-permute-done((f32[64,256]{1,0:T(8,128)S(1)}, f32[64,256]{1,0:T(8,128)S(1)}, u32[]{:S(2)}, u32[]{:S(2)}) %collective-permute-start.28) | collective-permute-done | bytes 65568 | tf_op jit(solution)/shard_map/ppermute | solution.py:18
  120.4 1.2 collective-permute-start.29
  121.6 1.6 %collective-permute-start.30 = (f32[16,256]{1,0:T(8,128)S(1)}, f32[16,256]{1,0:T(8,128)S(1)}, u32[]{:S(2)}, u32[]{:S(2)}) collective-permute-start(f32[16,256]{1,0:T(8,128)S(1)} %get-tuple-element.84), channel_id=1, source_target_pairs={{0,8},{4,12},{8,0},{12,4},{16,24},{20,28},{24,16},{28,20},{32,40},... | collective-permute-start | bytes 49160 | tf_op jit(solution)/shard_map/ppermute | solution.py:18
  123.2 3.8 %collective-permute-start.31 = (f32[16,256]{1,0:T(8,128)S(1)}, f32[16,256]{1,0:T(8,128)S(1)}, u32[]{:S(2)}, u32[]{:S(2)}) collective-permute-start(f32[16,256]{1,0:T(8,128)S(1)} %get-tuple-element.85), channel_id=1, source_target_pairs={{0,12},{4,8},{8,4},{12,0},{16,28},{20,24},{24,20},{28,16},{32,44},... | collective-permute-start | bytes 49160 | tf_op jit(solution)/shard_map/ppermute | solution.py:18
  127.0 2.3 %collective-permute-done.30 = f32[16,256]{1,0:T(8,128)S(1)} collective-permute-done((f32[16,256]{1,0:T(8,128)S(1)}, f32[16,256]{1,0:T(8,128)S(1)}, u32[]{:S(2)}, u32[]{:S(2)}) %collective-permute-start.30) | collective-permute-done | bytes 16416 | tf_op jit(solution)/shard_map/ppermute | solution.py:18
  (46 shorter events, 2.1 us)
Async XLA Ops:
  0.6 30.5 %copy-start.3 = (s32[1,8,8]{2,1,0:T(8,128)S(1)}, s32[1,8,8]{2,1,0:T(8,128)}, u32[]{:S(2)}) copy-start(s32[1,8,8]{2,1,0:T(8,128)} %param.6) | copy-start | bytes 772
  4.4 14.4 %collective-permute-start = (f32[128,256]{1,0:T(8,128)S(1)}, f32[128,256]{1,0:T(8,128)S(1)}, u32[]{:S(2)}, u32[]{:S(2)}) collective-permute-start(f32[128,256]{1,0:T(8,128)S(1)} %get-tuple-element.44), channel_id=1, source_target_pairs={{0,32},{4,36},{8,40},{12,44},{16,48},{20,52},{24,56},{28,60},{32,0... | collective-permute-start | bytes 393224 | tf_op jit(solution)/shard_map/ppermute | solution.py:18
  7.5 11.3 %collective-permute-start.1 = (f32[128,256]{1,0:T(8,128)S(1)}, f32[128,256]{1,0:T(8,128)S(1)}, u32[]{:S(2)}, u32[]{:S(2)}) collective-permute-start(f32[128,256]{1,0:T(8,128)S(1)} %get-tuple-element.45), channel_id=1, source_target_pairs={{0,48},{4,52},{8,56},{12,60},{16,32},{20,36},{24,40},{28,44},{32,1... | collective-permute-start | bytes 393224 | tf_op jit(solution)/shard_map/ppermute | solution.py:18
  8.6 29.8 %copy-start.1 = (f32[1024,256]{1,0:T(8,128)S(1)}, f32[1024,256]{1,0:T(8,128)}, u32[]{:S(2)}) copy-start(f32[1024,256]{1,0:T(8,128)} %p_hbm.3) | copy-start | bytes 3145732
  8.6 29.8 %copy-start.2 = (f32[1024,1024]{1,0:T(8,128)S(1)}, f32[1024,1024]{1,0:T(8,128)}, u32[]{:S(2)}) copy-start(f32[1024,1024]{1,0:T(8,128)} %param.5) | copy-start | bytes 12582916
  8.6 10.1 %collective-permute-start.2 = (f32[64,256]{1,0:T(8,128)S(1)}, f32[64,256]{1,0:T(8,128)S(1)}, u32[]{:S(2)}, u32[]{:S(2)}) collective-permute-start(f32[64,256]{1,0:T(8,128)S(1)} %get-tuple-element.47), channel_id=1, source_target_pairs={{0,16},{4,20},{8,24},{12,28},{16,0},{20,4},{24,8},{28,12},{32,48},... | collective-permute-start | bytes 196616 | tf_op jit(solution)/shard_map/ppermute | solution.py:18
  11.8 21.7 %collective-permute-start.6 = (f32[128,256]{1,0:T(8,128)S(1)}, f32[128,256]{1,0:T(8,128)S(1)}, u32[]{:S(2)}, u32[]{:S(2)}) collective-permute-start(f32[128,256]{1,0:T(8,128)S(1)} %get-tuple-element.48), channel_id=1, source_target_pairs={{0,4},{4,0},{8,12},{12,8},{16,20},{20,16},{24,28},{28,24},{32,36},... | collective-permute-start | bytes 393224 | tf_op jit(solution)/shard_map/ppermute | solution.py:18
  15.2 9.3 %collective-permute-start.9 = (f32[128,256]{1,0:T(8,128)S(1)}, f32[128,256]{1,0:T(8,128)S(1)}, u32[]{:S(2)}, u32[]{:S(2)}) collective-permute-start(f32[128,256]{1,0:T(8,128)S(1)} %get-tuple-element.54), channel_id=1, source_target_pairs={{0,12},{4,8},{8,4},{12,0},{16,28},{20,24},{24,20},{28,16},{32,44},... | collective-permute-start | bytes 393224 | tf_op jit(solution)/shard_map/ppermute | solution.py:18
  18.8 12.3 %collective-permute-start.5 = (f32[32,256]{1,0:T(8,128)S(1)}, f32[32,256]{1,0:T(8,128)S(1)}, u32[]{:S(2)}, u32[]{:S(2)}) collective-permute-start(f32[32,256]{1,0:T(8,128)S(1)} %get-tuple-element.89), channel_id=1, source_target_pairs={{0,192},{4,196},{8,200},{12,204},{16,208},{20,212},{24,216},{28,22... | collective-permute-start | bytes 98312 | tf_op jit(solution)/shard_map/ppermute | solution.py:18
  21.9 9.2 %collective-permute-start.4 = (f32[32,256]{1,0:T(8,128)S(1)}, f32[32,256]{1,0:T(8,128)S(1)}, u32[]{:S(2)}, u32[]{:S(2)}) collective-permute-start(f32[32,256]{1,0:T(8,128)S(1)} %get-tuple-element.89), channel_id=1, source_target_pairs={{0,128},{4,132},{8,136},{12,140},{16,144},{20,148},{24,152},{28,15... | collective-permute-start | bytes 98312 | tf_op jit(solution)/shard_map/ppermute | solution.py:18
  24.5 11.8 %collective-permute-start.10 = (f32[128,256]{1,0:T(8,128)S(1)}, f32[128,256]{1,0:T(8,128)S(1)}, u32[]{:S(2)}, u32[]{:S(2)}) collective-permute-start(f32[128,256]{1,0:T(8,128)S(1)} %add.46), channel_id=1, source_target_pairs={{0,8},{4,12},{8,0},{12,4},{16,24},{20,28},{24,16},{28,20},{32,40},... | collective-permute-start | bytes 393224 | tf_op jit(solution)/shard_map/ppermute | solution.py:18
  29.6 3.9 %collective-permute-start.3 = (f32[32,256]{1,0:T(8,128)S(1)}, f32[32,256]{1,0:T(8,128)S(1)}, u32[]{:S(2)}, u32[]{:S(2)}) collective-permute-start(f32[32,256]{1,0:T(8,128)S(1)} %get-tuple-element.88), channel_id=1, source_target_pairs={{0,64},{4,68},{8,72},{12,76},{16,80},{20,84},{24,88},{28,92},{32,9... | collective-permute-start | bytes 98312 | tf_op jit(solution)/shard_map/ppermute | solution.py:18
  33.5 7.4 %collective-permute-start.7 = (f32[128,256]{1,0:T(8,128)S(1)}, f32[128,256]{1,0:T(8,128)S(1)}, u32[]{:S(2)}, u32[]{:S(2)}) collective-permute-start(f32[128,256]{1,0:T(8,128)S(1)} %pad_maximum_fusion), channel_id=1, source_target_pairs={{0,4},{4,0},{8,12},{12,8},{16,20},{20,16},{24,28},{28,24},{32,36},... | collective-permute-start | bytes 393224 | tf_op jit(solution)/shard_map/ppermute | solution.py:18
  36.3 7.7 %collective-permute-start.11 = (f32[128,256]{1,0:T(8,128)S(1)}, f32[128,256]{1,0:T(8,128)S(1)}, u32[]{:S(2)}, u32[]{:S(2)}) collective-permute-start(f32[128,256]{1,0:T(8,128)S(1)} %add.47), channel_id=1, source_target_pairs={{0,16},{4,20},{8,24},{12,28},{16,0},{20,4},{24,8},{28,12},{32,48},... | collective-permute-start | bytes 393224 | tf_op jit(solution)/shard_map/ppermute | solution.py:18
  38.5 5.6 %copy-start = (f32[6,1024,128]{2,1,0:T(8,128)S(1)}, f32[6,1024,128]{2,1,0:T(8,128)}, u32[]{:S(2)}) copy-start(f32[6,1024,128]{2,1,0:T(8,128)} %u_ref.1) | copy-start | bytes 9437188
  40.9 10.7 %collective-permute-start.8 = (f32[128,256]{1,0:T(8,128)S(1)}, f32[128,256]{1,0:T(8,128)S(1)}, u32[]{:S(2)}, u32[]{:S(2)}) collective-permute-start(f32[128,256]{1,0:T(8,128)S(1)} %add.44), channel_id=1, source_target_pairs={{0,8},{4,12},{8,0},{12,4},{16,24},{20,28},{24,16},{28,20},{32,40},... | collective-permute-start | bytes 393224 | tf_op jit(solution)/shard_map/ppermute | solution.py:18
  51.6 11.8 %collective-permute-start.13 = (f32[128,256]{1,0:T(8,128)S(1)}, f32[128,256]{1,0:T(8,128)S(1)}, u32[]{:S(2)}, u32[]{:S(2)}) collective-permute-start(f32[128,256]{1,0:T(8,128)S(1)} %get-tuple-element.61), channel_id=1, source_target_pairs={{0,12},{4,8},{8,4},{12,0},{16,28},{20,24},{24,20},{28,16},{32,44},... | collective-permute-start | bytes 393224 | tf_op jit(solution)/shard_map/ppermute | solution.py:18
  54.0 12.1 %collective-permute-start.12 = (f32[128,256]{1,0:T(8,128)S(1)}, f32[128,256]{1,0:T(8,128)S(1)}, u32[]{:S(2)}, u32[]{:S(2)}) collective-permute-start(f32[128,256]{1,0:T(8,128)S(1)} %get-tuple-element.61), channel_id=1, source_target_pairs={{0,8},{4,12},{8,0},{12,4},{16,24},{20,28},{24,16},{28,20},{32,40},... | collective-permute-start | bytes 393224 | tf_op jit(solution)/shard_map/ppermute | solution.py:18
  58.8 8.7 %collective-permute-start.14 = (f32[128,256]{1,0:T(8,128)S(1)}, f32[128,256]{1,0:T(8,128)S(1)}, u32[]{:S(2)}, u32[]{:S(2)}) collective-permute-start(f32[128,256]{1,0:T(8,128)S(1)} %add.45.q0), channel_id=1, source_target_pairs={{0,16},{4,20},{8,24},{12,28},{16,0},{20,4},{24,8},{28,12},{32,48},... | collective-permute-start | bytes 393224 | tf_op jit(solution)/shard_map/ppermute | solution.py:18
  59.6 6.6 %collective-permute-start.16 = (f32[64,256]{1,0:T(8,128)S(1)}, f32[64,256]{1,0:T(8,128)S(1)}, u32[]{:S(2)}, u32[]{:S(2)}) collective-permute-start(f32[64,256]{1,0:T(8,128)S(1)} %slice.28), channel_id=1, source_target_pairs={{0,48},{4,52},{8,56},{12,60},{16,32},{20,36},{24,40},{28,44},{32,1... | collective-permute-start | bytes 196616 | tf_op jit(solution)/shard_map/ppermute | solution.py:18
  61.7 5.8 %collective-permute-start.15 = (f32[64,256]{1,0:T(8,128)S(1)}, f32[64,256]{1,0:T(8,128)S(1)}, u32[]{:S(2)}, u32[]{:S(2)}) collective-permute-start(f32[64,256]{1,0:T(8,128)S(1)} %slice.28), channel_id=1, source_target_pairs={{0,32},{4,36},{8,40},{12,44},{16,48},{20,52},{24,56},{28,60},{32,0... | collective-permute-start | bytes 196616 | tf_op jit(solution)/shard_map/ppermute | solution.py:18
  69.5 2.7 %collective-permute-start.18 = (f32[1024,256]{1,0:T(8,128)S(1)}, f32[1024,256]{1,0:T(8,128)S(1)}, u32[]{:S(2)}, u32[]{:S(2)}) collective-permute-start(f32[1024,256]{1,0:T(8,128)S(1)} %get-tuple-element.64.refs_0_), channel_id=1, source_target_pairs={{0,1},{1,0},{2,3},{3,2},{4,5},{5,4},{6,7},{7,6},{8,9},{9,8},{10,11... | collective-permute-start | bytes 3145736 | tf_op jit(solution)/shard_map/ppermute | solution.py:18
  69.5 25.6 %collective-permute-start.17 = (f32[1024,256]{1,0:T(8,128)S(1)}, f32[1024,256]{1,0:T(8,128)S(1)}, u32[]{:S(2)}, u32[]{:S(2)}) collective-permute-start(f32[1024,256]{1,0:T(8,128)S(1)} %get-tuple-element.64.refs_0_), channel_id=1, source_target_pairs={{0,2},{1,3},{2,0},{3,1},{4,6},{5,7},{6,4},{7,5},{8,10},{9,11},{10,... | collective-permute-start | bytes 3145736 | tf_op jit(solution)/shard_map/ppermute | solution.py:18
  73.2 21.8 %collective-permute-start.19 = (f32[2,64,256]{2,1,0:T(8,128)S(1)}, f32[2,64,256]{2,1,0:T(8,128)S(1)}, u32[]{:S(2)}, u32[]{:S(2)}) collective-permute-start(f32[2,64,256]{2,1,0:T(8,128)S(1)} %get-tuple-element.66), channel_id=1, source_target_pairs={{0,16},{4,20},{8,24},{12,28},{16,0},{20,4},{24,8},{28,12},{32,48},... | collective-permute-start | bytes 393224 | tf_op jit(solution)/shard_map/ppermute | solution.py:18
  73.9 21.1 %collective-permute-start.20 = (f32[2,64,256]{2,1,0:T(8,128)S(1)}, f32[2,64,256]{2,1,0:T(8,128)S(1)}, u32[]{:S(2)}, u32[]{:S(2)}) collective-permute-start(f32[2,64,256]{2,1,0:T(8,128)S(1)} %get-tuple-element.67), channel_id=1, source_target_pairs={{0,32},{4,36},{8,40},{12,44},{16,48},{20,52},{24,56},{28,60},{32,0... | collective-permute-start | bytes 393224 | tf_op jit(solution)/shard_map/ppermute | solution.py:18
  75.9 19.1 %collective-permute-start.21 = (f32[2,64,256]{2,1,0:T(8,128)S(1)}, f32[2,64,256]{2,1,0:T(8,128)S(1)}, u32[]{:S(2)}, u32[]{:S(2)}) collective-permute-start(f32[2,64,256]{2,1,0:T(8,128)S(1)} %get-tuple-element.68), channel_id=1, source_target_pairs={{0,48},{4,52},{8,56},{12,60},{16,32},{20,36},{24,40},{28,44},{32,1... | collective-permute-start | bytes 393224 | tf_op jit(solution)/shard_map/ppermute | solution.py:18
  95.1 2.7 %collective-permute-start.22 = (f32[1024,256]{1,0:T(8,128)S(1)}, f32[1024,256]{1,0:T(8,128)S(1)}, u32[]{:S(2)}, u32[]{:S(2)}) collective-permute-start(f32[1024,256]{1,0:T(8,128)S(1)} %collective-permute-done.17.refs_1_), channel_id=1, source_target_pairs={{0,1},{1,0},{2,3},{3,2},{4,5},{5,4},{6,7},{7,6},{8,9},{9,8},{10,11... | collective-permute-start | bytes 3145736 | tf_op jit(solution)/shard_map/ppermute | solution.py:18
  98.9 6.4 %collective-permute-start.23 = (f32[2,64,256]{2,1,0:T(8,128)S(1)}, f32[2,64,256]{2,1,0:T(8,128)S(1)}, u32[]{:S(2)}, u32[]{:S(2)}) collective-permute-start(f32[2,64,256]{2,1,0:T(8,128)S(1)} %get-tuple-element.75), channel_id=1, source_target_pairs={{0,16},{4,20},{8,24},{12,28},{16,0},{20,4},{24,8},{28,12},{32,48},... | collective-permute-start | bytes 393224 | tf_op jit(solution)/shard_map/ppermute | solution.py:18
  99.6 8.4 %collective-permute-start.24 = (f32[2,64,256]{2,1,0:T(8,128)S(1)}, f32[2,64,256]{2,1,0:T(8,128)S(1)}, u32[]{:S(2)}, u32[]{:S(2)}) collective-permute-start(f32[2,64,256]{2,1,0:T(8,128)S(1)} %get-tuple-element.76), channel_id=1, source_target_pairs={{0,32},{4,36},{8,40},{12,44},{16,48},{20,52},{24,56},{28,60},{32,0... | collective-permute-start | bytes 393224 | tf_op jit(solution)/shard_map/ppermute | solution.py:18
  101.6 8.7 %collective-permute-start.25 = (f32[2,64,256]{2,1,0:T(8,128)S(1)}, f32[2,64,256]{2,1,0:T(8,128)S(1)}, u32[]{:S(2)}, u32[]{:S(2)}) collective-permute-start(f32[2,64,256]{2,1,0:T(8,128)S(1)} %get-tuple-element.77), channel_id=1, source_target_pairs={{0,48},{4,52},{8,56},{12,60},{16,32},{20,36},{24,40},{28,44},{32,1... | collective-permute-start | bytes 393224 | tf_op jit(solution)/shard_map/ppermute | solution.py:18
  110.4 4.8 %collective-permute-start.26 = (f32[64,256]{1,0:T(8,128)S(1)}, f32[64,256]{1,0:T(8,128)S(1)}, u32[]{:S(2)}, u32[]{:S(2)}) collective-permute-start(f32[64,256]{1,0:T(8,128)S(1)} %get-tuple-element.79), channel_id=1, source_target_pairs={{0,64},{4,68},{8,72},{12,76},{16,80},{20,84},{24,88},{28,92},{32,9... | collective-permute-start | bytes 196616 | tf_op jit(solution)/shard_map/ppermute | solution.py:18
  112.0 5.9 %collective-permute-start.27 = (f32[64,256]{1,0:T(8,128)S(1)}, f32[64,256]{1,0:T(8,128)S(1)}, u32[]{:S(2)}, u32[]{:S(2)}) collective-permute-start(f32[64,256]{1,0:T(8,128)S(1)} %get-tuple-element.80), channel_id=1, source_target_pairs={{0,128},{4,132},{8,136},{12,140},{16,144},{20,148},{24,152},{28,15... | collective-permute-start | bytes 196616 | tf_op jit(solution)/shard_map/ppermute | solution.py:18
  114.9 5.5 %collective-permute-start.28 = (f32[64,256]{1,0:T(8,128)S(1)}, f32[64,256]{1,0:T(8,128)S(1)}, u32[]{:S(2)}, u32[]{:S(2)}) collective-permute-start(f32[64,256]{1,0:T(8,128)S(1)} %get-tuple-element.81), channel_id=1, source_target_pairs={{0,192},{4,196},{8,200},{12,204},{16,208},{20,212},{24,216},{28,22... | collective-permute-start | bytes 196616 | tf_op jit(solution)/shard_map/ppermute | solution.py:18
  120.4 6.6 %collective-permute-start.29 = (f32[16,256]{1,0:T(8,128)S(1)}, f32[16,256]{1,0:T(8,128)S(1)}, u32[]{:S(2)}, u32[]{:S(2)}) collective-permute-start(f32[16,256]{1,0:T(8,128)S(1)} %get-tuple-element.83), channel_id=1, source_target_pairs={{0,4},{4,0},{8,12},{12,8},{16,20},{20,16},{24,28},{28,24},{32,36},... | collective-permute-start | bytes 49160 | tf_op jit(solution)/shard_map/ppermute | solution.py:18
  121.6 7.6 %collective-permute-start.30 = (f32[16,256]{1,0:T(8,128)S(1)}, f32[16,256]{1,0:T(8,128)S(1)}, u32[]{:S(2)}, u32[]{:S(2)}) collective-permute-start(f32[16,256]{1,0:T(8,128)S(1)} %get-tuple-element.84), channel_id=1, source_target_pairs={{0,8},{4,12},{8,0},{12,4},{16,24},{20,28},{24,16},{28,20},{32,40},... | collective-permute-start | bytes 49160 | tf_op jit(solution)/shard_map/ppermute | solution.py:18
  123.2 6.0 %collective-permute-start.31 = (f32[16,256]{1,0:T(8,128)S(1)}, f32[16,256]{1,0:T(8,128)S(1)}, u32[]{:S(2)}, u32[]{:S(2)}) collective-permute-start(f32[16,256]{1,0:T(8,128)S(1)} %get-tuple-element.85), channel_id=1, source_target_pairs={{0,12},{4,8},{8,4},{12,0},{16,28},{20,24},{24,20},{28,16},{32,44},... | collective-permute-start | bytes 49160 | tf_op jit(solution)/shard_map/ppermute | solution.py:18

commit v5 on v3

--- a/solution.py
+++ b/solution.py
@@ -112,13 +112,13 @@
     )
 
 
-LATE = (1, 3, 4, 5)
-
-
-def prepare(near, rows, zero, two):
-    def body(n_ref, u_ref, z_ref, t_ref, out, high, low):
-        early = jnp.concatenate([u_ref[0], u_ref[2]], axis=1)
-        nodes = jnp.concatenate([z_ref[...], t_ref[...]], axis=0)
+LATE = (0, 3, 4, 5)
+
+
+def prepare(near, rows, one, one_more, two):
+    def body(n_ref, u_ref, o_ref, m_ref, t_ref, out, high, low):
+        early = jnp.concatenate([u_ref[1], u_ref[2]], axis=1)
+        nodes = jnp.concatenate([o_ref[...] + m_ref[...], t_ref[...]], axis=0)
         out[...] = n_ref[...] + dot3(split(early), split(nodes), MATMUL)
         high[...], low[...] = split(jnp.concatenate([u_ref[t] for t in LATE], axis=1))
 
@@ -136,20 +136,21 @@
         [
             tiled(wide),
             pl.BlockSpec((levels, tile, rank), lambda i: (0, i, 0)),
-            whole(zero.shape),
+            whole(one.shape),
+            whole(one_more.shape),
             whole(two.shape),
         ],
-        [near, rows, zero, two],
+        [near, rows, one, one_more, two],
         flops=12 * rank * points * wide,
         grid=(points // tile,),
         out_specs=[tiled(wide), tiled(len(LATE) * rank), tiled(len(LATE) * rank)],
     )
 
 
-def expand(base, rows_high, rows_low, one, part, part1, part2, part3):
-    def body(b_ref, h_ref, l_ref, o_ref, q0, q1, q2, q3, out, held, total):
+def expand(base, rows_high, rows_low, zero, part, part1, part2, part3):
+    def body(b_ref, h_ref, l_ref, z_ref, q0, q1, q2, q3, out, held, total):
         _, x, _ = place()
-        total[0:128] = o_ref[...]
+        total[0:128] = z_ref[...]
         for k, ref in ((0, q0), (1, q1)):
             total[pl.ds(pl.multiple_of(128 + ((x ^ k) & 1) * 64, 64), 64)] = ref[:64]
         for k, ref in ((0, q0), (1, q1), (2, q2), (3, q3)):
@@ -163,7 +164,7 @@
 
     points, wide = base.shape
     depth = rows_high.shape[1]
-    given = [base, rows_high, rows_low, one, part, part1, part2, part3]
+    given = [base, rows_high, rows_low, zero, part, part1, part2, part3]
     return call(
         body,
         shapes(base.shape, base.shape),
@@ -223,19 +224,21 @@
     )
 
 
-def cut_z(ins):
+def cut_z(ins, shift):
     rows, wide = ins[0].shape
+    half = rows // 2
 
     def body(*refs):
-        ins, outs, total = refs[:4], refs[4:8], refs[8]
+        *given, keep, give, total = refs
         _, _, z = place()
-        total[...] = (ins[0][...] + ins[1][...]) + (ins[2][...] + ins[3][...])
-        for k, out in enumerate(outs):
-            out[...] = total[pl.ds(pl.multiple_of((z ^ k) * (rows // 4), rows // 4), rows // 4)]
-
-    return call(
-        body,
-        shapes(*[(rows // 4, wide)] * 4),
+        side = (z >> shift) & 1
+        total[...] = functools.reduce(jnp.add, [ref[...] for ref in given])
+        keep[...] = total[pl.ds(pl.multiple_of(side * half, half), half)]
+        give[...] = total[pl.ds(pl.multiple_of((1 - side) * half, half), half)]
+
+    return call(
+        body,
+        shapes(*[(half, wide)] * 2),
         [whole(i.shape) for i in ins],
         list(ins),
         [pltpu.VMEM((rows, wide), F32)],
@@ -260,28 +263,26 @@
     keep, *sent = project_high(column_factor_stack, probes)
     _, one, two, three = around([keep, *sent], 4)
     low0, low1, low2 = project_low(column_factor_stack, probes)
-    two_a = swap(low2, "leaf", 3)
-    one_a = swap(low1, "leaf", 2)
-    node0 = swap(low0, "leaf", 1)
-    low2 = low2 + two_a
+    low2 = low2 + swap(low2, "leaf", 1)
     part3 = two[:64] + three[:64]
     upper = keep + one + two[64:] + three[64:]
     part4 = swap(upper[:32], "leaf", 16)
     five = upper[32:]
     part5 = swap(five, "leaf", 32) + swap(five, "leaf", 48)
     part = jnp.concatenate([part3, part4, part5])
-    node2 = low2 + swap(low2, "leaf", 2)
-    node2 = swap(node2, "leaf", 4)
-    part, node0, one_a = lax.optimization_barrier((part, node0, one_a))
+    low2 = low2 + swap(low2, "leaf", 3)
+    node2 = swap(low2, "leaf", 4)
+    part, low1 = lax.optimization_barrier((part, low1))
     part = part + swap(part, "leaf", 1)
-    part, near = lax.optimization_barrier((part, near))
-    part = part + swap(part, "leaf", 2)
-    late = prepare(near, row_factor_stack, node0, node2)
-    part, low1, *late = lax.optimization_barrier((part, low1, *late))
+    node1 = swap(low1, "leaf", 3)
+    part, node1, near = lax.optimization_barrier((part, node1, near))
+    part = part + swap(part, "leaf", 3)
+    node1_more = swap(node1, "leaf", 1)
+    part, low0 = lax.optimization_barrier((part, low0))
     gathered = [swap(part, "leaf", 4), swap(part[64:], "leaf", 8), swap(part[64:], "leaf", 12)]
-    node1 = one_a + swap(low1, "leaf", 3)
-
-    result, applied = expand(*late, node1, part, *gathered)
+    node0 = swap(low0, "leaf", 1)
+    late = prepare(near, row_factor_stack, node1, node1_more, node2)
+    result, applied = expand(*late, node0, part, *gathered)
 
     far = swap(applied, "probe", 2)
     beside = swap(applied, "probe", 1)
@@ -290,8 +291,9 @@
     across = swap(far, "probe", 1)
     second = around(gram([far, across], applied), 4)
     blocks = around(cut_y(first, second), 16)
-    blocks = around(cut_z(blocks), 1)
-    total = (blocks[0] + blocks[1]) + (blocks[2] + blocks[3])
+    keep, give = cut_z(blocks, 1)
+    keep, give = cut_z([keep, swap(give, "leaf", 3)], 0)
+    total = keep + swap(give, "leaf", 1)
     return result, total / (leaf_points * lax.axis_size("leaf"))
 
 

time: 133 us -> 120 us (0.902)
  waiting for transfers between devices: 59.2 us -> 50.1 us
  starting transfers between devices: 58.8 us -> 55.1 us
    ppermute x32 -> x31, waiting for transfers between devices: 59.2 us -> 50.1 us  [swap(): return lax.ppermute(value, axis, pairs)]
    ppermute x32 -> x31, starting transfers between devices: 58.8 us -> 55.1 us  [swap(): return lax.ppermute(value, axis, pairs)]
    pallas_call x8 -> x9, Pallas kernels: 9.03 us -> 9.05 us  [call(): pl.pallas_call(body, out_shape=outs, grid=grid, in_specs=specs, out_specs...]
  transfers between devices with their start and end apart: 32 -> 31, of which waited for: 16 -> 17; matrix products, arithmetic and copies ran while one was open for 2% -> 2% of each run, Pallas kernels for 3% -> 3%
where the time goes in v5:
time: 120 us
  starting transfers between devices  55.1 us (46%)
  waiting for transfers between devices  50.1 us (42%)
  Pallas kernels  9.05 us (8%)
  matrix products  2.39 us (2%)
  local copies, waits for them, and re-layouts  1.73 us (1%)
    ppermute x31, starting transfers between devices, swap(): return lax.ppermute(value, axis, pairs)  55.1 us
    ppermute x31, waiting for transfers between devices, swap(): return lax.ppermute(value, axis, pairs)  50.1 us
    pallas_call x9, Pallas kernels, call(): pl.pallas_call(body, out_shape=outs, grid=grid, in_specs=specs, out_specs...  9.05 us
  transfers between devices with their start and end apart: 31, of which 17 were waited for; matrix products, arithmetic and copies ran while one was open for 2% of the time, Pallas kernels for 3%

profile of v5, /device:TPU:32, one launch (start us, length us, event | category | flops | bytes accessed | tf_op | source)
XLA Modules:
  0.0 119.9 jit_solution(17797621184783150194)
XLA Ops:
  0.7 1.4 %copy-done.1 = f32[1024,256]{1,0:T(8,128)S(1)} copy-done((f32[1024,256]{1,0:T(8,128)S(1)}, f32[1024,256]{1,0:T(8,128)}, u32[]{:S(2)}) %copy-start.1) | copy-done | bytes 1048600
  2.0 2.3 %shard_map.68 = (f32[64,256]{1,0:T(8,128)S(1)}, f32[64,256]{1,0:T(8,128)S(1)}, f32[128,256]{1,0:T(8,128)S(1)}, f32[128,256]{1,0:T(8,128)S(1)}) custom-call(f32[6,1024,128]{2,1,0:T(8,128)} %c_ref.3, f32[1024,256]{1,0:T(8,128)S(1)} %copy-done.1), custom_call_target="tpu_custom_call" | custom-call | flops 603979776 | bytes 4587520 | tf_op jit(solution)/shard_map/pallas_call | solution.py:49
  4.4 3.1 %collective-permute-start = (f32[128,256]{1,0:T(8,128)S(1)}, f32[128,256]{1,0:T(8,128)S(1)}, u32[]{:S(2)}, u32[]{:S(2)}) collective-permute-start(f32[128,256]{1,0:T(8,128)S(1)} %get-tuple-element.42), channel_id=1, source_target_pairs={{0,32},{4,36},{8,40},{12,44},{16,48},{20,52},{24,56},{28,60},{32,0... | collective-permute-start | bytes 393224 | tf_op jit(solution)/shard_map/ppermute | solution.py:18
  7.5 1.2 collective-permute-start.1
  8.6 0.8 shard_map.69
  9.5 3.3 %collective-permute-start.9 = (f32[128,256]{1,0:T(8,128)S(1)}, f32[128,256]{1,0:T(8,128)S(1)}, u32[]{:S(2)}, u32[]{:S(2)}) collective-permute-start(f32[128,256]{1,0:T(8,128)S(1)} %get-tuple-element.51), channel_id=1, source_target_pairs={{0,4},{4,0},{8,12},{12,8},{16,20},{20,16},{24,28},{28,24},{32,36},... | collective-permute-start | bytes 393224 | tf_op jit(solution)/shard_map/ppermute | solution.py:18
  12.9 1.1 collective-permute-done.1
  14.0 3.1 %collective-permute-start.5 = (f32[32,256]{1,0:T(8,128)S(1)}, f32[32,256]{1,0:T(8,128)S(1)}, u32[]{:S(2)}, u32[]{:S(2)}) collective-permute-start(f32[32,256]{1,0:T(8,128)S(1)} %get-tuple-element.85), channel_id=1, source_target_pairs={{0,192},{4,196},{8,200},{12,204},{16,208},{20,212},{24,216},{28,22... | collective-permute-start | bytes 98312 | tf_op jit(solution)/shard_map/ppermute | solution.py:18
  17.1 0.6 collective-permute-start.4
  18.3 5.5 %collective-permute-start.10 = (f32[128,256]{1,0:T(8,128)S(1)}, f32[128,256]{1,0:T(8,128)S(1)}, u32[]{:S(2)}, u32[]{:S(2)}) collective-permute-start(f32[128,256]{1,0:T(8,128)S(1)} %add.36), channel_id=1, source_target_pairs={{0,12},{4,8},{8,4},{12,0},{16,28},{20,24},{24,20},{28,16},{32,44},... | collective-permute-start | bytes 393224 | tf_op jit(solution)/shard_map/ppermute | solution.py:18
  23.8 4.3 %collective-permute-start.7 = (f32[128,256]{1,0:T(8,128)S(1)}, f32[128,256]{1,0:T(8,128)S(1)}, u32[]{:S(2)}, u32[]{:S(2)}) collective-permute-start(f32[128,256]{1,0:T(8,128)S(1)} %get-tuple-element.48), channel_id=1, source_target_pairs={{0,12},{4,8},{8,4},{12,0},{16,28},{20,24},{24,20},{28,16},{32,44},... | collective-permute-start | bytes 393224 | tf_op jit(solution)/shard_map/ppermute | solution.py:18
  28.1 1.5 %collective-permute-start.6 = (f32[128,256]{1,0:T(8,128)S(1)}, f32[128,256]{1,0:T(8,128)S(1)}, u32[]{:S(2)}, u32[]{:S(2)}) collective-permute-start(f32[128,256]{1,0:T(8,128)S(1)} %pad_maximum_fusion), channel_id=1, source_target_pairs={{0,4},{4,0},{8,12},{12,8},{16,20},{20,16},{24,28},{28,24},{32,36},... | collective-permute-start | bytes 393224 | tf_op jit(solution)/shard_map/ppermute | solution.py:18
  29.9 2.4 %fusion.n_ref = f32[1024,256]{1,0:T(8,128)S(1)} fusion(f32[1024,256]{1,0:T(8,128)S(1)} %copy-done.1, f32[1024,1024]{1,0:T(8,128)S(1)} %copy-done.3, f32[128,8,8,128]{3,2,1,0:T(8,128)S(1)} %bitcast.8), kind=kOutput, calls=%fused_computation.1 | convolution fusion | flops 1611661312 | bytes 10485760 | tf_op jit(solution)/shard_map/dot_general | solution.py:261
  32.3 4.0 %collective-permute-done.6 = f32[128,256]{1,0:T(8,128)S(1)} collective-permute-done((f32[128,256]{1,0:T(8,128)S(1)}, f32[128,256]{1,0:T(8,128)S(1)}, u32[]{:S(2)}, u32[]{:S(2)}) %collective-permute-start.6) | collective-permute-done | bytes 131104 | tf_op jit(solution)/shard_map/ppermute | solution.py:18
  36.4 2.7 %collective-permute-start.11 = (f32[128,256]{1,0:T(8,128)S(1)}, f32[128,256]{1,0:T(8,128)S(1)}, u32[]{:S(2)}, u32[]{:S(2)}) collective-permute-start(f32[128,256]{1,0:T(8,128)S(1)} %add.37), channel_id=1, source_target_pairs={{0,16},{4,20},{8,24},{12,28},{16,0},{20,4},{24,8},{28,12},{32,48},... | collective-permute-start | bytes 393224 | tf_op jit(solution)/shard_map/ppermute | solution.py:18
  39.1 3.0 %collective-permute-start.8 = (f32[128,256]{1,0:T(8,128)S(1)}, f32[128,256]{1,0:T(8,128)S(1)}, u32[]{:S(2)}, u32[]{:S(2)}) collective-permute-start(f32[128,256]{1,0:T(8,128)S(1)} %collective-permute-done.7.o_ref), channel_id=1, source_target_pairs={{0,4},{4,0},{8,12},{12,8},{16,20},{20,16},{24,28},{28,24},{32,36},... | collective-permute-start | bytes 393224 | tf_op jit(solution)/shard_map/ppermute | solution.py:18
  42.1 2.5 %collective-permute-done.12 = f32[128,256]{1,0:T(8,128)S(1)} collective-permute-done((f32[128,256]{1,0:T(8,128)S(1)}, f32[128,256]{1,0:T(8,128)S(1)}, u32[]{:S(2)}, u32[]{:S(2)}) %collective-permute-start.12) | collective-permute-done | bytes 131104 | tf_op jit(solution)/shard_map/ppermute | solution.py:18
  44.8 2.3 %collective-permute-start.14 = (f32[128,256]{1,0:T(8,128)S(1)}, f32[128,256]{1,0:T(8,128)S(1)}, u32[]{:S(2)}, u32[]{:S(2)}) collective-permute-start(f32[128,256]{1,0:T(8,128)S(1)} %add.38.q0), channel_id=1, source_target_pairs={{0,16},{4,20},{8,24},{12,28},{16,0},{20,4},{24,8},{28,12},{32,48},... | collective-permute-start | bytes 393224 | tf_op jit(solution)/shard_map/ppermute | solution.py:18
  47.2 1.2 %collective-permute-start.16 = (f32[64,256]{1,0:T(8,128)S(1)}, f32[64,256]{1,0:T(8,128)S(1)}, u32[]{:S(2)}, u32[]{:S(2)}) collective-permute-start(f32[64,256]{1,0:T(8,128)S(1)} %slice.28), channel_id=1, source_target_pairs={{0,48},{4,52},{8,56},{12,60},{16,32},{20,36},{24,40},{28,44},{32,1... | collective-permute-start | bytes 196616 | tf_op jit(solution)/shard_map/ppermute | solution.py:18
  48.4 1.5 %collective-permute-start.15 = (f32[64,256]{1,0:T(8,128)S(1)}, f32[64,256]{1,0:T(8,128)S(1)}, u32[]{:S(2)}, u32[]{:S(2)}) collective-permute-start(f32[64,256]{1,0:T(8,128)S(1)} %slice.28), channel_id=1, source_target_pairs={{0,32},{4,36},{8,40},{12,44},{16,48},{20,52},{24,56},{28,60},{32,0... | collective-permute-start | bytes 196616 | tf_op jit(solution)/shard_map/ppermute | solution.py:18
  50.0 1.6 %shard_map.70 = (f32[1024,256]{1,0:T(8,128)S(1)}, bf16[1024,512]{1,0:T(8,128)(2,1)S(1)}, bf16[1024,512]{1,0:T(8,128)(2,1)S(1)}) custom-call(f32[1024,256]{1,0:T(8,128)S(1)} %fusion.n_ref, f32[6,1024,128]{2,1,0:T(8,128)S(1)} %copy-done.2, f32[128,256]{1,0:T(8,128)S(1)} %collective-permute-done.7.o_ref, f32[128,256]{1,0:T(8,128)S(1)} %collective-permute-done.8.m_ref, ...), custom_call_target="tpu_custom_call" | custom-call | flops 402653184 | bytes 9830400 | tf_op jit(solution)/shard_map/pallas_call | solution.py:49
  51.6 1.3 %collective-permute-done.16.q3 = f32[64,256]{1,0:T(8,128)S(1)} collective-permute-done((f32[64,256]{1,0:T(8,128)S(1)}, f32[64,256]{1,0:T(8,128)S(1)}, u32[]{:S(2)}, u32[]{:S(2)}) %collective-permute-start.16) | collective-permute-done | bytes 65568 | tf_op jit(solution)/shard_map/ppermute | solution.py:18
  52.9 1.3 %collective-permute-done.15.q2 = f32[64,256]{1,0:T(8,128)S(1)} collective-permute-done((f32[64,256]{1,0:T(8,128)S(1)}, f32[64,256]{1,0:T(8,128)S(1)}, u32[]{:S(2)}, u32[]{:S(2)}) %collective-permute-start.15) | collective-permute-done | bytes 65568 | tf_op jit(solution)/shard_map/ppermute | solution.py:18
  54.2 2.0 %shard_map.71 = (f32[1024,256]{1,0:T(8,128)}, f32[1024,256]{1,0:T(8,128)S(1)}) custom-call(f32[1024,256]{1,0:T(8,128)S(1)} %get-tuple-element.52.b_ref, bf16[1024,512]{1,0:T(8,128)(2,1)S(1)} %get-tuple-element.53.h_ref, bf16[1024,512]{1,0:T(8,128)(2,1)S(1)} %get-tuple-element.54.l_ref, f32[128,256]{1,0:T(8,128)S(1)} %collective-permute-done.13.z_ref, ...), custom_call_target="tpu_custom_call" | custom-call | flops 805306368 | bytes 7864320 | tf_op jit(solution)/shard_map/pallas_call | solution.py:49
  56.2 2.1 %collective-permute-start.17 = (f32[1024,256]{1,0:T(8,128)S(1)}, f32[1024,256]{1,0:T(8,128)S(1)}, u32[]{:S(2)}, u32[]{:S(2)}) collective-permute-start(f32[1024,256]{1,0:T(8,128)S(1)} %get-tuple-element.60.refs_0_), channel_id=1, source_target_pairs={{0,2},{1,3},{2,0},{3,1},{4,6},{5,7},{6,4},{7,5},{8,10},{9,11},{10,... | collective-permute-start | bytes 3145736 | tf_op jit(solution)/shard_map/ppermute | solution.py:18
  58.2 0.6 collective-permute-done.18.refs_1_
  58.8 1.1 shard_map.72
  59.9 1.4 %collective-permute-start.19 = (f32[2,64,256]{2,1,0:T(8,128)S(1)}, f32[2,64,256]{2,1,0:T(8,128)S(1)}, u32[]{:S(2)}, u32[]{:S(2)}) collective-permute-start(f32[2,64,256]{2,1,0:T(8,128)S(1)} %get-tuple-element.62), channel_id=1, source_target_pairs={{0,16},{4,20},{8,24},{12,28},{16,0},{20,4},{24,8},{28,12},{32,48},... | collective-permute-start | bytes 393224 | tf_op jit(solution)/shard_map/ppermute | solution.py:18
  61.3 2.2 %collective-permute-start.20 = (f32[2,64,256]{2,1,0:T(8,128)S(1)}, f32[2,64,256]{2,1,0:T(8,128)S(1)}, u32[]{:S(2)}, u32[]{:S(2)}) collective-permute-start(f32[2,64,256]{2,1,0:T(8,128)S(1)} %get-tuple-element.63), channel_id=1, source_target_pairs={{0,32},{4,36},{8,40},{12,44},{16,48},{20,52},{24,56},{28,60},{32,0... | collective-permute-start | bytes 393224 | tf_op jit(solution)/shard_map/ppermute | solution.py:18
  63.5 1.2 collective-permute-start.21
  64.7 17.4 %collective-permute-done.17.refs_1_ = f32[1024,256]{1,0:T(8,128)S(1)} collective-permute-done((f32[1024,256]{1,0:T(8,128)S(1)}, f32[1024,256]{1,0:T(8,128)S(1)}, u32[]{:S(2)}, u32[]{:S(2)}) %collective-permute-start.17) | collective-permute-done | bytes 1048608 | tf_op jit(solution)/shard_map/ppermute | solution.py:18
  82.2 2.6 %collective-permute-done.22.refs_2_ = f32[1024,256]{1,0:T(8,128)S(1)} collective-permute-done((f32[1024,256]{1,0:T(8,128)S(1)}, f32[1024,256]{1,0:T(8,128)S(1)}, u32[]{:S(2)}, u32[]{:S(2)}) %collective-permute-start.22) | collective-permute-done | bytes 1048608 | tf_op jit(solution)/shard_map/ppermute | solution.py:18
  84.8 1.1 shard_map.73
  85.9 1.4 %collective-permute-start.23 = (f32[2,64,256]{2,1,0:T(8,128)S(1)}, f32[2,64,256]{2,1,0:T(8,128)S(1)}, u32[]{:S(2)}, u32[]{:S(2)}) collective-permute-start(f32[2,64,256]{2,1,0:T(8,128)S(1)} %get-tuple-element.71), channel_id=1, source_target_pairs={{0,16},{4,20},{8,24},{12,28},{16,0},{20,4},{24,8},{28,12},{32,48},... | collective-permute-start | bytes 393224 | tf_op jit(solution)/shard_map/ppermute | solution.py:18
  87.3 2.2 %collective-permute-start.24 = (f32[2,64,256]{2,1,0:T(8,128)S(1)}, f32[2,64,256]{2,1,0:T(8,128)S(1)}, u32[]{:S(2)}, u32[]{:S(2)}) collective-permute-start(f32[2,64,256]{2,1,0:T(8,128)S(1)} %get-tuple-element.72), channel_id=1, source_target_pairs={{0,32},{4,36},{8,40},{12,44},{16,48},{20,52},{24,56},{28,60},{32,0... | collective-permute-start | bytes 393224 | tf_op jit(solution)/shard_map/ppermute | solution.py:18
  89.5 1.2 collective-permute-start.25
  90.7 1.6 %collective-permute-done.23.refs_5_ = f32[2,64,256]{2,1,0:T(8,128)S(1)} collective-permute-done((f32[2,64,256]{2,1,0:T(8,128)S(1)}, f32[2,64,256]{2,1,0:T(8,128)S(1)}, u32[]{:S(2)}, u32[]{:S(2)}) %collective-permute-start.23) | collective-permute-done | bytes 131104 | tf_op jit(solution)/shard_map/ppermute | solution.py:18
  92.3 3.6 %collective-permute-done.24.refs_6_ = f32[2,64,256]{2,1,0:T(8,128)S(1)} collective-permute-done((f32[2,64,256]{2,1,0:T(8,128)S(1)}, f32[2,64,256]{2,1,0:T(8,128)S(1)}, u32[]{:S(2)}, u32[]{:S(2)}) %collective-permute-start.24) | collective-permute-done | bytes 131104 | tf_op jit(solution)/shard_map/ppermute | solution.py:18
  95.9 2.2 %collective-permute-done.25.refs_7_ = f32[2,64,256]{2,1,0:T(8,128)S(1)} collective-permute-done((f32[2,64,256]{2,1,0:T(8,128)S(1)}, f32[2,64,256]{2,1,0:T(8,128)S(1)}, u32[]{:S(2)}, u32[]{:S(2)}) %collective-permute-start.25) | collective-permute-done | bytes 131104 | tf_op jit(solution)/shard_map/ppermute | solution.py:18
  98.2 1.8 %collective-permute-start.26 = (f32[64,256]{1,0:T(8,128)S(1)}, f32[64,256]{1,0:T(8,128)S(1)}, u32[]{:S(2)}, u32[]{:S(2)}) collective-permute-start(f32[64,256]{1,0:T(8,128)S(1)} %get-tuple-element.75), channel_id=1, source_target_pairs={{0,64},{4,68},{8,72},{12,76},{16,80},{20,84},{24,88},{28,92},{32,9... | collective-permute-start | bytes 196616 | tf_op jit(solution)/shard_map/ppermute | solution.py:18
  100.0 2.9 %collective-permute-start.27 = (f32[64,256]{1,0:T(8,128)S(1)}, f32[64,256]{1,0:T(8,128)S(1)}, u32[]{:S(2)}, u32[]{:S(2)}) collective-permute-start(f32[64,256]{1,0:T(8,128)S(1)} %get-tuple-element.76), channel_id=1, source_target_pairs={{0,128},{4,132},{8,136},{12,140},{16,144},{20,148},{24,152},{28,15... | collective-permute-start | bytes 196616 | tf_op jit(solution)/shard_map/ppermute | solution.py:18
  103.0 2.9 %collective-permute-done.27.refs_2_ = f32[64,256]{1,0:T(8,128)S(1)} collective-permute-done((f32[64,256]{1,0:T(8,128)S(1)}, f32[64,256]{1,0:T(8,128)S(1)}, u32[]{:S(2)}, u32[]{:S(2)}) %collective-permute-start.27) | collective-permute-done | bytes 65568 | tf_op jit(solution)/shard_map/ppermute | solution.py:18
  105.9 2.5 %collective-permute-done.28.refs_3_ = f32[64,256]{1,0:T(8,128)S(1)} collective-permute-done((f32[64,256]{1,0:T(8,128)S(1)}, f32[64,256]{1,0:T(8,128)S(1)}, u32[]{:S(2)}, u32[]{:S(2)}) %collective-permute-start.28) | collective-permute-done | bytes 65568 | tf_op jit(solution)/shard_map/ppermute | solution.py:18
  108.4 2.2 %collective-permute-start.29 = (f32[32,256]{1,0:T(8,128)S(1)}, f32[32,256]{1,0:T(8,128)S(1)}, u32[]{:S(2)}, u32[]{:S(2)}) collective-permute-start(f32[32,256]{1,0:T(8,128)S(1)} %get-tuple-element.79), channel_id=1, source_target_pairs={{0,12},{4,8},{8,4},{12,0},{16,28},{20,24},{24,20},{28,16},{32,44},... | collective-permute-start | bytes 98312 | tf_op jit(solution)/shard_map/ppermute | solution.py:18
  110.7 3.9 %collective-permute-done.29.refs_1_ = f32[32,256]{1,0:T(8,128)S(1)} collective-permute-done((f32[32,256]{1,0:T(8,128)S(1)}, f32[32,256]{1,0:T(8,128)S(1)}, u32[]{:S(2)}, u32[]{:S(2)}) %collective-permute-start.29) | collective-permute-done | bytes 32800 | tf_op jit(solution)/shard_map/ppermute | solution.py:18
  114.6 2.3 %collective-permute-start.30 = (f32[16,256]{1,0:T(8,128)S(1)}, f32[16,256]{1,0:T(8,128)S(1)}, u32[]{:S(2)}, u32[]{:S(2)}) collective-permute-start(f32[16,256]{1,0:T(8,128)S(1)} %get-tuple-element.81), channel_id=1, source_target_pairs={{0,4},{4,0},{8,12},{12,8},{16,20},{20,16},{24,28},{28,24},{32,36},... | collective-permute-start | bytes 49160 | tf_op jit(solution)/shard_map/ppermute | solution.py:18
  116.8 2.4 %collective-permute-done.30 = f32[16,256]{1,0:T(8,128)S(1)} collective-permute-done((f32[16,256]{1,0:T(8,128)S(1)}, f32[16,256]{1,0:T(8,128)S(1)}, u32[]{:S(2)}, u32[]{:S(2)}) %collective-permute-start.30) | collective-permute-done | bytes 16416 | tf_op jit(solution)/shard_map/ppermute | solution.py:18
  119.3 0.6 add_multiply_fusion
  (46 shorter events, 1.8 us)
Async XLA Ops:
  0.6 8.0 %copy-start = (f32[6,1024,128]{2,1,0:T(8,128)S(1)}, f32[6,1024,128]{2,1,0:T(8,128)}, u32[]{:S(2)}) copy-start(f32[6,1024,128]{2,1,0:T(8,128)} %c_ref.3) | copy-start | bytes 9437188
  0.6 1.4 %copy-start.1 = (f32[1024,256]{1,0:T(8,128)S(1)}, f32[1024,256]{1,0:T(8,128)}, u32[]{:S(2)}) copy-start(f32[1024,256]{1,0:T(8,128)} %p_ref.3) | copy-start | bytes 3145732
  2.0 16.2 %copy-start.4 = (s32[1,8,8]{2,1,0:T(8,128)S(1)}, s32[1,8,8]{2,1,0:T(8,128)}, u32[]{:S(2)}) copy-start(s32[1,8,8]{2,1,0:T(8,128)} %param.6) | copy-start | bytes 772
  4.4 8.5 %collective-permute-start = (f32[128,256]{1,0:T(8,128)S(1)}, f32[128,256]{1,0:T(8,128)S(1)}, u32[]{:S(2)}, u32[]{:S(2)}) collective-permute-start(f32[128,256]{1,0:T(8,128)S(1)} %get-tuple-element.42), channel_id=1, source_target_pairs={{0,32},{4,36},{8,40},{12,44},{16,48},{20,52},{24,56},{28,60},{32,0... | collective-permute-start | bytes 393224 | tf_op jit(solution)/shard_map/ppermute | solution.py:18
  7.5 6.5 %collective-permute-start.1 = (f32[128,256]{1,0:T(8,128)S(1)}, f32[128,256]{1,0:T(8,128)S(1)}, u32[]{:S(2)}, u32[]{:S(2)}) collective-permute-start(f32[128,256]{1,0:T(8,128)S(1)} %get-tuple-element.43), channel_id=1, source_target_pairs={{0,48},{4,52},{8,56},{12,60},{16,32},{20,36},{24,40},{28,44},{32,1... | collective-permute-start | bytes 393224 | tf_op jit(solution)/shard_map/ppermute | solution.py:18
  8.6 21.3 %copy-start.3 = (f32[1024,1024]{1,0:T(8,128)S(1)}, f32[1024,1024]{1,0:T(8,128)}, u32[]{:S(2)}) copy-start(f32[1024,1024]{1,0:T(8,128)} %param.5) | copy-start | bytes 12582916
  8.6 4.3 %collective-permute-start.2 = (f32[64,256]{1,0:T(8,128)S(1)}, f32[64,256]{1,0:T(8,128)S(1)}, u32[]{:S(2)}, u32[]{:S(2)}) collective-permute-start(f32[64,256]{1,0:T(8,128)S(1)} %get-tuple-element.45), channel_id=1, source_target_pairs={{0,16},{4,20},{8,24},{12,28},{16,0},{20,4},{24,8},{28,12},{32,48},... | collective-permute-start | bytes 196616 | tf_op jit(solution)/shard_map/ppermute | solution.py:18
  9.5 8.8 %collective-permute-start.9 = (f32[128,256]{1,0:T(8,128)S(1)}, f32[128,256]{1,0:T(8,128)S(1)}, u32[]{:S(2)}, u32[]{:S(2)}) collective-permute-start(f32[128,256]{1,0:T(8,128)S(1)} %get-tuple-element.51), channel_id=1, source_target_pairs={{0,4},{4,0},{8,12},{12,8},{16,20},{20,16},{24,28},{28,24},{32,36},... | collective-permute-start | bytes 393224 | tf_op jit(solution)/shard_map/ppermute | solution.py:18
  14.0 9.7 %collective-permute-start.5 = (f32[32,256]{1,0:T(8,128)S(1)}, f32[32,256]{1,0:T(8,128)S(1)}, u32[]{:S(2)}, u32[]{:S(2)}) collective-permute-start(f32[32,256]{1,0:T(8,128)S(1)} %get-tuple-element.85), channel_id=1, source_target_pairs={{0,192},{4,196},{8,200},{12,204},{16,208},{20,212},{24,216},{28,22... | collective-permute-start | bytes 98312 | tf_op jit(solution)/shard_map/ppermute | solution.py:18
  17.1 6.6 %collective-permute-start.4 = (f32[32,256]{1,0:T(8,128)S(1)}, f32[32,256]{1,0:T(8,128)S(1)}, u32[]{:S(2)}, u32[]{:S(2)}) collective-permute-start(f32[32,256]{1,0:T(8,128)S(1)} %get-tuple-element.85), channel_id=1, source_target_pairs={{0,128},{4,132},{8,136},{12,140},{16,144},{20,148},{24,152},{28,15... | collective-permute-start | bytes 98312 | tf_op jit(solution)/shard_map/ppermute | solution.py:18
  17.8 6.0 %collective-permute-start.3 = (f32[32,256]{1,0:T(8,128)S(1)}, f32[32,256]{1,0:T(8,128)S(1)}, u32[]{:S(2)}, u32[]{:S(2)}) collective-permute-start(f32[32,256]{1,0:T(8,128)S(1)} %get-tuple-element.84), channel_id=1, source_target_pairs={{0,64},{4,68},{8,72},{12,76},{16,80},{20,84},{24,88},{28,92},{32,9... | collective-permute-start | bytes 98312 | tf_op jit(solution)/shard_map/ppermute | solution.py:18
  18.3 18.1 %collective-permute-start.10 = (f32[128,256]{1,0:T(8,128)S(1)}, f32[128,256]{1,0:T(8,128)S(1)}, u32[]{:S(2)}, u32[]{:S(2)}) collective-permute-start(f32[128,256]{1,0:T(8,128)S(1)} %add.36), channel_id=1, source_target_pairs={{0,12},{4,8},{8,4},{12,0},{16,28},{20,24},{24,20},{28,16},{32,44},... | collective-permute-start | bytes 393224 | tf_op jit(solution)/shard_map/ppermute | solution.py:18
  23.8 12.5 %collective-permute-start.7 = (f32[128,256]{1,0:T(8,128)S(1)}, f32[128,256]{1,0:T(8,128)S(1)}, u32[]{:S(2)}, u32[]{:S(2)}) collective-permute-start(f32[128,256]{1,0:T(8,128)S(1)} %get-tuple-element.48), channel_id=1, source_target_pairs={{0,12},{4,8},{8,4},{12,0},{16,28},{20,24},{24,20},{28,16},{32,44},... | collective-permute-start | bytes 393224 | tf_op jit(solution)/shard_map/ppermute | solution.py:18
  28.1 8.2 %collective-permute-start.6 = (f32[128,256]{1,0:T(8,128)S(1)}, f32[128,256]{1,0:T(8,128)S(1)}, u32[]{:S(2)}, u32[]{:S(2)}) collective-permute-start(f32[128,256]{1,0:T(8,128)S(1)} %pad_maximum_fusion), channel_id=1, source_target_pairs={{0,4},{4,0},{8,12},{12,8},{16,20},{20,16},{24,28},{28,24},{32,36},... | collective-permute-start | bytes 393224 | tf_op jit(solution)/shard_map/ppermute | solution.py:18
  29.9 20.1 %copy-start.2 = (f32[6,1024,128]{2,1,0:T(8,128)S(1)}, f32[6,1024,128]{2,1,0:T(8,128)}, u32[]{:S(2)}) copy-start(f32[6,1024,128]{2,1,0:T(8,128)} %u_ref.1) | copy-start | bytes 9437188
  36.3 8.3 %collective-permute-start.12 = (f32[128,256]{1,0:T(8,128)S(1)}, f32[128,256]{1,0:T(8,128)S(1)}, u32[]{:S(2)}, u32[]{:S(2)}) collective-permute-start(f32[128,256]{1,0:T(8,128)S(1)} %add.35), channel_id=1, source_target_pairs={{0,12},{4,8},{8,4},{12,0},{16,28},{20,24},{24,20},{28,16},{32,44},... | collective-permute-start | bytes 393224 | tf_op jit(solution)/shard_map/ppermute | solution.py:18
  36.4 12.0 %collective-permute-start.11 = (f32[128,256]{1,0:T(8,128)S(1)}, f32[128,256]{1,0:T(8,128)S(1)}, u32[]{:S(2)}, u32[]{:S(2)}) collective-permute-start(f32[128,256]{1,0:T(8,128)S(1)} %add.37), channel_id=1, source_target_pairs={{0,16},{4,20},{8,24},{12,28},{16,0},{20,4},{24,8},{28,12},{32,48},... | collective-permute-start | bytes 393224 | tf_op jit(solution)/shard_map/ppermute | solution.py:18
  39.1 10.9 %collective-permute-start.8 = (f32[128,256]{1,0:T(8,128)S(1)}, f32[128,256]{1,0:T(8,128)S(1)}, u32[]{:S(2)}, u32[]{:S(2)}) collective-permute-start(f32[128,256]{1,0:T(8,128)S(1)} %collective-permute-done.7.o_ref), channel_id=1, source_target_pairs={{0,4},{4,0},{8,12},{12,8},{16,20},{20,16},{24,28},{28,24},{32,36},... | collective-permute-start | bytes 393224 | tf_op jit(solution)/shard_map/ppermute | solution.py:18
  44.6 9.6 %collective-permute-start.13 = (f32[128,256]{1,0:T(8,128)S(1)}, f32[128,256]{1,0:T(8,128)S(1)}, u32[]{:S(2)}, u32[]{:S(2)}) collective-permute-start(f32[128,256]{1,0:T(8,128)S(1)} %get-tuple-element.57), channel_id=1, source_target_pairs={{0,4},{4,0},{8,12},{12,8},{16,20},{20,16},{24,28},{28,24},{32,36},... | collective-permute-start | bytes 393224 | tf_op jit(solution)/shard_map/ppermute | solution.py:18
  44.8 9.3 %collective-permute-start.14 = (f32[128,256]{1,0:T(8,128)S(1)}, f32[128,256]{1,0:T(8,128)S(1)}, u32[]{:S(2)}, u32[]{:S(2)}) collective-permute-start(f32[128,256]{1,0:T(8,128)S(1)} %add.38.q0), channel_id=1, source_target_pairs={{0,16},{4,20},{8,24},{12,28},{16,0},{20,4},{24,8},{28,12},{32,48},... | collective-permute-start | bytes 393224 | tf_op jit(solution)/shard_map/ppermute | solution.py:18
  47.2 5.7 %collective-permute-start.16 = (f32[64,256]{1,0:T(8,128)S(1)}, f32[64,256]{1,0:T(8,128)S(1)}, u32[]{:S(2)}, u32[]{:S(2)}) collective-permute-start(f32[64,256]{1,0:T(8,128)S(1)} %slice.28), channel_id=1, source_target_pairs={{0,48},{4,52},{8,56},{12,60},{16,32},{20,36},{24,40},{28,44},{32,1... | collective-permute-start | bytes 196616 | tf_op jit(solution)/shard_map/ppermute | solution.py:18
  48.4 5.8 %collective-permute-start.15 = (f32[64,256]{1,0:T(8,128)S(1)}, f32[64,256]{1,0:T(8,128)S(1)}, u32[]{:S(2)}, u32[]{:S(2)}) collective-permute-start(f32[64,256]{1,0:T(8,128)S(1)} %slice.28), channel_id=1, source_target_pairs={{0,32},{4,36},{8,40},{12,44},{16,48},{20,52},{24,56},{28,60},{32,0... | collective-permute-start | bytes 196616 | tf_op jit(solution)/shard_map/ppermute | solution.py:18
  56.2 2.7 %collective-permute-start.18 = (f32[1024,256]{1,0:T(8,128)S(1)}, f32[1024,256]{1,0:T(8,128)S(1)}, u32[]{:S(2)}, u32[]{:S(2)}) collective-permute-start(f32[1024,256]{1,0:T(8,128)S(1)} %get-tuple-element.60.refs_0_), channel_id=1, source_target_pairs={{0,1},{1,0},{2,3},{3,2},{4,5},{5,4},{6,7},{7,6},{8,9},{9,8},{10,11... | collective-permute-start | bytes 3145736 | tf_op jit(solution)/shard_map/ppermute | solution.py:18
  56.2 25.9 %collective-permute-start.17 = (f32[1024,256]{1,0:T(8,128)S(1)}, f32[1024,256]{1,0:T(8,128)S(1)}, u32[]{:S(2)}, u32[]{:S(2)}) collective-permute-start(f32[1024,256]{1,0:T(8,128)S(1)} %get-tuple-element.60.refs_0_), channel_id=1, source_target_pairs={{0,2},{1,3},{2,0},{3,1},{4,6},{5,7},{6,4},{7,5},{8,10},{9,11},{10,... | collective-permute-start | bytes 3145736 | tf_op jit(solution)/shard_map/ppermute | solution.py:18
  59.9 22.2 %collective-permute-start.19 = (f32[2,64,256]{2,1,0:T(8,128)S(1)}, f32[2,64,256]{2,1,0:T(8,128)S(1)}, u32[]{:S(2)}, u32[]{:S(2)}) collective-permute-start(f32[2,64,256]{2,1,0:T(8,128)S(1)} %get-tuple-element.62), channel_id=1, source_target_pairs={{0,16},{4,20},{8,24},{12,28},{16,0},{20,4},{24,8},{28,12},{32,48},... | collective-permute-start | bytes 393224 | tf_op jit(solution)/shard_map/ppermute | solution.py:18
  61.3 20.8 %collective-permute-start.20 = (f32[2,64,256]{2,1,0:T(8,128)S(1)}, f32[2,64,256]{2,1,0:T(8,128)S(1)}, u32[]{:S(2)}, u32[]{:S(2)}) collective-permute-start(f32[2,64,256]{2,1,0:T(8,128)S(1)} %get-tuple-element.63), channel_id=1, source_target_pairs={{0,32},{4,36},{8,40},{12,44},{16,48},{20,52},{24,56},{28,60},{32,0... | collective-permute-start | bytes 393224 | tf_op jit(solution)/shard_map/ppermute | solution.py:18
  63.5 18.6 %collective-permute-start.21 = (f32[2,64,256]{2,1,0:T(8,128)S(1)}, f32[2,64,256]{2,1,0:T(8,128)S(1)}, u32[]{:S(2)}, u32[]{:S(2)}) collective-permute-start(f32[2,64,256]{2,1,0:T(8,128)S(1)} %get-tuple-element.64), channel_id=1, source_target_pairs={{0,48},{4,52},{8,56},{12,60},{16,32},{20,36},{24,40},{28,44},{32,1... | collective-permute-start | bytes 393224 | tf_op jit(solution)/shard_map/ppermute | solution.py:18
  82.1 2.7 %collective-permute-start.22 = (f32[1024,256]{1,0:T(8,128)S(1)}, f32[1024,256]{1,0:T(8,128)S(1)}, u32[]{:S(2)}, u32[]{:S(2)}) collective-permute-start(f32[1024,256]{1,0:T(8,128)S(1)} %collective-permute-done.17.refs_1_), channel_id=1, source_target_pairs={{0,1},{1,0},{2,3},{3,2},{4,5},{5,4},{6,7},{7,6},{8,9},{9,8},{10,11... | collective-permute-start | bytes 3145736 | tf_op jit(solution)/shard_map/ppermute | solution.py:18
  85.9 6.4 %collective-permute-start.23 = (f32[2,64,256]{2,1,0:T(8,128)S(1)}, f32[2,64,256]{2,1,0:T(8,128)S(1)}, u32[]{:S(2)}, u32[]{:S(2)}) collective-permute-start(f32[2,64,256]{2,1,0:T(8,128)S(1)} %get-tuple-element.71), channel_id=1, source_target_pairs={{0,16},{4,20},{8,24},{12,28},{16,0},{20,4},{24,8},{28,12},{32,48},... | collective-permute-start | bytes 393224 | tf_op jit(solution)/shard_map/ppermute | solution.py:18
  87.3 8.6 %collective-permute-start.24 = (f32[2,64,256]{2,1,0:T(8,128)S(1)}, f32[2,64,256]{2,1,0:T(8,128)S(1)}, u32[]{:S(2)}, u32[]{:S(2)}) collective-permute-start(f32[2,64,256]{2,1,0:T(8,128)S(1)} %get-tuple-element.72), channel_id=1, source_target_pairs={{0,32},{4,36},{8,40},{12,44},{16,48},{20,52},{24,56},{28,60},{32,0... | collective-permute-start | bytes 393224 | tf_op jit(solution)/shard_map/ppermute | solution.py:18
  89.5 8.7 %collective-permute-start.25 = (f32[2,64,256]{2,1,0:T(8,128)S(1)}, f32[2,64,256]{2,1,0:T(8,128)S(1)}, u32[]{:S(2)}, u32[]{:S(2)}) collective-permute-start(f32[2,64,256]{2,1,0:T(8,128)S(1)} %get-tuple-element.73), channel_id=1, source_target_pairs={{0,48},{4,52},{8,56},{12,60},{16,32},{20,36},{24,40},{28,44},{32,1... | collective-permute-start | bytes 393224 | tf_op jit(solution)/shard_map/ppermute | solution.py:18
  98.2 4.8 %collective-permute-start.26 = (f32[64,256]{1,0:T(8,128)S(1)}, f32[64,256]{1,0:T(8,128)S(1)}, u32[]{:S(2)}, u32[]{:S(2)}) collective-permute-start(f32[64,256]{1,0:T(8,128)S(1)} %get-tuple-element.75), channel_id=1, source_target_pairs={{0,64},{4,68},{8,72},{12,76},{16,80},{20,84},{24,88},{28,92},{32,9... | collective-permute-start | bytes 196616 | tf_op jit(solution)/shard_map/ppermute | solution.py:18
  100.0 5.8 %collective-permute-start.27 = (f32[64,256]{1,0:T(8,128)S(1)}, f32[64,256]{1,0:T(8,128)S(1)}, u32[]{:S(2)}, u32[]{:S(2)}) collective-permute-start(f32[64,256]{1,0:T(8,128)S(1)} %get-tuple-element.76), channel_id=1, source_target_pairs={{0,128},{4,132},{8,136},{12,140},{16,144},{20,148},{24,152},{28,15... | collective-permute-start | bytes 196616 | tf_op jit(solution)/shard_map/ppermute | solution.py:18
  102.9 5.5 %collective-permute-start.28 = (f32[64,256]{1,0:T(8,128)S(1)}, f32[64,256]{1,0:T(8,128)S(1)}, u32[]{:S(2)}, u32[]{:S(2)}) collective-permute-start(f32[64,256]{1,0:T(8,128)S(1)} %get-tuple-element.77), channel_id=1, source_target_pairs={{0,192},{4,196},{8,200},{12,204},{16,208},{20,212},{24,216},{28,22... | collective-permute-start | bytes 196616 | tf_op jit(solution)/shard_map/ppermute | solution.py:18
  108.4 6.1 %collective-permute-start.29 = (f32[32,256]{1,0:T(8,128)S(1)}, f32[32,256]{1,0:T(8,128)S(1)}, u32[]{:S(2)}, u32[]{:S(2)}) collective-permute-start(f32[32,256]{1,0:T(8,128)S(1)} %get-tuple-element.79), channel_id=1, source_target_pairs={{0,12},{4,8},{8,4},{12,0},{16,28},{20,24},{24,20},{28,16},{32,44},... | collective-permute-start | bytes 98312 | tf_op jit(solution)/shard_map/ppermute | solution.py:18
  114.6 4.7 %collective-permute-start.30 = (f32[16,256]{1,0:T(8,128)S(1)}, f32[16,256]{1,0:T(8,128)S(1)}, u32[]{:S(2)}, u32[]{:S(2)}) collective-permute-start(f32[16,256]{1,0:T(8,128)S(1)} %get-tuple-element.81), channel_id=1, source_target_pairs={{0,4},{4,0},{8,12},{12,8},{16,20},{20,16},{24,28},{28,24},{32,36},... | collective-permute-start | bytes 49160 | tf_op jit(solution)/shard_map/ppermute | solution.py:18

commit v6 on v5

--- a/solution.py
+++ b/solution.py
@@ -10,7 +10,7 @@
 HIGH = lax.Precision.HIGH
 F32 = jnp.float32
 LIMIT = 40 * 2**20
-MOST = 52 * 2**20
+MOST = 53 * 2**20
 
 
 def swap(value, axis, mask):
@@ -63,12 +63,61 @@
     return leaf >> 4, (leaf >> 2) & 3, leaf & 3
 
 
+CUTS = 4
+
+
+def project(columns, probes, first, outs, emit):
+    _, points, rank = columns.shape
+    wide = probes.shape[1]
+    piece = points // CUTS
+
+    def body(c_hbm, p_hbm, *refs):
+        *results, held, given, total, sems = refs
+        copies = [
+            pltpu.make_async_copy(
+                p_hbm.at[pl.ds(i * piece, piece)], given.at[pl.ds(i * piece, piece)], sems.at[0, i]
+            )
+            for i in range(CUTS)
+        ]
+        for level in range(3):
+            for i in range(CUTS):
+                copies.append(
+                    pltpu.make_async_copy(
+                        c_hbm.at[first + level, pl.ds(i * piece, piece)],
+                        held.at[level, pl.ds(i * piece, piece)],
+                        sems.at[level + 1, i],
+                    )
+                )
+        for copy in copies:
+            copy.start()
+        for copy in copies[:CUTS]:
+            copy.wait()
+        right = split(given[...])
+        for level in range(3):
+            for copy in copies[(level + 1) * CUTS:(level + 2) * CUTS]:
+                copy.wait()
+            total[level] = dot3(split(held[level]), right, ROWS)
+        emit(total, *results)
+
+    return call(
+        body,
+        outs,
+        [pl.BlockSpec(memory_space=pltpu.HBM)] * 2,
+        [columns, probes],
+        [
+            pltpu.VMEM((3, points, rank), F32),
+            pltpu.VMEM((points, wide), F32),
+            pltpu.VMEM((3, rank, wide), F32),
+            pltpu.SemaphoreType.DMA((4, CUTS)),
+        ],
+        flops=18 * points * rank * wide,
+        limit=MOST,
+    )
+
+
 def project_high(columns, probes):
-    def body(c_ref, p_ref, keep, one, two, three, total):
+    def emit(total, keep, one, two, three):
         _, x, _ = place()
-        right = split(p_ref[...])
-        for level in range(3):
-            total[level] = dot3(split(c_ref[level]), right, ROWS)
         for part, out in ((1, one), (2, two), (3, three)):
             base = 0 if part == 1 else 64
             if part > 1:
@@ -81,35 +130,18 @@
         keep[:32] = total[1, pl.ds(row, 32)]
         keep[32:] = total[2, pl.ds(row, 32)]
 
-    _, points, rank = columns.shape
     wide = probes.shape[1]
-    return call(
-        body,
-        shapes((64, wide), (64, wide), (128, wide), (128, wide)),
-        [pl.BlockSpec((3, points, rank), lambda _: (1, 0, 0)), whole(probes.shape)],
-        [columns, probes],
-        [pltpu.VMEM((3, rank, wide), F32)],
-        flops=18 * points * rank * wide,
-        limit=MOST,
-    )
+    outs = shapes((64, wide), (64, wide), (128, wide), (128, wide))
+    return project(columns, probes, 3, outs, emit)
 
 
 def project_low(columns, probes):
-    def body(c_ref, p_ref, *outs):
-        right = split(p_ref[...])
+    def emit(total, *outs):
         for level, out in enumerate(outs):
-            out[...] = dot3(split(c_ref[level]), right, ROWS)
-
-    _, points, rank = columns.shape
-    wide = probes.shape[1]
-    return call(
-        body,
-        shapes(*[(rank, wide)] * 3),
-        [pl.BlockSpec((3, points, rank), lambda _: (0, 0, 0)), whole(probes.shape)],
-        [columns, probes],
-        flops=18 * points * rank * wide,
-        limit=LIMIT,
-    )
+            out[...] = total[level]
+
+    outs = shapes(*[(columns.shape[2], probes.shape[1])] * 3)
+    return project(columns, probes, 0, outs, emit)
 
 
 LATE = (0, 3, 4, 5)
@@ -249,7 +281,7 @@
     return [parts[0]] + [swap(parts[k], "leaf", k * scale) for k in (1, 2, 3)]
 
 
-def local(leaf_blocks, block_mask, row_factor_stack, column_factor_stack, probes):
+def near_product(leaf_blocks, block_mask, probes):
     leaf_points = leaf_blocks.shape[1]
     side = block_mask.shape[1]
     span = leaf_points // side
@@ -258,8 +290,11 @@
     masked = (
         leaf_blocks.reshape(side, span, side, span) * weights[:, None, :, None]
     ).reshape(leaf_points, leaf_points)
-    near = jnp.dot(masked, probes, precision=HIGH, preferred_element_type=F32)
-
+    return jnp.dot(masked, probes, precision=HIGH, preferred_element_type=F32)
+
+
+def local(leaf_blocks, block_mask, row_factor_stack, column_factor_stack, probes):
+    leaf_points = leaf_blocks.shape[1]
     keep, *sent = project_high(column_factor_stack, probes)
     _, one, two, three = around([keep, *sent], 4)
     low0, low1, low2 = project_low(column_factor_stack, probes)
@@ -272,10 +307,12 @@
     part = jnp.concatenate([part3, part4, part5])
     low2 = low2 + swap(low2, "leaf", 3)
     node2 = swap(low2, "leaf", 4)
-    part, low1 = lax.optimization_barrier((part, low1))
+    part, blocks, low1 = lax.optimization_barrier((part, leaf_blocks, low1))
+    near = near_product(blocks, block_mask, probes)
     part = part + swap(part, "leaf", 1)
+    near, low1 = lax.optimization_barrier((near, low1))
     node1 = swap(low1, "leaf", 3)
-    part, node1, near = lax.optimization_barrier((part, node1, near))
+    part, near = lax.optimization_barrier((part, near))
     part = part + swap(part, "leaf", 3)
     node1_more = swap(node1, "leaf", 1)
     part, low0 = lax.optimization_barrier((part, low0))

time: 120 us -> 120 us (level)
  Pallas kernels: 9.05 us -> 12.3 us
  starting transfers between devices: 55.1 us -> 53 us
  local copies, waits for them, and re-layouts: 1.73 us -> 0.36 us
    pallas_call x9, Pallas kernels: 9.05 us -> 12.3 us  [call(): pl.pallas_call(body, out_shape=outs, grid=grid, in_specs=specs, out_specs...]
    ppermute x31, starting transfers between devices: 55.1 us -> 53 us  [swap(): return lax.ppermute(value, axis, pairs)]
    unnamed x10 -> x8, local copies, waits for them, and re-layouts: 1.39 us -> 0.02 us
  transfers between devices with their start and end apart: 31 -> 31, of which waited for: 17 -> 17; matrix products, arithmetic and copies ran while one was open for 2% -> 2% of each run, Pallas kernels for 3% -> 5%
where the time goes in v6:
time: 120 us; the launch traced here: 119 us
  starting transfers between devices  53 us (44%)
  waiting for transfers between devices  49.2 us (41%)
  Pallas kernels  12.3 us (10%)
  matrix products  2.39 us (2%)
    ppermute x31, starting transfers between devices, swap(): return lax.ppermute(value, axis, pairs)  53 us
    ppermute x31, waiting for transfers between devices, swap(): return lax.ppermute(value, axis, pairs)  49.2 us
    pallas_call x9, Pallas kernels, call(): pl.pallas_call(body, out_shape=outs, grid=grid, in_specs=specs, out_specs...  12.3 us
  transfers between devices with their start and end apart: 31, of which 17 were waited for; matrix products, arithmetic and copies ran while one was open for 2% of the time, Pallas kernels for 5%

profile of v6, /device:TPU:32, one launch (start us, length us, event | category | flops | bytes accessed | tf_op | source)
XLA Modules:
  0.0 118.8 jit_solution(7758160829965886134)
XLA Ops:
  0.6 3.1 %shard_map.68 = (f32[64,256]{1,0:T(8,128)S(1)}, f32[64,256]{1,0:T(8,128)S(1)}, f32[128,256]{1,0:T(8,128)S(1)}, f32[128,256]{1,0:T(8,128)S(1)}) custom-call(f32[6,1024,128]{2,1,0:T(8,128)} %c_hbm.3, f32[1024,256]{1,0:T(8,128)} %p_hbm.3), custom_call_target="tpu_custom_call" | custom-call | flops 603979776 | bytes 4587520 | tf_op jit(solution)/shard_map/pallas_call | solution.py:49
  3.8 3.1 %collective-permute-start = (f32[128,256]{1,0:T(8,128)S(1)}, f32[128,256]{1,0:T(8,128)S(1)}, u32[]{:S(2)}, u32[]{:S(2)}) collective-permute-start(f32[128,256]{1,0:T(8,128)S(1)} %get-tuple-element.44), channel_id=1, source_target_pairs={{0,32},{4,36},{8,40},{12,44},{16,48},{20,52},{24,56},{28,60},{32,0... | collective-permute-start | bytes 393224 | tf_op jit(solution)/shard_map/ppermute | solution.py:18
  6.9 1.1 collective-permute-start.1
  8.0 3.3 %shard_map.69 = (f32[128,256]{1,0:T(8,128)S(1)}, f32[128,256]{1,0:T(8,128)S(1)}, f32[128,256]{1,0:T(8,128)S(1)}) custom-call(f32[6,1024,128]{2,1,0:T(8,128)} %c_hbm.3, f32[1024,256]{1,0:T(8,128)} %p_hbm.3), custom_call_target="tpu_custom_call" | custom-call | flops 603979776 | bytes 4587520 | tf_op jit(solution)/shard_map/pallas_call | solution.py:49
  11.3 3.4 %collective-permute-start.9 = (f32[128,256]{1,0:T(8,128)S(1)}, f32[128,256]{1,0:T(8,128)S(1)}, u32[]{:S(2)}, u32[]{:S(2)}) collective-permute-start(f32[128,256]{1,0:T(8,128)S(1)} %get-tuple-element.55), channel_id=1, source_target_pairs={{0,4},{4,0},{8,12},{12,8},{16,20},{20,16},{24,28},{28,24},{32,36},... | collective-permute-start | bytes 393224 | tf_op jit(solution)/shard_map/ppermute | solution.py:18
  14.8 3.1 %collective-permute-start.5 = (f32[32,256]{1,0:T(8,128)S(1)}, f32[32,256]{1,0:T(8,128)S(1)}, u32[]{:S(2)}, u32[]{:S(2)}) collective-permute-start(f32[32,256]{1,0:T(8,128)S(1)} %get-tuple-element.89), channel_id=1, source_target_pairs={{0,192},{4,196},{8,200},{12,204},{16,208},{20,212},{24,216},{28,22... | collective-permute-start | bytes 98312 | tf_op jit(solution)/shard_map/ppermute | solution.py:18
  17.8 0.6 collective-permute-start.4
  18.5 0.5 collective-permute-start.3
  19.3 6.1 %collective-permute-start.10 = (f32[128,256]{1,0:T(8,128)S(1)}, f32[128,256]{1,0:T(8,128)S(1)}, u32[]{:S(2)}, u32[]{:S(2)}) collective-permute-start(f32[128,256]{1,0:T(8,128)S(1)} %add.36), channel_id=1, source_target_pairs={{0,12},{4,8},{8,4},{12,0},{16,28},{20,24},{24,20},{28,16},{32,44},... | collective-permute-start | bytes 393224 | tf_op jit(solution)/shard_map/ppermute | solution.py:18
  25.5 0.3 mul.11
  25.9 2.4 %fusion.n_ref = f32[1024,256]{1,0:T(8,128)S(1)} fusion(f32[1024,256]{1,0:T(8,128)S(1)} %copy-done.1, f32[1024,1024]{1,0:T(8,128)S(1)} %copy-done.2, f32[128,8,8,128]{3,2,1,0:T(8,128)S(1)} %bitcast.8), kind=kOutput, calls=%fused_computation.1 | convolution fusion | flops 1611661312 | bytes 10485760 | tf_op jit(solution)/shard_map/dot_general | solution.py:293
  28.3 3.5 %collective-permute-start.7 = (f32[128,256]{1,0:T(8,128)S(1)}, f32[128,256]{1,0:T(8,128)S(1)}, u32[]{:S(2)}, u32[]{:S(2)}) collective-permute-start(f32[128,256]{1,0:T(8,128)S(1)} %get-tuple-element.54), channel_id=1, source_target_pairs={{0,12},{4,8},{8,4},{12,0},{16,28},{20,24},{24,20},{28,16},{32,44},... | collective-permute-start | bytes 393224 | tf_op jit(solution)/shard_map/ppermute | solution.py:18
  31.8 3.0 %collective-permute-done.6 = f32[128,256]{1,0:T(8,128)S(1)} collective-permute-done((f32[128,256]{1,0:T(8,128)S(1)}, f32[128,256]{1,0:T(8,128)S(1)}, u32[]{:S(2)}, u32[]{:S(2)}) %collective-permute-start.6) | collective-permute-done | bytes 131104 | tf_op jit(solution)/shard_map/ppermute | solution.py:18
  34.9 0.6 collective-permute-start.12
  35.5 2.2 %collective-permute-start.11 = (f32[128,256]{1,0:T(8,128)S(1)}, f32[128,256]{1,0:T(8,128)S(1)}, u32[]{:S(2)}, u32[]{:S(2)}) collective-permute-start(f32[128,256]{1,0:T(8,128)S(1)} %add.37), channel_id=1, source_target_pairs={{0,16},{4,20},{8,24},{12,28},{16,0},{20,4},{24,8},{28,12},{32,48},... | collective-permute-start | bytes 393224 | tf_op jit(solution)/shard_map/ppermute | solution.py:18
  37.7 4.0 %collective-permute-done.7.o_ref = f32[128,256]{1,0:T(8,128)S(1)} collective-permute-done((f32[128,256]{1,0:T(8,128)S(1)}, f32[128,256]{1,0:T(8,128)S(1)}, u32[]{:S(2)}, u32[]{:S(2)}) %collective-permute-start.7) | collective-permute-done | bytes 131104 | tf_op jit(solution)/shard_map/ppermute | solution.py:18
  41.7 2.3 %collective-permute-done.12 = f32[128,256]{1,0:T(8,128)S(1)} collective-permute-done((f32[128,256]{1,0:T(8,128)S(1)}, f32[128,256]{1,0:T(8,128)S(1)}, u32[]{:S(2)}, u32[]{:S(2)}) %collective-permute-start.12) | collective-permute-done | bytes 131104 | tf_op jit(solution)/shard_map/ppermute | solution.py:18
  44.0 0.7 collective-permute-start.13
  44.7 1.6 %collective-permute-start.14 = (f32[128,256]{1,0:T(8,128)S(1)}, f32[128,256]{1,0:T(8,128)S(1)}, u32[]{:S(2)}, u32[]{:S(2)}) collective-permute-start(f32[128,256]{1,0:T(8,128)S(1)} %add.38.q0), channel_id=1, source_target_pairs={{0,16},{4,20},{8,24},{12,28},{16,0},{20,4},{24,8},{28,12},{32,48},... | collective-permute-start | bytes 393224 | tf_op jit(solution)/shard_map/ppermute | solution.py:18
  46.3 1.6 %collective-permute-start.16 = (f32[64,256]{1,0:T(8,128)S(1)}, f32[64,256]{1,0:T(8,128)S(1)}, u32[]{:S(2)}, u32[]{:S(2)}) collective-permute-start(f32[64,256]{1,0:T(8,128)S(1)} %slice.28), channel_id=1, source_target_pairs={{0,48},{4,52},{8,56},{12,60},{16,32},{20,36},{24,40},{28,44},{32,1... | collective-permute-start | bytes 196616 | tf_op jit(solution)/shard_map/ppermute | solution.py:18
  47.9 0.9 collective-permute-start.15
  48.9 1.6 %shard_map.70 = (f32[1024,256]{1,0:T(8,128)S(1)}, bf16[1024,512]{1,0:T(8,128)(2,1)S(1)}, bf16[1024,512]{1,0:T(8,128)(2,1)S(1)}) custom-call(f32[1024,256]{1,0:T(8,128)S(1)} %fusion.n_ref, f32[6,1024,128]{2,1,0:T(8,128)S(1)} %copy-done, f32[128,256]{1,0:T(8,128)S(1)} %collective-permute-done.7.o_ref, f32[128,256]{1,0:T(8,128)S(1)} %collective-permute-done.8.m_ref, ...), custom_call_target="tpu_custom_call" | custom-call | flops 402653184 | bytes 9830400 | tf_op jit(solution)/shard_map/pallas_call | solution.py:49
  50.6 1.9 %collective-permute-done.16.q3 = f32[64,256]{1,0:T(8,128)S(1)} collective-permute-done((f32[64,256]{1,0:T(8,128)S(1)}, f32[64,256]{1,0:T(8,128)S(1)}, u32[]{:S(2)}, u32[]{:S(2)}) %collective-permute-start.16) | collective-permute-done | bytes 65568 | tf_op jit(solution)/shard_map/ppermute | solution.py:18
  52.5 1.2 %collective-permute-done.15.q2 = f32[64,256]{1,0:T(8,128)S(1)} collective-permute-done((f32[64,256]{1,0:T(8,128)S(1)}, f32[64,256]{1,0:T(8,128)S(1)}, u32[]{:S(2)}, u32[]{:S(2)}) %collective-permute-start.15) | collective-permute-done | bytes 65568 | tf_op jit(solution)/shard_map/ppermute | solution.py:18
  53.7 2.0 %shard_map.71 = (f32[1024,256]{1,0:T(8,128)}, f32[1024,256]{1,0:T(8,128)S(1)}) custom-call(f32[1024,256]{1,0:T(8,128)S(1)} %get-tuple-element.56.b_ref, bf16[1024,512]{1,0:T(8,128)(2,1)S(1)} %get-tuple-element.57.h_ref, bf16[1024,512]{1,0:T(8,128)(2,1)S(1)} %get-tuple-element.58.l_ref, f32[128,256]{1,0:T(8,128)S(1)} %collective-permute-done.13.z_ref, ...), custom_call_target="tpu_custom_call" | custom-call | flops 805306368 | bytes 7864320 | tf_op jit(solution)/shard_map/pallas_call | solution.py:49
  55.7 2.4 %collective-permute-start.17 = (f32[1024,256]{1,0:T(8,128)S(1)}, f32[1024,256]{1,0:T(8,128)S(1)}, u32[]{:S(2)}, u32[]{:S(2)}) collective-permute-start(f32[1024,256]{1,0:T(8,128)S(1)} %get-tuple-element.64.refs_0_), channel_id=1, source_target_pairs={{0,2},{1,3},{2,0},{3,1},{4,6},{5,7},{6,4},{7,5},{8,10},{9,11},{10,... | collective-permute-start | bytes 3145736 | tf_op jit(solution)/shard_map/ppermute | solution.py:18
  58.3 1.1 shard_map.72
  59.4 0.7 collective-permute-start.19
  60.2 2.4 %collective-permute-start.20 = (f32[2,64,256]{2,1,0:T(8,128)S(1)}, f32[2,64,256]{2,1,0:T(8,128)S(1)}, u32[]{:S(2)}, u32[]{:S(2)}) collective-permute-start(f32[2,64,256]{2,1,0:T(8,128)S(1)} %get-tuple-element.67), channel_id=1, source_target_pairs={{0,32},{4,36},{8,40},{12,44},{16,48},{20,52},{24,56},{28,60},{32,0... | collective-permute-start | bytes 393224 | tf_op jit(solution)/shard_map/ppermute | solution.py:18
  62.6 1.6 %collective-permute-start.21 = (f32[2,64,256]{2,1,0:T(8,128)S(1)}, f32[2,64,256]{2,1,0:T(8,128)S(1)}, u32[]{:S(2)}, u32[]{:S(2)}) collective-permute-start(f32[2,64,256]{2,1,0:T(8,128)S(1)} %get-tuple-element.68), channel_id=1, source_target_pairs={{0,48},{4,52},{8,56},{12,60},{16,32},{20,36},{24,40},{28,44},{32,1... | collective-permute-start | bytes 393224 | tf_op jit(solution)/shard_map/ppermute | solution.py:18
  64.2 17.7 %collective-permute-done.17.refs_1_ = f32[1024,256]{1,0:T(8,128)S(1)} collective-permute-done((f32[1024,256]{1,0:T(8,128)S(1)}, f32[1024,256]{1,0:T(8,128)S(1)}, u32[]{:S(2)}, u32[]{:S(2)}) %collective-permute-start.17) | collective-permute-done | bytes 1048608 | tf_op jit(solution)/shard_map/ppermute | solution.py:18
  82.0 2.6 %collective-permute-done.22.refs_2_ = f32[1024,256]{1,0:T(8,128)S(1)} collective-permute-done((f32[1024,256]{1,0:T(8,128)S(1)}, f32[1024,256]{1,0:T(8,128)S(1)}, u32[]{:S(2)}, u32[]{:S(2)}) %collective-permute-start.22) | collective-permute-done | bytes 1048608 | tf_op jit(solution)/shard_map/ppermute | solution.py:18
  84.7 1.1 shard_map.73
  85.9 2.7 %collective-permute-start.24 = (f32[2,64,256]{2,1,0:T(8,128)S(1)}, f32[2,64,256]{2,1,0:T(8,128)S(1)}, u32[]{:S(2)}, u32[]{:S(2)}) collective-permute-start(f32[2,64,256]{2,1,0:T(8,128)S(1)} %get-tuple-element.76), channel_id=1, source_target_pairs={{0,32},{4,36},{8,40},{12,44},{16,48},{20,52},{24,56},{28,60},{32,0... | collective-permute-start | bytes 393224 | tf_op jit(solution)/shard_map/ppermute | solution.py:18
  88.7 1.9 %collective-permute-start.25 = (f32[2,64,256]{2,1,0:T(8,128)S(1)}, f32[2,64,256]{2,1,0:T(8,128)S(1)}, u32[]{:S(2)}, u32[]{:S(2)}) collective-permute-start(f32[2,64,256]{2,1,0:T(8,128)S(1)} %get-tuple-element.77), channel_id=1, source_target_pairs={{0,48},{4,52},{8,56},{12,60},{16,32},{20,36},{24,40},{28,44},{32,1... | collective-permute-start | bytes 393224 | tf_op jit(solution)/shard_map/ppermute | solution.py:18
  90.5 1.6 %collective-permute-done.23.refs_5_ = f32[2,64,256]{2,1,0:T(8,128)S(1)} collective-permute-done((f32[2,64,256]{2,1,0:T(8,128)S(1)}, f32[2,64,256]{2,1,0:T(8,128)S(1)}, u32[]{:S(2)}, u32[]{:S(2)}) %collective-permute-start.23) | collective-permute-done | bytes 131104 | tf_op jit(solution)/shard_map/ppermute | solution.py:18
  92.2 2.9 %collective-permute-done.24.refs_6_ = f32[2,64,256]{2,1,0:T(8,128)S(1)} collective-permute-done((f32[2,64,256]{2,1,0:T(8,128)S(1)}, f32[2,64,256]{2,1,0:T(8,128)S(1)}, u32[]{:S(2)}, u32[]{:S(2)}) %collective-permute-start.24) | collective-permute-done | bytes 131104 | tf_op jit(solution)/shard_map/ppermute | solution.py:18
  95.1 2.2 %collective-permute-done.25.refs_7_ = f32[2,64,256]{2,1,0:T(8,128)S(1)} collective-permute-done((f32[2,64,256]{2,1,0:T(8,128)S(1)}, f32[2,64,256]{2,1,0:T(8,128)S(1)}, u32[]{:S(2)}, u32[]{:S(2)}) %collective-permute-start.25) | collective-permute-done | bytes 131104 | tf_op jit(solution)/shard_map/ppermute | solution.py:18
  97.4 1.2 %collective-permute-start.26 = (f32[64,256]{1,0:T(8,128)S(1)}, f32[64,256]{1,0:T(8,128)S(1)}, u32[]{:S(2)}, u32[]{:S(2)}) collective-permute-start(f32[64,256]{1,0:T(8,128)S(1)} %get-tuple-element.79), channel_id=1, source_target_pairs={{0,64},{4,68},{8,72},{12,76},{16,80},{20,84},{24,88},{28,92},{32,9... | collective-permute-start | bytes 196616 | tf_op jit(solution)/shard_map/ppermute | solution.py:18
  98.6 2.9 %collective-permute-start.27 = (f32[64,256]{1,0:T(8,128)S(1)}, f32[64,256]{1,0:T(8,128)S(1)}, u32[]{:S(2)}, u32[]{:S(2)}) collective-permute-start(f32[64,256]{1,0:T(8,128)S(1)} %get-tuple-element.80), channel_id=1, source_target_pairs={{0,128},{4,132},{8,136},{12,140},{16,144},{20,148},{24,152},{28,15... | collective-permute-start | bytes 196616 | tf_op jit(solution)/shard_map/ppermute | solution.py:18
  101.5 0.7 collective-permute-start.28
  102.2 2.3 %collective-permute-done.27.refs_2_ = f32[64,256]{1,0:T(8,128)S(1)} collective-permute-done((f32[64,256]{1,0:T(8,128)S(1)}, f32[64,256]{1,0:T(8,128)S(1)}, u32[]{:S(2)}, u32[]{:S(2)}) %collective-permute-start.27) | collective-permute-done | bytes 65568 | tf_op jit(solution)/shard_map/ppermute | solution.py:18
  104.4 2.5 %collective-permute-done.28.refs_3_ = f32[64,256]{1,0:T(8,128)S(1)} collective-permute-done((f32[64,256]{1,0:T(8,128)S(1)}, f32[64,256]{1,0:T(8,128)S(1)}, u32[]{:S(2)}, u32[]{:S(2)}) %collective-permute-start.28) | collective-permute-done | bytes 65568 | tf_op jit(solution)/shard_map/ppermute | solution.py:18
  107.0 4.5 %collective-permute-start.29 = (f32[32,256]{1,0:T(8,128)S(1)}, f32[32,256]{1,0:T(8,128)S(1)}, u32[]{:S(2)}, u32[]{:S(2)}) collective-permute-start(f32[32,256]{1,0:T(8,128)S(1)} %get-tuple-element.83), channel_id=1, source_target_pairs={{0,12},{4,8},{8,4},{12,0},{16,28},{20,24},{24,20},{28,16},{32,44},... | collective-permute-start | bytes 98312 | tf_op jit(solution)/shard_map/ppermute | solution.py:18
  111.5 1.9 %collective-permute-done.29.refs_1_ = f32[32,256]{1,0:T(8,128)S(1)} collective-permute-done((f32[32,256]{1,0:T(8,128)S(1)}, f32[32,256]{1,0:T(8,128)S(1)}, u32[]{:S(2)}, u32[]{:S(2)}) %collective-permute-start.29) | collective-permute-done | bytes 32800 | tf_op jit(solution)/shard_map/ppermute | solution.py:18
  113.4 2.5 %collective-permute-start.30 = (f32[16,256]{1,0:T(8,128)S(1)}, f32[16,256]{1,0:T(8,128)S(1)}, u32[]{:S(2)}, u32[]{:S(2)}) collective-permute-start(f32[16,256]{1,0:T(8,128)S(1)} %get-tuple-element.85), channel_id=1, source_target_pairs={{0,4},{4,0},{8,12},{12,8},{16,20},{20,16},{24,28},{28,24},{32,36},... | collective-permute-start | bytes 49160 | tf_op jit(solution)/shard_map/ppermute | solution.py:18
  115.9 2.3 %collective-permute-done.30 = f32[16,256]{1,0:T(8,128)S(1)} collective-permute-done((f32[16,256]{1,0:T(8,128)S(1)}, f32[16,256]{1,0:T(8,128)S(1)}, u32[]{:S(2)}, u32[]{:S(2)}) %collective-permute-start.30) | collective-permute-done | bytes 16416 | tf_op jit(solution)/shard_map/ppermute | solution.py:18
  118.2 0.6 add_multiply_fusion
  (44 shorter events, 1.4 us)
Async XLA Ops:
  0.6 18.3 %copy-start.3 = (s32[1,8,8]{2,1,0:T(8,128)S(1)}, s32[1,8,8]{2,1,0:T(8,128)}, u32[]{:S(2)}) copy-start(s32[1,8,8]{2,1,0:T(8,128)} %param.6) | copy-start | bytes 772
  3.8 10.9 %collective-permute-start = (f32[128,256]{1,0:T(8,128)S(1)}, f32[128,256]{1,0:T(8,128)S(1)}, u32[]{:S(2)}, u32[]{:S(2)}) collective-permute-start(f32[128,256]{1,0:T(8,128)S(1)} %get-tuple-element.44), channel_id=1, source_target_pairs={{0,32},{4,36},{8,40},{12,44},{16,48},{20,52},{24,56},{28,60},{32,0... | collective-permute-start | bytes 393224 | tf_op jit(solution)/shard_map/ppermute | solution.py:18
  6.9 7.8 %collective-permute-start.1 = (f32[128,256]{1,0:T(8,128)S(1)}, f32[128,256]{1,0:T(8,128)S(1)}, u32[]{:S(2)}, u32[]{:S(2)}) collective-permute-start(f32[128,256]{1,0:T(8,128)S(1)} %get-tuple-element.45), channel_id=1, source_target_pairs={{0,48},{4,52},{8,56},{12,60},{16,32},{20,36},{24,40},{28,44},{32,1... | collective-permute-start | bytes 393224 | tf_op jit(solution)/shard_map/ppermute | solution.py:18
  8.0 17.8 %copy-start.1 = (f32[1024,256]{1,0:T(8,128)S(1)}, f32[1024,256]{1,0:T(8,128)}, u32[]{:S(2)}) copy-start(f32[1024,256]{1,0:T(8,128)} %p_hbm.3) | copy-start | bytes 3145732
  8.0 17.8 %copy-start.2 = (f32[1024,1024]{1,0:T(8,128)S(1)}, f32[1024,1024]{1,0:T(8,128)}, u32[]{:S(2)}) copy-start(f32[1024,1024]{1,0:T(8,128)} %param.5) | copy-start | bytes 12582916
  8.0 6.7 %collective-permute-start.2 = (f32[64,256]{1,0:T(8,128)S(1)}, f32[64,256]{1,0:T(8,128)S(1)}, u32[]{:S(2)}, u32[]{:S(2)}) collective-permute-start(f32[64,256]{1,0:T(8,128)S(1)} %get-tuple-element.47), channel_id=1, source_target_pairs={{0,16},{4,20},{8,24},{12,28},{16,0},{20,4},{24,8},{28,12},{32,48},... | collective-permute-start | bytes 196616 | tf_op jit(solution)/shard_map/ppermute | solution.py:18
  11.3 7.9 %collective-permute-start.9 = (f32[128,256]{1,0:T(8,128)S(1)}, f32[128,256]{1,0:T(8,128)S(1)}, u32[]{:S(2)}, u32[]{:S(2)}) collective-permute-start(f32[128,256]{1,0:T(8,128)S(1)} %get-tuple-element.55), channel_id=1, source_target_pairs={{0,4},{4,0},{8,12},{12,8},{16,20},{20,16},{24,28},{28,24},{32,36},... | collective-permute-start | bytes 393224 | tf_op jit(solution)/shard_map/ppermute | solution.py:18
  14.8 10.6 %collective-permute-start.5 = (f32[32,256]{1,0:T(8,128)S(1)}, f32[32,256]{1,0:T(8,128)S(1)}, u32[]{:S(2)}, u32[]{:S(2)}) collective-permute-start(f32[32,256]{1,0:T(8,128)S(1)} %get-tuple-element.89), channel_id=1, source_target_pairs={{0,192},{4,196},{8,200},{12,204},{16,208},{20,212},{24,216},{28,22... | collective-permute-start | bytes 98312 | tf_op jit(solution)/shard_map/ppermute | solution.py:18
  17.8 7.5 %collective-permute-start.4 = (f32[32,256]{1,0:T(8,128)S(1)}, f32[32,256]{1,0:T(8,128)S(1)}, u32[]{:S(2)}, u32[]{:S(2)}) collective-permute-start(f32[32,256]{1,0:T(8,128)S(1)} %get-tuple-element.89), channel_id=1, source_target_pairs={{0,128},{4,132},{8,136},{12,140},{16,144},{20,148},{24,152},{28,15... | collective-permute-start | bytes 98312 | tf_op jit(solution)/shard_map/ppermute | solution.py:18
  18.5 6.9 %collective-permute-start.3 = (f32[32,256]{1,0:T(8,128)S(1)}, f32[32,256]{1,0:T(8,128)S(1)}, u32[]{:S(2)}, u32[]{:S(2)}) collective-permute-start(f32[32,256]{1,0:T(8,128)S(1)} %get-tuple-element.88), channel_id=1, source_target_pairs={{0,64},{4,68},{8,72},{12,76},{16,80},{20,84},{24,88},{28,92},{32,9... | collective-permute-start | bytes 98312 | tf_op jit(solution)/shard_map/ppermute | solution.py:18
  19.3 16.3 %collective-permute-start.10 = (f32[128,256]{1,0:T(8,128)S(1)}, f32[128,256]{1,0:T(8,128)S(1)}, u32[]{:S(2)}, u32[]{:S(2)}) collective-permute-start(f32[128,256]{1,0:T(8,128)S(1)} %add.36), channel_id=1, source_target_pairs={{0,12},{4,8},{8,4},{12,0},{16,28},{20,24},{24,20},{28,16},{32,44},... | collective-permute-start | bytes 393224 | tf_op jit(solution)/shard_map/ppermute | solution.py:18
  25.4 9.5 %collective-permute-start.6 = (f32[128,256]{1,0:T(8,128)S(1)}, f32[128,256]{1,0:T(8,128)S(1)}, u32[]{:S(2)}, u32[]{:S(2)}) collective-permute-start(f32[128,256]{1,0:T(8,128)S(1)} %pad_maximum_fusion), channel_id=1, source_target_pairs={{0,4},{4,0},{8,12},{12,8},{16,20},{20,16},{24,28},{28,24},{32,36},... | collective-permute-start | bytes 393224 | tf_op jit(solution)/shard_map/ppermute | solution.py:18
  25.9 23.1 %copy-start = (f32[6,1024,128]{2,1,0:T(8,128)S(1)}, f32[6,1024,128]{2,1,0:T(8,128)}, u32[]{:S(2)}) copy-start(f32[6,1024,128]{2,1,0:T(8,128)} %u_ref.1) | copy-start | bytes 9437188
  28.3 13.4 %collective-permute-start.7 = (f32[128,256]{1,0:T(8,128)S(1)}, f32[128,256]{1,0:T(8,128)S(1)}, u32[]{:S(2)}, u32[]{:S(2)}) collective-permute-start(f32[128,256]{1,0:T(8,128)S(1)} %get-tuple-element.54), channel_id=1, source_target_pairs={{0,12},{4,8},{8,4},{12,0},{16,28},{20,24},{24,20},{28,16},{32,44},... | collective-permute-start | bytes 393224 | tf_op jit(solution)/shard_map/ppermute | solution.py:18
  34.9 9.1 %collective-permute-start.12 = (f32[128,256]{1,0:T(8,128)S(1)}, f32[128,256]{1,0:T(8,128)S(1)}, u32[]{:S(2)}, u32[]{:S(2)}) collective-permute-start(f32[128,256]{1,0:T(8,128)S(1)} %add.35), channel_id=1, source_target_pairs={{0,12},{4,8},{8,4},{12,0},{16,28},{20,24},{24,20},{28,16},{32,44},... | collective-permute-start | bytes 393224 | tf_op jit(solution)/shard_map/ppermute | solution.py:18
  35.5 12.4 %collective-permute-start.11 = (f32[128,256]{1,0:T(8,128)S(1)}, f32[128,256]{1,0:T(8,128)S(1)}, u32[]{:S(2)}, u32[]{:S(2)}) collective-permute-start(f32[128,256]{1,0:T(8,128)S(1)} %add.37), channel_id=1, source_target_pairs={{0,16},{4,20},{8,24},{12,28},{16,0},{20,4},{24,8},{28,12},{32,48},... | collective-permute-start | bytes 393224 | tf_op jit(solution)/shard_map/ppermute | solution.py:18
  41.7 7.3 %collective-permute-start.8 = (f32[128,256]{1,0:T(8,128)S(1)}, f32[128,256]{1,0:T(8,128)S(1)}, u32[]{:S(2)}, u32[]{:S(2)}) collective-permute-start(f32[128,256]{1,0:T(8,128)S(1)} %collective-permute-done.7.o_ref), channel_id=1, source_target_pairs={{0,4},{4,0},{8,12},{12,8},{16,20},{20,16},{24,28},{28,24},{32,36},... | collective-permute-start | bytes 393224 | tf_op jit(solution)/shard_map/ppermute | solution.py:18
  44.0 9.7 %collective-permute-start.13 = (f32[128,256]{1,0:T(8,128)S(1)}, f32[128,256]{1,0:T(8,128)S(1)}, u32[]{:S(2)}, u32[]{:S(2)}) collective-permute-start(f32[128,256]{1,0:T(8,128)S(1)} %get-tuple-element.61), channel_id=1, source_target_pairs={{0,4},{4,0},{8,12},{12,8},{16,20},{20,16},{24,28},{28,24},{32,36},... | collective-permute-start | bytes 393224 | tf_op jit(solution)/shard_map/ppermute | solution.py:18
  44.7 9.0 %collective-permute-start.14 = (f32[128,256]{1,0:T(8,128)S(1)}, f32[128,256]{1,0:T(8,128)S(1)}, u32[]{:S(2)}, u32[]{:S(2)}) collective-permute-start(f32[128,256]{1,0:T(8,128)S(1)} %add.38.q0), channel_id=1, source_target_pairs={{0,16},{4,20},{8,24},{12,28},{16,0},{20,4},{24,8},{28,12},{32,48},... | collective-permute-start | bytes 393224 | tf_op jit(solution)/shard_map/ppermute | solution.py:18
  46.3 6.2 %collective-permute-start.16 = (f32[64,256]{1,0:T(8,128)S(1)}, f32[64,256]{1,0:T(8,128)S(1)}, u32[]{:S(2)}, u32[]{:S(2)}) collective-permute-start(f32[64,256]{1,0:T(8,128)S(1)} %slice.28), channel_id=1, source_target_pairs={{0,48},{4,52},{8,56},{12,60},{16,32},{20,36},{24,40},{28,44},{32,1... | collective-permute-start | bytes 196616 | tf_op jit(solution)/shard_map/ppermute | solution.py:18
  47.9 5.8 %collective-permute-start.15 = (f32[64,256]{1,0:T(8,128)S(1)}, f32[64,256]{1,0:T(8,128)S(1)}, u32[]{:S(2)}, u32[]{:S(2)}) collective-permute-start(f32[64,256]{1,0:T(8,128)S(1)} %slice.28), channel_id=1, source_target_pairs={{0,32},{4,36},{8,40},{12,44},{16,48},{20,52},{24,56},{28,60},{32,0... | collective-permute-start | bytes 196616 | tf_op jit(solution)/shard_map/ppermute | solution.py:18
  55.7 2.7 %collective-permute-start.18 = (f32[1024,256]{1,0:T(8,128)S(1)}, f32[1024,256]{1,0:T(8,128)S(1)}, u32[]{:S(2)}, u32[]{:S(2)}) collective-permute-start(f32[1024,256]{1,0:T(8,128)S(1)} %get-tuple-element.64.refs_0_), channel_id=1, source_target_pairs={{0,1},{1,0},{2,3},{3,2},{4,5},{5,4},{6,7},{7,6},{8,9},{9,8},{10,11... | collective-permute-start | bytes 3145736 | tf_op jit(solution)/shard_map/ppermute | solution.py:18
  55.7 26.2 %collective-permute-start.17 = (f32[1024,256]{1,0:T(8,128)S(1)}, f32[1024,256]{1,0:T(8,128)S(1)}, u32[]{:S(2)}, u32[]{:S(2)}) collective-permute-start(f32[1024,256]{1,0:T(8,128)S(1)} %get-tuple-element.64.refs_0_), channel_id=1, source_target_pairs={{0,2},{1,3},{2,0},{3,1},{4,6},{5,7},{6,4},{7,5},{8,10},{9,11},{10,... | collective-permute-start | bytes 3145736 | tf_op jit(solution)/shard_map/ppermute | solution.py:18
  59.4 22.5 %collective-permute-start.19 = (f32[2,64,256]{2,1,0:T(8,128)S(1)}, f32[2,64,256]{2,1,0:T(8,128)S(1)}, u32[]{:S(2)}, u32[]{:S(2)}) collective-permute-start(f32[2,64,256]{2,1,0:T(8,128)S(1)} %get-tuple-element.66), channel_id=1, source_target_pairs={{0,16},{4,20},{8,24},{12,28},{16,0},{20,4},{24,8},{28,12},{32,48},... | collective-permute-start | bytes 393224 | tf_op jit(solution)/shard_map/ppermute | solution.py:18
  60.2 21.7 %collective-permute-start.20 = (f32[2,64,256]{2,1,0:T(8,128)S(1)}, f32[2,64,256]{2,1,0:T(8,128)S(1)}, u32[]{:S(2)}, u32[]{:S(2)}) collective-permute-start(f32[2,64,256]{2,1,0:T(8,128)S(1)} %get-tuple-element.67), channel_id=1, source_target_pairs={{0,32},{4,36},{8,40},{12,44},{16,48},{20,52},{24,56},{28,60},{32,0... | collective-permute-start | bytes 393224 | tf_op jit(solution)/shard_map/ppermute | solution.py:18
  62.6 19.3 %collective-permute-start.21 = (f32[2,64,256]{2,1,0:T(8,128)S(1)}, f32[2,64,256]{2,1,0:T(8,128)S(1)}, u32[]{:S(2)}, u32[]{:S(2)}) collective-permute-start(f32[2,64,256]{2,1,0:T(8,128)S(1)} %get-tuple-element.68), channel_id=1, source_target_pairs={{0,48},{4,52},{8,56},{12,60},{16,32},{20,36},{24,40},{28,44},{32,1... | collective-permute-start | bytes 393224 | tf_op jit(solution)/shard_map/ppermute | solution.py:18
  81.9 2.7 %collective-permute-start.22 = (f32[1024,256]{1,0:T(8,128)S(1)}, f32[1024,256]{1,0:T(8,128)S(1)}, u32[]{:S(2)}, u32[]{:S(2)}) collective-permute-start(f32[1024,256]{1,0:T(8,128)S(1)} %collective-permute-done.17.refs_1_), channel_id=1, source_target_pairs={{0,1},{1,0},{2,3},{3,2},{4,5},{5,4},{6,7},{7,6},{8,9},{9,8},{10,11... | collective-permute-start | bytes 3145736 | tf_op jit(solution)/shard_map/ppermute | solution.py:18
  85.7 6.4 %collective-permute-start.23 = (f32[2,64,256]{2,1,0:T(8,128)S(1)}, f32[2,64,256]{2,1,0:T(8,128)S(1)}, u32[]{:S(2)}, u32[]{:S(2)}) collective-permute-start(f32[2,64,256]{2,1,0:T(8,128)S(1)} %get-tuple-element.75), channel_id=1, source_target_pairs={{0,16},{4,20},{8,24},{12,28},{16,0},{20,4},{24,8},{28,12},{32,48},... | collective-permute-start | bytes 393224 | tf_op jit(solution)/shard_map/ppermute | solution.py:18
  85.9 9.2 %collective-permute-start.24 = (f32[2,64,256]{2,1,0:T(8,128)S(1)}, f32[2,64,256]{2,1,0:T(8,128)S(1)}, u32[]{:S(2)}, u32[]{:S(2)}) collective-permute-start(f32[2,64,256]{2,1,0:T(8,128)S(1)} %get-tuple-element.76), channel_id=1, source_target_pairs={{0,32},{4,36},{8,40},{12,44},{16,48},{20,52},{24,56},{28,60},{32,0... | collective-permute-start | bytes 393224 | tf_op jit(solution)/shard_map/ppermute | solution.py:18
  88.7 8.7 %collective-permute-start.25 = (f32[2,64,256]{2,1,0:T(8,128)S(1)}, f32[2,64,256]{2,1,0:T(8,128)S(1)}, u32[]{:S(2)}, u32[]{:S(2)}) collective-permute-start(f32[2,64,256]{2,1,0:T(8,128)S(1)} %get-tuple-element.77), channel_id=1, source_target_pairs={{0,48},{4,52},{8,56},{12,60},{16,32},{20,36},{24,40},{28,44},{32,1... | collective-permute-start | bytes 393224 | tf_op jit(solution)/shard_map/ppermute | solution.py:18
  97.4 4.8 %collective-permute-start.26 = (f32[64,256]{1,0:T(8,128)S(1)}, f32[64,256]{1,0:T(8,128)S(1)}, u32[]{:S(2)}, u32[]{:S(2)}) collective-permute-start(f32[64,256]{1,0:T(8,128)S(1)} %get-tuple-element.79), channel_id=1, source_target_pairs={{0,64},{4,68},{8,72},{12,76},{16,80},{20,84},{24,88},{28,92},{32,9... | collective-permute-start | bytes 196616 | tf_op jit(solution)/shard_map/ppermute | solution.py:18
  98.6 5.8 %collective-permute-start.27 = (f32[64,256]{1,0:T(8,128)S(1)}, f32[64,256]{1,0:T(8,128)S(1)}, u32[]{:S(2)}, u32[]{:S(2)}) collective-permute-start(f32[64,256]{1,0:T(8,128)S(1)} %get-tuple-element.80), channel_id=1, source_target_pairs={{0,128},{4,132},{8,136},{12,140},{16,144},{20,148},{24,152},{28,15... | collective-permute-start | bytes 196616 | tf_op jit(solution)/shard_map/ppermute | solution.py:18
  101.5 5.5 %collective-permute-start.28 = (f32[64,256]{1,0:T(8,128)S(1)}, f32[64,256]{1,0:T(8,128)S(1)}, u32[]{:S(2)}, u32[]{:S(2)}) collective-permute-start(f32[64,256]{1,0:T(8,128)S(1)} %get-tuple-element.81), channel_id=1, source_target_pairs={{0,192},{4,196},{8,200},{12,204},{16,208},{20,212},{24,216},{28,22... | collective-permute-start | bytes 196616 | tf_op jit(solution)/shard_map/ppermute | solution.py:18
  107.0 6.4 %collective-permute-start.29 = (f32[32,256]{1,0:T(8,128)S(1)}, f32[32,256]{1,0:T(8,128)S(1)}, u32[]{:S(2)}, u32[]{:S(2)}) collective-permute-start(f32[32,256]{1,0:T(8,128)S(1)} %get-tuple-element.83), channel_id=1, source_target_pairs={{0,12},{4,8},{8,4},{12,0},{16,28},{20,24},{24,20},{28,16},{32,44},... | collective-permute-start | bytes 98312 | tf_op jit(solution)/shard_map/ppermute | solution.py:18
  113.4 4.8 %collective-permute-start.30 = (f32[16,256]{1,0:T(8,128)S(1)}, f32[16,256]{1,0:T(8,128)S(1)}, u32[]{:S(2)}, u32[]{:S(2)}) collective-permute-start(f32[16,256]{1,0:T(8,128)S(1)} %get-tuple-element.85), channel_id=1, source_target_pairs={{0,4},{4,0},{8,12},{12,8},{16,20},{20,16},{24,28},{28,24},{32,36},... | collective-permute-start | bytes 49160 | tf_op jit(solution)/shard_map/ppermute | solution.py:18

commit v7 on v6

--- a/solution.py
+++ b/solution.py
@@ -179,8 +179,26 @@
     )
 
 
+def chunks(value):
+    left, right = value[:, :128], value[:, 128:]
+    group = lax.broadcasted_iota(jnp.int32, left.shape, 1) // 32
+
+    def pick(*parts):
+        out = parts[3]
+        for k in (2, 1, 0):
+            out = jnp.where(group == k, parts[k], out)
+        return out
+
+    def turn(part, groups):
+        return pltpu.roll(part, groups * 32, 1) if groups else part
+
+    even = pick(left, turn(left, 3), turn(right, 2), turn(right, 1))
+    odd = pick(turn(left, 3), turn(left, 2), turn(right, 1), right)
+    return even, odd
+
+
 def expand(base, rows_high, rows_low, zero, part, part1, part2, part3):
-    def body(b_ref, h_ref, l_ref, z_ref, q0, q1, q2, q3, out, held, total):
+    def body(b_ref, h_ref, l_ref, z_ref, q0, q1, q2, q3, out, held, even, odd, total):
         _, x, _ = place()
         total[0:128] = z_ref[...]
         for k, ref in ((0, q0), (1, q1)):
@@ -191,15 +209,17 @@
             total[pl.ds(256 + row, 32)] = ref[base:base + 32]
             total[pl.ds(384 + row, 32)] = ref[base + 32:base + 64]
         left = h_ref[...], l_ref[...]
-        held[...] = b_ref[...] + dot3(left, split(total[...]), MATMUL)
-        out[...] = held[...]
+        value = b_ref[...] + dot3(left, split(total[...]), MATMUL)
+        out[...] = value
+        held[...] = value
+        even[...], odd[...] = chunks(value)
 
     points, wide = base.shape
     depth = rows_high.shape[1]
     given = [base, rows_high, rows_low, zero, part, part1, part2, part3]
     return call(
         body,
-        shapes(base.shape, base.shape),
+        shapes(base.shape, base.shape, (points, wide // 2), (points, wide // 2)),
         [whole(g.shape) for g in given],
         given,
         [pltpu.VMEM((depth, wide), F32)],
@@ -209,6 +229,8 @@
 
 def gram(others, applied):
     wide = applied.shape[1]
+    tall = others[1].shape[1]
+    part = tall // 4
     given = [applied] if others[0] is applied else [applied, others[0]]
     given = given + [others[1]]
 
@@ -221,32 +243,37 @@
         total[0] = dot3(left, right, ROWS)
         total[1] = dot3(split(second[...]), right, ROWS)
         for k, out in enumerate(outs):
-            row = pl.multiple_of((x ^ k) * (wide // 4), wide // 4)
-            out[...] = total[:, pl.ds(row, wide // 4)]
-
-    return call(
-        body,
-        shapes(*[(2, wide // 4, wide)] * 4),
+            out[...] = total[:, pl.ds(pl.multiple_of((x ^ k) * part, part), part)]
+
+    return call(
+        body,
+        shapes(*[(2, part, wide)] * 4),
         [whole(g.shape) for g in given],
         given,
-        [pltpu.VMEM((2, wide, wide), F32)],
-        flops=12 * wide * wide * applied.shape[0],
-    )
-
-
-def cut_y(near, far):
+        [pltpu.VMEM((2, tall, wide), F32)],
+        flops=12 * tall * wide * applied.shape[0],
+    )
+
+
+def cut_y(near, far_even, far_odd):
     _, rows, wide = near[0].shape
+    half = rows // 2
 
     def body(*refs):
-        ins, outs, total = refs[:8], refs[8:12], refs[12]
+        ins, outs, total = refs[:12], refs[12:16], refs[16]
         y, _, _ = place()
         probe = lax.axis_index("probe")
-        total[:2] = (ins[0][...] + ins[1][...]) + (ins[2][...] + ins[3][...])
-        total[2:] = (ins[4][...] + ins[5][...]) + (ins[6][...] + ins[7][...])
+
+        def add(four):
+            return (four[0][...] + four[1][...]) + (four[2][...] + four[3][...])
+
+        total[:2] = add(ins[:4])
+        total[2:, :half] = add(ins[4:8])
+        total[2:, half:] = add(ins[8:])
         for k, out in enumerate(outs):
             out[...] = total[probe ^ y ^ k]
 
-    ins = [*near, *far]
+    ins = [*near, *far_even, *far_odd]
     return call(
         body,
         shapes(*[(rows, wide)] * 4),
@@ -319,15 +346,17 @@
     gathered = [swap(part, "leaf", 4), swap(part[64:], "leaf", 8), swap(part[64:], "leaf", 12)]
     node0 = swap(low0, "leaf", 1)
     late = prepare(near, row_factor_stack, node1, node1_more, node2)
-    result, applied = expand(*late, node0, part, *gathered)
-
-    far = swap(applied, "probe", 2)
+    result, applied, even, odd = expand(*late, node0, part, *gathered)
+
+    even = swap(even, "probe", 2)
+    odd = swap(odd, "probe", 2)
     beside = swap(applied, "probe", 1)
     first = around(gram([applied, beside], applied), 4)
-    far, *first = lax.optimization_barrier((far, *first))
-    across = swap(far, "probe", 1)
-    second = around(gram([far, across], applied), 4)
-    blocks = around(cut_y(first, second), 16)
+    even, *first = lax.optimization_barrier((even, *first))
+    second = around(gram([even, swap(even, "probe", 1)], applied), 4)
+    odd, *second = lax.optimization_barrier((odd, *second))
+    third = around(gram([odd, swap(odd, "probe", 1)], applied), 4)
+    blocks = around(cut_y(first, second, third), 16)
     keep, give = cut_z(blocks, 1)
     keep, give = cut_z([keep, swap(give, "leaf", 3)], 0)
     total = keep + swap(give, "leaf", 1)

time: 120 us -> 119 us (level); the launches traced: 119 us -> 119 us
  starting transfers between devices: 53 us -> 59.3 us
  waiting for transfers between devices: 49.2 us -> 43 us
    ppermute x31 -> x36, starting transfers between devices: 53 us -> 59.3 us  [swap(): return lax.ppermute(value, axis, pairs)]
    ppermute x31 -> x36, waiting for transfers between devices: 49.2 us -> 43 us  [swap(): return lax.ppermute(value, axis, pairs)]
    pallas_call x9 -> x10, Pallas kernels: 12.3 us -> 12.5 us  [call(): pl.pallas_call(body, out_shape=outs, grid=grid, in_specs=specs, out_specs...]
  transfers between devices with their start and end apart: 31 -> 36, of which waited for: 17 -> 19; matrix products, arithmetic and copies ran while one was open for 2% -> 2% of each run, Pallas kernels for 5% -> 6%
where the time goes in v7:
time: 119 us
  starting transfers between devices  59.3 us (50%)
  waiting for transfers between devices  43 us (36%)
  Pallas kernels  12.5 us (11%)
  matrix products  2.39 us (2%)
    ppermute x36, starting transfers between devices, swap(): return lax.ppermute(value, axis, pairs)  59.3 us
    ppermute x36, waiting for transfers between devices, swap(): return lax.ppermute(value, axis, pairs)  43 us
    pallas_call x10, Pallas kernels, call(): pl.pallas_call(body, out_shape=outs, grid=grid, in_specs=specs, out_specs...  12.5 us
    dot_general x1, matrix products, near_product(): return jnp.dot(masked, probes, precision=HIGH, preferred_element_type=F32)  2.39 us
  transfers between devices with their start and end apart: 36, of which 19 were waited for; matrix products, arithmetic and copies ran while one was open for 2% of the time, Pallas kernels for 6%

profile of v7, /device:TPU:32, one launch (start us, length us, event | category | flops | bytes accessed | tf_op | source)
XLA Modules:
  0.0 119.2 jit_solution(10065746657558477695)
XLA Ops:
  0.6 3.1 %shard_map.68 = (f32[64,256]{1,0:T(8,128)S(1)}, f32[64,256]{1,0:T(8,128)S(1)}, f32[128,256]{1,0:T(8,128)S(1)}, f32[128,256]{1,0:T(8,128)S(1)}) custom-call(f32[6,1024,128]{2,1,0:T(8,128)} %c_hbm.3, f32[1024,256]{1,0:T(8,128)} %p_hbm.3), custom_call_target="tpu_custom_call" | custom-call | flops 603979776 | bytes 4587520 | tf_op jit(solution)/shard_map/pallas_call | solution.py:49
  3.8 3.1 %collective-permute-start = (f32[128,256]{1,0:T(8,128)S(1)}, f32[128,256]{1,0:T(8,128)S(1)}, u32[]{:S(2)}, u32[]{:S(2)}) collective-permute-start(f32[128,256]{1,0:T(8,128)S(1)} %get-tuple-element.55), channel_id=1, source_target_pairs={{0,32},{4,36},{8,40},{12,44},{16,48},{20,52},{24,56},{28,60},{32,0... | collective-permute-start | bytes 393224 | tf_op jit(solution)/shard_map/ppermute | solution.py:18
  6.9 1.1 collective-permute-start.1
  8.0 3.3 %shard_map.69 = (f32[128,256]{1,0:T(8,128)S(1)}, f32[128,256]{1,0:T(8,128)S(1)}, f32[128,256]{1,0:T(8,128)S(1)}) custom-call(f32[6,1024,128]{2,1,0:T(8,128)} %c_hbm.3, f32[1024,256]{1,0:T(8,128)} %p_hbm.3), custom_call_target="tpu_custom_call" | custom-call | flops 603979776 | bytes 4587520 | tf_op jit(solution)/shard_map/pallas_call | solution.py:49
  11.3 3.4 %collective-permute-start.9 = (f32[128,256]{1,0:T(8,128)S(1)}, f32[128,256]{1,0:T(8,128)S(1)}, u32[]{:S(2)}, u32[]{:S(2)}) collective-permute-start(f32[128,256]{1,0:T(8,128)S(1)} %get-tuple-element.66), channel_id=1, source_target_pairs={{0,4},{4,0},{8,12},{12,8},{16,20},{20,16},{24,28},{28,24},{32,36},... | collective-permute-start | bytes 393224 | tf_op jit(solution)/shard_map/ppermute | solution.py:18
  14.8 3.1 %collective-permute-start.5 = (f32[32,256]{1,0:T(8,128)S(1)}, f32[32,256]{1,0:T(8,128)S(1)}, u32[]{:S(2)}, u32[]{:S(2)}) collective-permute-start(f32[32,256]{1,0:T(8,128)S(1)} %get-tuple-element.111), channel_id=1, source_target_pairs={{0,192},{4,196},{8,200},{12,204},{16,208},{20,212},{24,216},{28,22... | collective-permute-start | bytes 98312 | tf_op jit(solution)/shard_map/ppermute | solution.py:18
  17.8 0.6 collective-permute-start.4
  19.3 6.1 %collective-permute-start.10 = (f32[128,256]{1,0:T(8,128)S(1)}, f32[128,256]{1,0:T(8,128)S(1)}, u32[]{:S(2)}, u32[]{:S(2)}) collective-permute-start(f32[128,256]{1,0:T(8,128)S(1)} %add.36), channel_id=1, source_target_pairs={{0,12},{4,8},{8,4},{12,0},{16,28},{20,24},{24,20},{28,16},{32,44},... | collective-permute-start | bytes 393224 | tf_op jit(solution)/shard_map/ppermute | solution.py:18
  25.9 2.4 %fusion.n_ref = f32[1024,256]{1,0:T(8,128)S(1)} fusion(f32[1024,256]{1,0:T(8,128)S(1)} %copy-done.1, f32[1024,1024]{1,0:T(8,128)S(1)} %copy-done.2, f32[128,8,8,128]{3,2,1,0:T(8,128)S(1)} %bitcast.8), kind=kOutput, calls=%fused_computation.1 | convolution fusion | flops 1611661312 | bytes 10485760 | tf_op jit(solution)/shard_map/dot_general | solution.py:320
  28.3 3.5 %collective-permute-start.7 = (f32[128,256]{1,0:T(8,128)S(1)}, f32[128,256]{1,0:T(8,128)S(1)}, u32[]{:S(2)}, u32[]{:S(2)}) collective-permute-start(f32[128,256]{1,0:T(8,128)S(1)} %get-tuple-element.65), channel_id=1, source_target_pairs={{0,12},{4,8},{8,4},{12,0},{16,28},{20,24},{24,20},{28,16},{32,44},... | collective-permute-start | bytes 393224 | tf_op jit(solution)/shard_map/ppermute | solution.py:18
  31.8 3.0 %collective-permute-done.6 = f32[128,256]{1,0:T(8,128)S(1)} collective-permute-done((f32[128,256]{1,0:T(8,128)S(1)}, f32[128,256]{1,0:T(8,128)S(1)}, u32[]{:S(2)}, u32[]{:S(2)}) %collective-permute-start.6) | collective-permute-done | bytes 131104 | tf_op jit(solution)/shard_map/ppermute | solution.py:18
  34.9 0.6 collective-permute-start.12
  35.5 2.2 %collective-permute-start.11 = (f32[128,256]{1,0:T(8,128)S(1)}, f32[128,256]{1,0:T(8,128)S(1)}, u32[]{:S(2)}, u32[]{:S(2)}) collective-permute-start(f32[128,256]{1,0:T(8,128)S(1)} %add.37), channel_id=1, source_target_pairs={{0,16},{4,20},{8,24},{12,28},{16,0},{20,4},{24,8},{28,12},{32,48},... | collective-permute-start | bytes 393224 | tf_op jit(solution)/shard_map/ppermute | solution.py:18
  37.7 4.0 %collective-permute-done.7.o_ref = f32[128,256]{1,0:T(8,128)S(1)} collective-permute-done((f32[128,256]{1,0:T(8,128)S(1)}, f32[128,256]{1,0:T(8,128)S(1)}, u32[]{:S(2)}, u32[]{:S(2)}) %collective-permute-start.7) | collective-permute-done | bytes 131104 | tf_op jit(solution)/shard_map/ppermute | solution.py:18
  41.7 2.3 %collective-permute-done.12 = f32[128,256]{1,0:T(8,128)S(1)} collective-permute-done((f32[128,256]{1,0:T(8,128)S(1)}, f32[128,256]{1,0:T(8,128)S(1)}, u32[]{:S(2)}, u32[]{:S(2)}) %collective-permute-start.12) | collective-permute-done | bytes 131104 | tf_op jit(solution)/shard_map/ppermute | solution.py:18
  44.0 0.7 collective-permute-start.13
  44.7 1.6 %collective-permute-start.14 = (f32[128,256]{1,0:T(8,128)S(1)}, f32[128,256]{1,0:T(8,128)S(1)}, u32[]{:S(2)}, u32[]{:S(2)}) collective-permute-start(f32[128,256]{1,0:T(8,128)S(1)} %add.38.q0), channel_id=1, source_target_pairs={{0,16},{4,20},{8,24},{12,28},{16,0},{20,4},{24,8},{28,12},{32,48},... | collective-permute-start | bytes 393224 | tf_op jit(solution)/shard_map/ppermute | solution.py:18
  46.3 1.6 %collective-permute-start.16 = (f32[64,256]{1,0:T(8,128)S(1)}, f32[64,256]{1,0:T(8,128)S(1)}, u32[]{:S(2)}, u32[]{:S(2)}) collective-permute-start(f32[64,256]{1,0:T(8,128)S(1)} %slice.28), channel_id=1, source_target_pairs={{0,48},{4,52},{8,56},{12,60},{16,32},{20,36},{24,40},{28,44},{32,1... | collective-permute-start | bytes 196616 | tf_op jit(solution)/shard_map/ppermute | solution.py:18
  47.9 0.9 collective-permute-start.15
  48.9 1.6 %shard_map.70 = (f32[1024,256]{1,0:T(8,128)S(1)}, bf16[1024,512]{1,0:T(8,128)(2,1)S(1)}, bf16[1024,512]{1,0:T(8,128)(2,1)S(1)}) custom-call(f32[1024,256]{1,0:T(8,128)S(1)} %fusion.n_ref, f32[6,1024,128]{2,1,0:T(8,128)S(1)} %copy-done, f32[128,256]{1,0:T(8,128)S(1)} %collective-permute-done.7.o_ref, f32[128,256]{1,0:T(8,128)S(1)} %collective-permute-done.8.m_ref, ...), custom_call_target="tpu_custom_call" | custom-call | flops 402653184 | bytes 9830400 | tf_op jit(solution)/shard_map/pallas_call | solution.py:49
  50.6 1.9 %collective-permute-done.16.q3 = f32[64,256]{1,0:T(8,128)S(1)} collective-permute-done((f32[64,256]{1,0:T(8,128)S(1)}, f32[64,256]{1,0:T(8,128)S(1)}, u32[]{:S(2)}, u32[]{:S(2)}) %collective-permute-start.16) | collective-permute-done | bytes 65568 | tf_op jit(solution)/shard_map/ppermute | solution.py:18
  52.5 1.2 %collective-permute-done.15.q2 = f32[64,256]{1,0:T(8,128)S(1)} collective-permute-done((f32[64,256]{1,0:T(8,128)S(1)}, f32[64,256]{1,0:T(8,128)S(1)}, u32[]{:S(2)}, u32[]{:S(2)}) %collective-permute-start.15) | collective-permute-done | bytes 65568 | tf_op jit(solution)/shard_map/ppermute | solution.py:18
  53.7 2.0 %shard_map.71 = (f32[1024,256]{1,0:T(8,128)}, f32[1024,256]{1,0:T(8,128)S(1)}, f32[1024,128]{1,0:T(8,128)S(1)}, f32[1024,128]{1,0:T(8,128)S(1)}) custom-call(f32[1024,256]{1,0:T(8,128)S(1)} %get-tuple-element.67.b_ref, bf16[1024,512]{1,0:T(8,128)(2,1)S(1)} %get-tuple-element.68.h_ref, bf16[1024,512]{1,0:T(8,128)(2,1)S(1)} %get-tuple-element.69.l_ref, ...), custom_call_target="tpu_custom_call" | custom-call | flops 805306368 | bytes 8912896 | tf_op jit(solution)/shard_map/pallas_call | solution.py:49
  55.7 2.4 %collective-permute-start.17 = (f32[1024,128]{1,0:T(8,128)S(1)}, f32[1024,128]{1,0:T(8,128)S(1)}, u32[]{:S(2)}, u32[]{:S(2)}) collective-permute-start(f32[1024,128]{1,0:T(8,128)S(1)} %get-tuple-element.75), channel_id=1, source_target_pairs={{0,2},{1,3},{2,0},{3,1},{4,6},{5,7},{6,4},{7,5},{8,10},{9,11},{10,... | collective-permute-start | bytes 1572872 | tf_op jit(solution)/shard_map/ppermute | solution.py:18
  58.3 1.1 shard_map.72
  59.4 0.7 collective-permute-start.19
  60.2 2.4 %collective-permute-start.20 = (f32[2,64,256]{2,1,0:T(8,128)S(1)}, f32[2,64,256]{2,1,0:T(8,128)S(1)}, u32[]{:S(2)}, u32[]{:S(2)}) collective-permute-start(f32[2,64,256]{2,1,0:T(8,128)S(1)} %get-tuple-element.79), channel_id=1, source_target_pairs={{0,32},{4,36},{8,40},{12,44},{16,48},{20,52},{24,56},{28,60},{32,0... | collective-permute-start | bytes 393224 | tf_op jit(solution)/shard_map/ppermute | solution.py:18
  62.6 1.6 %collective-permute-start.21 = (f32[2,64,256]{2,1,0:T(8,128)S(1)}, f32[2,64,256]{2,1,0:T(8,128)S(1)}, u32[]{:S(2)}, u32[]{:S(2)}) collective-permute-start(f32[2,64,256]{2,1,0:T(8,128)S(1)} %get-tuple-element.80), channel_id=1, source_target_pairs={{0,48},{4,52},{8,56},{12,60},{16,32},{20,36},{24,40},{28,44},{32,1... | collective-permute-start | bytes 393224 | tf_op jit(solution)/shard_map/ppermute | solution.py:18
  64.2 6.5 %collective-permute-done.17.refs_1_ = f32[1024,128]{1,0:T(8,128)S(1)} collective-permute-done((f32[1024,128]{1,0:T(8,128)S(1)}, f32[1024,128]{1,0:T(8,128)S(1)}, u32[]{:S(2)}, u32[]{:S(2)}) %collective-permute-start.17) | collective-permute-done | bytes 524320 | tf_op jit(solution)/shard_map/ppermute | solution.py:18
  71.2 2.2 %collective-permute-start.22 = (f32[1024,128]{1,0:T(8,128)S(1)}, f32[1024,128]{1,0:T(8,128)S(1)}, u32[]{:S(2)}, u32[]{:S(2)}) collective-permute-start(f32[1024,128]{1,0:T(8,128)S(1)} %get-tuple-element.85), channel_id=1, source_target_pairs={{0,2},{1,3},{2,0},{3,1},{4,6},{5,7},{6,4},{7,5},{8,10},{9,11},{10,... | collective-permute-start | bytes 1572872 | tf_op jit(solution)/shard_map/ppermute | solution.py:18
  73.4 0.7 shard_map.73
  74.2 3.3 %collective-permute-start.25 = (f32[2,32,256]{2,1,0:T(8,128)S(1)}, f32[2,32,256]{2,1,0:T(8,128)S(1)}, u32[]{:S(2)}, u32[]{:S(2)}) collective-permute-start(f32[2,32,256]{2,1,0:T(8,128)S(1)} %get-tuple-element.89), channel_id=1, source_target_pairs={{0,32},{4,36},{8,40},{12,44},{16,48},{20,52},{24,56},{28,60},{32,0... | collective-permute-start | bytes 196616 | tf_op jit(solution)/shard_map/ppermute | solution.py:18
  77.5 1.4 %collective-permute-start.26 = (f32[2,32,256]{2,1,0:T(8,128)S(1)}, f32[2,32,256]{2,1,0:T(8,128)S(1)}, u32[]{:S(2)}, u32[]{:S(2)}) collective-permute-start(f32[2,32,256]{2,1,0:T(8,128)S(1)} %get-tuple-element.90), channel_id=1, source_target_pairs={{0,48},{4,52},{8,56},{12,60},{16,32},{20,36},{24,40},{28,44},{32,1... | collective-permute-start | bytes 196616 | tf_op jit(solution)/shard_map/ppermute | solution.py:18
  78.9 7.1 %collective-permute-done.22.refs_1_ = f32[1024,128]{1,0:T(8,128)S(1)} collective-permute-done((f32[1024,128]{1,0:T(8,128)S(1)}, f32[1024,128]{1,0:T(8,128)S(1)}, u32[]{:S(2)}, u32[]{:S(2)}) %collective-permute-start.22) | collective-permute-done | bytes 524320 | tf_op jit(solution)/shard_map/ppermute | solution.py:18
  86.1 1.9 %collective-permute-done.27.refs_2_ = f32[1024,128]{1,0:T(8,128)S(1)} collective-permute-done((f32[1024,128]{1,0:T(8,128)S(1)}, f32[1024,128]{1,0:T(8,128)S(1)}, u32[]{:S(2)}, u32[]{:S(2)}) %collective-permute-start.27) | collective-permute-done | bytes 524320 | tf_op jit(solution)/shard_map/ppermute | solution.py:18
  88.0 0.6 shard_map.74
  89.0 3.3 %collective-permute-start.29 = (f32[2,32,256]{2,1,0:T(8,128)S(1)}, f32[2,32,256]{2,1,0:T(8,128)S(1)}, u32[]{:S(2)}, u32[]{:S(2)}) collective-permute-start(f32[2,32,256]{2,1,0:T(8,128)S(1)} %get-tuple-element.98), channel_id=1, source_target_pairs={{0,32},{4,36},{8,40},{12,44},{16,48},{20,52},{24,56},{28,60},{32,0... | collective-permute-start | bytes 196616 | tf_op jit(solution)/shard_map/ppermute | solution.py:18
  92.3 1.4 %collective-permute-start.30 = (f32[2,32,256]{2,1,0:T(8,128)S(1)}, f32[2,32,256]{2,1,0:T(8,128)S(1)}, u32[]{:S(2)}, u32[]{:S(2)}) collective-permute-start(f32[2,32,256]{2,1,0:T(8,128)S(1)} %get-tuple-element.99), channel_id=1, source_target_pairs={{0,48},{4,52},{8,56},{12,60},{16,32},{20,36},{24,40},{28,44},{32,1... | collective-permute-start | bytes 196616 | tf_op jit(solution)/shard_map/ppermute | solution.py:18
  93.9 1.9 %collective-permute-done.29.refs_10_ = f32[2,32,256]{2,1,0:T(8,128)S(1)} collective-permute-done((f32[2,32,256]{2,1,0:T(8,128)S(1)}, f32[2,32,256]{2,1,0:T(8,128)S(1)}, u32[]{:S(2)}, u32[]{:S(2)}) %collective-permute-start.29) | collective-permute-done | bytes 65568 | tf_op jit(solution)/shard_map/ppermute | solution.py:18
  95.8 1.9 %collective-permute-done.30.refs_11_ = f32[2,32,256]{2,1,0:T(8,128)S(1)} collective-permute-done((f32[2,32,256]{2,1,0:T(8,128)S(1)}, f32[2,32,256]{2,1,0:T(8,128)S(1)}, u32[]{:S(2)}, u32[]{:S(2)}) %collective-permute-start.30) | collective-permute-done | bytes 65568 | tf_op jit(solution)/shard_map/ppermute | solution.py:18
  97.8 1.4 %collective-permute-start.31 = (f32[64,256]{1,0:T(8,128)S(1)}, f32[64,256]{1,0:T(8,128)S(1)}, u32[]{:S(2)}, u32[]{:S(2)}) collective-permute-start(f32[64,256]{1,0:T(8,128)S(1)} %get-tuple-element.101), channel_id=1, source_target_pairs={{0,64},{4,68},{8,72},{12,76},{16,80},{20,84},{24,88},{28,92},{32,9... | collective-permute-start | bytes 196616 | tf_op jit(solution)/shard_map/ppermute | solution.py:18
  99.3 2.9 %collective-permute-start.32 = (f32[64,256]{1,0:T(8,128)S(1)}, f32[64,256]{1,0:T(8,128)S(1)}, u32[]{:S(2)}, u32[]{:S(2)}) collective-permute-start(f32[64,256]{1,0:T(8,128)S(1)} %get-tuple-element.102), channel_id=1, source_target_pairs={{0,128},{4,132},{8,136},{12,140},{16,144},{20,148},{24,152},{28,15... | collective-permute-start | bytes 196616 | tf_op jit(solution)/shard_map/ppermute | solution.py:18
  102.7 2.5 %collective-permute-done.32.refs_2_ = f32[64,256]{1,0:T(8,128)S(1)} collective-permute-done((f32[64,256]{1,0:T(8,128)S(1)}, f32[64,256]{1,0:T(8,128)S(1)}, u32[]{:S(2)}, u32[]{:S(2)}) %collective-permute-start.32) | collective-permute-done | bytes 65568 | tf_op jit(solution)/shard_map/ppermute | solution.py:18
  105.2 2.4 %collective-permute-done.33.refs_3_ = f32[64,256]{1,0:T(8,128)S(1)} collective-permute-done((f32[64,256]{1,0:T(8,128)S(1)}, f32[64,256]{1,0:T(8,128)S(1)}, u32[]{:S(2)}, u32[]{:S(2)}) %collective-permute-start.33) | collective-permute-done | bytes 65568 | tf_op jit(solution)/shard_map/ppermute | solution.py:18
  107.7 3.8 %collective-permute-start.34 = (f32[32,256]{1,0:T(8,128)S(1)}, f32[32,256]{1,0:T(8,128)S(1)}, u32[]{:S(2)}, u32[]{:S(2)}) collective-permute-start(f32[32,256]{1,0:T(8,128)S(1)} %get-tuple-element.105), channel_id=1, source_target_pairs={{0,12},{4,8},{8,4},{12,0},{16,28},{20,24},{24,20},{28,16},{32,44},... | collective-permute-start | bytes 98312 | tf_op jit(solution)/shard_map/ppermute | solution.py:18
  111.5 2.3 %collective-permute-done.34.refs_1_ = f32[32,256]{1,0:T(8,128)S(1)} collective-permute-done((f32[32,256]{1,0:T(8,128)S(1)}, f32[32,256]{1,0:T(8,128)S(1)}, u32[]{:S(2)}, u32[]{:S(2)}) %collective-permute-start.34) | collective-permute-done | bytes 32800 | tf_op jit(solution)/shard_map/ppermute | solution.py:18
  113.8 2.3 %collective-permute-start.35 = (f32[16,256]{1,0:T(8,128)S(1)}, f32[16,256]{1,0:T(8,128)S(1)}, u32[]{:S(2)}, u32[]{:S(2)}) collective-permute-start(f32[16,256]{1,0:T(8,128)S(1)} %get-tuple-element.107), channel_id=1, source_target_pairs={{0,4},{4,0},{8,12},{12,8},{16,20},{20,16},{24,28},{28,24},{32,36},... | collective-permute-start | bytes 49160 | tf_op jit(solution)/shard_map/ppermute | solution.py:18
  116.1 2.4 %collective-permute-done.35 = f32[16,256]{1,0:T(8,128)S(1)} collective-permute-done((f32[16,256]{1,0:T(8,128)S(1)}, f32[16,256]{1,0:T(8,128)S(1)}, u32[]{:S(2)}, u32[]{:S(2)}) %collective-permute-start.35) | collective-permute-done | bytes 16416 | tf_op jit(solution)/shard_map/ppermute | solution.py:18
  (55 shorter events, 4.3 us)
Async XLA Ops:
  0.6 18.3 %copy-start.3 = (s32[1,8,8]{2,1,0:T(8,128)S(1)}, s32[1,8,8]{2,1,0:T(8,128)}, u32[]{:S(2)}) copy-start(s32[1,8,8]{2,1,0:T(8,128)} %param.6) | copy-start | bytes 772
  3.8 10.9 %collective-permute-start = (f32[128,256]{1,0:T(8,128)S(1)}, f32[128,256]{1,0:T(8,128)S(1)}, u32[]{:S(2)}, u32[]{:S(2)}) collective-permute-start(f32[128,256]{1,0:T(8,128)S(1)} %get-tuple-element.55), channel_id=1, source_target_pairs={{0,32},{4,36},{8,40},{12,44},{16,48},{20,52},{24,56},{28,60},{32,0... | collective-permute-start | bytes 393224 | tf_op jit(solution)/shard_map/ppermute | solution.py:18
  6.9 7.8 %collective-permute-start.1 = (f32[128,256]{1,0:T(8,128)S(1)}, f32[128,256]{1,0:T(8,128)S(1)}, u32[]{:S(2)}, u32[]{:S(2)}) collective-permute-start(f32[128,256]{1,0:T(8,128)S(1)} %get-tuple-element.56), channel_id=1, source_target_pairs={{0,48},{4,52},{8,56},{12,60},{16,32},{20,36},{24,40},{28,44},{32,1... | collective-permute-start | bytes 393224 | tf_op jit(solution)/shard_map/ppermute | solution.py:18
  8.0 17.8 %copy-start.1 = (f32[1024,256]{1,0:T(8,128)S(1)}, f32[1024,256]{1,0:T(8,128)}, u32[]{:S(2)}) copy-start(f32[1024,256]{1,0:T(8,128)} %p_hbm.3) | copy-start | bytes 3145732
  8.0 17.8 %copy-start.2 = (f32[1024,1024]{1,0:T(8,128)S(1)}, f32[1024,1024]{1,0:T(8,128)}, u32[]{:S(2)}) copy-start(f32[1024,1024]{1,0:T(8,128)} %param.5) | copy-start | bytes 12582916
  8.0 6.7 %collective-permute-start.2 = (f32[64,256]{1,0:T(8,128)S(1)}, f32[64,256]{1,0:T(8,128)S(1)}, u32[]{:S(2)}, u32[]{:S(2)}) collective-permute-start(f32[64,256]{1,0:T(8,128)S(1)} %get-tuple-element.58), channel_id=1, source_target_pairs={{0,16},{4,20},{8,24},{12,28},{16,0},{20,4},{24,8},{28,12},{32,48},... | collective-permute-start | bytes 196616 | tf_op jit(solution)/shard_map/ppermute | solution.py:18
  11.3 7.9 %collective-permute-start.9 = (f32[128,256]{1,0:T(8,128)S(1)}, f32[128,256]{1,0:T(8,128)S(1)}, u32[]{:S(2)}, u32[]{:S(2)}) collective-permute-start(f32[128,256]{1,0:T(8,128)S(1)} %get-tuple-element.66), channel_id=1, source_target_pairs={{0,4},{4,0},{8,12},{12,8},{16,20},{20,16},{24,28},{28,24},{32,36},... | collective-permute-start | bytes 393224 | tf_op jit(solution)/shard_map/ppermute | solution.py:18
  14.8 10.6 %collective-permute-start.5 = (f32[32,256]{1,0:T(8,128)S(1)}, f32[32,256]{1,0:T(8,128)S(1)}, u32[]{:S(2)}, u32[]{:S(2)}) collective-permute-start(f32[32,256]{1,0:T(8,128)S(1)} %get-tuple-element.111), channel_id=1, source_target_pairs={{0,192},{4,196},{8,200},{12,204},{16,208},{20,212},{24,216},{28,22... | collective-permute-start | bytes 98312 | tf_op jit(solution)/shard_map/ppermute | solution.py:18
  17.8 7.5 %collective-permute-start.4 = (f32[32,256]{1,0:T(8,128)S(1)}, f32[32,256]{1,0:T(8,128)S(1)}, u32[]{:S(2)}, u32[]{:S(2)}) collective-permute-start(f32[32,256]{1,0:T(8,128)S(1)} %get-tuple-element.111), channel_id=1, source_target_pairs={{0,128},{4,132},{8,136},{12,140},{16,144},{20,148},{24,152},{28,15... | collective-permute-start | bytes 98312 | tf_op jit(solution)/shard_map/ppermute | solution.py:18
  18.5 6.9 %collective-permute-start.3 = (f32[32,256]{1,0:T(8,128)S(1)}, f32[32,256]{1,0:T(8,128)S(1)}, u32[]{:S(2)}, u32[]{:S(2)}) collective-permute-start(f32[32,256]{1,0:T(8,128)S(1)} %get-tuple-element.110), channel_id=1, source_target_pairs={{0,64},{4,68},{8,72},{12,76},{16,80},{20,84},{24,88},{28,92},{32,9... | collective-permute-start | bytes 98312 | tf_op jit(solution)/shard_map/ppermute | solution.py:18
  19.3 16.3 %collective-permute-start.10 = (f32[128,256]{1,0:T(8,128)S(1)}, f32[128,256]{1,0:T(8,128)S(1)}, u32[]{:S(2)}, u32[]{:S(2)}) collective-permute-start(f32[128,256]{1,0:T(8,128)S(1)} %add.36), channel_id=1, source_target_pairs={{0,12},{4,8},{8,4},{12,0},{16,28},{20,24},{24,20},{28,16},{32,44},... | collective-permute-start | bytes 393224 | tf_op jit(solution)/shard_map/ppermute | solution.py:18
  25.4 9.5 %collective-permute-start.6 = (f32[128,256]{1,0:T(8,128)S(1)}, f32[128,256]{1,0:T(8,128)S(1)}, u32[]{:S(2)}, u32[]{:S(2)}) collective-permute-start(f32[128,256]{1,0:T(8,128)S(1)} %pad_maximum_fusion), channel_id=1, source_target_pairs={{0,4},{4,0},{8,12},{12,8},{16,20},{20,16},{24,28},{28,24},{32,36},... | collective-permute-start | bytes 393224 | tf_op jit(solution)/shard_map/ppermute | solution.py:18
  25.9 23.1 %copy-start = (f32[6,1024,128]{2,1,0:T(8,128)S(1)}, f32[6,1024,128]{2,1,0:T(8,128)}, u32[]{:S(2)}) copy-start(f32[6,1024,128]{2,1,0:T(8,128)} %u_ref.1) | copy-start | bytes 9437188
  28.3 13.4 %collective-permute-start.7 = (f32[128,256]{1,0:T(8,128)S(1)}, f32[128,256]{1,0:T(8,128)S(1)}, u32[]{:S(2)}, u32[]{:S(2)}) collective-permute-start(f32[128,256]{1,0:T(8,128)S(1)} %get-tuple-element.65), channel_id=1, source_target_pairs={{0,12},{4,8},{8,4},{12,0},{16,28},{20,24},{24,20},{28,16},{32,44},... | collective-permute-start | bytes 393224 | tf_op jit(solution)/shard_map/ppermute | solution.py:18
  34.9 9.1 %collective-permute-start.12 = (f32[128,256]{1,0:T(8,128)S(1)}, f32[128,256]{1,0:T(8,128)S(1)}, u32[]{:S(2)}, u32[]{:S(2)}) collective-permute-start(f32[128,256]{1,0:T(8,128)S(1)} %add.35), channel_id=1, source_target_pairs={{0,12},{4,8},{8,4},{12,0},{16,28},{20,24},{24,20},{28,16},{32,44},... | collective-permute-start | bytes 393224 | tf_op jit(solution)/shard_map/ppermute | solution.py:18
  35.5 12.4 %collective-permute-start.11 = (f32[128,256]{1,0:T(8,128)S(1)}, f32[128,256]{1,0:T(8,128)S(1)}, u32[]{:S(2)}, u32[]{:S(2)}) collective-permute-start(f32[128,256]{1,0:T(8,128)S(1)} %add.37), channel_id=1, source_target_pairs={{0,16},{4,20},{8,24},{12,28},{16,0},{20,4},{24,8},{28,12},{32,48},... | collective-permute-start | bytes 393224 | tf_op jit(solution)/shard_map/ppermute | solution.py:18
  41.7 7.3 %collective-permute-start.8 = (f32[128,256]{1,0:T(8,128)S(1)}, f32[128,256]{1,0:T(8,128)S(1)}, u32[]{:S(2)}, u32[]{:S(2)}) collective-permute-start(f32[128,256]{1,0:T(8,128)S(1)} %collective-permute-done.7.o_ref), channel_id=1, source_target_pairs={{0,4},{4,0},{8,12},{12,8},{16,20},{20,16},{24,28},{28,24},{32,36},... | collective-permute-start | bytes 393224 | tf_op jit(solution)/shard_map/ppermute | solution.py:18
  44.0 9.7 %collective-permute-start.13 = (f32[128,256]{1,0:T(8,128)S(1)}, f32[128,256]{1,0:T(8,128)S(1)}, u32[]{:S(2)}, u32[]{:S(2)}) collective-permute-start(f32[128,256]{1,0:T(8,128)S(1)} %get-tuple-element.72), channel_id=1, source_target_pairs={{0,4},{4,0},{8,12},{12,8},{16,20},{20,16},{24,28},{28,24},{32,36},... | collective-permute-start | bytes 393224 | tf_op jit(solution)/shard_map/ppermute | solution.py:18
  44.7 9.0 %collective-permute-start.14 = (f32[128,256]{1,0:T(8,128)S(1)}, f32[128,256]{1,0:T(8,128)S(1)}, u32[]{:S(2)}, u32[]{:S(2)}) collective-permute-start(f32[128,256]{1,0:T(8,128)S(1)} %add.38.q0), channel_id=1, source_target_pairs={{0,16},{4,20},{8,24},{12,28},{16,0},{20,4},{24,8},{28,12},{32,48},... | collective-permute-start | bytes 393224 | tf_op jit(solution)/shard_map/ppermute | solution.py:18
  46.3 6.2 %collective-permute-start.16 = (f32[64,256]{1,0:T(8,128)S(1)}, f32[64,256]{1,0:T(8,128)S(1)}, u32[]{:S(2)}, u32[]{:S(2)}) collective-permute-start(f32[64,256]{1,0:T(8,128)S(1)} %slice.28), channel_id=1, source_target_pairs={{0,48},{4,52},{8,56},{12,60},{16,32},{20,36},{24,40},{28,44},{32,1... | collective-permute-start | bytes 196616 | tf_op jit(solution)/shard_map/ppermute | solution.py:18
  47.9 5.8 %collective-permute-start.15 = (f32[64,256]{1,0:T(8,128)S(1)}, f32[64,256]{1,0:T(8,128)S(1)}, u32[]{:S(2)}, u32[]{:S(2)}) collective-permute-start(f32[64,256]{1,0:T(8,128)S(1)} %slice.28), channel_id=1, source_target_pairs={{0,32},{4,36},{8,40},{12,44},{16,48},{20,52},{24,56},{28,60},{32,0... | collective-permute-start | bytes 196616 | tf_op jit(solution)/shard_map/ppermute | solution.py:18
  55.7 2.7 %collective-permute-start.18 = (f32[1024,256]{1,0:T(8,128)S(1)}, f32[1024,256]{1,0:T(8,128)S(1)}, u32[]{:S(2)}, u32[]{:S(2)}) collective-permute-start(f32[1024,256]{1,0:T(8,128)S(1)} %get-tuple-element.76.refs_0_), channel_id=1, source_target_pairs={{0,1},{1,0},{2,3},{3,2},{4,5},{5,4},{6,7},{7,6},{8,9},{9,8},{10,11... | collective-permute-start | bytes 3145736 | tf_op jit(solution)/shard_map/ppermute | solution.py:18
  55.7 15.0 %collective-permute-start.17 = (f32[1024,128]{1,0:T(8,128)S(1)}, f32[1024,128]{1,0:T(8,128)S(1)}, u32[]{:S(2)}, u32[]{:S(2)}) collective-permute-start(f32[1024,128]{1,0:T(8,128)S(1)} %get-tuple-element.75), channel_id=1, source_target_pairs={{0,2},{1,3},{2,0},{3,1},{4,6},{5,7},{6,4},{7,5},{8,10},{9,11},{10,... | collective-permute-start | bytes 1572872 | tf_op jit(solution)/shard_map/ppermute | solution.py:18
  59.4 11.2 %collective-permute-start.19 = (f32[2,64,256]{2,1,0:T(8,128)S(1)}, f32[2,64,256]{2,1,0:T(8,128)S(1)}, u32[]{:S(2)}, u32[]{:S(2)}) collective-permute-start(f32[2,64,256]{2,1,0:T(8,128)S(1)} %get-tuple-element.78), channel_id=1, source_target_pairs={{0,16},{4,20},{8,24},{12,28},{16,0},{20,4},{24,8},{28,12},{32,48},... | collective-permute-start | bytes 393224 | tf_op jit(solution)/shard_map/ppermute | solution.py:18
  60.2 10.5 %collective-permute-start.20 = (f32[2,64,256]{2,1,0:T(8,128)S(1)}, f32[2,64,256]{2,1,0:T(8,128)S(1)}, u32[]{:S(2)}, u32[]{:S(2)}) collective-permute-start(f32[2,64,256]{2,1,0:T(8,128)S(1)} %get-tuple-element.79), channel_id=1, source_target_pairs={{0,32},{4,36},{8,40},{12,44},{16,48},{20,52},{24,56},{28,60},{32,0... | collective-permute-start | bytes 393224 | tf_op jit(solution)/shard_map/ppermute | solution.py:18
  62.6 8.7 %collective-permute-start.21 = (f32[2,64,256]{2,1,0:T(8,128)S(1)}, f32[2,64,256]{2,1,0:T(8,128)S(1)}, u32[]{:S(2)}, u32[]{:S(2)}) collective-permute-start(f32[2,64,256]{2,1,0:T(8,128)S(1)} %get-tuple-element.80), channel_id=1, source_target_pairs={{0,48},{4,52},{8,56},{12,60},{16,32},{20,36},{24,40},{28,44},{32,1... | collective-permute-start | bytes 393224 | tf_op jit(solution)/shard_map/ppermute | solution.py:18
  71.2 2.2 %collective-permute-start.23 = (f32[1024,128]{1,0:T(8,128)S(1)}, f32[1024,128]{1,0:T(8,128)S(1)}, u32[]{:S(2)}, u32[]{:S(2)}) collective-permute-start(f32[1024,128]{1,0:T(8,128)S(1)} %collective-permute-done.17.refs_1_), channel_id=1, source_target_pairs={{0,1},{1,0},{2,3},{3,2},{4,5},{5,4},{6,7},{7,6},{8,9},{9,8},{10,11... | collective-permute-start | bytes 1572872 | tf_op jit(solution)/shard_map/ppermute | solution.py:18
  71.2 14.7 %collective-permute-start.22 = (f32[1024,128]{1,0:T(8,128)S(1)}, f32[1024,128]{1,0:T(8,128)S(1)}, u32[]{:S(2)}, u32[]{:S(2)}) collective-permute-start(f32[1024,128]{1,0:T(8,128)S(1)} %get-tuple-element.85), channel_id=1, source_target_pairs={{0,2},{1,3},{2,0},{3,1},{4,6},{5,7},{6,4},{7,5},{8,10},{9,11},{10,... | collective-permute-start | bytes 1572872 | tf_op jit(solution)/shard_map/ppermute | solution.py:18
  74.1 11.9 %collective-permute-start.24 = (f32[2,32,256]{2,1,0:T(8,128)S(1)}, f32[2,32,256]{2,1,0:T(8,128)S(1)}, u32[]{:S(2)}, u32[]{:S(2)}) collective-permute-start(f32[2,32,256]{2,1,0:T(8,128)S(1)} %get-tuple-element.88), channel_id=1, source_target_pairs={{0,16},{4,20},{8,24},{12,28},{16,0},{20,4},{24,8},{28,12},{32,48},... | collective-permute-start | bytes 196616 | tf_op jit(solution)/shard_map/ppermute | solution.py:18
  74.2 11.8 %collective-permute-start.25 = (f32[2,32,256]{2,1,0:T(8,128)S(1)}, f32[2,32,256]{2,1,0:T(8,128)S(1)}, u32[]{:S(2)}, u32[]{:S(2)}) collective-permute-start(f32[2,32,256]{2,1,0:T(8,128)S(1)} %get-tuple-element.89), channel_id=1, source_target_pairs={{0,32},{4,36},{8,40},{12,44},{16,48},{20,52},{24,56},{28,60},{32,0... | collective-permute-start | bytes 196616 | tf_op jit(solution)/shard_map/ppermute | solution.py:18
  77.5 8.5 %collective-permute-start.26 = (f32[2,32,256]{2,1,0:T(8,128)S(1)}, f32[2,32,256]{2,1,0:T(8,128)S(1)}, u32[]{:S(2)}, u32[]{:S(2)}) collective-permute-start(f32[2,32,256]{2,1,0:T(8,128)S(1)} %get-tuple-element.90), channel_id=1, source_target_pairs={{0,48},{4,52},{8,56},{12,60},{16,32},{20,36},{24,40},{28,44},{32,1... | collective-permute-start | bytes 196616 | tf_op jit(solution)/shard_map/ppermute | solution.py:18
  86.0 2.0 %collective-permute-start.27 = (f32[1024,128]{1,0:T(8,128)S(1)}, f32[1024,128]{1,0:T(8,128)S(1)}, u32[]{:S(2)}, u32[]{:S(2)}) collective-permute-start(f32[1024,128]{1,0:T(8,128)S(1)} %collective-permute-done.22.refs_1_), channel_id=1, source_target_pairs={{0,1},{1,0},{2,3},{3,2},{4,5},{5,4},{6,7},{7,6},{8,9},{9,8},{10,11... | collective-permute-start | bytes 1572872 | tf_op jit(solution)/shard_map/ppermute | solution.py:18
  88.7 5.2 %collective-permute-start.28 = (f32[2,32,256]{2,1,0:T(8,128)S(1)}, f32[2,32,256]{2,1,0:T(8,128)S(1)}, u32[]{:S(2)}, u32[]{:S(2)}) collective-permute-start(f32[2,32,256]{2,1,0:T(8,128)S(1)} %get-tuple-element.97), channel_id=1, source_target_pairs={{0,16},{4,20},{8,24},{12,28},{16,0},{20,4},{24,8},{28,12},{32,48},... | collective-permute-start | bytes 196616 | tf_op jit(solution)/shard_map/ppermute | solution.py:18
  89.0 6.8 %collective-permute-start.29 = (f32[2,32,256]{2,1,0:T(8,128)S(1)}, f32[2,32,256]{2,1,0:T(8,128)S(1)}, u32[]{:S(2)}, u32[]{:S(2)}) collective-permute-start(f32[2,32,256]{2,1,0:T(8,128)S(1)} %get-tuple-element.98), channel_id=1, source_target_pairs={{0,32},{4,36},{8,40},{12,44},{16,48},{20,52},{24,56},{28,60},{32,0... | collective-permute-start | bytes 196616 | tf_op jit(solution)/shard_map/ppermute | solution.py:18
  92.3 5.5 %collective-permute-start.30 = (f32[2,32,256]{2,1,0:T(8,128)S(1)}, f32[2,32,256]{2,1,0:T(8,128)S(1)}, u32[]{:S(2)}, u32[]{:S(2)}) collective-permute-start(f32[2,32,256]{2,1,0:T(8,128)S(1)} %get-tuple-element.99), channel_id=1, source_target_pairs={{0,48},{4,52},{8,56},{12,60},{16,32},{20,36},{24,40},{28,44},{32,1... | collective-permute-start | bytes 196616 | tf_op jit(solution)/shard_map/ppermute | solution.py:18
  97.8 4.8 %collective-permute-start.31 = (f32[64,256]{1,0:T(8,128)S(1)}, f32[64,256]{1,0:T(8,128)S(1)}, u32[]{:S(2)}, u32[]{:S(2)}) collective-permute-start(f32[64,256]{1,0:T(8,128)S(1)} %get-tuple-element.101), channel_id=1, source_target_pairs={{0,64},{4,68},{8,72},{12,76},{16,80},{20,84},{24,88},{28,92},{32,9... | collective-permute-start | bytes 196616 | tf_op jit(solution)/shard_map/ppermute | solution.py:18
  99.3 5.9 %collective-permute-start.32 = (f32[64,256]{1,0:T(8,128)S(1)}, f32[64,256]{1,0:T(8,128)S(1)}, u32[]{:S(2)}, u32[]{:S(2)}) collective-permute-start(f32[64,256]{1,0:T(8,128)S(1)} %get-tuple-element.102), channel_id=1, source_target_pairs={{0,128},{4,132},{8,136},{12,140},{16,144},{20,148},{24,152},{28,15... | collective-permute-start | bytes 196616 | tf_op jit(solution)/shard_map/ppermute | solution.py:18
  102.2 5.5 %collective-permute-start.33 = (f32[64,256]{1,0:T(8,128)S(1)}, f32[64,256]{1,0:T(8,128)S(1)}, u32[]{:S(2)}, u32[]{:S(2)}) collective-permute-start(f32[64,256]{1,0:T(8,128)S(1)} %get-tuple-element.103), channel_id=1, source_target_pairs={{0,192},{4,196},{8,200},{12,204},{16,208},{20,212},{24,216},{28,22... | collective-permute-start | bytes 196616 | tf_op jit(solution)/shard_map/ppermute | solution.py:18
  107.7 6.1 %collective-permute-start.34 = (f32[32,256]{1,0:T(8,128)S(1)}, f32[32,256]{1,0:T(8,128)S(1)}, u32[]{:S(2)}, u32[]{:S(2)}) collective-permute-start(f32[32,256]{1,0:T(8,128)S(1)} %get-tuple-element.105), channel_id=1, source_target_pairs={{0,12},{4,8},{8,4},{12,0},{16,28},{20,24},{24,20},{28,16},{32,44},... | collective-permute-start | bytes 98312 | tf_op jit(solution)/shard_map/ppermute | solution.py:18
  113.8 4.7 %collective-permute-start.35 = (f32[16,256]{1,0:T(8,128)S(1)}, f32[16,256]{1,0:T(8,128)S(1)}, u32[]{:S(2)}, u32[]{:S(2)}) collective-permute-start(f32[16,256]{1,0:T(8,128)S(1)} %get-tuple-element.107), channel_id=1, source_target_pairs={{0,4},{4,0},{8,12},{12,8},{16,20},{20,16},{24,28},{28,24},{32,36},... | collective-permute-start | bytes 49160 | tf_op jit(solution)/shard_map/ppermute | solution.py:18

commit v8 on v7

--- a/solution.py
+++ b/solution.py
@@ -227,21 +227,25 @@
     )
 
 
-def gram(others, applied):
-    wide = applied.shape[1]
-    tall = others[1].shape[1]
+def gram(left, first, second):
+    wide = first.shape[1]
+    near = left is first
+    tall = left.shape[1]
     part = tall // 4
-    given = [applied] if others[0] is applied else [applied, others[0]]
-    given = given + [others[1]]
+    given = [first, second] if near else [first, second, left]
 
     def body(*refs):
-        (a_ref, first), second = (refs[0], refs[len(given) - 2]), refs[len(given) - 1]
+        a_ref, b_ref = refs[0], refs[1]
         outs, total = refs[len(given):-1], refs[-1]
         _, x, _ = place()
-        right = split(a_ref[...])
-        left = right if first is a_ref else split(first[...])
-        total[0] = dot3(left, right, ROWS)
-        total[1] = dot3(split(second[...]), right, ROWS)
+        mine, beside = split(a_ref[...]), split(b_ref[...])
+        if near:
+            pairs = (mine, mine), (beside, mine)
+        else:
+            rows = split(refs[2][...])
+            pairs = (rows, mine), (rows, beside)
+        for k, (up, down) in enumerate(pairs):
+            total[k] = dot3(up, down, ROWS)
         for k, out in enumerate(outs):
             out[...] = total[:, pl.ds(pl.multiple_of((x ^ k) * part, part), part)]
 
@@ -251,35 +255,49 @@
         [whole(g.shape) for g in given],
         given,
         [pltpu.VMEM((2, tall, wide), F32)],
-        flops=12 * tall * wide * applied.shape[0],
-    )
-
-
-def cut_y(near, far_even, far_odd):
+        flops=12 * tall * wide * first.shape[0],
+    )
+
+
+def add_x(near, far_even, far_odd):
     _, rows, wide = near[0].shape
     half = rows // 2
 
     def body(*refs):
-        ins, outs, total = refs[:12], refs[12:16], refs[16]
+        ins, mine, give = refs[:12], refs[12], refs[13]
+
+        def add(four, block):
+            return (four[0][block] + four[1][block]) + (four[2][block] + four[3][block])
+
+        for block in range(2):
+            mine[block] = add(ins[:4], block)
+        mine[2, :half] = add(ins[4:8], 0)
+        mine[2, half:] = add(ins[8:], 0)
+        give[:half] = add(ins[4:8], 1)
+        give[half:] = add(ins[8:], 1)
+
+    ins = [*near, *far_even, *far_odd]
+    return call(body, shapes((3, rows, wide), (rows, wide)), [whole(i.shape) for i in ins], ins)
+
+
+def cut_y(mine, got):
+    blocks, rows, wide = mine.shape
+
+    def body(mine_ref, got_ref, *refs):
+        *outs, total = refs
         y, _, _ = place()
         probe = lax.axis_index("probe")
-
-        def add(four):
-            return (four[0][...] + four[1][...]) + (four[2][...] + four[3][...])
-
-        total[:2] = add(ins[:4])
-        total[2:, :half] = add(ins[4:8])
-        total[2:, half:] = add(ins[8:])
+        total[:blocks] = mine_ref[...]
+        total[blocks] = got_ref[...]
         for k, out in enumerate(outs):
             out[...] = total[probe ^ y ^ k]
 
-    ins = [*near, *far_even, *far_odd]
     return call(
         body,
         shapes(*[(rows, wide)] * 4),
-        [whole(i.shape) for i in ins],
-        ins,
-        [pltpu.VMEM((4, rows, wide), F32)],
+        [whole(mine.shape), whole(got.shape)],
+        [mine, got],
+        [pltpu.VMEM((blocks + 1, rows, wide), F32)],
     )
 
 
@@ -351,12 +369,13 @@
     even = swap(even, "probe", 2)
     odd = swap(odd, "probe", 2)
     beside = swap(applied, "probe", 1)
-    first = around(gram([applied, beside], applied), 4)
+    first = around(gram(applied, applied, beside), 4)
     even, *first = lax.optimization_barrier((even, *first))
-    second = around(gram([even, swap(even, "probe", 1)], applied), 4)
+    second = around(gram(even, applied, beside), 4)
     odd, *second = lax.optimization_barrier((odd, *second))
-    third = around(gram([odd, swap(odd, "probe", 1)], applied), 4)
-    blocks = around(cut_y(first, second, third), 16)
+    third = around(gram(odd, applied, beside), 4)
+    mine, give = add_x(first, second, third)
+    blocks = around(cut_y(mine, swap(give, "probe", 1)), 16)
     keep, give = cut_z(blocks, 1)
     keep, give = cut_z([keep, swap(give, "leaf", 3)], 0)
     total = keep + swap(give, "leaf", 1)

time: 119 us -> 115 us (0.966); the launches traced: 119 us -> 114 us
  waiting for transfers between devices: 43 us -> 39.1 us
  starting transfers between devices: 59.3 us -> 57.8 us
    ppermute x36 -> x35, waiting for transfers between devices: 43 us -> 39.1 us  [swap(): return lax.ppermute(value, axis, pairs)]
    ppermute x36 -> x35, starting transfers between devices: 59.3 us -> 57.8 us  [swap(): return lax.ppermute(value, axis, pairs)]
    pallas_call x10 -> x11, Pallas kernels: 12.5 us -> 12.7 us  [call(): pl.pallas_call(body, out_shape=outs, grid=grid, in_specs=specs, out_specs...]
  transfers between devices with their start and end apart: 36 -> 35, of which waited for: 19 -> 18; matrix products, arithmetic and copies ran while one was open for 2% -> 3% of each run, Pallas kernels for 6% -> 6%
where the time goes in v8:
time: 115 us; the launch traced here: 114 us
  starting transfers between devices  57.8 us (50%)
  waiting for transfers between devices  39.1 us (34%)
  Pallas kernels  12.7 us (11%)
  matrix products  2.39 us (2%)
    ppermute x35, starting transfers between devices, swap(): return lax.ppermute(value, axis, pairs)  57.8 us
    ppermute x35, waiting for transfers between devices, swap(): return lax.ppermute(value, axis, pairs)  39.1 us
    pallas_call x11, Pallas kernels, call(): pl.pallas_call(body, out_shape=outs, grid=grid, in_specs=specs, out_specs...  12.7 us
    dot_general x1, matrix products, near_product(): return jnp.dot(masked, probes, precision=HIGH, preferred_element_type=F32)  2.39 us
  transfers between devices with their start and end apart: 35, of which 18 were waited for; matrix products, arithmetic and copies ran while one was open for 3% of the time, Pallas kernels for 6%

profile of v8, /device:TPU:32, one launch (start us, length us, event | category | flops | bytes accessed | tf_op | source)
XLA Modules:
  0.0 113.9 jit_solution(2669002277899003264)
XLA Ops:
  0.6 3.1 %shard_map.68 = (f32[64,256]{1,0:T(8,128)S(1)}, f32[64,256]{1,0:T(8,128)S(1)}, f32[128,256]{1,0:T(8,128)S(1)}, f32[128,256]{1,0:T(8,128)S(1)}) custom-call(f32[6,1024,128]{2,1,0:T(8,128)} %c_hbm.3, f32[1024,256]{1,0:T(8,128)} %p_hbm.3), custom_call_target="tpu_custom_call" | custom-call | flops 603979776 | bytes 4587520 | tf_op jit(solution)/shard_map/pallas_call | solution.py:49
  3.8 3.1 %collective-permute-start = (f32[128,256]{1,0:T(8,128)S(1)}, f32[128,256]{1,0:T(8,128)S(1)}, u32[]{:S(2)}, u32[]{:S(2)}) collective-permute-start(f32[128,256]{1,0:T(8,128)S(1)} %get-tuple-element.57), channel_id=1, source_target_pairs={{0,32},{4,36},{8,40},{12,44},{16,48},{20,52},{24,56},{28,60},{32,0... | collective-permute-start | bytes 393224 | tf_op jit(solution)/shard_map/ppermute | solution.py:18
  6.9 1.1 collective-permute-start.1
  8.0 3.3 %shard_map.69 = (f32[128,256]{1,0:T(8,128)S(1)}, f32[128,256]{1,0:T(8,128)S(1)}, f32[128,256]{1,0:T(8,128)S(1)}) custom-call(f32[6,1024,128]{2,1,0:T(8,128)} %c_hbm.3, f32[1024,256]{1,0:T(8,128)} %p_hbm.3), custom_call_target="tpu_custom_call" | custom-call | flops 603979776 | bytes 4587520 | tf_op jit(solution)/shard_map/pallas_call | solution.py:49
  11.3 3.4 %collective-permute-start.9 = (f32[128,256]{1,0:T(8,128)S(1)}, f32[128,256]{1,0:T(8,128)S(1)}, u32[]{:S(2)}, u32[]{:S(2)}) collective-permute-start(f32[128,256]{1,0:T(8,128)S(1)} %get-tuple-element.68), channel_id=1, source_target_pairs={{0,4},{4,0},{8,12},{12,8},{16,20},{20,16},{24,28},{28,24},{32,36},... | collective-permute-start | bytes 393224 | tf_op jit(solution)/shard_map/ppermute | solution.py:18
  14.8 3.1 %collective-permute-start.5 = (f32[32,256]{1,0:T(8,128)S(1)}, f32[32,256]{1,0:T(8,128)S(1)}, u32[]{:S(2)}, u32[]{:S(2)}) collective-permute-start(f32[32,256]{1,0:T(8,128)S(1)} %get-tuple-element.115), channel_id=1, source_target_pairs={{0,192},{4,196},{8,200},{12,204},{16,208},{20,212},{24,216},{28,22... | collective-permute-start | bytes 98312 | tf_op jit(solution)/shard_map/ppermute | solution.py:18
  17.8 0.6 collective-permute-start.4
  19.3 6.1 %collective-permute-start.10 = (f32[128,256]{1,0:T(8,128)S(1)}, f32[128,256]{1,0:T(8,128)S(1)}, u32[]{:S(2)}, u32[]{:S(2)}) collective-permute-start(f32[128,256]{1,0:T(8,128)S(1)} %add.36), channel_id=1, source_target_pairs={{0,12},{4,8},{8,4},{12,0},{16,28},{20,24},{24,20},{28,16},{32,44},... | collective-permute-start | bytes 393224 | tf_op jit(solution)/shard_map/ppermute | solution.py:18
  25.9 2.4 %fusion.n_ref = f32[1024,256]{1,0:T(8,128)S(1)} fusion(f32[1024,256]{1,0:T(8,128)S(1)} %copy-done.1, f32[1024,1024]{1,0:T(8,128)S(1)} %copy-done.2, f32[128,8,8,128]{3,2,1,0:T(8,128)S(1)} %bitcast.8), kind=kOutput, calls=%fused_computation.1 | convolution fusion | flops 1611661312 | bytes 10485760 | tf_op jit(solution)/shard_map/dot_general | solution.py:338
  28.3 3.5 %collective-permute-start.7 = (f32[128,256]{1,0:T(8,128)S(1)}, f32[128,256]{1,0:T(8,128)S(1)}, u32[]{:S(2)}, u32[]{:S(2)}) collective-permute-start(f32[128,256]{1,0:T(8,128)S(1)} %get-tuple-element.67), channel_id=1, source_target_pairs={{0,12},{4,8},{8,4},{12,0},{16,28},{20,24},{24,20},{28,16},{32,44},... | collective-permute-start | bytes 393224 | tf_op jit(solution)/shard_map/ppermute | solution.py:18
  31.8 3.0 %collective-permute-done.6 = f32[128,256]{1,0:T(8,128)S(1)} collective-permute-done((f32[128,256]{1,0:T(8,128)S(1)}, f32[128,256]{1,0:T(8,128)S(1)}, u32[]{:S(2)}, u32[]{:S(2)}) %collective-permute-start.6) | collective-permute-done | bytes 131104 | tf_op jit(solution)/shard_map/ppermute | solution.py:18
  34.9 0.6 collective-permute-start.12
  35.5 2.2 %collective-permute-start.11 = (f32[128,256]{1,0:T(8,128)S(1)}, f32[128,256]{1,0:T(8,128)S(1)}, u32[]{:S(2)}, u32[]{:S(2)}) collective-permute-start(f32[128,256]{1,0:T(8,128)S(1)} %add.37), channel_id=1, source_target_pairs={{0,16},{4,20},{8,24},{12,28},{16,0},{20,4},{24,8},{28,12},{32,48},... | collective-permute-start | bytes 393224 | tf_op jit(solution)/shard_map/ppermute | solution.py:18
  37.7 4.0 %collective-permute-done.7.o_ref = f32[128,256]{1,0:T(8,128)S(1)} collective-permute-done((f32[128,256]{1,0:T(8,128)S(1)}, f32[128,256]{1,0:T(8,128)S(1)}, u32[]{:S(2)}, u32[]{:S(2)}) %collective-permute-start.7) | collective-permute-done | bytes 131104 | tf_op jit(solution)/shard_map/ppermute | solution.py:18
  41.7 2.3 %collective-permute-done.12 = f32[128,256]{1,0:T(8,128)S(1)} collective-permute-done((f32[128,256]{1,0:T(8,128)S(1)}, f32[128,256]{1,0:T(8,128)S(1)}, u32[]{:S(2)}, u32[]{:S(2)}) %collective-permute-start.12) | collective-permute-done | bytes 131104 | tf_op jit(solution)/shard_map/ppermute | solution.py:18
  44.0 0.7 collective-permute-start.13
  44.7 1.6 %collective-permute-start.14 = (f32[128,256]{1,0:T(8,128)S(1)}, f32[128,256]{1,0:T(8,128)S(1)}, u32[]{:S(2)}, u32[]{:S(2)}) collective-permute-start(f32[128,256]{1,0:T(8,128)S(1)} %add.38.q0), channel_id=1, source_target_pairs={{0,16},{4,20},{8,24},{12,28},{16,0},{20,4},{24,8},{28,12},{32,48},... | collective-permute-start | bytes 393224 | tf_op jit(solution)/shard_map/ppermute | solution.py:18
  46.3 1.6 %collective-permute-start.16 = (f32[64,256]{1,0:T(8,128)S(1)}, f32[64,256]{1,0:T(8,128)S(1)}, u32[]{:S(2)}, u32[]{:S(2)}) collective-permute-start(f32[64,256]{1,0:T(8,128)S(1)} %slice.28), channel_id=1, source_target_pairs={{0,48},{4,52},{8,56},{12,60},{16,32},{20,36},{24,40},{28,44},{32,1... | collective-permute-start | bytes 196616 | tf_op jit(solution)/shard_map/ppermute | solution.py:18
  47.9 0.9 collective-permute-start.15
  48.9 1.6 %shard_map.70 = (f32[1024,256]{1,0:T(8,128)S(1)}, bf16[1024,512]{1,0:T(8,128)(2,1)S(1)}, bf16[1024,512]{1,0:T(8,128)(2,1)S(1)}) custom-call(f32[1024,256]{1,0:T(8,128)S(1)} %fusion.n_ref, f32[6,1024,128]{2,1,0:T(8,128)S(1)} %copy-done, f32[128,256]{1,0:T(8,128)S(1)} %collective-permute-done.7.o_ref, f32[128,256]{1,0:T(8,128)S(1)} %collective-permute-done.8.m_ref, ...), custom_call_target="tpu_custom_call" | custom-call | flops 402653184 | bytes 9830400 | tf_op jit(solution)/shard_map/pallas_call | solution.py:49
  50.6 1.9 %collective-permute-done.16.q3 = f32[64,256]{1,0:T(8,128)S(1)} collective-permute-done((f32[64,256]{1,0:T(8,128)S(1)}, f32[64,256]{1,0:T(8,128)S(1)}, u32[]{:S(2)}, u32[]{:S(2)}) %collective-permute-start.16) | collective-permute-done | bytes 65568 | tf_op jit(solution)/shard_map/ppermute | solution.py:18
  52.5 1.2 %collective-permute-done.15.q2 = f32[64,256]{1,0:T(8,128)S(1)} collective-permute-done((f32[64,256]{1,0:T(8,128)S(1)}, f32[64,256]{1,0:T(8,128)S(1)}, u32[]{:S(2)}, u32[]{:S(2)}) %collective-permute-start.15) | collective-permute-done | bytes 65568 | tf_op jit(solution)/shard_map/ppermute | solution.py:18
  53.7 2.0 %shard_map.71 = (f32[1024,256]{1,0:T(8,128)}, f32[1024,256]{1,0:T(8,128)S(1)}, f32[1024,128]{1,0:T(8,128)S(1)}, f32[1024,128]{1,0:T(8,128)S(1)}) custom-call(f32[1024,256]{1,0:T(8,128)S(1)} %get-tuple-element.69.b_ref, bf16[1024,512]{1,0:T(8,128)(2,1)S(1)} %get-tuple-element.70.h_ref, bf16[1024,512]{1,0:T(8,128)(2,1)S(1)} %get-tuple-element.71.l_ref, ...), custom_call_target="tpu_custom_call" | custom-call | flops 805306368 | bytes 8912896 | tf_op jit(solution)/shard_map/pallas_call | solution.py:49
  55.7 2.4 %collective-permute-start.17 = (f32[1024,128]{1,0:T(8,128)S(1)}, f32[1024,128]{1,0:T(8,128)S(1)}, u32[]{:S(2)}, u32[]{:S(2)}) collective-permute-start(f32[1024,128]{1,0:T(8,128)S(1)} %get-tuple-element.77), channel_id=1, source_target_pairs={{0,2},{1,3},{2,0},{3,1},{4,6},{5,7},{6,4},{7,5},{8,10},{9,11},{10,... | collective-permute-start | bytes 1572872 | tf_op jit(solution)/shard_map/ppermute | solution.py:18
  58.3 1.1 shard_map.72
  59.4 0.7 collective-permute-start.19
  60.2 2.4 %collective-permute-start.20 = (f32[2,64,256]{2,1,0:T(8,128)S(1)}, f32[2,64,256]{2,1,0:T(8,128)S(1)}, u32[]{:S(2)}, u32[]{:S(2)}) collective-permute-start(f32[2,64,256]{2,1,0:T(8,128)S(1)} %get-tuple-element.81), channel_id=1, source_target_pairs={{0,32},{4,36},{8,40},{12,44},{16,48},{20,52},{24,56},{28,60},{32,0... | collective-permute-start | bytes 393224 | tf_op jit(solution)/shard_map/ppermute | solution.py:18
  62.6 1.6 %collective-permute-start.21 = (f32[2,64,256]{2,1,0:T(8,128)S(1)}, f32[2,64,256]{2,1,0:T(8,128)S(1)}, u32[]{:S(2)}, u32[]{:S(2)}) collective-permute-start(f32[2,64,256]{2,1,0:T(8,128)S(1)} %get-tuple-element.82), channel_id=1, source_target_pairs={{0,48},{4,52},{8,56},{12,60},{16,32},{20,36},{24,40},{28,44},{32,1... | collective-permute-start | bytes 393224 | tf_op jit(solution)/shard_map/ppermute | solution.py:18
  64.2 6.6 %collective-permute-done.17.refs_2_ = f32[1024,128]{1,0:T(8,128)S(1)} collective-permute-done((f32[1024,128]{1,0:T(8,128)S(1)}, f32[1024,128]{1,0:T(8,128)S(1)}, u32[]{:S(2)}, u32[]{:S(2)}) %collective-permute-start.17) | collective-permute-done | bytes 524320 | tf_op jit(solution)/shard_map/ppermute | solution.py:18
  71.2 0.7 shard_map.73
  72.1 3.1 %collective-permute-start.24 = (f32[2,32,256]{2,1,0:T(8,128)S(1)}, f32[2,32,256]{2,1,0:T(8,128)S(1)}, u32[]{:S(2)}, u32[]{:S(2)}) collective-permute-start(f32[2,32,256]{2,1,0:T(8,128)S(1)} %get-tuple-element.91), channel_id=1, source_target_pairs={{0,32},{4,36},{8,40},{12,44},{16,48},{20,52},{24,56},{28,60},{32,0... | collective-permute-start | bytes 196616 | tf_op jit(solution)/shard_map/ppermute | solution.py:18
  75.1 1.6 %collective-permute-start.25 = (f32[2,32,256]{2,1,0:T(8,128)S(1)}, f32[2,32,256]{2,1,0:T(8,128)S(1)}, u32[]{:S(2)}, u32[]{:S(2)}) collective-permute-start(f32[2,32,256]{2,1,0:T(8,128)S(1)} %get-tuple-element.92), channel_id=1, source_target_pairs={{0,48},{4,52},{8,56},{12,60},{16,32},{20,36},{24,40},{28,44},{32,1... | collective-permute-start | bytes 196616 | tf_op jit(solution)/shard_map/ppermute | solution.py:18
  76.7 5.2 %collective-permute-done.22.refs_2_ = f32[1024,128]{1,0:T(8,128)S(1)} collective-permute-done((f32[1024,128]{1,0:T(8,128)S(1)}, f32[1024,128]{1,0:T(8,128)S(1)}, u32[]{:S(2)}, u32[]{:S(2)}) %collective-permute-start.22) | collective-permute-done | bytes 524320 | tf_op jit(solution)/shard_map/ppermute | solution.py:18
  81.9 0.7 shard_map.74
  82.8 2.7 %collective-permute-start.27 = (f32[2,32,256]{2,1,0:T(8,128)S(1)}, f32[2,32,256]{2,1,0:T(8,128)S(1)}, u32[]{:S(2)}, u32[]{:S(2)}) collective-permute-start(f32[2,32,256]{2,1,0:T(8,128)S(1)} %get-tuple-element.100), channel_id=1, source_target_pairs={{0,32},{4,36},{8,40},{12,44},{16,48},{20,52},{24,56},{28,60},{32,0... | collective-permute-start | bytes 196616 | tf_op jit(solution)/shard_map/ppermute | solution.py:18
  85.6 1.9 %collective-permute-start.28 = (f32[2,32,256]{2,1,0:T(8,128)S(1)}, f32[2,32,256]{2,1,0:T(8,128)S(1)}, u32[]{:S(2)}, u32[]{:S(2)}) collective-permute-start(f32[2,32,256]{2,1,0:T(8,128)S(1)} %get-tuple-element.101), channel_id=1, source_target_pairs={{0,48},{4,52},{8,56},{12,60},{16,32},{20,36},{24,40},{28,44},{32,1... | collective-permute-start | bytes 196616 | tf_op jit(solution)/shard_map/ppermute | solution.py:18
  87.4 1.8 %collective-permute-done.27.refs_10_ = f32[2,32,256]{2,1,0:T(8,128)S(1)} collective-permute-done((f32[2,32,256]{2,1,0:T(8,128)S(1)}, f32[2,32,256]{2,1,0:T(8,128)S(1)}, u32[]{:S(2)}, u32[]{:S(2)}) %collective-permute-start.27) | collective-permute-done | bytes 65568 | tf_op jit(solution)/shard_map/ppermute | solution.py:18
  89.2 1.8 %collective-permute-done.28.refs_11_ = f32[2,32,256]{2,1,0:T(8,128)S(1)} collective-permute-done((f32[2,32,256]{2,1,0:T(8,128)S(1)}, f32[2,32,256]{2,1,0:T(8,128)S(1)}, u32[]{:S(2)}, u32[]{:S(2)}) %collective-permute-start.28) | collective-permute-done | bytes 65568 | tf_op jit(solution)/shard_map/ppermute | solution.py:18
  91.2 1.2 %collective-permute-done.29.got_ref = f32[64,256]{1,0:T(8,128)S(1)} collective-permute-done((f32[64,256]{1,0:T(8,128)S(1)}, f32[64,256]{1,0:T(8,128)S(1)}, u32[]{:S(2)}, u32[]{:S(2)}) %collective-permute-start.29) | collective-permute-done | bytes 65568 | tf_op jit(solution)/shard_map/ppermute | solution.py:18
  92.5 1.2 %collective-permute-start.30 = (f32[64,256]{1,0:T(8,128)S(1)}, f32[64,256]{1,0:T(8,128)S(1)}, u32[]{:S(2)}, u32[]{:S(2)}) collective-permute-start(f32[64,256]{1,0:T(8,128)S(1)} %get-tuple-element.105), channel_id=1, source_target_pairs={{0,64},{4,68},{8,72},{12,76},{16,80},{20,84},{24,88},{28,92},{32,9... | collective-permute-start | bytes 196616 | tf_op jit(solution)/shard_map/ppermute | solution.py:18
  93.7 2.9 %collective-permute-start.31 = (f32[64,256]{1,0:T(8,128)S(1)}, f32[64,256]{1,0:T(8,128)S(1)}, u32[]{:S(2)}, u32[]{:S(2)}) collective-permute-start(f32[64,256]{1,0:T(8,128)S(1)} %get-tuple-element.106), channel_id=1, source_target_pairs={{0,128},{4,132},{8,136},{12,140},{16,144},{20,148},{24,152},{28,15... | collective-permute-start | bytes 196616 | tf_op jit(solution)/shard_map/ppermute | solution.py:18
  96.5 0.7 collective-permute-start.32
  97.3 2.8 %collective-permute-done.31.refs_2_ = f32[64,256]{1,0:T(8,128)S(1)} collective-permute-done((f32[64,256]{1,0:T(8,128)S(1)}, f32[64,256]{1,0:T(8,128)S(1)}, u32[]{:S(2)}, u32[]{:S(2)}) %collective-permute-start.31) | collective-permute-done | bytes 65568 | tf_op jit(solution)/shard_map/ppermute | solution.py:18
  100.1 1.9 %collective-permute-done.32.refs_3_ = f32[64,256]{1,0:T(8,128)S(1)} collective-permute-done((f32[64,256]{1,0:T(8,128)S(1)}, f32[64,256]{1,0:T(8,128)S(1)}, u32[]{:S(2)}, u32[]{:S(2)}) %collective-permute-start.32) | collective-permute-done | bytes 65568 | tf_op jit(solution)/shard_map/ppermute | solution.py:18
  102.0 4.5 %collective-permute-start.33 = (f32[32,256]{1,0:T(8,128)S(1)}, f32[32,256]{1,0:T(8,128)S(1)}, u32[]{:S(2)}, u32[]{:S(2)}) collective-permute-start(f32[32,256]{1,0:T(8,128)S(1)} %get-tuple-element.109), channel_id=1, source_target_pairs={{0,12},{4,8},{8,4},{12,0},{16,28},{20,24},{24,20},{28,16},{32,44},... | collective-permute-start | bytes 98312 | tf_op jit(solution)/shard_map/ppermute | solution.py:18
  106.6 1.9 %collective-permute-done.33.refs_1_ = f32[32,256]{1,0:T(8,128)S(1)} collective-permute-done((f32[32,256]{1,0:T(8,128)S(1)}, f32[32,256]{1,0:T(8,128)S(1)}, u32[]{:S(2)}, u32[]{:S(2)}) %collective-permute-start.33) | collective-permute-done | bytes 32800 | tf_op jit(solution)/shard_map/ppermute | solution.py:18
  108.5 2.5 %collective-permute-start.34 = (f32[16,256]{1,0:T(8,128)S(1)}, f32[16,256]{1,0:T(8,128)S(1)}, u32[]{:S(2)}, u32[]{:S(2)}) collective-permute-start(f32[16,256]{1,0:T(8,128)S(1)} %get-tuple-element.111), channel_id=1, source_target_pairs={{0,4},{4,0},{8,12},{12,8},{16,20},{20,16},{24,28},{28,24},{32,36},... | collective-permute-start | bytes 49160 | tf_op jit(solution)/shard_map/ppermute | solution.py:18
  111.0 2.3 %collective-permute-done.34 = f32[16,256]{1,0:T(8,128)S(1)} collective-permute-done((f32[16,256]{1,0:T(8,128)S(1)}, f32[16,256]{1,0:T(8,128)S(1)}, u32[]{:S(2)}, u32[]{:S(2)}) %collective-permute-start.34) | collective-permute-done | bytes 16416 | tf_op jit(solution)/shard_map/ppermute | solution.py:18
  (54 shorter events, 3.3 us)
Async XLA Ops:
  0.6 18.3 %copy-start.3 = (s32[1,8,8]{2,1,0:T(8,128)S(1)}, s32[1,8,8]{2,1,0:T(8,128)}, u32[]{:S(2)}) copy-start(s32[1,8,8]{2,1,0:T(8,128)} %param.6) | copy-start | bytes 772
  3.8 10.9 %collective-permute-start = (f32[128,256]{1,0:T(8,128)S(1)}, f32[128,256]{1,0:T(8,128)S(1)}, u32[]{:S(2)}, u32[]{:S(2)}) collective-permute-start(f32[128,256]{1,0:T(8,128)S(1)} %get-tuple-element.57), channel_id=1, source_target_pairs={{0,32},{4,36},{8,40},{12,44},{16,48},{20,52},{24,56},{28,60},{32,0... | collective-permute-start | bytes 393224 | tf_op jit(solution)/shard_map/ppermute | solution.py:18
  6.9 7.8 %collective-permute-start.1 = (f32[128,256]{1,0:T(8,128)S(1)}, f32[128,256]{1,0:T(8,128)S(1)}, u32[]{:S(2)}, u32[]{:S(2)}) collective-permute-start(f32[128,256]{1,0:T(8,128)S(1)} %get-tuple-element.58), channel_id=1, source_target_pairs={{0,48},{4,52},{8,56},{12,60},{16,32},{20,36},{24,40},{28,44},{32,1... | collective-permute-start | bytes 393224 | tf_op jit(solution)/shard_map/ppermute | solution.py:18
  8.0 17.8 %copy-start.1 = (f32[1024,256]{1,0:T(8,128)S(1)}, f32[1024,256]{1,0:T(8,128)}, u32[]{:S(2)}) copy-start(f32[1024,256]{1,0:T(8,128)} %p_hbm.3) | copy-start | bytes 3145732
  8.0 17.8 %copy-start.2 = (f32[1024,1024]{1,0:T(8,128)S(1)}, f32[1024,1024]{1,0:T(8,128)}, u32[]{:S(2)}) copy-start(f32[1024,1024]{1,0:T(8,128)} %param.5) | copy-start | bytes 12582916
  8.0 6.7 %collective-permute-start.2 = (f32[64,256]{1,0:T(8,128)S(1)}, f32[64,256]{1,0:T(8,128)S(1)}, u32[]{:S(2)}, u32[]{:S(2)}) collective-permute-start(f32[64,256]{1,0:T(8,128)S(1)} %get-tuple-element.60), channel_id=1, source_target_pairs={{0,16},{4,20},{8,24},{12,28},{16,0},{20,4},{24,8},{28,12},{32,48},... | collective-permute-start | bytes 196616 | tf_op jit(solution)/shard_map/ppermute | solution.py:18
  11.3 7.9 %collective-permute-start.9 = (f32[128,256]{1,0:T(8,128)S(1)}, f32[128,256]{1,0:T(8,128)S(1)}, u32[]{:S(2)}, u32[]{:S(2)}) collective-permute-start(f32[128,256]{1,0:T(8,128)S(1)} %get-tuple-element.68), channel_id=1, source_target_pairs={{0,4},{4,0},{8,12},{12,8},{16,20},{20,16},{24,28},{28,24},{32,36},... | collective-permute-start | bytes 393224 | tf_op jit(solution)/shard_map/ppermute | solution.py:18
  14.8 10.6 %collective-permute-start.5 = (f32[32,256]{1,0:T(8,128)S(1)}, f32[32,256]{1,0:T(8,128)S(1)}, u32[]{:S(2)}, u32[]{:S(2)}) collective-permute-start(f32[32,256]{1,0:T(8,128)S(1)} %get-tuple-element.115), channel_id=1, source_target_pairs={{0,192},{4,196},{8,200},{12,204},{16,208},{20,212},{24,216},{28,22... | collective-permute-start | bytes 98312 | tf_op jit(solution)/shard_map/ppermute | solution.py:18
  17.8 7.5 %collective-permute-start.4 = (f32[32,256]{1,0:T(8,128)S(1)}, f32[32,256]{1,0:T(8,128)S(1)}, u32[]{:S(2)}, u32[]{:S(2)}) collective-permute-start(f32[32,256]{1,0:T(8,128)S(1)} %get-tuple-element.115), channel_id=1, source_target_pairs={{0,128},{4,132},{8,136},{12,140},{16,144},{20,148},{24,152},{28,15... | collective-permute-start | bytes 98312 | tf_op jit(solution)/shard_map/ppermute | solution.py:18
  18.5 6.9 %collective-permute-start.3 = (f32[32,256]{1,0:T(8,128)S(1)}, f32[32,256]{1,0:T(8,128)S(1)}, u32[]{:S(2)}, u32[]{:S(2)}) collective-permute-start(f32[32,256]{1,0:T(8,128)S(1)} %get-tuple-element.114), channel_id=1, source_target_pairs={{0,64},{4,68},{8,72},{12,76},{16,80},{20,84},{24,88},{28,92},{32,9... | collective-permute-start | bytes 98312 | tf_op jit(solution)/shard_map/ppermute | solution.py:18
  19.3 16.3 %collective-permute-start.10 = (f32[128,256]{1,0:T(8,128)S(1)}, f32[128,256]{1,0:T(8,128)S(1)}, u32[]{:S(2)}, u32[]{:S(2)}) collective-permute-start(f32[128,256]{1,0:T(8,128)S(1)} %add.36), channel_id=1, source_target_pairs={{0,12},{4,8},{8,4},{12,0},{16,28},{20,24},{24,20},{28,16},{32,44},... | collective-permute-start | bytes 393224 | tf_op jit(solution)/shard_map/ppermute | solution.py:18
  25.4 9.5 %collective-permute-start.6 = (f32[128,256]{1,0:T(8,128)S(1)}, f32[128,256]{1,0:T(8,128)S(1)}, u32[]{:S(2)}, u32[]{:S(2)}) collective-permute-start(f32[128,256]{1,0:T(8,128)S(1)} %pad_maximum_fusion), channel_id=1, source_target_pairs={{0,4},{4,0},{8,12},{12,8},{16,20},{20,16},{24,28},{28,24},{32,36},... | collective-permute-start | bytes 393224 | tf_op jit(solution)/shard_map/ppermute | solution.py:18
  25.9 23.1 %copy-start = (f32[6,1024,128]{2,1,0:T(8,128)S(1)}, f32[6,1024,128]{2,1,0:T(8,128)}, u32[]{:S(2)}) copy-start(f32[6,1024,128]{2,1,0:T(8,128)} %u_ref.1) | copy-start | bytes 9437188
  28.3 13.4 %collective-permute-start.7 = (f32[128,256]{1,0:T(8,128)S(1)}, f32[128,256]{1,0:T(8,128)S(1)}, u32[]{:S(2)}, u32[]{:S(2)}) collective-permute-start(f32[128,256]{1,0:T(8,128)S(1)} %get-tuple-element.67), channel_id=1, source_target_pairs={{0,12},{4,8},{8,4},{12,0},{16,28},{20,24},{24,20},{28,16},{32,44},... | collective-permute-start | bytes 393224 | tf_op jit(solution)/shard_map/ppermute | solution.py:18
  34.9 9.1 %collective-permute-start.12 = (f32[128,256]{1,0:T(8,128)S(1)}, f32[128,256]{1,0:T(8,128)S(1)}, u32[]{:S(2)}, u32[]{:S(2)}) collective-permute-start(f32[128,256]{1,0:T(8,128)S(1)} %add.35), channel_id=1, source_target_pairs={{0,12},{4,8},{8,4},{12,0},{16,28},{20,24},{24,20},{28,16},{32,44},... | collective-permute-start | bytes 393224 | tf_op jit(solution)/shard_map/ppermute | solution.py:18
  35.5 12.4 %collective-permute-start.11 = (f32[128,256]{1,0:T(8,128)S(1)}, f32[128,256]{1,0:T(8,128)S(1)}, u32[]{:S(2)}, u32[]{:S(2)}) collective-permute-start(f32[128,256]{1,0:T(8,128)S(1)} %add.37), channel_id=1, source_target_pairs={{0,16},{4,20},{8,24},{12,28},{16,0},{20,4},{24,8},{28,12},{32,48},... | collective-permute-start | bytes 393224 | tf_op jit(solution)/shard_map/ppermute | solution.py:18
  41.7 7.3 %collective-permute-start.8 = (f32[128,256]{1,0:T(8,128)S(1)}, f32[128,256]{1,0:T(8,128)S(1)}, u32[]{:S(2)}, u32[]{:S(2)}) collective-permute-start(f32[128,256]{1,0:T(8,128)S(1)} %collective-permute-done.7.o_ref), channel_id=1, source_target_pairs={{0,4},{4,0},{8,12},{12,8},{16,20},{20,16},{24,28},{28,24},{32,36},... | collective-permute-start | bytes 393224 | tf_op jit(solution)/shard_map/ppermute | solution.py:18
  44.0 9.7 %collective-permute-start.13 = (f32[128,256]{1,0:T(8,128)S(1)}, f32[128,256]{1,0:T(8,128)S(1)}, u32[]{:S(2)}, u32[]{:S(2)}) collective-permute-start(f32[128,256]{1,0:T(8,128)S(1)} %get-tuple-element.74), channel_id=1, source_target_pairs={{0,4},{4,0},{8,12},{12,8},{16,20},{20,16},{24,28},{28,24},{32,36},... | collective-permute-start | bytes 393224 | tf_op jit(solution)/shard_map/ppermute | solution.py:18
  44.7 9.0 %collective-permute-start.14 = (f32[128,256]{1,0:T(8,128)S(1)}, f32[128,256]{1,0:T(8,128)S(1)}, u32[]{:S(2)}, u32[]{:S(2)}) collective-permute-start(f32[128,256]{1,0:T(8,128)S(1)} %add.38.q0), channel_id=1, source_target_pairs={{0,16},{4,20},{8,24},{12,28},{16,0},{20,4},{24,8},{28,12},{32,48},... | collective-permute-start | bytes 393224 | tf_op jit(solution)/shard_map/ppermute | solution.py:18
  46.3 6.2 %collective-permute-start.16 = (f32[64,256]{1,0:T(8,128)S(1)}, f32[64,256]{1,0:T(8,128)S(1)}, u32[]{:S(2)}, u32[]{:S(2)}) collective-permute-start(f32[64,256]{1,0:T(8,128)S(1)} %slice.28), channel_id=1, source_target_pairs={{0,48},{4,52},{8,56},{12,60},{16,32},{20,36},{24,40},{28,44},{32,1... | collective-permute-start | bytes 196616 | tf_op jit(solution)/shard_map/ppermute | solution.py:18
  47.9 5.8 %collective-permute-start.15 = (f32[64,256]{1,0:T(8,128)S(1)}, f32[64,256]{1,0:T(8,128)S(1)}, u32[]{:S(2)}, u32[]{:S(2)}) collective-permute-start(f32[64,256]{1,0:T(8,128)S(1)} %slice.28), channel_id=1, source_target_pairs={{0,32},{4,36},{8,40},{12,44},{16,48},{20,52},{24,56},{28,60},{32,0... | collective-permute-start | bytes 196616 | tf_op jit(solution)/shard_map/ppermute | solution.py:18
  55.7 2.7 %collective-permute-start.18 = (f32[1024,256]{1,0:T(8,128)S(1)}, f32[1024,256]{1,0:T(8,128)S(1)}, u32[]{:S(2)}, u32[]{:S(2)}) collective-permute-start(f32[1024,256]{1,0:T(8,128)S(1)} %get-tuple-element.78.refs_0_), channel_id=1, source_target_pairs={{0,1},{1,0},{2,3},{3,2},{4,5},{5,4},{6,7},{7,6},{8,9},{9,8},{10,11... | collective-permute-start | bytes 3145736 | tf_op jit(solution)/shard_map/ppermute | solution.py:18
  55.7 15.2 %collective-permute-start.17 = (f32[1024,128]{1,0:T(8,128)S(1)}, f32[1024,128]{1,0:T(8,128)S(1)}, u32[]{:S(2)}, u32[]{:S(2)}) collective-permute-start(f32[1024,128]{1,0:T(8,128)S(1)} %get-tuple-element.77), channel_id=1, source_target_pairs={{0,2},{1,3},{2,0},{3,1},{4,6},{5,7},{6,4},{7,5},{8,10},{9,11},{10,... | collective-permute-start | bytes 1572872 | tf_op jit(solution)/shard_map/ppermute | solution.py:18
  58.1 23.8 %collective-permute-start.22 = (f32[1024,128]{1,0:T(8,128)S(1)}, f32[1024,128]{1,0:T(8,128)S(1)}, u32[]{:S(2)}, u32[]{:S(2)}) collective-permute-start(f32[1024,128]{1,0:T(8,128)S(1)} %get-tuple-element.87), channel_id=1, source_target_pairs={{0,2},{1,3},{2,0},{3,1},{4,6},{5,7},{6,4},{7,5},{8,10},{9,11},{10,... | collective-permute-start | bytes 1572872 | tf_op jit(solution)/shard_map/ppermute | solution.py:18
  59.4 11.4 %collective-permute-start.19 = (f32[2,64,256]{2,1,0:T(8,128)S(1)}, f32[2,64,256]{2,1,0:T(8,128)S(1)}, u32[]{:S(2)}, u32[]{:S(2)}) collective-permute-start(f32[2,64,256]{2,1,0:T(8,128)S(1)} %get-tuple-element.80), channel_id=1, source_target_pairs={{0,16},{4,20},{8,24},{12,28},{16,0},{20,4},{24,8},{28,12},{32,48},... | collective-permute-start | bytes 393224 | tf_op jit(solution)/shard_map/ppermute | solution.py:18
  60.2 10.7 %collective-permute-start.20 = (f32[2,64,256]{2,1,0:T(8,128)S(1)}, f32[2,64,256]{2,1,0:T(8,128)S(1)}, u32[]{:S(2)}, u32[]{:S(2)}) collective-permute-start(f32[2,64,256]{2,1,0:T(8,128)S(1)} %get-tuple-element.81), channel_id=1, source_target_pairs={{0,32},{4,36},{8,40},{12,44},{16,48},{20,52},{24,56},{28,60},{32,0... | collective-permute-start | bytes 393224 | tf_op jit(solution)/shard_map/ppermute | solution.py:18
  62.6 8.7 %collective-permute-start.21 = (f32[2,64,256]{2,1,0:T(8,128)S(1)}, f32[2,64,256]{2,1,0:T(8,128)S(1)}, u32[]{:S(2)}, u32[]{:S(2)}) collective-permute-start(f32[2,64,256]{2,1,0:T(8,128)S(1)} %get-tuple-element.82), channel_id=1, source_target_pairs={{0,48},{4,52},{8,56},{12,60},{16,32},{20,36},{24,40},{28,44},{32,1... | collective-permute-start | bytes 393224 | tf_op jit(solution)/shard_map/ppermute | solution.py:18
  72.0 10.0 %collective-permute-start.23 = (f32[2,32,256]{2,1,0:T(8,128)S(1)}, f32[2,32,256]{2,1,0:T(8,128)S(1)}, u32[]{:S(2)}, u32[]{:S(2)}) collective-permute-start(f32[2,32,256]{2,1,0:T(8,128)S(1)} %get-tuple-element.90), channel_id=1, source_target_pairs={{0,16},{4,20},{8,24},{12,28},{16,0},{20,4},{24,8},{28,12},{32,48},... | collective-permute-start | bytes 196616 | tf_op jit(solution)/shard_map/ppermute | solution.py:18
  72.1 9.9 %collective-permute-start.24 = (f32[2,32,256]{2,1,0:T(8,128)S(1)}, f32[2,32,256]{2,1,0:T(8,128)S(1)}, u32[]{:S(2)}, u32[]{:S(2)}) collective-permute-start(f32[2,32,256]{2,1,0:T(8,128)S(1)} %get-tuple-element.91), channel_id=1, source_target_pairs={{0,32},{4,36},{8,40},{12,44},{16,48},{20,52},{24,56},{28,60},{32,0... | collective-permute-start | bytes 196616 | tf_op jit(solution)/shard_map/ppermute | solution.py:18
  75.1 6.8 %collective-permute-start.25 = (f32[2,32,256]{2,1,0:T(8,128)S(1)}, f32[2,32,256]{2,1,0:T(8,128)S(1)}, u32[]{:S(2)}, u32[]{:S(2)}) collective-permute-start(f32[2,32,256]{2,1,0:T(8,128)S(1)} %get-tuple-element.92), channel_id=1, source_target_pairs={{0,48},{4,52},{8,56},{12,60},{16,32},{20,36},{24,40},{28,44},{32,1... | collective-permute-start | bytes 196616 | tf_op jit(solution)/shard_map/ppermute | solution.py:18
  82.6 4.8 %collective-permute-start.26 = (f32[2,32,256]{2,1,0:T(8,128)S(1)}, f32[2,32,256]{2,1,0:T(8,128)S(1)}, u32[]{:S(2)}, u32[]{:S(2)}) collective-permute-start(f32[2,32,256]{2,1,0:T(8,128)S(1)} %get-tuple-element.99), channel_id=1, source_target_pairs={{0,16},{4,20},{8,24},{12,28},{16,0},{20,4},{24,8},{28,12},{32,48},... | collective-permute-start | bytes 196616 | tf_op jit(solution)/shard_map/ppermute | solution.py:18
  82.8 6.4 %collective-permute-start.27 = (f32[2,32,256]{2,1,0:T(8,128)S(1)}, f32[2,32,256]{2,1,0:T(8,128)S(1)}, u32[]{:S(2)}, u32[]{:S(2)}) collective-permute-start(f32[2,32,256]{2,1,0:T(8,128)S(1)} %get-tuple-element.100), channel_id=1, source_target_pairs={{0,32},{4,36},{8,40},{12,44},{16,48},{20,52},{24,56},{28,60},{32,0... | collective-permute-start | bytes 196616 | tf_op jit(solution)/shard_map/ppermute | solution.py:18
  85.6 5.5 %collective-permute-start.28 = (f32[2,32,256]{2,1,0:T(8,128)S(1)}, f32[2,32,256]{2,1,0:T(8,128)S(1)}, u32[]{:S(2)}, u32[]{:S(2)}) collective-permute-start(f32[2,32,256]{2,1,0:T(8,128)S(1)} %get-tuple-element.101), channel_id=1, source_target_pairs={{0,48},{4,52},{8,56},{12,60},{16,32},{20,36},{24,40},{28,44},{32,1... | collective-permute-start | bytes 196616 | tf_op jit(solution)/shard_map/ppermute | solution.py:18
  91.1 1.3 %collective-permute-start.29 = (f32[64,256]{1,0:T(8,128)S(1)}, f32[64,256]{1,0:T(8,128)S(1)}, u32[]{:S(2)}, u32[]{:S(2)}) collective-permute-start(f32[64,256]{1,0:T(8,128)S(1)} %get-tuple-element.103), channel_id=1, source_target_pairs={{0,1},{1,0},{2,3},{3,2},{4,5},{5,4},{6,7},{7,6},{8,9},{9,8},{10,11... | collective-permute-start | bytes 196616 | tf_op jit(solution)/shard_map/ppermute | solution.py:18
  92.5 4.8 %collective-permute-start.30 = (f32[64,256]{1,0:T(8,128)S(1)}, f32[64,256]{1,0:T(8,128)S(1)}, u32[]{:S(2)}, u32[]{:S(2)}) collective-permute-start(f32[64,256]{1,0:T(8,128)S(1)} %get-tuple-element.105), channel_id=1, source_target_pairs={{0,64},{4,68},{8,72},{12,76},{16,80},{20,84},{24,88},{28,92},{32,9... | collective-permute-start | bytes 196616 | tf_op jit(solution)/shard_map/ppermute | solution.py:18
  93.7 6.4 %collective-permute-start.31 = (f32[64,256]{1,0:T(8,128)S(1)}, f32[64,256]{1,0:T(8,128)S(1)}, u32[]{:S(2)}, u32[]{:S(2)}) collective-permute-start(f32[64,256]{1,0:T(8,128)S(1)} %get-tuple-element.106), channel_id=1, source_target_pairs={{0,128},{4,132},{8,136},{12,140},{16,144},{20,148},{24,152},{28,15... | collective-permute-start | bytes 196616 | tf_op jit(solution)/shard_map/ppermute | solution.py:18
  96.5 5.5 %collective-permute-start.32 = (f32[64,256]{1,0:T(8,128)S(1)}, f32[64,256]{1,0:T(8,128)S(1)}, u32[]{:S(2)}, u32[]{:S(2)}) collective-permute-start(f32[64,256]{1,0:T(8,128)S(1)} %get-tuple-element.107), channel_id=1, source_target_pairs={{0,192},{4,196},{8,200},{12,204},{16,208},{20,212},{24,216},{28,22... | collective-permute-start | bytes 196616 | tf_op jit(solution)/shard_map/ppermute | solution.py:18
  102.0 6.4 %collective-permute-start.33 = (f32[32,256]{1,0:T(8,128)S(1)}, f32[32,256]{1,0:T(8,128)S(1)}, u32[]{:S(2)}, u32[]{:S(2)}) collective-permute-start(f32[32,256]{1,0:T(8,128)S(1)} %get-tuple-element.109), channel_id=1, source_target_pairs={{0,12},{4,8},{8,4},{12,0},{16,28},{20,24},{24,20},{28,16},{32,44},... | collective-permute-start | bytes 98312 | tf_op jit(solution)/shard_map/ppermute | solution.py:18
  108.5 4.8 %collective-permute-start.34 = (f32[16,256]{1,0:T(8,128)S(1)}, f32[16,256]{1,0:T(8,128)S(1)}, u32[]{:S(2)}, u32[]{:S(2)}) collective-permute-start(f32[16,256]{1,0:T(8,128)S(1)} %get-tuple-element.111), channel_id=1, source_target_pairs={{0,4},{4,0},{8,12},{12,8},{16,20},{20,16},{24,28},{28,24},{32,36},... | collective-permute-start | bytes 49160 | tf_op jit(solution)/shard_map/ppermute | solution.py:18

commit v9 on v8

--- a/solution.py
+++ b/solution.py
@@ -144,14 +144,12 @@
     return project(columns, probes, 0, outs, emit)
 
 
-LATE = (0, 3, 4, 5)
-
-
-def prepare(near, rows, one, one_more, two):
-    def body(n_ref, u_ref, o_ref, m_ref, t_ref, out, high, low):
-        early = jnp.concatenate([u_ref[1], u_ref[2]], axis=1)
-        nodes = jnp.concatenate([o_ref[...] + m_ref[...], t_ref[...]], axis=0)
-        out[...] = n_ref[...] + dot3(split(early), split(nodes), MATMUL)
+LATE = (0, 1, 3, 4, 5)
+
+
+def prepare(near, rows, two):
+    def body(n_ref, u_ref, t_ref, out, high, low):
+        out[...] = n_ref[...] + dot3(split(u_ref[2]), split(t_ref[...]), MATMUL)
         high[...], low[...] = split(jnp.concatenate([u_ref[t] for t in LATE], axis=1))
 
     levels, points, rank = rows.shape
@@ -168,12 +166,10 @@
         [
             tiled(wide),
             pl.BlockSpec((levels, tile, rank), lambda i: (0, i, 0)),
-            whole(one.shape),
-            whole(one_more.shape),
             whole(two.shape),
         ],
-        [near, rows, one, one_more, two],
-        flops=12 * rank * points * wide,
+        [near, rows, two],
+        flops=6 * rank * points * wide,
         grid=(points // tile,),
         out_specs=[tiled(wide), tiled(len(LATE) * rank), tiled(len(LATE) * rank)],
     )
@@ -197,17 +193,20 @@
     return even, odd
 
 
-def expand(base, rows_high, rows_low, zero, part, part1, part2, part3):
-    def body(b_ref, h_ref, l_ref, z_ref, q0, q1, q2, q3, out, held, even, odd, total):
+def expand(base, rows_high, rows_low, zero, one, one_more, part, part1, part2, part3):
+    def body(
+        b_ref, h_ref, l_ref, z_ref, o_ref, m_ref, q0, q1, q2, q3, out, held, even, odd, total
+    ):
         _, x, _ = place()
         total[0:128] = z_ref[...]
+        total[128:256] = o_ref[...] + m_ref[...]
         for k, ref in ((0, q0), (1, q1)):
-            total[pl.ds(pl.multiple_of(128 + ((x ^ k) & 1) * 64, 64), 64)] = ref[:64]
+            total[pl.ds(pl.multiple_of(256 + ((x ^ k) & 1) * 64, 64), 64)] = ref[:64]
         for k, ref in ((0, q0), (1, q1), (2, q2), (3, q3)):
             base = 64 if k < 2 else 0
             row = pl.multiple_of((x ^ k) * 32, 32)
-            total[pl.ds(256 + row, 32)] = ref[base:base + 32]
-            total[pl.ds(384 + row, 32)] = ref[base + 32:base + 64]
+            total[pl.ds(384 + row, 32)] = ref[base:base + 32]
+            total[pl.ds(512 + row, 32)] = ref[base + 32:base + 64]
         left = h_ref[...], l_ref[...]
         value = b_ref[...] + dot3(left, split(total[...]), MATMUL)
         out[...] = value
@@ -216,7 +215,7 @@
 
     points, wide = base.shape
     depth = rows_high.shape[1]
-    given = [base, rows_high, rows_low, zero, part, part1, part2, part3]
+    given = [base, rows_high, rows_low, zero, one, one_more, part, part1, part2, part3]
     return call(
         body,
         shapes(base.shape, base.shape, (points, wide // 2), (points, wide // 2)),
@@ -359,12 +358,13 @@
     node1 = swap(low1, "leaf", 3)
     part, near = lax.optimization_barrier((part, near))
     part = part + swap(part, "leaf", 3)
+    node1, low0 = lax.optimization_barrier((node1, low0))
     node1_more = swap(node1, "leaf", 1)
-    part, low0 = lax.optimization_barrier((part, low0))
+    node0 = swap(low0, "leaf", 1)
+    late = prepare(near, row_factor_stack, node2)
+    part, *late = lax.optimization_barrier((part, *late))
     gathered = [swap(part, "leaf", 4), swap(part[64:], "leaf", 8), swap(part[64:], "leaf", 12)]
-    node0 = swap(low0, "leaf", 1)
-    late = prepare(near, row_factor_stack, node1, node1_more, node2)
-    result, applied, even, odd = expand(*late, node0, part, *gathered)
+    result, applied, even, odd = expand(*late, node0, node1, node1_more, part, *gathered)
 
     even = swap(even, "probe", 2)
     odd = swap(odd, "probe", 2)

time: 115 us -> 114 us (level); the launches traced: 114 us -> 114 us
  starting transfers between devices: 57.8 us -> 59.7 us
  waiting for transfers between devices: 39.1 us -> 37.2 us
    ppermute x35, waiting for transfers between devices: 39.1 us -> 37.2 us  [swap(): return lax.ppermute(value, axis, pairs)]
    ppermute x35, starting transfers between devices: 57.8 us -> 59.7 us  [swap(): return lax.ppermute(value, axis, pairs)]
  transfers between devices with their start and end apart: 35 -> 35, of which waited for: 18 -> 16; matrix products, arithmetic and copies ran while one was open for 3% -> 2% of each run, Pallas kernels for 6% -> 6%
where the time goes in v9:
time: 114 us
  starting transfers between devices  59.7 us (52%)
  waiting for transfers between devices  37.2 us (33%)
  Pallas kernels  13.1 us (11%)
  matrix products  2.39 us (2%)
    ppermute x35, starting transfers between devices, swap(): return lax.ppermute(value, axis, pairs)  59.7 us
    ppermute x35, waiting for transfers between devices, swap(): return lax.ppermute(value, axis, pairs)  37.2 us
    pallas_call x11, Pallas kernels, call(): pl.pallas_call(body, out_shape=outs, grid=grid, in_specs=specs, out_specs...  13.1 us
    dot_general x1, matrix products, near_product(): return jnp.dot(masked, probes, precision=HIGH, preferred_element_type=F32)  2.39 us
  transfers between devices with their start and end apart: 35, of which 16 were waited for; matrix products, arithmetic and copies ran while one was open for 2% of the time, Pallas kernels for 6%

profile of v9, /device:TPU:32, one launch (start us, length us, event | category | flops | bytes accessed | tf_op | source)
XLA Modules:
  0.0 114.3 jit_solution(3300258529511625753)
XLA Ops:
  0.6 3.1 %shard_map.68 = (f32[64,256]{1,0:T(8,128)S(1)}, f32[64,256]{1,0:T(8,128)S(1)}, f32[128,256]{1,0:T(8,128)S(1)}, f32[128,256]{1,0:T(8,128)S(1)}) custom-call(f32[6,1024,128]{2,1,0:T(8,128)} %c_hbm.3, f32[1024,256]{1,0:T(8,128)} %p_hbm.3), custom_call_target="tpu_custom_call" | custom-call | flops 603979776 | bytes 4587520 | tf_op jit(solution)/shard_map/pallas_call | solution.py:49
  3.8 3.1 %collective-permute-start = (f32[128,256]{1,0:T(8,128)S(1)}, f32[128,256]{1,0:T(8,128)S(1)}, u32[]{:S(2)}, u32[]{:S(2)}) collective-permute-start(f32[128,256]{1,0:T(8,128)S(1)} %get-tuple-element.61), channel_id=1, source_target_pairs={{0,32},{4,36},{8,40},{12,44},{16,48},{20,52},{24,56},{28,60},{32,0... | collective-permute-start | bytes 393224 | tf_op jit(solution)/shard_map/ppermute | solution.py:18
  6.9 1.1 collective-permute-start.1
  8.0 3.3 %shard_map.69 = (f32[128,256]{1,0:T(8,128)S(1)}, f32[128,256]{1,0:T(8,128)S(1)}, f32[128,256]{1,0:T(8,128)S(1)}) custom-call(f32[6,1024,128]{2,1,0:T(8,128)} %c_hbm.3, f32[1024,256]{1,0:T(8,128)} %p_hbm.3), custom_call_target="tpu_custom_call" | custom-call | flops 603979776 | bytes 4587520 | tf_op jit(solution)/shard_map/pallas_call | solution.py:49
  11.3 3.4 %collective-permute-start.8 = (f32[128,256]{1,0:T(8,128)S(1)}, f32[128,256]{1,0:T(8,128)S(1)}, u32[]{:S(2)}, u32[]{:S(2)}) collective-permute-start(f32[128,256]{1,0:T(8,128)S(1)} %get-tuple-element.72), channel_id=1, source_target_pairs={{0,4},{4,0},{8,12},{12,8},{16,20},{20,16},{24,28},{28,24},{32,36},... | collective-permute-start | bytes 393224 | tf_op jit(solution)/shard_map/ppermute | solution.py:18
  14.8 3.1 %collective-permute-start.5 = (f32[32,256]{1,0:T(8,128)S(1)}, f32[32,256]{1,0:T(8,128)S(1)}, u32[]{:S(2)}, u32[]{:S(2)}) collective-permute-start(f32[32,256]{1,0:T(8,128)S(1)} %get-tuple-element.123), channel_id=1, source_target_pairs={{0,192},{4,196},{8,200},{12,204},{16,208},{20,212},{24,216},{28,22... | collective-permute-start | bytes 98312 | tf_op jit(solution)/shard_map/ppermute | solution.py:18
  17.8 0.6 collective-permute-start.4
  18.5 0.5 collective-permute-start.3
  19.3 6.1 %collective-permute-start.9 = (f32[128,256]{1,0:T(8,128)S(1)}, f32[128,256]{1,0:T(8,128)S(1)}, u32[]{:S(2)}, u32[]{:S(2)}) collective-permute-start(f32[128,256]{1,0:T(8,128)S(1)} %add.37), channel_id=1, source_target_pairs={{0,12},{4,8},{8,4},{12,0},{16,28},{20,24},{24,20},{28,16},{32,44},... | collective-permute-start | bytes 393224 | tf_op jit(solution)/shard_map/ppermute | solution.py:18
  25.9 2.4 %fusion.n_ref = f32[1024,256]{1,0:T(8,128)S(1)} fusion(f32[1024,256]{1,0:T(8,128)S(1)} %copy-done.1, f32[1024,1024]{1,0:T(8,128)S(1)} %copy-done.2, f32[128,8,8,128]{3,2,1,0:T(8,128)S(1)} %bitcast.8), kind=kOutput, calls=%fused_computation.1 | convolution fusion | flops 1611661312 | bytes 10485760 | tf_op jit(solution)/shard_map/dot_general | solution.py:337
  28.3 3.5 %collective-permute-start.11 = (f32[128,256]{1,0:T(8,128)S(1)}, f32[128,256]{1,0:T(8,128)S(1)}, u32[]{:S(2)}, u32[]{:S(2)}) collective-permute-start(f32[128,256]{1,0:T(8,128)S(1)} %get-tuple-element.79), channel_id=1, source_target_pairs={{0,12},{4,8},{8,4},{12,0},{16,28},{20,24},{24,20},{28,16},{32,44},... | collective-permute-start | bytes 393224 | tf_op jit(solution)/shard_map/ppermute | solution.py:18
  31.8 1.6 %collective-permute-start.10 = (f32[128,256]{1,0:T(8,128)S(1)}, f32[128,256]{1,0:T(8,128)S(1)}, u32[]{:S(2)}, u32[]{:S(2)}) collective-permute-start(f32[128,256]{1,0:T(8,128)S(1)} %add.38), channel_id=1, source_target_pairs={{0,16},{4,20},{8,24},{12,28},{16,0},{20,4},{24,8},{28,12},{32,48},... | collective-permute-start | bytes 393224 | tf_op jit(solution)/shard_map/ppermute | solution.py:18
  33.4 1.4 %collective-permute-done.6 = f32[128,256]{1,0:T(8,128)S(1)} collective-permute-done((f32[128,256]{1,0:T(8,128)S(1)}, f32[128,256]{1,0:T(8,128)S(1)}, u32[]{:S(2)}, u32[]{:S(2)}) %collective-permute-start.6) | collective-permute-done | bytes 131104 | tf_op jit(solution)/shard_map/ppermute | solution.py:18
  34.9 2.6 %collective-permute-start.7 = (f32[128,256]{1,0:T(8,128)S(1)}, f32[128,256]{1,0:T(8,128)S(1)}, u32[]{:S(2)}, u32[]{:S(2)}) collective-permute-start(f32[128,256]{1,0:T(8,128)S(1)} %add.35), channel_id=1, source_target_pairs={{0,12},{4,8},{8,4},{12,0},{16,28},{20,24},{24,20},{28,16},{32,44},... | collective-permute-start | bytes 393224 | tf_op jit(solution)/shard_map/ppermute | solution.py:18
  37.5 2.7 %collective-permute-done.11.o_ref = f32[128,256]{1,0:T(8,128)S(1)} collective-permute-done((f32[128,256]{1,0:T(8,128)S(1)}, f32[128,256]{1,0:T(8,128)S(1)}, u32[]{:S(2)}, u32[]{:S(2)}) %collective-permute-start.11) | collective-permute-done | bytes 131104 | tf_op jit(solution)/shard_map/ppermute | solution.py:18
  40.3 2.9 %collective-permute-start.13 = (f32[128,256]{1,0:T(8,128)S(1)}, f32[128,256]{1,0:T(8,128)S(1)}, u32[]{:S(2)}, u32[]{:S(2)}) collective-permute-start(f32[128,256]{1,0:T(8,128)S(1)} %collective-permute-done.11.o_ref), channel_id=1, source_target_pairs={{0,4},{4,0},{8,12},{12,8},{16,20},{20,16},{24,28},{28,24},{32,36},... | collective-permute-start | bytes 393224 | tf_op jit(solution)/shard_map/ppermute | solution.py:18
  43.2 1.7 %shard_map.70 = (f32[1024,256]{1,0:T(8,128)S(1)}, bf16[1024,640]{1,0:T(8,128)(2,1)S(1)}, bf16[1024,640]{1,0:T(8,128)(2,1)S(1)}) custom-call(f32[1024,256]{1,0:T(8,128)S(1)} %fusion.n_ref, f32[6,1024,128]{2,1,0:T(8,128)S(1)} %copy-done, f32[128,256]{1,0:T(8,128)S(1)} %collective-permute-done.10.t_ref), custom_call_target="tpu_custom_call" | custom-call | flops 201326592 | bytes 10616832 | tf_op jit(solution)/shard_map/pallas_call | solution.py:49
  45.0 3.1 %collective-permute-start.14 = (f32[128,256]{1,0:T(8,128)S(1)}, f32[128,256]{1,0:T(8,128)S(1)}, u32[]{:S(2)}, u32[]{:S(2)}) collective-permute-start(f32[128,256]{1,0:T(8,128)S(1)} %add.36.q0), channel_id=1, source_target_pairs={{0,16},{4,20},{8,24},{12,28},{16,0},{20,4},{24,8},{28,12},{32,48},... | collective-permute-start | bytes 393224 | tf_op jit(solution)/shard_map/ppermute | solution.py:18
  48.1 2.1 %collective-permute-start.15 = (f32[64,256]{1,0:T(8,128)S(1)}, f32[64,256]{1,0:T(8,128)S(1)}, u32[]{:S(2)}, u32[]{:S(2)}) collective-permute-start(f32[64,256]{1,0:T(8,128)S(1)} %slice.28), channel_id=1, source_target_pairs={{0,32},{4,36},{8,40},{12,44},{16,48},{20,52},{24,56},{28,60},{32,0... | collective-permute-start | bytes 196616 | tf_op jit(solution)/shard_map/ppermute | solution.py:18
  50.2 4.0 %collective-permute-done.16.q3 = f32[64,256]{1,0:T(8,128)S(1)} collective-permute-done((f32[64,256]{1,0:T(8,128)S(1)}, f32[64,256]{1,0:T(8,128)S(1)}, u32[]{:S(2)}, u32[]{:S(2)}) %collective-permute-start.16) | collective-permute-done | bytes 65568 | tf_op jit(solution)/shard_map/ppermute | solution.py:18
  54.2 2.4 %shard_map.71 = (f32[1024,256]{1,0:T(8,128)}, f32[1024,256]{1,0:T(8,128)S(1)}, f32[1024,128]{1,0:T(8,128)S(1)}, f32[1024,128]{1,0:T(8,128)S(1)}) custom-call(f32[1024,256]{1,0:T(8,128)S(1)} %get-tuple-element.76.b_ref, bf16[1024,640]{1,0:T(8,128)(2,1)S(1)} %get-tuple-element.77.h_ref, bf16[1024,640]{1,0:T(8,128)(2,1)S(1)} %get-tuple-element.78.l_ref, ...), custom_call_target="tpu_custom_call" | custom-call | flops 1006632960 | bytes 10223616 | tf_op jit(solution)/shard_map/pallas_call | solution.py:49
  56.8 1.8 %collective-permute-start.22 = (f32[1024,128]{1,0:T(8,128)S(1)}, f32[1024,128]{1,0:T(8,128)S(1)}, u32[]{:S(2)}, u32[]{:S(2)}) collective-permute-start(f32[1024,128]{1,0:T(8,128)S(1)} %get-tuple-element.95), channel_id=1, source_target_pairs={{0,2},{1,3},{2,0},{3,1},{4,6},{5,7},{6,4},{7,5},{8,10},{9,11},{10,... | collective-permute-start | bytes 1572872 | tf_op jit(solution)/shard_map/ppermute | solution.py:18
  58.6 0.6 collective-permute-done.18.refs_1_
  59.3 1.1 shard_map.72
  60.3 0.8 collective-permute-start.19
  61.1 3.6 %collective-permute-start.20 = (f32[2,64,256]{2,1,0:T(8,128)S(1)}, f32[2,64,256]{2,1,0:T(8,128)S(1)}, u32[]{:S(2)}, u32[]{:S(2)}) collective-permute-start(f32[2,64,256]{2,1,0:T(8,128)S(1)} %get-tuple-element.89), channel_id=1, source_target_pairs={{0,32},{4,36},{8,40},{12,44},{16,48},{20,52},{24,56},{28,60},{32,0... | collective-permute-start | bytes 393224 | tf_op jit(solution)/shard_map/ppermute | solution.py:18
  65.1 6.2 %collective-permute-done.17.refs_2_ = f32[1024,128]{1,0:T(8,128)S(1)} collective-permute-done((f32[1024,128]{1,0:T(8,128)S(1)}, f32[1024,128]{1,0:T(8,128)S(1)}, u32[]{:S(2)}, u32[]{:S(2)}) %collective-permute-start.17) | collective-permute-done | bytes 524320 | tf_op jit(solution)/shard_map/ppermute | solution.py:18
  71.3 2.1 %collective-permute-done.21.refs_3_ = f32[2,64,256]{2,1,0:T(8,128)S(1)} collective-permute-done((f32[2,64,256]{2,1,0:T(8,128)S(1)}, f32[2,64,256]{2,1,0:T(8,128)S(1)}, u32[]{:S(2)}, u32[]{:S(2)}) %collective-permute-start.21) | collective-permute-done | bytes 131104 | tf_op jit(solution)/shard_map/ppermute | solution.py:18
  73.4 0.7 shard_map.73
  74.2 2.2 %collective-permute-start.24 = (f32[2,32,256]{2,1,0:T(8,128)S(1)}, f32[2,32,256]{2,1,0:T(8,128)S(1)}, u32[]{:S(2)}, u32[]{:S(2)}) collective-permute-start(f32[2,32,256]{2,1,0:T(8,128)S(1)} %get-tuple-element.99), channel_id=1, source_target_pairs={{0,32},{4,36},{8,40},{12,44},{16,48},{20,52},{24,56},{28,60},{32,0... | collective-permute-start | bytes 196616 | tf_op jit(solution)/shard_map/ppermute | solution.py:18
  76.4 2.5 %collective-permute-start.25 = (f32[2,32,256]{2,1,0:T(8,128)S(1)}, f32[2,32,256]{2,1,0:T(8,128)S(1)}, u32[]{:S(2)}, u32[]{:S(2)}) collective-permute-start(f32[2,32,256]{2,1,0:T(8,128)S(1)} %get-tuple-element.100), channel_id=1, source_target_pairs={{0,48},{4,52},{8,56},{12,60},{16,32},{20,36},{24,40},{28,44},{32,1... | collective-permute-start | bytes 196616 | tf_op jit(solution)/shard_map/ppermute | solution.py:18
  78.9 3.3 %collective-permute-done.22.refs_2_ = f32[1024,128]{1,0:T(8,128)S(1)} collective-permute-done((f32[1024,128]{1,0:T(8,128)S(1)}, f32[1024,128]{1,0:T(8,128)S(1)}, u32[]{:S(2)}, u32[]{:S(2)}) %collective-permute-start.22) | collective-permute-done | bytes 524320 | tf_op jit(solution)/shard_map/ppermute | solution.py:18
  82.2 0.7 shard_map.74
  82.9 0.8 collective-permute-start.26
  83.7 3.6 %collective-permute-start.27 = (f32[2,32,256]{2,1,0:T(8,128)S(1)}, f32[2,32,256]{2,1,0:T(8,128)S(1)}, u32[]{:S(2)}, u32[]{:S(2)}) collective-permute-start(f32[2,32,256]{2,1,0:T(8,128)S(1)} %get-tuple-element.108), channel_id=1, source_target_pairs={{0,32},{4,36},{8,40},{12,44},{16,48},{20,52},{24,56},{28,60},{32,0... | collective-permute-start | bytes 196616 | tf_op jit(solution)/shard_map/ppermute | solution.py:18
  87.3 0.4 collective-permute-start.28
  87.7 2.7 %collective-permute-done.27.refs_10_ = f32[2,32,256]{2,1,0:T(8,128)S(1)} collective-permute-done((f32[2,32,256]{2,1,0:T(8,128)S(1)}, f32[2,32,256]{2,1,0:T(8,128)S(1)}, u32[]{:S(2)}, u32[]{:S(2)}) %collective-permute-start.27) | collective-permute-done | bytes 65568 | tf_op jit(solution)/shard_map/ppermute | solution.py:18
  90.4 2.4 %collective-permute-done.28.refs_11_ = f32[2,32,256]{2,1,0:T(8,128)S(1)} collective-permute-done((f32[2,32,256]{2,1,0:T(8,128)S(1)}, f32[2,32,256]{2,1,0:T(8,128)S(1)}, u32[]{:S(2)}, u32[]{:S(2)}) %collective-permute-start.28) | collective-permute-done | bytes 65568 | tf_op jit(solution)/shard_map/ppermute | solution.py:18
  92.9 1.2 %collective-permute-done.29.got_ref = f32[64,256]{1,0:T(8,128)S(1)} collective-permute-done((f32[64,256]{1,0:T(8,128)S(1)}, f32[64,256]{1,0:T(8,128)S(1)}, u32[]{:S(2)}, u32[]{:S(2)}) %collective-permute-start.29) | collective-permute-done | bytes 65568 | tf_op jit(solution)/shard_map/ppermute | solution.py:18
  94.5 2.6 %collective-permute-start.31 = (f32[64,256]{1,0:T(8,128)S(1)}, f32[64,256]{1,0:T(8,128)S(1)}, u32[]{:S(2)}, u32[]{:S(2)}) collective-permute-start(f32[64,256]{1,0:T(8,128)S(1)} %get-tuple-element.114), channel_id=1, source_target_pairs={{0,128},{4,132},{8,136},{12,140},{16,144},{20,148},{24,152},{28,15... | collective-permute-start | bytes 196616 | tf_op jit(solution)/shard_map/ppermute | solution.py:18
  97.0 2.0 %collective-permute-start.32 = (f32[64,256]{1,0:T(8,128)S(1)}, f32[64,256]{1,0:T(8,128)S(1)}, u32[]{:S(2)}, u32[]{:S(2)}) collective-permute-start(f32[64,256]{1,0:T(8,128)S(1)} %get-tuple-element.115), channel_id=1, source_target_pairs={{0,192},{4,196},{8,200},{12,204},{16,208},{20,212},{24,216},{28,22... | collective-permute-start | bytes 196616 | tf_op jit(solution)/shard_map/ppermute | solution.py:18
  99.2 1.5 %collective-permute-done.31.refs_2_ = f32[64,256]{1,0:T(8,128)S(1)} collective-permute-done((f32[64,256]{1,0:T(8,128)S(1)}, f32[64,256]{1,0:T(8,128)S(1)}, u32[]{:S(2)}, u32[]{:S(2)}) %collective-permute-start.31) | collective-permute-done | bytes 65568 | tf_op jit(solution)/shard_map/ppermute | solution.py:18
  100.7 1.8 %collective-permute-done.32.refs_3_ = f32[64,256]{1,0:T(8,128)S(1)} collective-permute-done((f32[64,256]{1,0:T(8,128)S(1)}, f32[64,256]{1,0:T(8,128)S(1)}, u32[]{:S(2)}, u32[]{:S(2)}) %collective-permute-start.32) | collective-permute-done | bytes 65568 | tf_op jit(solution)/shard_map/ppermute | solution.py:18
  102.5 2.9 %collective-permute-start.33 = (f32[32,256]{1,0:T(8,128)S(1)}, f32[32,256]{1,0:T(8,128)S(1)}, u32[]{:S(2)}, u32[]{:S(2)}) collective-permute-start(f32[32,256]{1,0:T(8,128)S(1)} %get-tuple-element.117), channel_id=1, source_target_pairs={{0,12},{4,8},{8,4},{12,0},{16,28},{20,24},{24,20},{28,16},{32,44},... | collective-permute-start | bytes 98312 | tf_op jit(solution)/shard_map/ppermute | solution.py:18
  105.4 3.5 %collective-permute-done.33.refs_1_ = f32[32,256]{1,0:T(8,128)S(1)} collective-permute-done((f32[32,256]{1,0:T(8,128)S(1)}, f32[32,256]{1,0:T(8,128)S(1)}, u32[]{:S(2)}, u32[]{:S(2)}) %collective-permute-start.33) | collective-permute-done | bytes 32800 | tf_op jit(solution)/shard_map/ppermute | solution.py:18
  109.0 1.6 %collective-permute-start.34 = (f32[16,256]{1,0:T(8,128)S(1)}, f32[16,256]{1,0:T(8,128)S(1)}, u32[]{:S(2)}, u32[]{:S(2)}) collective-permute-start(f32[16,256]{1,0:T(8,128)S(1)} %get-tuple-element.119), channel_id=1, source_target_pairs={{0,4},{4,0},{8,12},{12,8},{16,20},{20,16},{24,28},{28,24},{32,36},... | collective-permute-start | bytes 49160 | tf_op jit(solution)/shard_map/ppermute | solution.py:18
  110.6 3.1 %collective-permute-done.34 = f32[16,256]{1,0:T(8,128)S(1)} collective-permute-done((f32[16,256]{1,0:T(8,128)S(1)}, f32[16,256]{1,0:T(8,128)S(1)}, u32[]{:S(2)}, u32[]{:S(2)}) %collective-permute-start.34) | collective-permute-done | bytes 16416 | tf_op jit(solution)/shard_map/ppermute | solution.py:18
  113.7 0.6 add_multiply_fusion
  (54 shorter events, 2.3 us)
Async XLA Ops:
  0.6 18.3 %copy-start.3 = (s32[1,8,8]{2,1,0:T(8,128)S(1)}, s32[1,8,8]{2,1,0:T(8,128)}, u32[]{:S(2)}) copy-start(s32[1,8,8]{2,1,0:T(8,128)} %param.6) | copy-start | bytes 772
  3.8 10.9 %collective-permute-start = (f32[128,256]{1,0:T(8,128)S(1)}, f32[128,256]{1,0:T(8,128)S(1)}, u32[]{:S(2)}, u32[]{:S(2)}) collective-permute-start(f32[128,256]{1,0:T(8,128)S(1)} %get-tuple-element.61), channel_id=1, source_target_pairs={{0,32},{4,36},{8,40},{12,44},{16,48},{20,52},{24,56},{28,60},{32,0... | collective-permute-start | bytes 393224 | tf_op jit(solution)/shard_map/ppermute | solution.py:18
  6.9 7.8 %collective-permute-start.1 = (f32[128,256]{1,0:T(8,128)S(1)}, f32[128,256]{1,0:T(8,128)S(1)}, u32[]{:S(2)}, u32[]{:S(2)}) collective-permute-start(f32[128,256]{1,0:T(8,128)S(1)} %get-tuple-element.62), channel_id=1, source_target_pairs={{0,48},{4,52},{8,56},{12,60},{16,32},{20,36},{24,40},{28,44},{32,1... | collective-permute-start | bytes 393224 | tf_op jit(solution)/shard_map/ppermute | solution.py:18
  8.0 17.8 %copy-start.1 = (f32[1024,256]{1,0:T(8,128)S(1)}, f32[1024,256]{1,0:T(8,128)}, u32[]{:S(2)}) copy-start(f32[1024,256]{1,0:T(8,128)} %p_hbm.3) | copy-start | bytes 3145732
  8.0 17.8 %copy-start.2 = (f32[1024,1024]{1,0:T(8,128)S(1)}, f32[1024,1024]{1,0:T(8,128)}, u32[]{:S(2)}) copy-start(f32[1024,1024]{1,0:T(8,128)} %param.5) | copy-start | bytes 12582916
  8.0 6.7 %collective-permute-start.2 = (f32[64,256]{1,0:T(8,128)S(1)}, f32[64,256]{1,0:T(8,128)S(1)}, u32[]{:S(2)}, u32[]{:S(2)}) collective-permute-start(f32[64,256]{1,0:T(8,128)S(1)} %get-tuple-element.64), channel_id=1, source_target_pairs={{0,16},{4,20},{8,24},{12,28},{16,0},{20,4},{24,8},{28,12},{32,48},... | collective-permute-start | bytes 196616 | tf_op jit(solution)/shard_map/ppermute | solution.py:18
  11.3 7.9 %collective-permute-start.8 = (f32[128,256]{1,0:T(8,128)S(1)}, f32[128,256]{1,0:T(8,128)S(1)}, u32[]{:S(2)}, u32[]{:S(2)}) collective-permute-start(f32[128,256]{1,0:T(8,128)S(1)} %get-tuple-element.72), channel_id=1, source_target_pairs={{0,4},{4,0},{8,12},{12,8},{16,20},{20,16},{24,28},{28,24},{32,36},... | collective-permute-start | bytes 393224 | tf_op jit(solution)/shard_map/ppermute | solution.py:18
  14.8 10.6 %collective-permute-start.5 = (f32[32,256]{1,0:T(8,128)S(1)}, f32[32,256]{1,0:T(8,128)S(1)}, u32[]{:S(2)}, u32[]{:S(2)}) collective-permute-start(f32[32,256]{1,0:T(8,128)S(1)} %get-tuple-element.123), channel_id=1, source_target_pairs={{0,192},{4,196},{8,200},{12,204},{16,208},{20,212},{24,216},{28,22... | collective-permute-start | bytes 98312 | tf_op jit(solution)/shard_map/ppermute | solution.py:18
  17.8 7.5 %collective-permute-start.4 = (f32[32,256]{1,0:T(8,128)S(1)}, f32[32,256]{1,0:T(8,128)S(1)}, u32[]{:S(2)}, u32[]{:S(2)}) collective-permute-start(f32[32,256]{1,0:T(8,128)S(1)} %get-tuple-element.123), channel_id=1, source_target_pairs={{0,128},{4,132},{8,136},{12,140},{16,144},{20,148},{24,152},{28,15... | collective-permute-start | bytes 98312 | tf_op jit(solution)/shard_map/ppermute | solution.py:18
  18.5 6.9 %collective-permute-start.3 = (f32[32,256]{1,0:T(8,128)S(1)}, f32[32,256]{1,0:T(8,128)S(1)}, u32[]{:S(2)}, u32[]{:S(2)}) collective-permute-start(f32[32,256]{1,0:T(8,128)S(1)} %get-tuple-element.122), channel_id=1, source_target_pairs={{0,64},{4,68},{8,72},{12,76},{16,80},{20,84},{24,88},{28,92},{32,9... | collective-permute-start | bytes 98312 | tf_op jit(solution)/shard_map/ppermute | solution.py:18
  19.3 12.6 %collective-permute-start.9 = (f32[128,256]{1,0:T(8,128)S(1)}, f32[128,256]{1,0:T(8,128)S(1)}, u32[]{:S(2)}, u32[]{:S(2)}) collective-permute-start(f32[128,256]{1,0:T(8,128)S(1)} %add.37), channel_id=1, source_target_pairs={{0,12},{4,8},{8,4},{12,0},{16,28},{20,24},{24,20},{28,16},{32,44},... | collective-permute-start | bytes 393224 | tf_op jit(solution)/shard_map/ppermute | solution.py:18
  25.4 9.5 %collective-permute-start.6 = (f32[128,256]{1,0:T(8,128)S(1)}, f32[128,256]{1,0:T(8,128)S(1)}, u32[]{:S(2)}, u32[]{:S(2)}) collective-permute-start(f32[128,256]{1,0:T(8,128)S(1)} %pad_maximum_fusion), channel_id=1, source_target_pairs={{0,4},{4,0},{8,12},{12,8},{16,20},{20,16},{24,28},{28,24},{32,36},... | collective-permute-start | bytes 393224 | tf_op jit(solution)/shard_map/ppermute | solution.py:18
  25.9 17.3 %copy-start = (f32[6,1024,128]{2,1,0:T(8,128)S(1)}, f32[6,1024,128]{2,1,0:T(8,128)}, u32[]{:S(2)}) copy-start(f32[6,1024,128]{2,1,0:T(8,128)} %u_ref.1) | copy-start | bytes 9437188
  28.3 12.0 %collective-permute-start.11 = (f32[128,256]{1,0:T(8,128)S(1)}, f32[128,256]{1,0:T(8,128)S(1)}, u32[]{:S(2)}, u32[]{:S(2)}) collective-permute-start(f32[128,256]{1,0:T(8,128)S(1)} %get-tuple-element.79), channel_id=1, source_target_pairs={{0,12},{4,8},{8,4},{12,0},{16,28},{20,24},{24,20},{28,16},{32,44},... | collective-permute-start | bytes 393224 | tf_op jit(solution)/shard_map/ppermute | solution.py:18
  31.8 11.3 %collective-permute-start.10 = (f32[128,256]{1,0:T(8,128)S(1)}, f32[128,256]{1,0:T(8,128)S(1)}, u32[]{:S(2)}, u32[]{:S(2)}) collective-permute-start(f32[128,256]{1,0:T(8,128)S(1)} %add.38), channel_id=1, source_target_pairs={{0,16},{4,20},{8,24},{12,28},{16,0},{20,4},{24,8},{28,12},{32,48},... | collective-permute-start | bytes 393224 | tf_op jit(solution)/shard_map/ppermute | solution.py:18
  34.9 10.0 %collective-permute-start.7 = (f32[128,256]{1,0:T(8,128)S(1)}, f32[128,256]{1,0:T(8,128)S(1)}, u32[]{:S(2)}, u32[]{:S(2)}) collective-permute-start(f32[128,256]{1,0:T(8,128)S(1)} %add.35), channel_id=1, source_target_pairs={{0,12},{4,8},{8,4},{12,0},{16,28},{20,24},{24,20},{28,16},{32,44},... | collective-permute-start | bytes 393224 | tf_op jit(solution)/shard_map/ppermute | solution.py:18
  40.3 9.9 %collective-permute-start.12 = (f32[128,256]{1,0:T(8,128)S(1)}, f32[128,256]{1,0:T(8,128)S(1)}, u32[]{:S(2)}, u32[]{:S(2)}) collective-permute-start(f32[128,256]{1,0:T(8,128)S(1)} %get-tuple-element.81), channel_id=1, source_target_pairs={{0,4},{4,0},{8,12},{12,8},{16,20},{20,16},{24,28},{28,24},{32,36},... | collective-permute-start | bytes 393224 | tf_op jit(solution)/shard_map/ppermute | solution.py:18
  40.3 9.9 %collective-permute-start.13 = (f32[128,256]{1,0:T(8,128)S(1)}, f32[128,256]{1,0:T(8,128)S(1)}, u32[]{:S(2)}, u32[]{:S(2)}) collective-permute-start(f32[128,256]{1,0:T(8,128)S(1)} %collective-permute-done.11.o_ref), channel_id=1, source_target_pairs={{0,4},{4,0},{8,12},{12,8},{16,20},{20,16},{24,28},{28,24},{32,36},... | collective-permute-start | bytes 393224 | tf_op jit(solution)/shard_map/ppermute | solution.py:18
  45.0 9.2 %collective-permute-start.14 = (f32[128,256]{1,0:T(8,128)S(1)}, f32[128,256]{1,0:T(8,128)S(1)}, u32[]{:S(2)}, u32[]{:S(2)}) collective-permute-start(f32[128,256]{1,0:T(8,128)S(1)} %add.36.q0), channel_id=1, source_target_pairs={{0,16},{4,20},{8,24},{12,28},{16,0},{20,4},{24,8},{28,12},{32,48},... | collective-permute-start | bytes 393224 | tf_op jit(solution)/shard_map/ppermute | solution.py:18
  48.0 6.2 %collective-permute-start.16 = (f32[64,256]{1,0:T(8,128)S(1)}, f32[64,256]{1,0:T(8,128)S(1)}, u32[]{:S(2)}, u32[]{:S(2)}) collective-permute-start(f32[64,256]{1,0:T(8,128)S(1)} %slice.28), channel_id=1, source_target_pairs={{0,48},{4,52},{8,56},{12,60},{16,32},{20,36},{24,40},{28,44},{32,1... | collective-permute-start | bytes 196616 | tf_op jit(solution)/shard_map/ppermute | solution.py:18
  48.1 6.1 %collective-permute-start.15 = (f32[64,256]{1,0:T(8,128)S(1)}, f32[64,256]{1,0:T(8,128)S(1)}, u32[]{:S(2)}, u32[]{:S(2)}) collective-permute-start(f32[64,256]{1,0:T(8,128)S(1)} %slice.28), channel_id=1, source_target_pairs={{0,32},{4,36},{8,40},{12,44},{16,48},{20,52},{24,56},{28,60},{32,0... | collective-permute-start | bytes 196616 | tf_op jit(solution)/shard_map/ppermute | solution.py:18
  56.6 2.7 %collective-permute-start.18 = (f32[1024,256]{1,0:T(8,128)S(1)}, f32[1024,256]{1,0:T(8,128)S(1)}, u32[]{:S(2)}, u32[]{:S(2)}) collective-permute-start(f32[1024,256]{1,0:T(8,128)S(1)} %get-tuple-element.86.refs_0_), channel_id=1, source_target_pairs={{0,1},{1,0},{2,3},{3,2},{4,5},{5,4},{6,7},{7,6},{8,9},{9,8},{10,11... | collective-permute-start | bytes 3145736 | tf_op jit(solution)/shard_map/ppermute | solution.py:18
  56.6 14.7 %collective-permute-start.17 = (f32[1024,128]{1,0:T(8,128)S(1)}, f32[1024,128]{1,0:T(8,128)S(1)}, u32[]{:S(2)}, u32[]{:S(2)}) collective-permute-start(f32[1024,128]{1,0:T(8,128)S(1)} %get-tuple-element.85), channel_id=1, source_target_pairs={{0,2},{1,3},{2,0},{3,1},{4,6},{5,7},{6,4},{7,5},{8,10},{9,11},{10,... | collective-permute-start | bytes 1572872 | tf_op jit(solution)/shard_map/ppermute | solution.py:18
  56.8 25.4 %collective-permute-start.22 = (f32[1024,128]{1,0:T(8,128)S(1)}, f32[1024,128]{1,0:T(8,128)S(1)}, u32[]{:S(2)}, u32[]{:S(2)}) collective-permute-start(f32[1024,128]{1,0:T(8,128)S(1)} %get-tuple-element.95), channel_id=1, source_target_pairs={{0,2},{1,3},{2,0},{3,1},{4,6},{5,7},{6,4},{7,5},{8,10},{9,11},{10,... | collective-permute-start | bytes 1572872 | tf_op jit(solution)/shard_map/ppermute | solution.py:18
  60.3 11.0 %collective-permute-start.19 = (f32[2,64,256]{2,1,0:T(8,128)S(1)}, f32[2,64,256]{2,1,0:T(8,128)S(1)}, u32[]{:S(2)}, u32[]{:S(2)}) collective-permute-start(f32[2,64,256]{2,1,0:T(8,128)S(1)} %get-tuple-element.88), channel_id=1, source_target_pairs={{0,16},{4,20},{8,24},{12,28},{16,0},{20,4},{24,8},{28,12},{32,48},... | collective-permute-start | bytes 393224 | tf_op jit(solution)/shard_map/ppermute | solution.py:18
  61.1 10.2 %collective-permute-start.20 = (f32[2,64,256]{2,1,0:T(8,128)S(1)}, f32[2,64,256]{2,1,0:T(8,128)S(1)}, u32[]{:S(2)}, u32[]{:S(2)}) collective-permute-start(f32[2,64,256]{2,1,0:T(8,128)S(1)} %get-tuple-element.89), channel_id=1, source_target_pairs={{0,32},{4,36},{8,40},{12,44},{16,48},{20,52},{24,56},{28,60},{32,0... | collective-permute-start | bytes 393224 | tf_op jit(solution)/shard_map/ppermute | solution.py:18
  64.7 8.7 %collective-permute-start.21 = (f32[2,64,256]{2,1,0:T(8,128)S(1)}, f32[2,64,256]{2,1,0:T(8,128)S(1)}, u32[]{:S(2)}, u32[]{:S(2)}) collective-permute-start(f32[2,64,256]{2,1,0:T(8,128)S(1)} %get-tuple-element.90), channel_id=1, source_target_pairs={{0,48},{4,52},{8,56},{12,60},{16,32},{20,36},{24,40},{28,44},{32,1... | collective-permute-start | bytes 393224 | tf_op jit(solution)/shard_map/ppermute | solution.py:18
  74.1 8.1 %collective-permute-start.23 = (f32[2,32,256]{2,1,0:T(8,128)S(1)}, f32[2,32,256]{2,1,0:T(8,128)S(1)}, u32[]{:S(2)}, u32[]{:S(2)}) collective-permute-start(f32[2,32,256]{2,1,0:T(8,128)S(1)} %get-tuple-element.98), channel_id=1, source_target_pairs={{0,16},{4,20},{8,24},{12,28},{16,0},{20,4},{24,8},{28,12},{32,48},... | collective-permute-start | bytes 196616 | tf_op jit(solution)/shard_map/ppermute | solution.py:18
  74.2 8.0 %collective-permute-start.24 = (f32[2,32,256]{2,1,0:T(8,128)S(1)}, f32[2,32,256]{2,1,0:T(8,128)S(1)}, u32[]{:S(2)}, u32[]{:S(2)}) collective-permute-start(f32[2,32,256]{2,1,0:T(8,128)S(1)} %get-tuple-element.99), channel_id=1, source_target_pairs={{0,32},{4,36},{8,40},{12,44},{16,48},{20,52},{24,56},{28,60},{32,0... | collective-permute-start | bytes 196616 | tf_op jit(solution)/shard_map/ppermute | solution.py:18
  76.4 5.8 %collective-permute-start.25 = (f32[2,32,256]{2,1,0:T(8,128)S(1)}, f32[2,32,256]{2,1,0:T(8,128)S(1)}, u32[]{:S(2)}, u32[]{:S(2)}) collective-permute-start(f32[2,32,256]{2,1,0:T(8,128)S(1)} %get-tuple-element.100), channel_id=1, source_target_pairs={{0,48},{4,52},{8,56},{12,60},{16,32},{20,36},{24,40},{28,44},{32,1... | collective-permute-start | bytes 196616 | tf_op jit(solution)/shard_map/ppermute | solution.py:18
  82.9 4.8 %collective-permute-start.26 = (f32[2,32,256]{2,1,0:T(8,128)S(1)}, f32[2,32,256]{2,1,0:T(8,128)S(1)}, u32[]{:S(2)}, u32[]{:S(2)}) collective-permute-start(f32[2,32,256]{2,1,0:T(8,128)S(1)} %get-tuple-element.107), channel_id=1, source_target_pairs={{0,16},{4,20},{8,24},{12,28},{16,0},{20,4},{24,8},{28,12},{32,48},... | collective-permute-start | bytes 196616 | tf_op jit(solution)/shard_map/ppermute | solution.py:18
  83.7 6.7 %collective-permute-start.27 = (f32[2,32,256]{2,1,0:T(8,128)S(1)}, f32[2,32,256]{2,1,0:T(8,128)S(1)}, u32[]{:S(2)}, u32[]{:S(2)}) collective-permute-start(f32[2,32,256]{2,1,0:T(8,128)S(1)} %get-tuple-element.108), channel_id=1, source_target_pairs={{0,32},{4,36},{8,40},{12,44},{16,48},{20,52},{24,56},{28,60},{32,0... | collective-permute-start | bytes 196616 | tf_op jit(solution)/shard_map/ppermute | solution.py:18
  87.3 5.5 %collective-permute-start.28 = (f32[2,32,256]{2,1,0:T(8,128)S(1)}, f32[2,32,256]{2,1,0:T(8,128)S(1)}, u32[]{:S(2)}, u32[]{:S(2)}) collective-permute-start(f32[2,32,256]{2,1,0:T(8,128)S(1)} %get-tuple-element.109), channel_id=1, source_target_pairs={{0,48},{4,52},{8,56},{12,60},{16,32},{20,36},{24,40},{28,44},{32,1... | collective-permute-start | bytes 196616 | tf_op jit(solution)/shard_map/ppermute | solution.py:18
  92.8 1.3 %collective-permute-start.29 = (f32[64,256]{1,0:T(8,128)S(1)}, f32[64,256]{1,0:T(8,128)S(1)}, u32[]{:S(2)}, u32[]{:S(2)}) collective-permute-start(f32[64,256]{1,0:T(8,128)S(1)} %get-tuple-element.111), channel_id=1, source_target_pairs={{0,1},{1,0},{2,3},{3,2},{4,5},{5,4},{6,7},{7,6},{8,9},{9,8},{10,11... | collective-permute-start | bytes 196616 | tf_op jit(solution)/shard_map/ppermute | solution.py:18
  94.2 5.0 %collective-permute-start.30 = (f32[64,256]{1,0:T(8,128)S(1)}, f32[64,256]{1,0:T(8,128)S(1)}, u32[]{:S(2)}, u32[]{:S(2)}) collective-permute-start(f32[64,256]{1,0:T(8,128)S(1)} %get-tuple-element.113), channel_id=1, source_target_pairs={{0,64},{4,68},{8,72},{12,76},{16,80},{20,84},{24,88},{28,92},{32,9... | collective-permute-start | bytes 196616 | tf_op jit(solution)/shard_map/ppermute | solution.py:18
  94.5 6.2 %collective-permute-start.31 = (f32[64,256]{1,0:T(8,128)S(1)}, f32[64,256]{1,0:T(8,128)S(1)}, u32[]{:S(2)}, u32[]{:S(2)}) collective-permute-start(f32[64,256]{1,0:T(8,128)S(1)} %get-tuple-element.114), channel_id=1, source_target_pairs={{0,128},{4,132},{8,136},{12,140},{16,144},{20,148},{24,152},{28,15... | collective-permute-start | bytes 196616 | tf_op jit(solution)/shard_map/ppermute | solution.py:18
  97.0 5.5 %collective-permute-start.32 = (f32[64,256]{1,0:T(8,128)S(1)}, f32[64,256]{1,0:T(8,128)S(1)}, u32[]{:S(2)}, u32[]{:S(2)}) collective-permute-start(f32[64,256]{1,0:T(8,128)S(1)} %get-tuple-element.115), channel_id=1, source_target_pairs={{0,192},{4,196},{8,200},{12,204},{16,208},{20,212},{24,216},{28,22... | collective-permute-start | bytes 196616 | tf_op jit(solution)/shard_map/ppermute | solution.py:18
  102.5 6.5 %collective-permute-start.33 = (f32[32,256]{1,0:T(8,128)S(1)}, f32[32,256]{1,0:T(8,128)S(1)}, u32[]{:S(2)}, u32[]{:S(2)}) collective-permute-start(f32[32,256]{1,0:T(8,128)S(1)} %get-tuple-element.117), channel_id=1, source_target_pairs={{0,12},{4,8},{8,4},{12,0},{16,28},{20,24},{24,20},{28,16},{32,44},... | collective-permute-start | bytes 98312 | tf_op jit(solution)/shard_map/ppermute | solution.py:18
  109.0 4.7 %collective-permute-start.34 = (f32[16,256]{1,0:T(8,128)S(1)}, f32[16,256]{1,0:T(8,128)S(1)}, u32[]{:S(2)}, u32[]{:S(2)}) collective-permute-start(f32[16,256]{1,0:T(8,128)S(1)} %get-tuple-element.119), channel_id=1, source_target_pairs={{0,4},{4,0},{8,12},{12,8},{16,20},{20,16},{24,28},{28,24},{32,36},... | collective-permute-start | bytes 49160 | tf_op jit(solution)/shard_map/ppermute | solution.py:18

commit v10 on v9

--- a/solution.py
+++ b/solution.py
@@ -195,7 +195,7 @@
 
 def expand(base, rows_high, rows_low, zero, one, one_more, part, part1, part2, part3):
     def body(
-        b_ref, h_ref, l_ref, z_ref, o_ref, m_ref, q0, q1, q2, q3, out, held, even, odd, total
+        b_ref, h_ref, l_ref, z_ref, o_ref, m_ref, q0, q1, q3, q2, out, held, even, odd, total
     ):
         _, x, _ = place()
         total[0:128] = z_ref[...]
@@ -215,7 +215,7 @@
 
     points, wide = base.shape
     depth = rows_high.shape[1]
-    given = [base, rows_high, rows_low, zero, one, one_more, part, part1, part2, part3]
+    given = [base, rows_high, rows_low, zero, one, one_more, part, part1, part3, part2]
     return call(
         body,
         shapes(base.shape, base.shape, (points, wide // 2), (points, wide // 2)),
@@ -322,7 +322,7 @@
 
 
 def around(parts, scale):
-    return [parts[0]] + [swap(parts[k], "leaf", k * scale) for k in (1, 2, 3)]
+    return [parts[0]] + [swap(parts[k], "leaf", k * scale) for k in (2, 1, 3)]
 
 
 def near_product(leaf_blocks, block_mask, probes):
@@ -340,7 +340,7 @@
 def local(leaf_blocks, block_mask, row_factor_stack, column_factor_stack, probes):
     leaf_points = leaf_blocks.shape[1]
     keep, *sent = project_high(column_factor_stack, probes)
-    _, one, two, three = around([keep, *sent], 4)
+    _, two, one, three = around([keep, *sent], 4)
     low0, low1, low2 = project_low(column_factor_stack, probes)
     low2 = low2 + swap(low2, "leaf", 1)
     part3 = two[:64] + three[:64]
@@ -350,25 +350,26 @@
     part5 = swap(five, "leaf", 32) + swap(five, "leaf", 48)
     part = jnp.concatenate([part3, part4, part5])
     low2 = low2 + swap(low2, "leaf", 3)
-    node2 = swap(low2, "leaf", 4)
     part, blocks, low1 = lax.optimization_barrier((part, leaf_blocks, low1))
     near = near_product(blocks, block_mask, probes)
     part = part + swap(part, "leaf", 1)
     near, low1 = lax.optimization_barrier((near, low1))
     node1 = swap(low1, "leaf", 3)
-    part, near = lax.optimization_barrier((part, near))
+    part, near, low2 = lax.optimization_barrier((part, near, low2))
     part = part + swap(part, "leaf", 3)
+    node2 = swap(low2, "leaf", 4)
     node1, low0 = lax.optimization_barrier((node1, low0))
     node1_more = swap(node1, "leaf", 1)
     node0 = swap(low0, "leaf", 1)
+    part, near, node2 = lax.optimization_barrier((part, near, node2))
     late = prepare(near, row_factor_stack, node2)
-    part, *late = lax.optimization_barrier((part, *late))
-    gathered = [swap(part, "leaf", 4), swap(part[64:], "leaf", 8), swap(part[64:], "leaf", 12)]
+    last = swap(part[64:], "leaf", 8)
+    gathered = [swap(part, "leaf", 4), last, swap(part[64:], "leaf", 12)]
     result, applied, even, odd = expand(*late, node0, node1, node1_more, part, *gathered)
 
+    beside = swap(applied, "probe", 1)
     even = swap(even, "probe", 2)
     odd = swap(odd, "probe", 2)
-    beside = swap(applied, "probe", 1)
     first = around(gram(applied, applied, beside), 4)
     even, *first = lax.optimization_barrier((even, *first))
     second = around(gram(even, applied, beside), 4)

time: 114 us -> 113 us (level)
  starting transfers between devices: 59.7 us -> 56.8 us
  waiting for transfers between devices: 37.2 us -> 39 us
    ppermute x35, starting transfers between devices: 59.7 us -> 56.8 us  [swap(): return lax.ppermute(value, axis, pairs)]
    ppermute x35, waiting for transfers between devices: 37.2 us -> 39 us  [swap(): return lax.ppermute(value, axis, pairs)]
  transfers between devices with their start and end apart: 35 -> 35, of which waited for: 16 -> 16; matrix products, arithmetic and copies ran while one was open for 2% -> 3% of each run, Pallas kernels for 6% -> 6%
where the time goes in v10:
time: 113 us
  starting transfers between devices  56.8 us (50%)
  waiting for transfers between devices  39 us (35%)
  Pallas kernels  13.1 us (12%)
  matrix products  2.39 us (2%)
    ppermute x35, starting transfers between devices, swap(): return lax.ppermute(value, axis, pairs)  56.8 us
    ppermute x35, waiting for transfers between devices, swap(): return lax.ppermute(value, axis, pairs)  39 us
    pallas_call x11, Pallas kernels, call(): pl.pallas_call(body, out_shape=outs, grid=grid, in_specs=specs, out_specs...  13.1 us
    dot_general x1, matrix products, near_product(): return jnp.dot(masked, probes, precision=HIGH, preferred_element_type=F32)  2.39 us
  transfers between devices with their start and end apart: 35, of which 16 were waited for; matrix products, arithmetic and copies ran while one was open for 3% of the time, Pallas kernels for 6%

profile of v10, /device:TPU:32, one launch (start us, length us, event | category | flops | bytes accessed | tf_op | source)
XLA Modules:
  0.0 113.2 jit_solution(8987746684674834638)
XLA Ops:
  0.6 3.1 %shard_map.68 = (f32[64,256]{1,0:T(8,128)S(1)}, f32[64,256]{1,0:T(8,128)S(1)}, f32[128,256]{1,0:T(8,128)S(1)}, f32[128,256]{1,0:T(8,128)S(1)}) custom-call(f32[6,1024,128]{2,1,0:T(8,128)} %c_hbm.3, f32[1024,256]{1,0:T(8,128)} %p_hbm.3), custom_call_target="tpu_custom_call" | custom-call | flops 603979776 | bytes 4587520 | tf_op jit(solution)/shard_map/pallas_call | solution.py:49
  3.8 3.1 %collective-permute-start = (f32[128,256]{1,0:T(8,128)S(1)}, f32[128,256]{1,0:T(8,128)S(1)}, u32[]{:S(2)}, u32[]{:S(2)}) collective-permute-start(f32[128,256]{1,0:T(8,128)S(1)} %get-tuple-element.61), channel_id=1, source_target_pairs={{0,32},{4,36},{8,40},{12,44},{16,48},{20,52},{24,56},{28,60},{32,0... | collective-permute-start | bytes 393224 | tf_op jit(solution)/shard_map/ppermute | solution.py:18
  6.9 1.1 %collective-permute-start.1 = (f32[128,256]{1,0:T(8,128)S(1)}, f32[128,256]{1,0:T(8,128)S(1)}, u32[]{:S(2)}, u32[]{:S(2)}) collective-permute-start(f32[128,256]{1,0:T(8,128)S(1)} %get-tuple-element.62), channel_id=1, source_target_pairs={{0,48},{4,52},{8,56},{12,60},{16,32},{20,36},{24,40},{28,44},{32,1... | collective-permute-start | bytes 393224 | tf_op jit(solution)/shard_map/ppermute | solution.py:18
  8.0 3.3 %shard_map.69 = (f32[128,256]{1,0:T(8,128)S(1)}, f32[128,256]{1,0:T(8,128)S(1)}, f32[128,256]{1,0:T(8,128)S(1)}) custom-call(f32[6,1024,128]{2,1,0:T(8,128)} %c_hbm.3, f32[1024,256]{1,0:T(8,128)} %p_hbm.3), custom_call_target="tpu_custom_call" | custom-call | flops 603979776 | bytes 4587520 | tf_op jit(solution)/shard_map/pallas_call | solution.py:49
  11.3 3.4 %collective-permute-start.7 = (f32[128,256]{1,0:T(8,128)S(1)}, f32[128,256]{1,0:T(8,128)S(1)}, u32[]{:S(2)}, u32[]{:S(2)}) collective-permute-start(f32[128,256]{1,0:T(8,128)S(1)} %get-tuple-element.70), channel_id=1, source_target_pairs={{0,4},{4,0},{8,12},{12,8},{16,20},{20,16},{24,28},{28,24},{32,36},... | collective-permute-start | bytes 393224 | tf_op jit(solution)/shard_map/ppermute | solution.py:18
  14.8 3.1 %collective-permute-start.5 = (f32[32,256]{1,0:T(8,128)S(1)}, f32[32,256]{1,0:T(8,128)S(1)}, u32[]{:S(2)}, u32[]{:S(2)}) collective-permute-start(f32[32,256]{1,0:T(8,128)S(1)} %get-tuple-element.123), channel_id=1, source_target_pairs={{0,192},{4,196},{8,200},{12,204},{16,208},{20,212},{24,216},{28,22... | collective-permute-start | bytes 98312 | tf_op jit(solution)/shard_map/ppermute | solution.py:18
  19.3 6.1 %collective-permute-start.8 = (f32[128,256]{1,0:T(8,128)S(1)}, f32[128,256]{1,0:T(8,128)S(1)}, u32[]{:S(2)}, u32[]{:S(2)}) collective-permute-start(f32[128,256]{1,0:T(8,128)S(1)} %add.36), channel_id=1, source_target_pairs={{0,12},{4,8},{8,4},{12,0},{16,28},{20,24},{24,20},{28,16},{32,44},... | collective-permute-start | bytes 393224 | tf_op jit(solution)/shard_map/ppermute | solution.py:18
  25.9 2.4 %fusion.n_ref = f32[1024,256]{1,0:T(8,128)S(1)} fusion(f32[1024,256]{1,0:T(8,128)S(1)} %copy-done.1, f32[1024,1024]{1,0:T(8,128)S(1)} %copy-done.2, f32[128,8,8,128]{3,2,1,0:T(8,128)S(1)} %bitcast.8), kind=kOutput, calls=%fused_computation.1 | convolution fusion | flops 1611661312 | bytes 10485760 | tf_op jit(solution)/shard_map/dot_general | solution.py:337
  28.3 3.5 %collective-permute-start.11 = (f32[128,256]{1,0:T(8,128)S(1)}, f32[128,256]{1,0:T(8,128)S(1)}, u32[]{:S(2)}, u32[]{:S(2)}) collective-permute-start(f32[128,256]{1,0:T(8,128)S(1)} %get-tuple-element.79), channel_id=1, source_target_pairs={{0,12},{4,8},{8,4},{12,0},{16,28},{20,24},{24,20},{28,16},{32,44},... | collective-permute-start | bytes 393224 | tf_op jit(solution)/shard_map/ppermute | solution.py:18
  31.8 3.0 %collective-permute-done.6 = f32[128,256]{1,0:T(8,128)S(1)} collective-permute-done((f32[128,256]{1,0:T(8,128)S(1)}, f32[128,256]{1,0:T(8,128)S(1)}, u32[]{:S(2)}, u32[]{:S(2)}) %collective-permute-start.6) | collective-permute-done | bytes 131104 | tf_op jit(solution)/shard_map/ppermute | solution.py:18
  34.9 1.2 %collective-permute-start.9 = (f32[128,256]{1,0:T(8,128)S(1)}, f32[128,256]{1,0:T(8,128)S(1)}, u32[]{:S(2)}, u32[]{:S(2)}) collective-permute-start(f32[128,256]{1,0:T(8,128)S(1)} %add.35), channel_id=1, source_target_pairs={{0,12},{4,8},{8,4},{12,0},{16,28},{20,24},{24,20},{28,16},{32,44},... | collective-permute-start | bytes 393224 | tf_op jit(solution)/shard_map/ppermute | solution.py:18
  36.1 1.6 %collective-permute-start.10 = (f32[128,256]{1,0:T(8,128)S(1)}, f32[128,256]{1,0:T(8,128)S(1)}, u32[]{:S(2)}, u32[]{:S(2)}) collective-permute-start(f32[128,256]{1,0:T(8,128)S(1)} %add.37), channel_id=1, source_target_pairs={{0,16},{4,20},{8,24},{12,28},{16,0},{20,4},{24,8},{28,12},{32,48},... | collective-permute-start | bytes 393224 | tf_op jit(solution)/shard_map/ppermute | solution.py:18
  37.7 4.0 %collective-permute-done.11.o_ref = f32[128,256]{1,0:T(8,128)S(1)} collective-permute-done((f32[128,256]{1,0:T(8,128)S(1)}, f32[128,256]{1,0:T(8,128)S(1)}, u32[]{:S(2)}, u32[]{:S(2)}) %collective-permute-start.11) | collective-permute-done | bytes 131104 | tf_op jit(solution)/shard_map/ppermute | solution.py:18
  41.7 2.9 %collective-permute-start.13 = (f32[128,256]{1,0:T(8,128)S(1)}, f32[128,256]{1,0:T(8,128)S(1)}, u32[]{:S(2)}, u32[]{:S(2)}) collective-permute-start(f32[128,256]{1,0:T(8,128)S(1)} %collective-permute-done.11.o_ref), channel_id=1, source_target_pairs={{0,4},{4,0},{8,12},{12,8},{16,20},{20,16},{24,28},{28,24},{32,36},... | collective-permute-start | bytes 393224 | tf_op jit(solution)/shard_map/ppermute | solution.py:18
  44.6 1.7 %collective-permute-start.14 = (f32[128,256]{1,0:T(8,128)S(1)}, f32[128,256]{1,0:T(8,128)S(1)}, u32[]{:S(2)}, u32[]{:S(2)}) collective-permute-start(f32[128,256]{1,0:T(8,128)S(1)} %add.38.q0), channel_id=1, source_target_pairs={{0,16},{4,20},{8,24},{12,28},{16,0},{20,4},{24,8},{28,12},{32,48},... | collective-permute-start | bytes 393224 | tf_op jit(solution)/shard_map/ppermute | solution.py:18
  46.3 2.3 %collective-permute-start.16 = (f32[64,256]{1,0:T(8,128)S(1)}, f32[64,256]{1,0:T(8,128)S(1)}, u32[]{:S(2)}, u32[]{:S(2)}) collective-permute-start(f32[64,256]{1,0:T(8,128)S(1)} %slice.28), channel_id=1, source_target_pairs={{0,32},{4,36},{8,40},{12,44},{16,48},{20,52},{24,56},{28,60},{32,0... | collective-permute-start | bytes 196616 | tf_op jit(solution)/shard_map/ppermute | solution.py:18
  48.6 0.8 collective-permute-start.15
  49.4 1.7 %shard_map.70 = (f32[1024,256]{1,0:T(8,128)S(1)}, bf16[1024,640]{1,0:T(8,128)(2,1)S(1)}, bf16[1024,640]{1,0:T(8,128)(2,1)S(1)}) custom-call(f32[1024,256]{1,0:T(8,128)S(1)} %fusion.n_ref, f32[6,1024,128]{2,1,0:T(8,128)S(1)} %copy-done, f32[128,256]{1,0:T(8,128)S(1)} %collective-permute-done.10.t_ref), custom_call_target="tpu_custom_call" | custom-call | flops 201326592 | bytes 10616832 | tf_op jit(solution)/shard_map/pallas_call | solution.py:49
  51.2 1.2 %collective-permute-done.16.q2 = f32[64,256]{1,0:T(8,128)S(1)} collective-permute-done((f32[64,256]{1,0:T(8,128)S(1)}, f32[64,256]{1,0:T(8,128)S(1)}, u32[]{:S(2)}, u32[]{:S(2)}) %collective-permute-start.16) | collective-permute-done | bytes 65568 | tf_op jit(solution)/shard_map/ppermute | solution.py:18
  52.4 1.7 %collective-permute-done.15.q3 = f32[64,256]{1,0:T(8,128)S(1)} collective-permute-done((f32[64,256]{1,0:T(8,128)S(1)}, f32[64,256]{1,0:T(8,128)S(1)}, u32[]{:S(2)}, u32[]{:S(2)}) %collective-permute-start.15) | collective-permute-done | bytes 65568 | tf_op jit(solution)/shard_map/ppermute | solution.py:18
  54.0 2.4 %shard_map.71 = (f32[1024,256]{1,0:T(8,128)}, f32[1024,256]{1,0:T(8,128)S(1)}, f32[1024,128]{1,0:T(8,128)S(1)}, f32[1024,128]{1,0:T(8,128)S(1)}) custom-call(f32[1024,256]{1,0:T(8,128)S(1)} %get-tuple-element.76.b_ref, bf16[1024,640]{1,0:T(8,128)(2,1)S(1)} %get-tuple-element.77.h_ref, bf16[1024,640]{1,0:T(8,128)(2,1)S(1)} %get-tuple-element.78.l_ref, ...), custom_call_target="tpu_custom_call" | custom-call | flops 1006632960 | bytes 10223616 | tf_op jit(solution)/shard_map/pallas_call | solution.py:49
  56.5 2.0 %collective-permute-start.22 = (f32[1024,128]{1,0:T(8,128)S(1)}, f32[1024,128]{1,0:T(8,128)S(1)}, u32[]{:S(2)}, u32[]{:S(2)}) collective-permute-start(f32[1024,128]{1,0:T(8,128)S(1)} %get-tuple-element.95), channel_id=1, source_target_pairs={{0,2},{1,3},{2,0},{3,1},{4,6},{5,7},{6,4},{7,5},{8,10},{9,11},{10,... | collective-permute-start | bytes 1572872 | tf_op jit(solution)/shard_map/ppermute | solution.py:18
  59.1 1.1 shard_map.72
  60.2 0.8 collective-permute-start.19
  61.0 1.0 collective-permute-start.20
  62.0 2.4 %collective-permute-start.21 = (f32[2,64,256]{2,1,0:T(8,128)S(1)}, f32[2,64,256]{2,1,0:T(8,128)S(1)}, u32[]{:S(2)}, u32[]{:S(2)}) collective-permute-start(f32[2,64,256]{2,1,0:T(8,128)S(1)} %get-tuple-element.90), channel_id=1, source_target_pairs={{0,48},{4,52},{8,56},{12,60},{16,32},{20,36},{24,40},{28,44},{32,1... | collective-permute-start | bytes 393224 | tf_op jit(solution)/shard_map/ppermute | solution.py:18
  64.4 6.8 %collective-permute-done.17.refs_2_ = f32[1024,128]{1,0:T(8,128)S(1)} collective-permute-done((f32[1024,128]{1,0:T(8,128)S(1)}, f32[1024,128]{1,0:T(8,128)S(1)}, u32[]{:S(2)}, u32[]{:S(2)}) %collective-permute-start.17) | collective-permute-done | bytes 524320 | tf_op jit(solution)/shard_map/ppermute | solution.py:18
  71.2 0.7 shard_map.73
  71.9 0.8 collective-permute-start.23
  72.7 1.0 collective-permute-start.24
  73.7 2.4 %collective-permute-start.25 = (f32[2,32,256]{2,1,0:T(8,128)S(1)}, f32[2,32,256]{2,1,0:T(8,128)S(1)}, u32[]{:S(2)}, u32[]{:S(2)}) collective-permute-start(f32[2,32,256]{2,1,0:T(8,128)S(1)} %get-tuple-element.100), channel_id=1, source_target_pairs={{0,48},{4,52},{8,56},{12,60},{16,32},{20,36},{24,40},{28,44},{32,1... | collective-permute-start | bytes 196616 | tf_op jit(solution)/shard_map/ppermute | solution.py:18
  76.1 5.9 %collective-permute-done.22.refs_2_ = f32[1024,128]{1,0:T(8,128)S(1)} collective-permute-done((f32[1024,128]{1,0:T(8,128)S(1)}, f32[1024,128]{1,0:T(8,128)S(1)}, u32[]{:S(2)}, u32[]{:S(2)}) %collective-permute-start.22) | collective-permute-done | bytes 524320 | tf_op jit(solution)/shard_map/ppermute | solution.py:18
  82.0 0.7 shard_map.74
  82.7 0.8 collective-permute-start.26
  83.6 1.0 collective-permute-start.27
  84.5 2.4 %collective-permute-start.28 = (f32[2,32,256]{2,1,0:T(8,128)S(1)}, f32[2,32,256]{2,1,0:T(8,128)S(1)}, u32[]{:S(2)}, u32[]{:S(2)}) collective-permute-start(f32[2,32,256]{2,1,0:T(8,128)S(1)} %get-tuple-element.109), channel_id=1, source_target_pairs={{0,48},{4,52},{8,56},{12,60},{16,32},{20,36},{24,40},{28,44},{32,1... | collective-permute-start | bytes 196616 | tf_op jit(solution)/shard_map/ppermute | solution.py:18
  86.9 1.9 %collective-permute-done.26.refs_9_ = f32[2,32,256]{2,1,0:T(8,128)S(1)} collective-permute-done((f32[2,32,256]{2,1,0:T(8,128)S(1)}, f32[2,32,256]{2,1,0:T(8,128)S(1)}, u32[]{:S(2)}, u32[]{:S(2)}) %collective-permute-start.26) | collective-permute-done | bytes 65568 | tf_op jit(solution)/shard_map/ppermute | solution.py:18
  88.9 1.1 %collective-permute-done.28.refs_11_ = f32[2,32,256]{2,1,0:T(8,128)S(1)} collective-permute-done((f32[2,32,256]{2,1,0:T(8,128)S(1)}, f32[2,32,256]{2,1,0:T(8,128)S(1)}, u32[]{:S(2)}, u32[]{:S(2)}) %collective-permute-start.28) | collective-permute-done | bytes 65568 | tf_op jit(solution)/shard_map/ppermute | solution.py:18
  90.2 1.2 %collective-permute-done.29.got_ref = f32[64,256]{1,0:T(8,128)S(1)} collective-permute-done((f32[64,256]{1,0:T(8,128)S(1)}, f32[64,256]{1,0:T(8,128)S(1)}, u32[]{:S(2)}, u32[]{:S(2)}) %collective-permute-start.29) | collective-permute-done | bytes 65568 | tf_op jit(solution)/shard_map/ppermute | solution.py:18
  91.5 3.1 %collective-permute-start.30 = (f32[64,256]{1,0:T(8,128)S(1)}, f32[64,256]{1,0:T(8,128)S(1)}, u32[]{:S(2)}, u32[]{:S(2)}) collective-permute-start(f32[64,256]{1,0:T(8,128)S(1)} %get-tuple-element.113), channel_id=1, source_target_pairs={{0,128},{4,132},{8,136},{12,140},{16,144},{20,148},{24,152},{28,15... | collective-permute-start | bytes 196616 | tf_op jit(solution)/shard_map/ppermute | solution.py:18
  94.5 0.7 collective-permute-start.31
  95.6 1.7 %collective-permute-done.30.refs_1_ = f32[64,256]{1,0:T(8,128)S(1)} collective-permute-done((f32[64,256]{1,0:T(8,128)S(1)}, f32[64,256]{1,0:T(8,128)S(1)}, u32[]{:S(2)}, u32[]{:S(2)}) %collective-permute-start.30) | collective-permute-done | bytes 65568 | tf_op jit(solution)/shard_map/ppermute | solution.py:18
  97.3 1.5 %collective-permute-done.31.refs_2_ = f32[64,256]{1,0:T(8,128)S(1)} collective-permute-done((f32[64,256]{1,0:T(8,128)S(1)}, f32[64,256]{1,0:T(8,128)S(1)}, u32[]{:S(2)}, u32[]{:S(2)}) %collective-permute-start.31) | collective-permute-done | bytes 65568 | tf_op jit(solution)/shard_map/ppermute | solution.py:18
  98.8 1.8 %collective-permute-done.32.refs_3_ = f32[64,256]{1,0:T(8,128)S(1)} collective-permute-done((f32[64,256]{1,0:T(8,128)S(1)}, f32[64,256]{1,0:T(8,128)S(1)}, u32[]{:S(2)}, u32[]{:S(2)}) %collective-permute-start.32) | collective-permute-done | bytes 65568 | tf_op jit(solution)/shard_map/ppermute | solution.py:18
  100.7 5.2 %collective-permute-start.33 = (f32[32,256]{1,0:T(8,128)S(1)}, f32[32,256]{1,0:T(8,128)S(1)}, u32[]{:S(2)}, u32[]{:S(2)}) collective-permute-start(f32[32,256]{1,0:T(8,128)S(1)} %get-tuple-element.117), channel_id=1, source_target_pairs={{0,12},{4,8},{8,4},{12,0},{16,28},{20,24},{24,20},{28,16},{32,44},... | collective-permute-start | bytes 98312 | tf_op jit(solution)/shard_map/ppermute | solution.py:18
  105.9 2.0 %collective-permute-done.33.refs_1_ = f32[32,256]{1,0:T(8,128)S(1)} collective-permute-done((f32[32,256]{1,0:T(8,128)S(1)}, f32[32,256]{1,0:T(8,128)S(1)}, u32[]{:S(2)}, u32[]{:S(2)}) %collective-permute-start.33) | collective-permute-done | bytes 32800 | tf_op jit(solution)/shard_map/ppermute | solution.py:18
  107.9 0.7 collective-permute-start.34
  108.6 4.0 %collective-permute-done.34 = f32[16,256]{1,0:T(8,128)S(1)} collective-permute-done((f32[16,256]{1,0:T(8,128)S(1)}, f32[16,256]{1,0:T(8,128)S(1)}, u32[]{:S(2)}, u32[]{:S(2)}) %collective-permute-start.34) | collective-permute-done | bytes 16416 | tf_op jit(solution)/shard_map/ppermute | solution.py:18
  (54 shorter events, 3.9 us)
Async XLA Ops:
  0.6 18.3 %copy-start.3 = (s32[1,8,8]{2,1,0:T(8,128)S(1)}, s32[1,8,8]{2,1,0:T(8,128)}, u32[]{:S(2)}) copy-start(s32[1,8,8]{2,1,0:T(8,128)} %param.6) | copy-start | bytes 772
  3.8 10.9 %collective-permute-start = (f32[128,256]{1,0:T(8,128)S(1)}, f32[128,256]{1,0:T(8,128)S(1)}, u32[]{:S(2)}, u32[]{:S(2)}) collective-permute-start(f32[128,256]{1,0:T(8,128)S(1)} %get-tuple-element.61), channel_id=1, source_target_pairs={{0,32},{4,36},{8,40},{12,44},{16,48},{20,52},{24,56},{28,60},{32,0... | collective-permute-start | bytes 393224 | tf_op jit(solution)/shard_map/ppermute | solution.py:18
  6.9 7.8 %collective-permute-start.1 = (f32[128,256]{1,0:T(8,128)S(1)}, f32[128,256]{1,0:T(8,128)S(1)}, u32[]{:S(2)}, u32[]{:S(2)}) collective-permute-start(f32[128,256]{1,0:T(8,128)S(1)} %get-tuple-element.62), channel_id=1, source_target_pairs={{0,48},{4,52},{8,56},{12,60},{16,32},{20,36},{24,40},{28,44},{32,1... | collective-permute-start | bytes 393224 | tf_op jit(solution)/shard_map/ppermute | solution.py:18
  8.0 17.8 %copy-start.1 = (f32[1024,256]{1,0:T(8,128)S(1)}, f32[1024,256]{1,0:T(8,128)}, u32[]{:S(2)}) copy-start(f32[1024,256]{1,0:T(8,128)} %p_hbm.3) | copy-start | bytes 3145732
  8.0 17.8 %copy-start.2 = (f32[1024,1024]{1,0:T(8,128)S(1)}, f32[1024,1024]{1,0:T(8,128)}, u32[]{:S(2)}) copy-start(f32[1024,1024]{1,0:T(8,128)} %param.5) | copy-start | bytes 12582916
  8.0 6.7 %collective-permute-start.2 = (f32[64,256]{1,0:T(8,128)S(1)}, f32[64,256]{1,0:T(8,128)S(1)}, u32[]{:S(2)}, u32[]{:S(2)}) collective-permute-start(f32[64,256]{1,0:T(8,128)S(1)} %get-tuple-element.64), channel_id=1, source_target_pairs={{0,16},{4,20},{8,24},{12,28},{16,0},{20,4},{24,8},{28,12},{32,48},... | collective-permute-start | bytes 196616 | tf_op jit(solution)/shard_map/ppermute | solution.py:18
  11.3 7.9 %collective-permute-start.7 = (f32[128,256]{1,0:T(8,128)S(1)}, f32[128,256]{1,0:T(8,128)S(1)}, u32[]{:S(2)}, u32[]{:S(2)}) collective-permute-start(f32[128,256]{1,0:T(8,128)S(1)} %get-tuple-element.70), channel_id=1, source_target_pairs={{0,4},{4,0},{8,12},{12,8},{16,20},{20,16},{24,28},{28,24},{32,36},... | collective-permute-start | bytes 393224 | tf_op jit(solution)/shard_map/ppermute | solution.py:18
  14.8 10.6 %collective-permute-start.5 = (f32[32,256]{1,0:T(8,128)S(1)}, f32[32,256]{1,0:T(8,128)S(1)}, u32[]{:S(2)}, u32[]{:S(2)}) collective-permute-start(f32[32,256]{1,0:T(8,128)S(1)} %get-tuple-element.123), channel_id=1, source_target_pairs={{0,192},{4,196},{8,200},{12,204},{16,208},{20,212},{24,216},{28,22... | collective-permute-start | bytes 98312 | tf_op jit(solution)/shard_map/ppermute | solution.py:18
  17.8 7.5 %collective-permute-start.4 = (f32[32,256]{1,0:T(8,128)S(1)}, f32[32,256]{1,0:T(8,128)S(1)}, u32[]{:S(2)}, u32[]{:S(2)}) collective-permute-start(f32[32,256]{1,0:T(8,128)S(1)} %get-tuple-element.123), channel_id=1, source_target_pairs={{0,128},{4,132},{8,136},{12,140},{16,144},{20,148},{24,152},{28,15... | collective-permute-start | bytes 98312 | tf_op jit(solution)/shard_map/ppermute | solution.py:18
  18.5 6.9 %collective-permute-start.3 = (f32[32,256]{1,0:T(8,128)S(1)}, f32[32,256]{1,0:T(8,128)S(1)}, u32[]{:S(2)}, u32[]{:S(2)}) collective-permute-start(f32[32,256]{1,0:T(8,128)S(1)} %get-tuple-element.122), channel_id=1, source_target_pairs={{0,64},{4,68},{8,72},{12,76},{16,80},{20,84},{24,88},{28,92},{32,9... | collective-permute-start | bytes 98312 | tf_op jit(solution)/shard_map/ppermute | solution.py:18
  19.3 12.6 %collective-permute-start.8 = (f32[128,256]{1,0:T(8,128)S(1)}, f32[128,256]{1,0:T(8,128)S(1)}, u32[]{:S(2)}, u32[]{:S(2)}) collective-permute-start(f32[128,256]{1,0:T(8,128)S(1)} %add.36), channel_id=1, source_target_pairs={{0,12},{4,8},{8,4},{12,0},{16,28},{20,24},{24,20},{28,16},{32,44},... | collective-permute-start | bytes 393224 | tf_op jit(solution)/shard_map/ppermute | solution.py:18
  25.4 9.5 %collective-permute-start.6 = (f32[128,256]{1,0:T(8,128)S(1)}, f32[128,256]{1,0:T(8,128)S(1)}, u32[]{:S(2)}, u32[]{:S(2)}) collective-permute-start(f32[128,256]{1,0:T(8,128)S(1)} %pad_maximum_fusion), channel_id=1, source_target_pairs={{0,4},{4,0},{8,12},{12,8},{16,20},{20,16},{24,28},{28,24},{32,36},... | collective-permute-start | bytes 393224 | tf_op jit(solution)/shard_map/ppermute | solution.py:18
  25.9 23.5 %copy-start = (f32[6,1024,128]{2,1,0:T(8,128)S(1)}, f32[6,1024,128]{2,1,0:T(8,128)}, u32[]{:S(2)}) copy-start(f32[6,1024,128]{2,1,0:T(8,128)} %u_ref.1) | copy-start | bytes 9437188
  28.3 13.4 %collective-permute-start.11 = (f32[128,256]{1,0:T(8,128)S(1)}, f32[128,256]{1,0:T(8,128)S(1)}, u32[]{:S(2)}, u32[]{:S(2)}) collective-permute-start(f32[128,256]{1,0:T(8,128)S(1)} %get-tuple-element.79), channel_id=1, source_target_pairs={{0,12},{4,8},{8,4},{12,0},{16,28},{20,24},{24,20},{28,16},{32,44},... | collective-permute-start | bytes 393224 | tf_op jit(solution)/shard_map/ppermute | solution.py:18
  34.9 9.7 %collective-permute-start.9 = (f32[128,256]{1,0:T(8,128)S(1)}, f32[128,256]{1,0:T(8,128)S(1)}, u32[]{:S(2)}, u32[]{:S(2)}) collective-permute-start(f32[128,256]{1,0:T(8,128)S(1)} %add.35), channel_id=1, source_target_pairs={{0,12},{4,8},{8,4},{12,0},{16,28},{20,24},{24,20},{28,16},{32,44},... | collective-permute-start | bytes 393224 | tf_op jit(solution)/shard_map/ppermute | solution.py:18
  36.1 8.5 %collective-permute-start.10 = (f32[128,256]{1,0:T(8,128)S(1)}, f32[128,256]{1,0:T(8,128)S(1)}, u32[]{:S(2)}, u32[]{:S(2)}) collective-permute-start(f32[128,256]{1,0:T(8,128)S(1)} %add.37), channel_id=1, source_target_pairs={{0,16},{4,20},{8,24},{12,28},{16,0},{20,4},{24,8},{28,12},{32,48},... | collective-permute-start | bytes 393224 | tf_op jit(solution)/shard_map/ppermute | solution.py:18
  41.7 9.5 %collective-permute-start.12 = (f32[128,256]{1,0:T(8,128)S(1)}, f32[128,256]{1,0:T(8,128)S(1)}, u32[]{:S(2)}, u32[]{:S(2)}) collective-permute-start(f32[128,256]{1,0:T(8,128)S(1)} %get-tuple-element.81), channel_id=1, source_target_pairs={{0,4},{4,0},{8,12},{12,8},{16,20},{20,16},{24,28},{28,24},{32,36},... | collective-permute-start | bytes 393224 | tf_op jit(solution)/shard_map/ppermute | solution.py:18
  41.7 9.5 %collective-permute-start.13 = (f32[128,256]{1,0:T(8,128)S(1)}, f32[128,256]{1,0:T(8,128)S(1)}, u32[]{:S(2)}, u32[]{:S(2)}) collective-permute-start(f32[128,256]{1,0:T(8,128)S(1)} %collective-permute-done.11.o_ref), channel_id=1, source_target_pairs={{0,4},{4,0},{8,12},{12,8},{16,20},{20,16},{24,28},{28,24},{32,36},... | collective-permute-start | bytes 393224 | tf_op jit(solution)/shard_map/ppermute | solution.py:18
  44.6 9.4 %collective-permute-start.14 = (f32[128,256]{1,0:T(8,128)S(1)}, f32[128,256]{1,0:T(8,128)S(1)}, u32[]{:S(2)}, u32[]{:S(2)}) collective-permute-start(f32[128,256]{1,0:T(8,128)S(1)} %add.38.q0), channel_id=1, source_target_pairs={{0,16},{4,20},{8,24},{12,28},{16,0},{20,4},{24,8},{28,12},{32,48},... | collective-permute-start | bytes 393224 | tf_op jit(solution)/shard_map/ppermute | solution.py:18
  46.3 6.1 %collective-permute-start.16 = (f32[64,256]{1,0:T(8,128)S(1)}, f32[64,256]{1,0:T(8,128)S(1)}, u32[]{:S(2)}, u32[]{:S(2)}) collective-permute-start(f32[64,256]{1,0:T(8,128)S(1)} %slice.28), channel_id=1, source_target_pairs={{0,32},{4,36},{8,40},{12,44},{16,48},{20,52},{24,56},{28,60},{32,0... | collective-permute-start | bytes 196616 | tf_op jit(solution)/shard_map/ppermute | solution.py:18
  48.6 5.5 %collective-permute-start.15 = (f32[64,256]{1,0:T(8,128)S(1)}, f32[64,256]{1,0:T(8,128)S(1)}, u32[]{:S(2)}, u32[]{:S(2)}) collective-permute-start(f32[64,256]{1,0:T(8,128)S(1)} %slice.28), channel_id=1, source_target_pairs={{0,48},{4,52},{8,56},{12,60},{16,32},{20,36},{24,40},{28,44},{32,1... | collective-permute-start | bytes 196616 | tf_op jit(solution)/shard_map/ppermute | solution.py:18
  56.4 2.7 %collective-permute-start.18 = (f32[1024,256]{1,0:T(8,128)S(1)}, f32[1024,256]{1,0:T(8,128)S(1)}, u32[]{:S(2)}, u32[]{:S(2)}) collective-permute-start(f32[1024,256]{1,0:T(8,128)S(1)} %get-tuple-element.86.refs_0_), channel_id=1, source_target_pairs={{0,1},{1,0},{2,3},{3,2},{4,5},{5,4},{6,7},{7,6},{8,9},{9,8},{10,11... | collective-permute-start | bytes 3145736 | tf_op jit(solution)/shard_map/ppermute | solution.py:18
  56.5 14.7 %collective-permute-start.17 = (f32[1024,128]{1,0:T(8,128)S(1)}, f32[1024,128]{1,0:T(8,128)S(1)}, u32[]{:S(2)}, u32[]{:S(2)}) collective-permute-start(f32[1024,128]{1,0:T(8,128)S(1)} %get-tuple-element.85), channel_id=1, source_target_pairs={{0,2},{1,3},{2,0},{3,1},{4,6},{5,7},{6,4},{7,5},{8,10},{9,11},{10,... | collective-permute-start | bytes 1572872 | tf_op jit(solution)/shard_map/ppermute | solution.py:18
  56.5 25.6 %collective-permute-start.22 = (f32[1024,128]{1,0:T(8,128)S(1)}, f32[1024,128]{1,0:T(8,128)S(1)}, u32[]{:S(2)}, u32[]{:S(2)}) collective-permute-start(f32[1024,128]{1,0:T(8,128)S(1)} %get-tuple-element.95), channel_id=1, source_target_pairs={{0,2},{1,3},{2,0},{3,1},{4,6},{5,7},{6,4},{7,5},{8,10},{9,11},{10,... | collective-permute-start | bytes 1572872 | tf_op jit(solution)/shard_map/ppermute | solution.py:18
  60.2 11.0 %collective-permute-start.19 = (f32[2,64,256]{2,1,0:T(8,128)S(1)}, f32[2,64,256]{2,1,0:T(8,128)S(1)}, u32[]{:S(2)}, u32[]{:S(2)}) collective-permute-start(f32[2,64,256]{2,1,0:T(8,128)S(1)} %get-tuple-element.88), channel_id=1, source_target_pairs={{0,32},{4,36},{8,40},{12,44},{16,48},{20,52},{24,56},{28,60},{32,0... | collective-permute-start | bytes 393224 | tf_op jit(solution)/shard_map/ppermute | solution.py:18
  61.0 10.2 %collective-permute-start.20 = (f32[2,64,256]{2,1,0:T(8,128)S(1)}, f32[2,64,256]{2,1,0:T(8,128)S(1)}, u32[]{:S(2)}, u32[]{:S(2)}) collective-permute-start(f32[2,64,256]{2,1,0:T(8,128)S(1)} %get-tuple-element.89), channel_id=1, source_target_pairs={{0,16},{4,20},{8,24},{12,28},{16,0},{20,4},{24,8},{28,12},{32,48},... | collective-permute-start | bytes 393224 | tf_op jit(solution)/shard_map/ppermute | solution.py:18
  62.0 9.2 %collective-permute-start.21 = (f32[2,64,256]{2,1,0:T(8,128)S(1)}, f32[2,64,256]{2,1,0:T(8,128)S(1)}, u32[]{:S(2)}, u32[]{:S(2)}) collective-permute-start(f32[2,64,256]{2,1,0:T(8,128)S(1)} %get-tuple-element.90), channel_id=1, source_target_pairs={{0,48},{4,52},{8,56},{12,60},{16,32},{20,36},{24,40},{28,44},{32,1... | collective-permute-start | bytes 393224 | tf_op jit(solution)/shard_map/ppermute | solution.py:18
  71.9 10.1 %collective-permute-start.23 = (f32[2,32,256]{2,1,0:T(8,128)S(1)}, f32[2,32,256]{2,1,0:T(8,128)S(1)}, u32[]{:S(2)}, u32[]{:S(2)}) collective-permute-start(f32[2,32,256]{2,1,0:T(8,128)S(1)} %get-tuple-element.98), channel_id=1, source_target_pairs={{0,32},{4,36},{8,40},{12,44},{16,48},{20,52},{24,56},{28,60},{32,0... | collective-permute-start | bytes 196616 | tf_op jit(solution)/shard_map/ppermute | solution.py:18
  72.7 9.3 %collective-permute-start.24 = (f32[2,32,256]{2,1,0:T(8,128)S(1)}, f32[2,32,256]{2,1,0:T(8,128)S(1)}, u32[]{:S(2)}, u32[]{:S(2)}) collective-permute-start(f32[2,32,256]{2,1,0:T(8,128)S(1)} %get-tuple-element.99), channel_id=1, source_target_pairs={{0,16},{4,20},{8,24},{12,28},{16,0},{20,4},{24,8},{28,12},{32,48},... | collective-permute-start | bytes 196616 | tf_op jit(solution)/shard_map/ppermute | solution.py:18
  73.7 8.3 %collective-permute-start.25 = (f32[2,32,256]{2,1,0:T(8,128)S(1)}, f32[2,32,256]{2,1,0:T(8,128)S(1)}, u32[]{:S(2)}, u32[]{:S(2)}) collective-permute-start(f32[2,32,256]{2,1,0:T(8,128)S(1)} %get-tuple-element.100), channel_id=1, source_target_pairs={{0,48},{4,52},{8,56},{12,60},{16,32},{20,36},{24,40},{28,44},{32,1... | collective-permute-start | bytes 196616 | tf_op jit(solution)/shard_map/ppermute | solution.py:18
  82.7 6.1 %collective-permute-start.26 = (f32[2,32,256]{2,1,0:T(8,128)S(1)}, f32[2,32,256]{2,1,0:T(8,128)S(1)}, u32[]{:S(2)}, u32[]{:S(2)}) collective-permute-start(f32[2,32,256]{2,1,0:T(8,128)S(1)} %get-tuple-element.107), channel_id=1, source_target_pairs={{0,32},{4,36},{8,40},{12,44},{16,48},{20,52},{24,56},{28,60},{32,0... | collective-permute-start | bytes 196616 | tf_op jit(solution)/shard_map/ppermute | solution.py:18
  83.6 5.3 %collective-permute-start.27 = (f32[2,32,256]{2,1,0:T(8,128)S(1)}, f32[2,32,256]{2,1,0:T(8,128)S(1)}, u32[]{:S(2)}, u32[]{:S(2)}) collective-permute-start(f32[2,32,256]{2,1,0:T(8,128)S(1)} %get-tuple-element.108), channel_id=1, source_target_pairs={{0,16},{4,20},{8,24},{12,28},{16,0},{20,4},{24,8},{28,12},{32,48},... | collective-permute-start | bytes 196616 | tf_op jit(solution)/shard_map/ppermute | solution.py:18
  84.5 5.5 %collective-permute-start.28 = (f32[2,32,256]{2,1,0:T(8,128)S(1)}, f32[2,32,256]{2,1,0:T(8,128)S(1)}, u32[]{:S(2)}, u32[]{:S(2)}) collective-permute-start(f32[2,32,256]{2,1,0:T(8,128)S(1)} %get-tuple-element.109), channel_id=1, source_target_pairs={{0,48},{4,52},{8,56},{12,60},{16,32},{20,36},{24,40},{28,44},{32,1... | collective-permute-start | bytes 196616 | tf_op jit(solution)/shard_map/ppermute | solution.py:18
  90.1 1.3 %collective-permute-start.29 = (f32[64,256]{1,0:T(8,128)S(1)}, f32[64,256]{1,0:T(8,128)S(1)}, u32[]{:S(2)}, u32[]{:S(2)}) collective-permute-start(f32[64,256]{1,0:T(8,128)S(1)} %get-tuple-element.111), channel_id=1, source_target_pairs={{0,1},{1,0},{2,3},{3,2},{4,5},{5,4},{6,7},{7,6},{8,9},{9,8},{10,11... | collective-permute-start | bytes 196616 | tf_op jit(solution)/shard_map/ppermute | solution.py:18
  91.5 5.9 %collective-permute-start.30 = (f32[64,256]{1,0:T(8,128)S(1)}, f32[64,256]{1,0:T(8,128)S(1)}, u32[]{:S(2)}, u32[]{:S(2)}) collective-permute-start(f32[64,256]{1,0:T(8,128)S(1)} %get-tuple-element.113), channel_id=1, source_target_pairs={{0,128},{4,132},{8,136},{12,140},{16,144},{20,148},{24,152},{28,15... | collective-permute-start | bytes 196616 | tf_op jit(solution)/shard_map/ppermute | solution.py:18
  94.5 4.3 %collective-permute-start.31 = (f32[64,256]{1,0:T(8,128)S(1)}, f32[64,256]{1,0:T(8,128)S(1)}, u32[]{:S(2)}, u32[]{:S(2)}) collective-permute-start(f32[64,256]{1,0:T(8,128)S(1)} %get-tuple-element.114), channel_id=1, source_target_pairs={{0,64},{4,68},{8,72},{12,76},{16,80},{20,84},{24,88},{28,92},{32,9... | collective-permute-start | bytes 196616 | tf_op jit(solution)/shard_map/ppermute | solution.py:18
  95.2 5.5 %collective-permute-start.32 = (f32[64,256]{1,0:T(8,128)S(1)}, f32[64,256]{1,0:T(8,128)S(1)}, u32[]{:S(2)}, u32[]{:S(2)}) collective-permute-start(f32[64,256]{1,0:T(8,128)S(1)} %get-tuple-element.115), channel_id=1, source_target_pairs={{0,192},{4,196},{8,200},{12,204},{16,208},{20,212},{24,216},{28,22... | collective-permute-start | bytes 196616 | tf_op jit(solution)/shard_map/ppermute | solution.py:18
  100.7 7.2 %collective-permute-start.33 = (f32[32,256]{1,0:T(8,128)S(1)}, f32[32,256]{1,0:T(8,128)S(1)}, u32[]{:S(2)}, u32[]{:S(2)}) collective-permute-start(f32[32,256]{1,0:T(8,128)S(1)} %get-tuple-element.117), channel_id=1, source_target_pairs={{0,12},{4,8},{8,4},{12,0},{16,28},{20,24},{24,20},{28,16},{32,44},... | collective-permute-start | bytes 98312 | tf_op jit(solution)/shard_map/ppermute | solution.py:18
  107.9 4.7 %collective-permute-start.34 = (f32[16,256]{1,0:T(8,128)S(1)}, f32[16,256]{1,0:T(8,128)S(1)}, u32[]{:S(2)}, u32[]{:S(2)}) collective-permute-start(f32[16,256]{1,0:T(8,128)S(1)} %get-tuple-element.119), channel_id=1, source_target_pairs={{0,4},{4,0},{8,12},{12,8},{16,20},{20,16},{24,28},{28,24},{32,36},... | collective-permute-start | bytes 49160 | tf_op jit(solution)/shard_map/ppermute | solution.py:18

commit v11 on v10

--- a/solution.py
+++ b/solution.py
@@ -195,7 +195,7 @@
 
 def expand(base, rows_high, rows_low, zero, one, one_more, part, part1, part2, part3):
     def body(
-        b_ref, h_ref, l_ref, z_ref, o_ref, m_ref, q0, q1, q3, q2, out, held, even, odd, total
+        b_ref, h_ref, l_ref, z_ref, o_ref, m_ref, q0, q1, q3, q2, held, even, odd, total
     ):
         _, x, _ = place()
         total[0:128] = z_ref[...]
@@ -209,7 +209,6 @@
             total[pl.ds(512 + row, 32)] = ref[base + 32:base + 64]
         left = h_ref[...], l_ref[...]
         value = b_ref[...] + dot3(left, split(total[...]), MATMUL)
-        out[...] = value
         held[...] = value
         even[...], odd[...] = chunks(value)
 
@@ -218,7 +217,7 @@
     given = [base, rows_high, rows_low, zero, one, one_more, part, part1, part3, part2]
     return call(
         body,
-        shapes(base.shape, base.shape, (points, wide // 2), (points, wide // 2)),
+        shapes(base.shape, (points, wide // 2), (points, wide // 2)),
         [whole(g.shape) for g in given],
         given,
         [pltpu.VMEM((depth, wide), F32)],
@@ -245,12 +244,14 @@
             pairs = (rows, mine), (rows, beside)
         for k, (up, down) in enumerate(pairs):
             total[k] = dot3(up, down, ROWS)
-        for k, out in enumerate(outs):
+        for k, out in enumerate(outs[:4]):
             out[...] = total[:, pl.ds(pl.multiple_of((x ^ k) * part, part), part)]
-
-    return call(
-        body,
-        shapes(*[(2, part, wide)] * 4),
+        if near:
+            outs[4][...] = a_ref[...]
+
+    return call(
+        body,
+        shapes(*[(2, part, wide)] * 4, *[first.shape] * near),
         [whole(g.shape) for g in given],
         given,
         [pltpu.VMEM((2, tall, wide), F32)],
@@ -365,12 +366,13 @@
     late = prepare(near, row_factor_stack, node2)
     last = swap(part[64:], "leaf", 8)
     gathered = [swap(part, "leaf", 4), last, swap(part[64:], "leaf", 12)]
-    result, applied, even, odd = expand(*late, node0, node1, node1_more, part, *gathered)
+    applied, even, odd = expand(*late, node0, node1, node1_more, part, *gathered)
 
     beside = swap(applied, "probe", 1)
     even = swap(even, "probe", 2)
     odd = swap(odd, "probe", 2)
-    first = around(gram(applied, applied, beside), 4)
+    *first, result = gram(applied, applied, beside)
+    first = around(first, 4)
     even, *first = lax.optimization_barrier((even, *first))
     second = around(gram(even, applied, beside), 4)
     odd, *second = lax.optimization_barrier((odd, *second))

time: 113 us -> 113 us (level)
  transfers between devices with their start and end apart: 35 -> 35, of which waited for: 16 -> 16; matrix products, arithmetic and copies ran while one was open for 3% -> 3% of each run, Pallas kernels for 6% -> 7%
where the time goes in v11:
time: 113 us
  starting transfers between devices  57.1 us (51%)
  waiting for transfers between devices  38 us (34%)
  Pallas kernels  13.5 us (12%)
  matrix products  2.39 us (2%)
    ppermute x35, starting transfers between devices, swap(): return lax.ppermute(value, axis, pairs)  57.1 us
    ppermute x35, waiting for transfers between devices, swap(): return lax.ppermute(value, axis, pairs)  38 us
    pallas_call x11, Pallas kernels, call(): pl.pallas_call(body, out_shape=outs, grid=grid, in_specs=specs, out_specs...  13.5 us
    dot_general x1, matrix products, near_product(): return jnp.dot(masked, probes, precision=HIGH, preferred_element_type=F32)  2.39 us
  transfers between devices with their start and end apart: 35, of which 16 were waited for; matrix products, arithmetic and copies ran while one was open for 3% of the time, Pallas kernels for 7%

profile of v11, /device:TPU:32, one launch (start us, length us, event | category | flops | bytes accessed | tf_op | source)
XLA Modules:
  0.0 112.9 jit_solution(3436819700315229021)
XLA Ops:
  0.6 3.1 %shard_map.68 = (f32[64,256]{1,0:T(8,128)S(1)}, f32[64,256]{1,0:T(8,128)S(1)}, f32[128,256]{1,0:T(8,128)S(1)}, f32[128,256]{1,0:T(8,128)S(1)}) custom-call(f32[6,1024,128]{2,1,0:T(8,128)} %c_hbm.3, f32[1024,256]{1,0:T(8,128)} %p_hbm.3), custom_call_target="tpu_custom_call" | custom-call | flops 603979776 | bytes 4587520 | tf_op jit(solution)/shard_map/pallas_call | solution.py:49
  3.8 3.1 %collective-permute-start = (f32[128,256]{1,0:T(8,128)S(1)}, f32[128,256]{1,0:T(8,128)S(1)}, u32[]{:S(2)}, u32[]{:S(2)}) collective-permute-start(f32[128,256]{1,0:T(8,128)S(1)} %get-tuple-element.61), channel_id=1, source_target_pairs={{0,32},{4,36},{8,40},{12,44},{16,48},{20,52},{24,56},{28,60},{32,0... | collective-permute-start | bytes 393224 | tf_op jit(solution)/shard_map/ppermute | solution.py:18
  6.9 1.1 %collective-permute-start.1 = (f32[128,256]{1,0:T(8,128)S(1)}, f32[128,256]{1,0:T(8,128)S(1)}, u32[]{:S(2)}, u32[]{:S(2)}) collective-permute-start(f32[128,256]{1,0:T(8,128)S(1)} %get-tuple-element.62), channel_id=1, source_target_pairs={{0,48},{4,52},{8,56},{12,60},{16,32},{20,36},{24,40},{28,44},{32,1... | collective-permute-start | bytes 393224 | tf_op jit(solution)/shard_map/ppermute | solution.py:18
  8.0 3.3 %shard_map.69 = (f32[128,256]{1,0:T(8,128)S(1)}, f32[128,256]{1,0:T(8,128)S(1)}, f32[128,256]{1,0:T(8,128)S(1)}) custom-call(f32[6,1024,128]{2,1,0:T(8,128)} %c_hbm.3, f32[1024,256]{1,0:T(8,128)} %p_hbm.3), custom_call_target="tpu_custom_call" | custom-call | flops 603979776 | bytes 4587520 | tf_op jit(solution)/shard_map/pallas_call | solution.py:49
  11.3 3.4 %collective-permute-start.7 = (f32[128,256]{1,0:T(8,128)S(1)}, f32[128,256]{1,0:T(8,128)S(1)}, u32[]{:S(2)}, u32[]{:S(2)}) collective-permute-start(f32[128,256]{1,0:T(8,128)S(1)} %get-tuple-element.70), channel_id=1, source_target_pairs={{0,4},{4,0},{8,12},{12,8},{16,20},{20,16},{24,28},{28,24},{32,36},... | collective-permute-start | bytes 393224 | tf_op jit(solution)/shard_map/ppermute | solution.py:18
  14.8 3.1 %collective-permute-start.5 = (f32[32,256]{1,0:T(8,128)S(1)}, f32[32,256]{1,0:T(8,128)S(1)}, u32[]{:S(2)}, u32[]{:S(2)}) collective-permute-start(f32[32,256]{1,0:T(8,128)S(1)} %get-tuple-element.123), channel_id=1, source_target_pairs={{0,192},{4,196},{8,200},{12,204},{16,208},{20,212},{24,216},{28,22... | collective-permute-start | bytes 98312 | tf_op jit(solution)/shard_map/ppermute | solution.py:18
  19.3 6.1 %collective-permute-start.8 = (f32[128,256]{1,0:T(8,128)S(1)}, f32[128,256]{1,0:T(8,128)S(1)}, u32[]{:S(2)}, u32[]{:S(2)}) collective-permute-start(f32[128,256]{1,0:T(8,128)S(1)} %add.36), channel_id=1, source_target_pairs={{0,12},{4,8},{8,4},{12,0},{16,28},{20,24},{24,20},{28,16},{32,44},... | collective-permute-start | bytes 393224 | tf_op jit(solution)/shard_map/ppermute | solution.py:18
  25.9 2.4 %fusion.n_ref = f32[1024,256]{1,0:T(8,128)S(1)} fusion(f32[1024,256]{1,0:T(8,128)S(1)} %copy-done.1, f32[1024,1024]{1,0:T(8,128)S(1)} %copy-done.2, f32[128,8,8,128]{3,2,1,0:T(8,128)S(1)} %bitcast.8), kind=kOutput, calls=%fused_computation.1 | convolution fusion | flops 1611661312 | bytes 10485760 | tf_op jit(solution)/shard_map/dot_general | solution.py:338
  28.3 3.5 %collective-permute-start.11 = (f32[128,256]{1,0:T(8,128)S(1)}, f32[128,256]{1,0:T(8,128)S(1)}, u32[]{:S(2)}, u32[]{:S(2)}) collective-permute-start(f32[128,256]{1,0:T(8,128)S(1)} %get-tuple-element.79), channel_id=1, source_target_pairs={{0,12},{4,8},{8,4},{12,0},{16,28},{20,24},{24,20},{28,16},{32,44},... | collective-permute-start | bytes 393224 | tf_op jit(solution)/shard_map/ppermute | solution.py:18
  31.8 3.0 %collective-permute-done.6 = f32[128,256]{1,0:T(8,128)S(1)} collective-permute-done((f32[128,256]{1,0:T(8,128)S(1)}, f32[128,256]{1,0:T(8,128)S(1)}, u32[]{:S(2)}, u32[]{:S(2)}) %collective-permute-start.6) | collective-permute-done | bytes 131104 | tf_op jit(solution)/shard_map/ppermute | solution.py:18
  34.9 1.2 %collective-permute-start.9 = (f32[128,256]{1,0:T(8,128)S(1)}, f32[128,256]{1,0:T(8,128)S(1)}, u32[]{:S(2)}, u32[]{:S(2)}) collective-permute-start(f32[128,256]{1,0:T(8,128)S(1)} %add.35), channel_id=1, source_target_pairs={{0,12},{4,8},{8,4},{12,0},{16,28},{20,24},{24,20},{28,16},{32,44},... | collective-permute-start | bytes 393224 | tf_op jit(solution)/shard_map/ppermute | solution.py:18
  36.1 1.6 %collective-permute-start.10 = (f32[128,256]{1,0:T(8,128)S(1)}, f32[128,256]{1,0:T(8,128)S(1)}, u32[]{:S(2)}, u32[]{:S(2)}) collective-permute-start(f32[128,256]{1,0:T(8,128)S(1)} %add.37), channel_id=1, source_target_pairs={{0,16},{4,20},{8,24},{12,28},{16,0},{20,4},{24,8},{28,12},{32,48},... | collective-permute-start | bytes 393224 | tf_op jit(solution)/shard_map/ppermute | solution.py:18
  37.7 4.0 %collective-permute-done.11.o_ref = f32[128,256]{1,0:T(8,128)S(1)} collective-permute-done((f32[128,256]{1,0:T(8,128)S(1)}, f32[128,256]{1,0:T(8,128)S(1)}, u32[]{:S(2)}, u32[]{:S(2)}) %collective-permute-start.11) | collective-permute-done | bytes 131104 | tf_op jit(solution)/shard_map/ppermute | solution.py:18
  41.7 2.9 %collective-permute-start.13 = (f32[128,256]{1,0:T(8,128)S(1)}, f32[128,256]{1,0:T(8,128)S(1)}, u32[]{:S(2)}, u32[]{:S(2)}) collective-permute-start(f32[128,256]{1,0:T(8,128)S(1)} %collective-permute-done.11.o_ref), channel_id=1, source_target_pairs={{0,4},{4,0},{8,12},{12,8},{16,20},{20,16},{24,28},{28,24},{32,36},... | collective-permute-start | bytes 393224 | tf_op jit(solution)/shard_map/ppermute | solution.py:18
  44.6 1.7 %collective-permute-start.14 = (f32[128,256]{1,0:T(8,128)S(1)}, f32[128,256]{1,0:T(8,128)S(1)}, u32[]{:S(2)}, u32[]{:S(2)}) collective-permute-start(f32[128,256]{1,0:T(8,128)S(1)} %add.38.q0), channel_id=1, source_target_pairs={{0,16},{4,20},{8,24},{12,28},{16,0},{20,4},{24,8},{28,12},{32,48},... | collective-permute-start | bytes 393224 | tf_op jit(solution)/shard_map/ppermute | solution.py:18
  46.3 2.3 %collective-permute-start.16 = (f32[64,256]{1,0:T(8,128)S(1)}, f32[64,256]{1,0:T(8,128)S(1)}, u32[]{:S(2)}, u32[]{:S(2)}) collective-permute-start(f32[64,256]{1,0:T(8,128)S(1)} %slice.28), channel_id=1, source_target_pairs={{0,32},{4,36},{8,40},{12,44},{16,48},{20,52},{24,56},{28,60},{32,0... | collective-permute-start | bytes 196616 | tf_op jit(solution)/shard_map/ppermute | solution.py:18
  48.6 0.8 collective-permute-start.15
  49.4 1.7 %shard_map.70 = (f32[1024,256]{1,0:T(8,128)S(1)}, bf16[1024,640]{1,0:T(8,128)(2,1)S(1)}, bf16[1024,640]{1,0:T(8,128)(2,1)S(1)}) custom-call(f32[1024,256]{1,0:T(8,128)S(1)} %fusion.n_ref, f32[6,1024,128]{2,1,0:T(8,128)S(1)} %copy-done, f32[128,256]{1,0:T(8,128)S(1)} %collective-permute-done.10.t_ref), custom_call_target="tpu_custom_call" | custom-call | flops 201326592 | bytes 10616832 | tf_op jit(solution)/shard_map/pallas_call | solution.py:49
  51.2 1.2 %collective-permute-done.16.q2 = f32[64,256]{1,0:T(8,128)S(1)} collective-permute-done((f32[64,256]{1,0:T(8,128)S(1)}, f32[64,256]{1,0:T(8,128)S(1)}, u32[]{:S(2)}, u32[]{:S(2)}) %collective-permute-start.16) | collective-permute-done | bytes 65568 | tf_op jit(solution)/shard_map/ppermute | solution.py:18
  52.4 1.7 %collective-permute-done.15.q3 = f32[64,256]{1,0:T(8,128)S(1)} collective-permute-done((f32[64,256]{1,0:T(8,128)S(1)}, f32[64,256]{1,0:T(8,128)S(1)}, u32[]{:S(2)}, u32[]{:S(2)}) %collective-permute-start.15) | collective-permute-done | bytes 65568 | tf_op jit(solution)/shard_map/ppermute | solution.py:18
  54.0 1.8 %shard_map.71 = (f32[1024,256]{1,0:T(8,128)S(1)}, f32[1024,128]{1,0:T(8,128)S(1)}, f32[1024,128]{1,0:T(8,128)S(1)}) custom-call(f32[1024,256]{1,0:T(8,128)S(1)} %get-tuple-element.76.b_ref, bf16[1024,640]{1,0:T(8,128)(2,1)S(1)} %get-tuple-element.77.h_ref, bf16[1024,640]{1,0:T(8,128)(2,1)S(1)} %get-tuple-element.78.l_ref, ...), custom_call_target="tpu_custom_call" | custom-call | flops 1006632960 | bytes 9175040 | tf_op jit(solution)/shard_map/pallas_call | solution.py:49
  56.0 2.0 %collective-permute-start.22 = (f32[1024,128]{1,0:T(8,128)S(1)}, f32[1024,128]{1,0:T(8,128)S(1)}, u32[]{:S(2)}, u32[]{:S(2)}) collective-permute-start(f32[1024,128]{1,0:T(8,128)S(1)} %get-tuple-element.95), channel_id=1, source_target_pairs={{0,2},{1,3},{2,0},{3,1},{4,6},{5,7},{6,4},{7,5},{8,10},{9,11},{10,... | collective-permute-start | bytes 1572872 | tf_op jit(solution)/shard_map/ppermute | solution.py:18
  58.6 2.0 %shard_map.72 = (f32[2,64,256]{2,1,0:T(8,128)S(1)}, f32[2,64,256]{2,1,0:T(8,128)S(1)}, f32[2,64,256]{2,1,0:T(8,128)S(1)}, f32[2,64,256]{2,1,0:T(8,128)S(1)}, f32[1024,256]{1,0:T(8,128)}) custom-call(f32[1024,256]{1,0:T(8,128)S(1)} %get-tuple-element.84.refs_0_, f32[1024,256]{1,0:T(8,128)S(1)} %collective-permute-done.17.refs_1_), custom_call_target="tpu_custom_call" | custom-call | flops 805306368 | bytes 3670016 | tf_op jit(solution)/shard_map/pallas_call | solution.py:49
  60.6 0.7 collective-permute-start.19
  61.3 1.0 collective-permute-start.20
  62.3 2.4 %collective-permute-start.21 = (f32[2,64,256]{2,1,0:T(8,128)S(1)}, f32[2,64,256]{2,1,0:T(8,128)S(1)}, u32[]{:S(2)}, u32[]{:S(2)}) collective-permute-start(f32[2,64,256]{2,1,0:T(8,128)S(1)} %get-tuple-element.90), channel_id=1, source_target_pairs={{0,48},{4,52},{8,56},{12,60},{16,32},{20,36},{24,40},{28,44},{32,1... | collective-permute-start | bytes 393224 | tf_op jit(solution)/shard_map/ppermute | solution.py:18
  64.7 6.1 %collective-permute-done.18.refs_2_ = f32[1024,128]{1,0:T(8,128)S(1)} collective-permute-done((f32[1024,128]{1,0:T(8,128)S(1)}, f32[1024,128]{1,0:T(8,128)S(1)}, u32[]{:S(2)}, u32[]{:S(2)}) %collective-permute-start.18) | collective-permute-done | bytes 524320 | tf_op jit(solution)/shard_map/ppermute | solution.py:18
  70.7 0.7 shard_map.73
  71.5 0.8 collective-permute-start.23
  72.3 1.0 collective-permute-start.24
  73.3 2.4 %collective-permute-start.25 = (f32[2,32,256]{2,1,0:T(8,128)S(1)}, f32[2,32,256]{2,1,0:T(8,128)S(1)}, u32[]{:S(2)}, u32[]{:S(2)}) collective-permute-start(f32[2,32,256]{2,1,0:T(8,128)S(1)} %get-tuple-element.100), channel_id=1, source_target_pairs={{0,48},{4,52},{8,56},{12,60},{16,32},{20,36},{24,40},{28,44},{32,1... | collective-permute-start | bytes 196616 | tf_op jit(solution)/shard_map/ppermute | solution.py:18
  75.6 5.9 %collective-permute-done.22.refs_2_ = f32[1024,128]{1,0:T(8,128)S(1)} collective-permute-done((f32[1024,128]{1,0:T(8,128)S(1)}, f32[1024,128]{1,0:T(8,128)S(1)}, u32[]{:S(2)}, u32[]{:S(2)}) %collective-permute-start.22) | collective-permute-done | bytes 524320 | tf_op jit(solution)/shard_map/ppermute | solution.py:18
  81.5 0.7 shard_map.74
  82.2 1.1 collective-permute-start.26
  83.3 1.0 collective-permute-start.27
  84.2 2.4 %collective-permute-start.28 = (f32[2,32,256]{2,1,0:T(8,128)S(1)}, f32[2,32,256]{2,1,0:T(8,128)S(1)}, u32[]{:S(2)}, u32[]{:S(2)}) collective-permute-start(f32[2,32,256]{2,1,0:T(8,128)S(1)} %get-tuple-element.109), channel_id=1, source_target_pairs={{0,48},{4,52},{8,56},{12,60},{16,32},{20,36},{24,40},{28,44},{32,1... | collective-permute-start | bytes 196616 | tf_op jit(solution)/shard_map/ppermute | solution.py:18
  86.6 1.9 %collective-permute-done.26.refs_9_ = f32[2,32,256]{2,1,0:T(8,128)S(1)} collective-permute-done((f32[2,32,256]{2,1,0:T(8,128)S(1)}, f32[2,32,256]{2,1,0:T(8,128)S(1)}, u32[]{:S(2)}, u32[]{:S(2)}) %collective-permute-start.26) | collective-permute-done | bytes 65568 | tf_op jit(solution)/shard_map/ppermute | solution.py:18
  88.5 1.2 %collective-permute-done.28.refs_11_ = f32[2,32,256]{2,1,0:T(8,128)S(1)} collective-permute-done((f32[2,32,256]{2,1,0:T(8,128)S(1)}, f32[2,32,256]{2,1,0:T(8,128)S(1)}, u32[]{:S(2)}, u32[]{:S(2)}) %collective-permute-start.28) | collective-permute-done | bytes 65568 | tf_op jit(solution)/shard_map/ppermute | solution.py:18
  89.9 1.2 %collective-permute-done.29.got_ref = f32[64,256]{1,0:T(8,128)S(1)} collective-permute-done((f32[64,256]{1,0:T(8,128)S(1)}, f32[64,256]{1,0:T(8,128)S(1)}, u32[]{:S(2)}, u32[]{:S(2)}) %collective-permute-start.29) | collective-permute-done | bytes 65568 | tf_op jit(solution)/shard_map/ppermute | solution.py:18
  91.2 3.1 %collective-permute-start.30 = (f32[64,256]{1,0:T(8,128)S(1)}, f32[64,256]{1,0:T(8,128)S(1)}, u32[]{:S(2)}, u32[]{:S(2)}) collective-permute-start(f32[64,256]{1,0:T(8,128)S(1)} %get-tuple-element.113), channel_id=1, source_target_pairs={{0,128},{4,132},{8,136},{12,140},{16,144},{20,148},{24,152},{28,15... | collective-permute-start | bytes 196616 | tf_op jit(solution)/shard_map/ppermute | solution.py:18
  94.2 0.7 collective-permute-start.31
  95.3 1.7 %collective-permute-done.30.refs_1_ = f32[64,256]{1,0:T(8,128)S(1)} collective-permute-done((f32[64,256]{1,0:T(8,128)S(1)}, f32[64,256]{1,0:T(8,128)S(1)}, u32[]{:S(2)}, u32[]{:S(2)}) %collective-permute-start.30) | collective-permute-done | bytes 65568 | tf_op jit(solution)/shard_map/ppermute | solution.py:18
  97.0 1.5 %collective-permute-done.31.refs_2_ = f32[64,256]{1,0:T(8,128)S(1)} collective-permute-done((f32[64,256]{1,0:T(8,128)S(1)}, f32[64,256]{1,0:T(8,128)S(1)}, u32[]{:S(2)}, u32[]{:S(2)}) %collective-permute-start.31) | collective-permute-done | bytes 65568 | tf_op jit(solution)/shard_map/ppermute | solution.py:18
  98.5 1.8 %collective-permute-done.32.refs_3_ = f32[64,256]{1,0:T(8,128)S(1)} collective-permute-done((f32[64,256]{1,0:T(8,128)S(1)}, f32[64,256]{1,0:T(8,128)S(1)}, u32[]{:S(2)}, u32[]{:S(2)}) %collective-permute-start.32) | collective-permute-done | bytes 65568 | tf_op jit(solution)/shard_map/ppermute | solution.py:18
  100.4 5.2 %collective-permute-start.33 = (f32[32,256]{1,0:T(8,128)S(1)}, f32[32,256]{1,0:T(8,128)S(1)}, u32[]{:S(2)}, u32[]{:S(2)}) collective-permute-start(f32[32,256]{1,0:T(8,128)S(1)} %get-tuple-element.117), channel_id=1, source_target_pairs={{0,12},{4,8},{8,4},{12,0},{16,28},{20,24},{24,20},{28,16},{32,44},... | collective-permute-start | bytes 98312 | tf_op jit(solution)/shard_map/ppermute | solution.py:18
  105.6 2.0 %collective-permute-done.33.refs_1_ = f32[32,256]{1,0:T(8,128)S(1)} collective-permute-done((f32[32,256]{1,0:T(8,128)S(1)}, f32[32,256]{1,0:T(8,128)S(1)}, u32[]{:S(2)}, u32[]{:S(2)}) %collective-permute-start.33) | collective-permute-done | bytes 32800 | tf_op jit(solution)/shard_map/ppermute | solution.py:18
  107.6 0.7 collective-permute-start.34
  108.3 4.0 %collective-permute-done.34 = f32[16,256]{1,0:T(8,128)S(1)} collective-permute-done((f32[16,256]{1,0:T(8,128)S(1)}, f32[16,256]{1,0:T(8,128)S(1)}, u32[]{:S(2)}, u32[]{:S(2)}) %collective-permute-start.34) | collective-permute-done | bytes 16416 | tf_op jit(solution)/shard_map/ppermute | solution.py:18
  (54 shorter events, 4.0 us)
Async XLA Ops:
  0.6 18.3 %copy-start.3 = (s32[1,8,8]{2,1,0:T(8,128)S(1)}, s32[1,8,8]{2,1,0:T(8,128)}, u32[]{:S(2)}) copy-start(s32[1,8,8]{2,1,0:T(8,128)} %param.6) | copy-start | bytes 772
  3.8 10.9 %collective-permute-start = (f32[128,256]{1,0:T(8,128)S(1)}, f32[128,256]{1,0:T(8,128)S(1)}, u32[]{:S(2)}, u32[]{:S(2)}) collective-permute-start(f32[128,256]{1,0:T(8,128)S(1)} %get-tuple-element.61), channel_id=1, source_target_pairs={{0,32},{4,36},{8,40},{12,44},{16,48},{20,52},{24,56},{28,60},{32,0... | collective-permute-start | bytes 393224 | tf_op jit(solution)/shard_map/ppermute | solution.py:18
  6.9 7.8 %collective-permute-start.1 = (f32[128,256]{1,0:T(8,128)S(1)}, f32[128,256]{1,0:T(8,128)S(1)}, u32[]{:S(2)}, u32[]{:S(2)}) collective-permute-start(f32[128,256]{1,0:T(8,128)S(1)} %get-tuple-element.62), channel_id=1, source_target_pairs={{0,48},{4,52},{8,56},{12,60},{16,32},{20,36},{24,40},{28,44},{32,1... | collective-permute-start | bytes 393224 | tf_op jit(solution)/shard_map/ppermute | solution.py:18
  8.0 17.8 %copy-start.1 = (f32[1024,256]{1,0:T(8,128)S(1)}, f32[1024,256]{1,0:T(8,128)}, u32[]{:S(2)}) copy-start(f32[1024,256]{1,0:T(8,128)} %p_hbm.3) | copy-start | bytes 3145732
  8.0 17.8 %copy-start.2 = (f32[1024,1024]{1,0:T(8,128)S(1)}, f32[1024,1024]{1,0:T(8,128)}, u32[]{:S(2)}) copy-start(f32[1024,1024]{1,0:T(8,128)} %param.5) | copy-start | bytes 12582916
  8.0 6.7 %collective-permute-start.2 = (f32[64,256]{1,0:T(8,128)S(1)}, f32[64,256]{1,0:T(8,128)S(1)}, u32[]{:S(2)}, u32[]{:S(2)}) collective-permute-start(f32[64,256]{1,0:T(8,128)S(1)} %get-tuple-element.64), channel_id=1, source_target_pairs={{0,16},{4,20},{8,24},{12,28},{16,0},{20,4},{24,8},{28,12},{32,48},... | collective-permute-start | bytes 196616 | tf_op jit(solution)/shard_map/ppermute | solution.py:18
  11.3 7.9 %collective-permute-start.7 = (f32[128,256]{1,0:T(8,128)S(1)}, f32[128,256]{1,0:T(8,128)S(1)}, u32[]{:S(2)}, u32[]{:S(2)}) collective-permute-start(f32[128,256]{1,0:T(8,128)S(1)} %get-tuple-element.70), channel_id=1, source_target_pairs={{0,4},{4,0},{8,12},{12,8},{16,20},{20,16},{24,28},{28,24},{32,36},... | collective-permute-start | bytes 393224 | tf_op jit(solution)/shard_map/ppermute | solution.py:18
  14.8 10.6 %collective-permute-start.5 = (f32[32,256]{1,0:T(8,128)S(1)}, f32[32,256]{1,0:T(8,128)S(1)}, u32[]{:S(2)}, u32[]{:S(2)}) collective-permute-start(f32[32,256]{1,0:T(8,128)S(1)} %get-tuple-element.123), channel_id=1, source_target_pairs={{0,192},{4,196},{8,200},{12,204},{16,208},{20,212},{24,216},{28,22... | collective-permute-start | bytes 98312 | tf_op jit(solution)/shard_map/ppermute | solution.py:18
  17.8 7.5 %collective-permute-start.4 = (f32[32,256]{1,0:T(8,128)S(1)}, f32[32,256]{1,0:T(8,128)S(1)}, u32[]{:S(2)}, u32[]{:S(2)}) collective-permute-start(f32[32,256]{1,0:T(8,128)S(1)} %get-tuple-element.123), channel_id=1, source_target_pairs={{0,128},{4,132},{8,136},{12,140},{16,144},{20,148},{24,152},{28,15... | collective-permute-start | bytes 98312 | tf_op jit(solution)/shard_map/ppermute | solution.py:18
  18.5 6.9 %collective-permute-start.3 = (f32[32,256]{1,0:T(8,128)S(1)}, f32[32,256]{1,0:T(8,128)S(1)}, u32[]{:S(2)}, u32[]{:S(2)}) collective-permute-start(f32[32,256]{1,0:T(8,128)S(1)} %get-tuple-element.122), channel_id=1, source_target_pairs={{0,64},{4,68},{8,72},{12,76},{16,80},{20,84},{24,88},{28,92},{32,9... | collective-permute-start | bytes 98312 | tf_op jit(solution)/shard_map/ppermute | solution.py:18
  19.3 12.6 %collective-permute-start.8 = (f32[128,256]{1,0:T(8,128)S(1)}, f32[128,256]{1,0:T(8,128)S(1)}, u32[]{:S(2)}, u32[]{:S(2)}) collective-permute-start(f32[128,256]{1,0:T(8,128)S(1)} %add.36), channel_id=1, source_target_pairs={{0,12},{4,8},{8,4},{12,0},{16,28},{20,24},{24,20},{28,16},{32,44},... | collective-permute-start | bytes 393224 | tf_op jit(solution)/shard_map/ppermute | solution.py:18
  25.4 9.5 %collective-permute-start.6 = (f32[128,256]{1,0:T(8,128)S(1)}, f32[128,256]{1,0:T(8,128)S(1)}, u32[]{:S(2)}, u32[]{:S(2)}) collective-permute-start(f32[128,256]{1,0:T(8,128)S(1)} %pad_maximum_fusion), channel_id=1, source_target_pairs={{0,4},{4,0},{8,12},{12,8},{16,20},{20,16},{24,28},{28,24},{32,36},... | collective-permute-start | bytes 393224 | tf_op jit(solution)/shard_map/ppermute | solution.py:18
  25.9 23.5 %copy-start = (f32[6,1024,128]{2,1,0:T(8,128)S(1)}, f32[6,1024,128]{2,1,0:T(8,128)}, u32[]{:S(2)}) copy-start(f32[6,1024,128]{2,1,0:T(8,128)} %u_ref.1) | copy-start | bytes 9437188
  28.3 13.4 %collective-permute-start.11 = (f32[128,256]{1,0:T(8,128)S(1)}, f32[128,256]{1,0:T(8,128)S(1)}, u32[]{:S(2)}, u32[]{:S(2)}) collective-permute-start(f32[128,256]{1,0:T(8,128)S(1)} %get-tuple-element.79), channel_id=1, source_target_pairs={{0,12},{4,8},{8,4},{12,0},{16,28},{20,24},{24,20},{28,16},{32,44},... | collective-permute-start | bytes 393224 | tf_op jit(solution)/shard_map/ppermute | solution.py:18
  34.9 9.7 %collective-permute-start.9 = (f32[128,256]{1,0:T(8,128)S(1)}, f32[128,256]{1,0:T(8,128)S(1)}, u32[]{:S(2)}, u32[]{:S(2)}) collective-permute-start(f32[128,256]{1,0:T(8,128)S(1)} %add.35), channel_id=1, source_target_pairs={{0,12},{4,8},{8,4},{12,0},{16,28},{20,24},{24,20},{28,16},{32,44},... | collective-permute-start | bytes 393224 | tf_op jit(solution)/shard_map/ppermute | solution.py:18
  36.1 8.5 %collective-permute-start.10 = (f32[128,256]{1,0:T(8,128)S(1)}, f32[128,256]{1,0:T(8,128)S(1)}, u32[]{:S(2)}, u32[]{:S(2)}) collective-permute-start(f32[128,256]{1,0:T(8,128)S(1)} %add.37), channel_id=1, source_target_pairs={{0,16},{4,20},{8,24},{12,28},{16,0},{20,4},{24,8},{28,12},{32,48},... | collective-permute-start | bytes 393224 | tf_op jit(solution)/shard_map/ppermute | solution.py:18
  41.7 9.5 %collective-permute-start.12 = (f32[128,256]{1,0:T(8,128)S(1)}, f32[128,256]{1,0:T(8,128)S(1)}, u32[]{:S(2)}, u32[]{:S(2)}) collective-permute-start(f32[128,256]{1,0:T(8,128)S(1)} %get-tuple-element.81), channel_id=1, source_target_pairs={{0,4},{4,0},{8,12},{12,8},{16,20},{20,16},{24,28},{28,24},{32,36},... | collective-permute-start | bytes 393224 | tf_op jit(solution)/shard_map/ppermute | solution.py:18
  41.7 9.5 %collective-permute-start.13 = (f32[128,256]{1,0:T(8,128)S(1)}, f32[128,256]{1,0:T(8,128)S(1)}, u32[]{:S(2)}, u32[]{:S(2)}) collective-permute-start(f32[128,256]{1,0:T(8,128)S(1)} %collective-permute-done.11.o_ref), channel_id=1, source_target_pairs={{0,4},{4,0},{8,12},{12,8},{16,20},{20,16},{24,28},{28,24},{32,36},... | collective-permute-start | bytes 393224 | tf_op jit(solution)/shard_map/ppermute | solution.py:18
  44.6 9.4 %collective-permute-start.14 = (f32[128,256]{1,0:T(8,128)S(1)}, f32[128,256]{1,0:T(8,128)S(1)}, u32[]{:S(2)}, u32[]{:S(2)}) collective-permute-start(f32[128,256]{1,0:T(8,128)S(1)} %add.38.q0), channel_id=1, source_target_pairs={{0,16},{4,20},{8,24},{12,28},{16,0},{20,4},{24,8},{28,12},{32,48},... | collective-permute-start | bytes 393224 | tf_op jit(solution)/shard_map/ppermute | solution.py:18
  46.3 6.1 %collective-permute-start.16 = (f32[64,256]{1,0:T(8,128)S(1)}, f32[64,256]{1,0:T(8,128)S(1)}, u32[]{:S(2)}, u32[]{:S(2)}) collective-permute-start(f32[64,256]{1,0:T(8,128)S(1)} %slice.28), channel_id=1, source_target_pairs={{0,32},{4,36},{8,40},{12,44},{16,48},{20,52},{24,56},{28,60},{32,0... | collective-permute-start | bytes 196616 | tf_op jit(solution)/shard_map/ppermute | solution.py:18
  48.6 5.5 %collective-permute-start.15 = (f32[64,256]{1,0:T(8,128)S(1)}, f32[64,256]{1,0:T(8,128)S(1)}, u32[]{:S(2)}, u32[]{:S(2)}) collective-permute-start(f32[64,256]{1,0:T(8,128)S(1)} %slice.28), channel_id=1, source_target_pairs={{0,48},{4,52},{8,56},{12,60},{16,32},{20,36},{24,40},{28,44},{32,1... | collective-permute-start | bytes 196616 | tf_op jit(solution)/shard_map/ppermute | solution.py:18
  55.8 2.7 %collective-permute-start.17 = (f32[1024,256]{1,0:T(8,128)S(1)}, f32[1024,256]{1,0:T(8,128)S(1)}, u32[]{:S(2)}, u32[]{:S(2)}) collective-permute-start(f32[1024,256]{1,0:T(8,128)S(1)} %get-tuple-element.84.refs_0_), channel_id=1, source_target_pairs={{0,1},{1,0},{2,3},{3,2},{4,5},{5,4},{6,7},{7,6},{8,9},{9,8},{10,11... | collective-permute-start | bytes 3145736 | tf_op jit(solution)/shard_map/ppermute | solution.py:18
  55.9 14.8 %collective-permute-start.18 = (f32[1024,128]{1,0:T(8,128)S(1)}, f32[1024,128]{1,0:T(8,128)S(1)}, u32[]{:S(2)}, u32[]{:S(2)}) collective-permute-start(f32[1024,128]{1,0:T(8,128)S(1)} %get-tuple-element.86), channel_id=1, source_target_pairs={{0,2},{1,3},{2,0},{3,1},{4,6},{5,7},{6,4},{7,5},{8,10},{9,11},{10,... | collective-permute-start | bytes 1572872 | tf_op jit(solution)/shard_map/ppermute | solution.py:18
  56.0 25.5 %collective-permute-start.22 = (f32[1024,128]{1,0:T(8,128)S(1)}, f32[1024,128]{1,0:T(8,128)S(1)}, u32[]{:S(2)}, u32[]{:S(2)}) collective-permute-start(f32[1024,128]{1,0:T(8,128)S(1)} %get-tuple-element.95), channel_id=1, source_target_pairs={{0,2},{1,3},{2,0},{3,1},{4,6},{5,7},{6,4},{7,5},{8,10},{9,11},{10,... | collective-permute-start | bytes 1572872 | tf_op jit(solution)/shard_map/ppermute | solution.py:18
  60.6 10.2 %collective-permute-start.19 = (f32[2,64,256]{2,1,0:T(8,128)S(1)}, f32[2,64,256]{2,1,0:T(8,128)S(1)}, u32[]{:S(2)}, u32[]{:S(2)}) collective-permute-start(f32[2,64,256]{2,1,0:T(8,128)S(1)} %get-tuple-element.88), channel_id=1, source_target_pairs={{0,32},{4,36},{8,40},{12,44},{16,48},{20,52},{24,56},{28,60},{32,0... | collective-permute-start | bytes 393224 | tf_op jit(solution)/shard_map/ppermute | solution.py:18
  61.3 9.4 %collective-permute-start.20 = (f32[2,64,256]{2,1,0:T(8,128)S(1)}, f32[2,64,256]{2,1,0:T(8,128)S(1)}, u32[]{:S(2)}, u32[]{:S(2)}) collective-permute-start(f32[2,64,256]{2,1,0:T(8,128)S(1)} %get-tuple-element.89), channel_id=1, source_target_pairs={{0,16},{4,20},{8,24},{12,28},{16,0},{20,4},{24,8},{28,12},{32,48},... | collective-permute-start | bytes 393224 | tf_op jit(solution)/shard_map/ppermute | solution.py:18
  62.3 8.5 %collective-permute-start.21 = (f32[2,64,256]{2,1,0:T(8,128)S(1)}, f32[2,64,256]{2,1,0:T(8,128)S(1)}, u32[]{:S(2)}, u32[]{:S(2)}) collective-permute-start(f32[2,64,256]{2,1,0:T(8,128)S(1)} %get-tuple-element.90), channel_id=1, source_target_pairs={{0,48},{4,52},{8,56},{12,60},{16,32},{20,36},{24,40},{28,44},{32,1... | collective-permute-start | bytes 393224 | tf_op jit(solution)/shard_map/ppermute | solution.py:18
  71.5 10.0 %collective-permute-start.23 = (f32[2,32,256]{2,1,0:T(8,128)S(1)}, f32[2,32,256]{2,1,0:T(8,128)S(1)}, u32[]{:S(2)}, u32[]{:S(2)}) collective-permute-start(f32[2,32,256]{2,1,0:T(8,128)S(1)} %get-tuple-element.98), channel_id=1, source_target_pairs={{0,32},{4,36},{8,40},{12,44},{16,48},{20,52},{24,56},{28,60},{32,0... | collective-permute-start | bytes 196616 | tf_op jit(solution)/shard_map/ppermute | solution.py:18
  72.3 9.2 %collective-permute-start.24 = (f32[2,32,256]{2,1,0:T(8,128)S(1)}, f32[2,32,256]{2,1,0:T(8,128)S(1)}, u32[]{:S(2)}, u32[]{:S(2)}) collective-permute-start(f32[2,32,256]{2,1,0:T(8,128)S(1)} %get-tuple-element.99), channel_id=1, source_target_pairs={{0,16},{4,20},{8,24},{12,28},{16,0},{20,4},{24,8},{28,12},{32,48},... | collective-permute-start | bytes 196616 | tf_op jit(solution)/shard_map/ppermute | solution.py:18
  73.3 8.3 %collective-permute-start.25 = (f32[2,32,256]{2,1,0:T(8,128)S(1)}, f32[2,32,256]{2,1,0:T(8,128)S(1)}, u32[]{:S(2)}, u32[]{:S(2)}) collective-permute-start(f32[2,32,256]{2,1,0:T(8,128)S(1)} %get-tuple-element.100), channel_id=1, source_target_pairs={{0,48},{4,52},{8,56},{12,60},{16,32},{20,36},{24,40},{28,44},{32,1... | collective-permute-start | bytes 196616 | tf_op jit(solution)/shard_map/ppermute | solution.py:18
  82.2 6.3 %collective-permute-start.26 = (f32[2,32,256]{2,1,0:T(8,128)S(1)}, f32[2,32,256]{2,1,0:T(8,128)S(1)}, u32[]{:S(2)}, u32[]{:S(2)}) collective-permute-start(f32[2,32,256]{2,1,0:T(8,128)S(1)} %get-tuple-element.107), channel_id=1, source_target_pairs={{0,32},{4,36},{8,40},{12,44},{16,48},{20,52},{24,56},{28,60},{32,0... | collective-permute-start | bytes 196616 | tf_op jit(solution)/shard_map/ppermute | solution.py:18
  83.3 5.2 %collective-permute-start.27 = (f32[2,32,256]{2,1,0:T(8,128)S(1)}, f32[2,32,256]{2,1,0:T(8,128)S(1)}, u32[]{:S(2)}, u32[]{:S(2)}) collective-permute-start(f32[2,32,256]{2,1,0:T(8,128)S(1)} %get-tuple-element.108), channel_id=1, source_target_pairs={{0,16},{4,20},{8,24},{12,28},{16,0},{20,4},{24,8},{28,12},{32,48},... | collective-permute-start | bytes 196616 | tf_op jit(solution)/shard_map/ppermute | solution.py:18
  84.2 5.5 %collective-permute-start.28 = (f32[2,32,256]{2,1,0:T(8,128)S(1)}, f32[2,32,256]{2,1,0:T(8,128)S(1)}, u32[]{:S(2)}, u32[]{:S(2)}) collective-permute-start(f32[2,32,256]{2,1,0:T(8,128)S(1)} %get-tuple-element.109), channel_id=1, source_target_pairs={{0,48},{4,52},{8,56},{12,60},{16,32},{20,36},{24,40},{28,44},{32,1... | collective-permute-start | bytes 196616 | tf_op jit(solution)/shard_map/ppermute | solution.py:18
  89.8 1.3 %collective-permute-start.29 = (f32[64,256]{1,0:T(8,128)S(1)}, f32[64,256]{1,0:T(8,128)S(1)}, u32[]{:S(2)}, u32[]{:S(2)}) collective-permute-start(f32[64,256]{1,0:T(8,128)S(1)} %get-tuple-element.111), channel_id=1, source_target_pairs={{0,1},{1,0},{2,3},{3,2},{4,5},{5,4},{6,7},{7,6},{8,9},{9,8},{10,11... | collective-permute-start | bytes 196616 | tf_op jit(solution)/shard_map/ppermute | solution.py:18
  91.2 5.9 %collective-permute-start.30 = (f32[64,256]{1,0:T(8,128)S(1)}, f32[64,256]{1,0:T(8,128)S(1)}, u32[]{:S(2)}, u32[]{:S(2)}) collective-permute-start(f32[64,256]{1,0:T(8,128)S(1)} %get-tuple-element.113), channel_id=1, source_target_pairs={{0,128},{4,132},{8,136},{12,140},{16,144},{20,148},{24,152},{28,15... | collective-permute-start | bytes 196616 | tf_op jit(solution)/shard_map/ppermute | solution.py:18
  94.2 4.3 %collective-permute-start.31 = (f32[64,256]{1,0:T(8,128)S(1)}, f32[64,256]{1,0:T(8,128)S(1)}, u32[]{:S(2)}, u32[]{:S(2)}) collective-permute-start(f32[64,256]{1,0:T(8,128)S(1)} %get-tuple-element.114), channel_id=1, source_target_pairs={{0,64},{4,68},{8,72},{12,76},{16,80},{20,84},{24,88},{28,92},{32,9... | collective-permute-start | bytes 196616 | tf_op jit(solution)/shard_map/ppermute | solution.py:18
  94.9 5.5 %collective-permute-start.32 = (f32[64,256]{1,0:T(8,128)S(1)}, f32[64,256]{1,0:T(8,128)S(1)}, u32[]{:S(2)}, u32[]{:S(2)}) collective-permute-start(f32[64,256]{1,0:T(8,128)S(1)} %get-tuple-element.115), channel_id=1, source_target_pairs={{0,192},{4,196},{8,200},{12,204},{16,208},{20,212},{24,216},{28,22... | collective-permute-start | bytes 196616 | tf_op jit(solution)/shard_map/ppermute | solution.py:18
  100.4 7.2 %collective-permute-start.33 = (f32[32,256]{1,0:T(8,128)S(1)}, f32[32,256]{1,0:T(8,128)S(1)}, u32[]{:S(2)}, u32[]{:S(2)}) collective-permute-start(f32[32,256]{1,0:T(8,128)S(1)} %get-tuple-element.117), channel_id=1, source_target_pairs={{0,12},{4,8},{8,4},{12,0},{16,28},{20,24},{24,20},{28,16},{32,44},... | collective-permute-start | bytes 98312 | tf_op jit(solution)/shard_map/ppermute | solution.py:18
  107.6 4.7 %collective-permute-start.34 = (f32[16,256]{1,0:T(8,128)S(1)}, f32[16,256]{1,0:T(8,128)S(1)}, u32[]{:S(2)}, u32[]{:S(2)}) collective-permute-start(f32[16,256]{1,0:T(8,128)S(1)} %get-tuple-element.119), channel_id=1, source_target_pairs={{0,4},{4,0},{8,12},{12,8},{16,20},{20,16},{24,28},{28,24},{32,36},... | collective-permute-start | bytes 49160 | tf_op jit(solution)/shard_map/ppermute | solution.py:18

commit v12 on v11

--- a/solution.py
+++ b/solution.py
@@ -63,7 +63,7 @@
     return leaf >> 4, (leaf >> 2) & 3, leaf & 3
 
 
-CUTS = 4
+CUTS = 8
 
 
 def project(columns, probes, first, outs, emit):

time: 113 us -> 114 us (level)
  no operation moved by 1% of the time
where the time goes in v12:
time: 114 us; the launch traced here: 113 us
  starting transfers between devices  56.7 us (50%)
  waiting for transfers between devices  38.4 us (34%)
  Pallas kernels  14 us (12%)
  matrix products  2.39 us (2%)
    ppermute x35, starting transfers between devices, swap(): return lax.ppermute(value, axis, pairs)  56.7 us
    ppermute x35, waiting for transfers between devices, swap(): return lax.ppermute(value, axis, pairs)  38.4 us
    pallas_call x11, Pallas kernels, call(): pl.pallas_call(body, out_shape=outs, grid=grid, in_specs=specs, out_specs...  14 us
    dot_general x1, matrix products, near_product(): return jnp.dot(masked, probes, precision=HIGH, preferred_element_type=F32)  2.39 us
  transfers between devices with their start and end apart: 35, of which 16 were waited for; matrix products, arithmetic and copies ran while one was open for 3% of the time, Pallas kernels for 7%

profile of v12, /device:TPU:32, one launch (start us, length us, event | category | flops | bytes accessed | tf_op | source)
XLA Modules:
  0.0 113.4 jit_solution(10171235987103704258)
XLA Ops:
  0.6 3.4 %shard_map.68 = (f32[64,256]{1,0:T(8,128)S(1)}, f32[64,256]{1,0:T(8,128)S(1)}, f32[128,256]{1,0:T(8,128)S(1)}, f32[128,256]{1,0:T(8,128)S(1)}) custom-call(f32[6,1024,128]{2,1,0:T(8,128)} %c_hbm.3, f32[1024,256]{1,0:T(8,128)} %p_hbm.3), custom_call_target="tpu_custom_call" | custom-call | flops 603979776 | bytes 4587520 | tf_op jit(solution)/shard_map/pallas_call | solution.py:49
  4.0 3.1 %collective-permute-start = (f32[128,256]{1,0:T(8,128)S(1)}, f32[128,256]{1,0:T(8,128)S(1)}, u32[]{:S(2)}, u32[]{:S(2)}) collective-permute-start(f32[128,256]{1,0:T(8,128)S(1)} %get-tuple-element.61), channel_id=1, source_target_pairs={{0,32},{4,36},{8,40},{12,44},{16,48},{20,52},{24,56},{28,60},{32,0... | collective-permute-start | bytes 393224 | tf_op jit(solution)/shard_map/ppermute | solution.py:18
  7.2 1.1 %collective-permute-start.1 = (f32[128,256]{1,0:T(8,128)S(1)}, f32[128,256]{1,0:T(8,128)S(1)}, u32[]{:S(2)}, u32[]{:S(2)}) collective-permute-start(f32[128,256]{1,0:T(8,128)S(1)} %get-tuple-element.62), channel_id=1, source_target_pairs={{0,48},{4,52},{8,56},{12,60},{16,32},{20,36},{24,40},{28,44},{32,1... | collective-permute-start | bytes 393224 | tf_op jit(solution)/shard_map/ppermute | solution.py:18
  8.3 3.5 %shard_map.69 = (f32[128,256]{1,0:T(8,128)S(1)}, f32[128,256]{1,0:T(8,128)S(1)}, f32[128,256]{1,0:T(8,128)S(1)}) custom-call(f32[6,1024,128]{2,1,0:T(8,128)} %c_hbm.3, f32[1024,256]{1,0:T(8,128)} %p_hbm.3), custom_call_target="tpu_custom_call" | custom-call | flops 603979776 | bytes 4587520 | tf_op jit(solution)/shard_map/pallas_call | solution.py:49
  11.8 3.4 %collective-permute-start.7 = (f32[128,256]{1,0:T(8,128)S(1)}, f32[128,256]{1,0:T(8,128)S(1)}, u32[]{:S(2)}, u32[]{:S(2)}) collective-permute-start(f32[128,256]{1,0:T(8,128)S(1)} %get-tuple-element.70), channel_id=1, source_target_pairs={{0,4},{4,0},{8,12},{12,8},{16,20},{20,16},{24,28},{28,24},{32,36},... | collective-permute-start | bytes 393224 | tf_op jit(solution)/shard_map/ppermute | solution.py:18
  15.3 3.1 %collective-permute-start.5 = (f32[32,256]{1,0:T(8,128)S(1)}, f32[32,256]{1,0:T(8,128)S(1)}, u32[]{:S(2)}, u32[]{:S(2)}) collective-permute-start(f32[32,256]{1,0:T(8,128)S(1)} %get-tuple-element.123), channel_id=1, source_target_pairs={{0,192},{4,196},{8,200},{12,204},{16,208},{20,212},{24,216},{28,22... | collective-permute-start | bytes 98312 | tf_op jit(solution)/shard_map/ppermute | solution.py:18
  19.8 6.1 %collective-permute-start.8 = (f32[128,256]{1,0:T(8,128)S(1)}, f32[128,256]{1,0:T(8,128)S(1)}, u32[]{:S(2)}, u32[]{:S(2)}) collective-permute-start(f32[128,256]{1,0:T(8,128)S(1)} %add.36), channel_id=1, source_target_pairs={{0,12},{4,8},{8,4},{12,0},{16,28},{20,24},{24,20},{28,16},{32,44},... | collective-permute-start | bytes 393224 | tf_op jit(solution)/shard_map/ppermute | solution.py:18
  26.4 2.4 %fusion.n_ref = f32[1024,256]{1,0:T(8,128)S(1)} fusion(f32[1024,256]{1,0:T(8,128)S(1)} %copy-done.1, f32[1024,1024]{1,0:T(8,128)S(1)} %copy-done.2, f32[128,8,8,128]{3,2,1,0:T(8,128)S(1)} %bitcast.8), kind=kOutput, calls=%fused_computation.1 | convolution fusion | flops 1611661312 | bytes 10485760 | tf_op jit(solution)/shard_map/dot_general | solution.py:338
  28.8 3.3 %collective-permute-start.11 = (f32[128,256]{1,0:T(8,128)S(1)}, f32[128,256]{1,0:T(8,128)S(1)}, u32[]{:S(2)}, u32[]{:S(2)}) collective-permute-start(f32[128,256]{1,0:T(8,128)S(1)} %get-tuple-element.79), channel_id=1, source_target_pairs={{0,12},{4,8},{8,4},{12,0},{16,28},{20,24},{24,20},{28,16},{32,44},... | collective-permute-start | bytes 393224 | tf_op jit(solution)/shard_map/ppermute | solution.py:18
  32.1 3.3 %collective-permute-done.6 = f32[128,256]{1,0:T(8,128)S(1)} collective-permute-done((f32[128,256]{1,0:T(8,128)S(1)}, f32[128,256]{1,0:T(8,128)S(1)}, u32[]{:S(2)}, u32[]{:S(2)}) %collective-permute-start.6) | collective-permute-done | bytes 131104 | tf_op jit(solution)/shard_map/ppermute | solution.py:18
  35.4 1.2 %collective-permute-start.9 = (f32[128,256]{1,0:T(8,128)S(1)}, f32[128,256]{1,0:T(8,128)S(1)}, u32[]{:S(2)}, u32[]{:S(2)}) collective-permute-start(f32[128,256]{1,0:T(8,128)S(1)} %add.35), channel_id=1, source_target_pairs={{0,12},{4,8},{8,4},{12,0},{16,28},{20,24},{24,20},{28,16},{32,44},... | collective-permute-start | bytes 393224 | tf_op jit(solution)/shard_map/ppermute | solution.py:18
  36.6 1.4 %collective-permute-start.10 = (f32[128,256]{1,0:T(8,128)S(1)}, f32[128,256]{1,0:T(8,128)S(1)}, u32[]{:S(2)}, u32[]{:S(2)}) collective-permute-start(f32[128,256]{1,0:T(8,128)S(1)} %add.37), channel_id=1, source_target_pairs={{0,16},{4,20},{8,24},{12,28},{16,0},{20,4},{24,8},{28,12},{32,48},... | collective-permute-start | bytes 393224 | tf_op jit(solution)/shard_map/ppermute | solution.py:18
  38.0 4.3 %collective-permute-done.11.o_ref = f32[128,256]{1,0:T(8,128)S(1)} collective-permute-done((f32[128,256]{1,0:T(8,128)S(1)}, f32[128,256]{1,0:T(8,128)S(1)}, u32[]{:S(2)}, u32[]{:S(2)}) %collective-permute-start.11) | collective-permute-done | bytes 131104 | tf_op jit(solution)/shard_map/ppermute | solution.py:18
  42.3 2.9 %collective-permute-start.13 = (f32[128,256]{1,0:T(8,128)S(1)}, f32[128,256]{1,0:T(8,128)S(1)}, u32[]{:S(2)}, u32[]{:S(2)}) collective-permute-start(f32[128,256]{1,0:T(8,128)S(1)} %collective-permute-done.11.o_ref), channel_id=1, source_target_pairs={{0,4},{4,0},{8,12},{12,8},{16,20},{20,16},{24,28},{28,24},{32,36},... | collective-permute-start | bytes 393224 | tf_op jit(solution)/shard_map/ppermute | solution.py:18
  45.3 1.7 %collective-permute-start.14 = (f32[128,256]{1,0:T(8,128)S(1)}, f32[128,256]{1,0:T(8,128)S(1)}, u32[]{:S(2)}, u32[]{:S(2)}) collective-permute-start(f32[128,256]{1,0:T(8,128)S(1)} %add.38.q0), channel_id=1, source_target_pairs={{0,16},{4,20},{8,24},{12,28},{16,0},{20,4},{24,8},{28,12},{32,48},... | collective-permute-start | bytes 393224 | tf_op jit(solution)/shard_map/ppermute | solution.py:18
  47.0 2.1 %collective-permute-start.16 = (f32[64,256]{1,0:T(8,128)S(1)}, f32[64,256]{1,0:T(8,128)S(1)}, u32[]{:S(2)}, u32[]{:S(2)}) collective-permute-start(f32[64,256]{1,0:T(8,128)S(1)} %slice.28), channel_id=1, source_target_pairs={{0,32},{4,36},{8,40},{12,44},{16,48},{20,52},{24,56},{28,60},{32,0... | collective-permute-start | bytes 196616 | tf_op jit(solution)/shard_map/ppermute | solution.py:18
  49.0 1.0 collective-permute-start.15
  50.1 1.7 %shard_map.70 = (f32[1024,256]{1,0:T(8,128)S(1)}, bf16[1024,640]{1,0:T(8,128)(2,1)S(1)}, bf16[1024,640]{1,0:T(8,128)(2,1)S(1)}) custom-call(f32[1024,256]{1,0:T(8,128)S(1)} %fusion.n_ref, f32[6,1024,128]{2,1,0:T(8,128)S(1)} %copy-done, f32[128,256]{1,0:T(8,128)S(1)} %collective-permute-done.10.t_ref), custom_call_target="tpu_custom_call" | custom-call | flops 201326592 | bytes 10616832 | tf_op jit(solution)/shard_map/pallas_call | solution.py:49
  51.8 0.9 collective-permute-done.16.q2
  52.8 1.8 %collective-permute-done.15.q3 = f32[64,256]{1,0:T(8,128)S(1)} collective-permute-done((f32[64,256]{1,0:T(8,128)S(1)}, f32[64,256]{1,0:T(8,128)S(1)}, u32[]{:S(2)}, u32[]{:S(2)}) %collective-permute-start.15) | collective-permute-done | bytes 65568 | tf_op jit(solution)/shard_map/ppermute | solution.py:18
  54.5 1.8 %shard_map.71 = (f32[1024,256]{1,0:T(8,128)S(1)}, f32[1024,128]{1,0:T(8,128)S(1)}, f32[1024,128]{1,0:T(8,128)S(1)}) custom-call(f32[1024,256]{1,0:T(8,128)S(1)} %get-tuple-element.76.b_ref, bf16[1024,640]{1,0:T(8,128)(2,1)S(1)} %get-tuple-element.77.h_ref, bf16[1024,640]{1,0:T(8,128)(2,1)S(1)} %get-tuple-element.78.l_ref, ...), custom_call_target="tpu_custom_call" | custom-call | flops 1006632960 | bytes 9175040 | tf_op jit(solution)/shard_map/pallas_call | solution.py:49
  56.5 2.0 %collective-permute-start.22 = (f32[1024,128]{1,0:T(8,128)S(1)}, f32[1024,128]{1,0:T(8,128)S(1)}, u32[]{:S(2)}, u32[]{:S(2)}) collective-permute-start(f32[1024,128]{1,0:T(8,128)S(1)} %get-tuple-element.95), channel_id=1, source_target_pairs={{0,2},{1,3},{2,0},{3,1},{4,6},{5,7},{6,4},{7,5},{8,10},{9,11},{10,... | collective-permute-start | bytes 1572872 | tf_op jit(solution)/shard_map/ppermute | solution.py:18
  59.0 2.0 %shard_map.72 = (f32[2,64,256]{2,1,0:T(8,128)S(1)}, f32[2,64,256]{2,1,0:T(8,128)S(1)}, f32[2,64,256]{2,1,0:T(8,128)S(1)}, f32[2,64,256]{2,1,0:T(8,128)S(1)}, f32[1024,256]{1,0:T(8,128)}) custom-call(f32[1024,256]{1,0:T(8,128)S(1)} %get-tuple-element.84.refs_0_, f32[1024,256]{1,0:T(8,128)S(1)} %collective-permute-done.17.refs_1_), custom_call_target="tpu_custom_call" | custom-call | flops 805306368 | bytes 3670016 | tf_op jit(solution)/shard_map/pallas_call | solution.py:49
  61.1 1.0 collective-permute-start.19
  62.0 0.9 collective-permute-start.20
  63.0 2.2 %collective-permute-start.21 = (f32[2,64,256]{2,1,0:T(8,128)S(1)}, f32[2,64,256]{2,1,0:T(8,128)S(1)}, u32[]{:S(2)}, u32[]{:S(2)}) collective-permute-start(f32[2,64,256]{2,1,0:T(8,128)S(1)} %get-tuple-element.90), channel_id=1, source_target_pairs={{0,48},{4,52},{8,56},{12,60},{16,32},{20,36},{24,40},{28,44},{32,1... | collective-permute-start | bytes 393224 | tf_op jit(solution)/shard_map/ppermute | solution.py:18
  65.2 6.1 %collective-permute-done.18.refs_2_ = f32[1024,128]{1,0:T(8,128)S(1)} collective-permute-done((f32[1024,128]{1,0:T(8,128)S(1)}, f32[1024,128]{1,0:T(8,128)S(1)}, u32[]{:S(2)}, u32[]{:S(2)}) %collective-permute-start.18) | collective-permute-done | bytes 524320 | tf_op jit(solution)/shard_map/ppermute | solution.py:18
  71.2 0.7 shard_map.73
  71.9 1.1 collective-permute-start.23
  73.0 0.9 collective-permute-start.24
  73.9 2.2 %collective-permute-start.25 = (f32[2,32,256]{2,1,0:T(8,128)S(1)}, f32[2,32,256]{2,1,0:T(8,128)S(1)}, u32[]{:S(2)}, u32[]{:S(2)}) collective-permute-start(f32[2,32,256]{2,1,0:T(8,128)S(1)} %get-tuple-element.100), channel_id=1, source_target_pairs={{0,48},{4,52},{8,56},{12,60},{16,32},{20,36},{24,40},{28,44},{32,1... | collective-permute-start | bytes 196616 | tf_op jit(solution)/shard_map/ppermute | solution.py:18
  76.1 5.9 %collective-permute-done.22.refs_2_ = f32[1024,128]{1,0:T(8,128)S(1)} collective-permute-done((f32[1024,128]{1,0:T(8,128)S(1)}, f32[1024,128]{1,0:T(8,128)S(1)}, u32[]{:S(2)}, u32[]{:S(2)}) %collective-permute-start.22) | collective-permute-done | bytes 524320 | tf_op jit(solution)/shard_map/ppermute | solution.py:18
  82.0 0.7 shard_map.74
  82.7 1.3 %collective-permute-start.26 = (f32[2,32,256]{2,1,0:T(8,128)S(1)}, f32[2,32,256]{2,1,0:T(8,128)S(1)}, u32[]{:S(2)}, u32[]{:S(2)}) collective-permute-start(f32[2,32,256]{2,1,0:T(8,128)S(1)} %get-tuple-element.107), channel_id=1, source_target_pairs={{0,32},{4,36},{8,40},{12,44},{16,48},{20,52},{24,56},{28,60},{32,0... | collective-permute-start | bytes 196616 | tf_op jit(solution)/shard_map/ppermute | solution.py:18
  84.0 0.9 collective-permute-start.27
  84.9 2.2 %collective-permute-start.28 = (f32[2,32,256]{2,1,0:T(8,128)S(1)}, f32[2,32,256]{2,1,0:T(8,128)S(1)}, u32[]{:S(2)}, u32[]{:S(2)}) collective-permute-start(f32[2,32,256]{2,1,0:T(8,128)S(1)} %get-tuple-element.109), channel_id=1, source_target_pairs={{0,48},{4,52},{8,56},{12,60},{16,32},{20,36},{24,40},{28,44},{32,1... | collective-permute-start | bytes 196616 | tf_op jit(solution)/shard_map/ppermute | solution.py:18
  87.1 1.9 %collective-permute-done.26.refs_9_ = f32[2,32,256]{2,1,0:T(8,128)S(1)} collective-permute-done((f32[2,32,256]{2,1,0:T(8,128)S(1)}, f32[2,32,256]{2,1,0:T(8,128)S(1)}, u32[]{:S(2)}, u32[]{:S(2)}) %collective-permute-start.26) | collective-permute-done | bytes 65568 | tf_op jit(solution)/shard_map/ppermute | solution.py:18
  89.0 1.4 %collective-permute-done.28.refs_11_ = f32[2,32,256]{2,1,0:T(8,128)S(1)} collective-permute-done((f32[2,32,256]{2,1,0:T(8,128)S(1)}, f32[2,32,256]{2,1,0:T(8,128)S(1)}, u32[]{:S(2)}, u32[]{:S(2)}) %collective-permute-start.28) | collective-permute-done | bytes 65568 | tf_op jit(solution)/shard_map/ppermute | solution.py:18
  90.5 1.2 %collective-permute-done.29.got_ref = f32[64,256]{1,0:T(8,128)S(1)} collective-permute-done((f32[64,256]{1,0:T(8,128)S(1)}, f32[64,256]{1,0:T(8,128)S(1)}, u32[]{:S(2)}, u32[]{:S(2)}) %collective-permute-start.29) | collective-permute-done | bytes 65568 | tf_op jit(solution)/shard_map/ppermute | solution.py:18
  91.8 2.9 %collective-permute-start.30 = (f32[64,256]{1,0:T(8,128)S(1)}, f32[64,256]{1,0:T(8,128)S(1)}, u32[]{:S(2)}, u32[]{:S(2)}) collective-permute-start(f32[64,256]{1,0:T(8,128)S(1)} %get-tuple-element.113), channel_id=1, source_target_pairs={{0,128},{4,132},{8,136},{12,140},{16,144},{20,148},{24,152},{28,15... | collective-permute-start | bytes 196616 | tf_op jit(solution)/shard_map/ppermute | solution.py:18
  94.7 0.7 collective-permute-start.31
  96.0 1.7 %collective-permute-done.30.refs_1_ = f32[64,256]{1,0:T(8,128)S(1)} collective-permute-done((f32[64,256]{1,0:T(8,128)S(1)}, f32[64,256]{1,0:T(8,128)S(1)}, u32[]{:S(2)}, u32[]{:S(2)}) %collective-permute-start.30) | collective-permute-done | bytes 65568 | tf_op jit(solution)/shard_map/ppermute | solution.py:18
  97.7 1.3 %collective-permute-done.31.refs_2_ = f32[64,256]{1,0:T(8,128)S(1)} collective-permute-done((f32[64,256]{1,0:T(8,128)S(1)}, f32[64,256]{1,0:T(8,128)S(1)}, u32[]{:S(2)}, u32[]{:S(2)}) %collective-permute-start.31) | collective-permute-done | bytes 65568 | tf_op jit(solution)/shard_map/ppermute | solution.py:18
  99.1 1.8 %collective-permute-done.32.refs_3_ = f32[64,256]{1,0:T(8,128)S(1)} collective-permute-done((f32[64,256]{1,0:T(8,128)S(1)}, f32[64,256]{1,0:T(8,128)S(1)}, u32[]{:S(2)}, u32[]{:S(2)}) %collective-permute-start.32) | collective-permute-done | bytes 65568 | tf_op jit(solution)/shard_map/ppermute | solution.py:18
  100.9 5.2 %collective-permute-start.33 = (f32[32,256]{1,0:T(8,128)S(1)}, f32[32,256]{1,0:T(8,128)S(1)}, u32[]{:S(2)}, u32[]{:S(2)}) collective-permute-start(f32[32,256]{1,0:T(8,128)S(1)} %get-tuple-element.117), channel_id=1, source_target_pairs={{0,12},{4,8},{8,4},{12,0},{16,28},{20,24},{24,20},{28,16},{32,44},... | collective-permute-start | bytes 98312 | tf_op jit(solution)/shard_map/ppermute | solution.py:18
  106.1 1.9 %collective-permute-done.33.refs_1_ = f32[32,256]{1,0:T(8,128)S(1)} collective-permute-done((f32[32,256]{1,0:T(8,128)S(1)}, f32[32,256]{1,0:T(8,128)S(1)}, u32[]{:S(2)}, u32[]{:S(2)}) %collective-permute-start.33) | collective-permute-done | bytes 32800 | tf_op jit(solution)/shard_map/ppermute | solution.py:18
  108.1 0.7 collective-permute-start.34
  108.8 4.0 %collective-permute-done.34 = f32[16,256]{1,0:T(8,128)S(1)} collective-permute-done((f32[16,256]{1,0:T(8,128)S(1)}, f32[16,256]{1,0:T(8,128)S(1)}, u32[]{:S(2)}, u32[]{:S(2)}) %collective-permute-start.34) | collective-permute-done | bytes 16416 | tf_op jit(solution)/shard_map/ppermute | solution.py:18
  (54 shorter events, 4.2 us)
Async XLA Ops:
  0.6 18.8 %copy-start.3 = (s32[1,8,8]{2,1,0:T(8,128)S(1)}, s32[1,8,8]{2,1,0:T(8,128)}, u32[]{:S(2)}) copy-start(s32[1,8,8]{2,1,0:T(8,128)} %param.6) | copy-start | bytes 772
  4.0 11.2 %collective-permute-start = (f32[128,256]{1,0:T(8,128)S(1)}, f32[128,256]{1,0:T(8,128)S(1)}, u32[]{:S(2)}, u32[]{:S(2)}) collective-permute-start(f32[128,256]{1,0:T(8,128)S(1)} %get-tuple-element.61), channel_id=1, source_target_pairs={{0,32},{4,36},{8,40},{12,44},{16,48},{20,52},{24,56},{28,60},{32,0... | collective-permute-start | bytes 393224 | tf_op jit(solution)/shard_map/ppermute | solution.py:18
  7.2 8.0 %collective-permute-start.1 = (f32[128,256]{1,0:T(8,128)S(1)}, f32[128,256]{1,0:T(8,128)S(1)}, u32[]{:S(2)}, u32[]{:S(2)}) collective-permute-start(f32[128,256]{1,0:T(8,128)S(1)} %get-tuple-element.62), channel_id=1, source_target_pairs={{0,48},{4,52},{8,56},{12,60},{16,32},{20,36},{24,40},{28,44},{32,1... | collective-permute-start | bytes 393224 | tf_op jit(solution)/shard_map/ppermute | solution.py:18
  8.3 18.1 %copy-start.1 = (f32[1024,256]{1,0:T(8,128)S(1)}, f32[1024,256]{1,0:T(8,128)}, u32[]{:S(2)}) copy-start(f32[1024,256]{1,0:T(8,128)} %p_hbm.3) | copy-start | bytes 3145732
  8.3 18.1 %copy-start.2 = (f32[1024,1024]{1,0:T(8,128)S(1)}, f32[1024,1024]{1,0:T(8,128)}, u32[]{:S(2)}) copy-start(f32[1024,1024]{1,0:T(8,128)} %param.5) | copy-start | bytes 12582916
  8.3 6.9 %collective-permute-start.2 = (f32[64,256]{1,0:T(8,128)S(1)}, f32[64,256]{1,0:T(8,128)S(1)}, u32[]{:S(2)}, u32[]{:S(2)}) collective-permute-start(f32[64,256]{1,0:T(8,128)S(1)} %get-tuple-element.64), channel_id=1, source_target_pairs={{0,16},{4,20},{8,24},{12,28},{16,0},{20,4},{24,8},{28,12},{32,48},... | collective-permute-start | bytes 196616 | tf_op jit(solution)/shard_map/ppermute | solution.py:18
  11.8 7.9 %collective-permute-start.7 = (f32[128,256]{1,0:T(8,128)S(1)}, f32[128,256]{1,0:T(8,128)S(1)}, u32[]{:S(2)}, u32[]{:S(2)}) collective-permute-start(f32[128,256]{1,0:T(8,128)S(1)} %get-tuple-element.70), channel_id=1, source_target_pairs={{0,4},{4,0},{8,12},{12,8},{16,20},{20,16},{24,28},{28,24},{32,36},... | collective-permute-start | bytes 393224 | tf_op jit(solution)/shard_map/ppermute | solution.py:18
  15.3 10.6 %collective-permute-start.5 = (f32[32,256]{1,0:T(8,128)S(1)}, f32[32,256]{1,0:T(8,128)S(1)}, u32[]{:S(2)}, u32[]{:S(2)}) collective-permute-start(f32[32,256]{1,0:T(8,128)S(1)} %get-tuple-element.123), channel_id=1, source_target_pairs={{0,192},{4,196},{8,200},{12,204},{16,208},{20,212},{24,216},{28,22... | collective-permute-start | bytes 98312 | tf_op jit(solution)/shard_map/ppermute | solution.py:18
  18.4 7.5 %collective-permute-start.4 = (f32[32,256]{1,0:T(8,128)S(1)}, f32[32,256]{1,0:T(8,128)S(1)}, u32[]{:S(2)}, u32[]{:S(2)}) collective-permute-start(f32[32,256]{1,0:T(8,128)S(1)} %get-tuple-element.123), channel_id=1, source_target_pairs={{0,128},{4,132},{8,136},{12,140},{16,144},{20,148},{24,152},{28,15... | collective-permute-start | bytes 98312 | tf_op jit(solution)/shard_map/ppermute | solution.py:18
  19.0 6.9 %collective-permute-start.3 = (f32[32,256]{1,0:T(8,128)S(1)}, f32[32,256]{1,0:T(8,128)S(1)}, u32[]{:S(2)}, u32[]{:S(2)}) collective-permute-start(f32[32,256]{1,0:T(8,128)S(1)} %get-tuple-element.122), channel_id=1, source_target_pairs={{0,64},{4,68},{8,72},{12,76},{16,80},{20,84},{24,88},{28,92},{32,9... | collective-permute-start | bytes 98312 | tf_op jit(solution)/shard_map/ppermute | solution.py:18
  19.8 12.3 %collective-permute-start.8 = (f32[128,256]{1,0:T(8,128)S(1)}, f32[128,256]{1,0:T(8,128)S(1)}, u32[]{:S(2)}, u32[]{:S(2)}) collective-permute-start(f32[128,256]{1,0:T(8,128)S(1)} %add.36), channel_id=1, source_target_pairs={{0,12},{4,8},{8,4},{12,0},{16,28},{20,24},{24,20},{28,16},{32,44},... | collective-permute-start | bytes 393224 | tf_op jit(solution)/shard_map/ppermute | solution.py:18
  25.9 9.5 %collective-permute-start.6 = (f32[128,256]{1,0:T(8,128)S(1)}, f32[128,256]{1,0:T(8,128)S(1)}, u32[]{:S(2)}, u32[]{:S(2)}) collective-permute-start(f32[128,256]{1,0:T(8,128)S(1)} %pad_maximum_fusion), channel_id=1, source_target_pairs={{0,4},{4,0},{8,12},{12,8},{16,20},{20,16},{24,28},{28,24},{32,36},... | collective-permute-start | bytes 393224 | tf_op jit(solution)/shard_map/ppermute | solution.py:18
  26.4 23.7 %copy-start = (f32[6,1024,128]{2,1,0:T(8,128)S(1)}, f32[6,1024,128]{2,1,0:T(8,128)}, u32[]{:S(2)}) copy-start(f32[6,1024,128]{2,1,0:T(8,128)} %u_ref.1) | copy-start | bytes 9437188
  28.8 13.5 %collective-permute-start.11 = (f32[128,256]{1,0:T(8,128)S(1)}, f32[128,256]{1,0:T(8,128)S(1)}, u32[]{:S(2)}, u32[]{:S(2)}) collective-permute-start(f32[128,256]{1,0:T(8,128)S(1)} %get-tuple-element.79), channel_id=1, source_target_pairs={{0,12},{4,8},{8,4},{12,0},{16,28},{20,24},{24,20},{28,16},{32,44},... | collective-permute-start | bytes 393224 | tf_op jit(solution)/shard_map/ppermute | solution.py:18
  35.4 9.9 %collective-permute-start.9 = (f32[128,256]{1,0:T(8,128)S(1)}, f32[128,256]{1,0:T(8,128)S(1)}, u32[]{:S(2)}, u32[]{:S(2)}) collective-permute-start(f32[128,256]{1,0:T(8,128)S(1)} %add.35), channel_id=1, source_target_pairs={{0,12},{4,8},{8,4},{12,0},{16,28},{20,24},{24,20},{28,16},{32,44},... | collective-permute-start | bytes 393224 | tf_op jit(solution)/shard_map/ppermute | solution.py:18
  36.6 8.7 %collective-permute-start.10 = (f32[128,256]{1,0:T(8,128)S(1)}, f32[128,256]{1,0:T(8,128)S(1)}, u32[]{:S(2)}, u32[]{:S(2)}) collective-permute-start(f32[128,256]{1,0:T(8,128)S(1)} %add.37), channel_id=1, source_target_pairs={{0,16},{4,20},{8,24},{12,28},{16,0},{20,4},{24,8},{28,12},{32,48},... | collective-permute-start | bytes 393224 | tf_op jit(solution)/shard_map/ppermute | solution.py:18
  42.3 9.5 %collective-permute-start.12 = (f32[128,256]{1,0:T(8,128)S(1)}, f32[128,256]{1,0:T(8,128)S(1)}, u32[]{:S(2)}, u32[]{:S(2)}) collective-permute-start(f32[128,256]{1,0:T(8,128)S(1)} %get-tuple-element.81), channel_id=1, source_target_pairs={{0,4},{4,0},{8,12},{12,8},{16,20},{20,16},{24,28},{28,24},{32,36},... | collective-permute-start | bytes 393224 | tf_op jit(solution)/shard_map/ppermute | solution.py:18
  42.3 9.5 %collective-permute-start.13 = (f32[128,256]{1,0:T(8,128)S(1)}, f32[128,256]{1,0:T(8,128)S(1)}, u32[]{:S(2)}, u32[]{:S(2)}) collective-permute-start(f32[128,256]{1,0:T(8,128)S(1)} %collective-permute-done.11.o_ref), channel_id=1, source_target_pairs={{0,4},{4,0},{8,12},{12,8},{16,20},{20,16},{24,28},{28,24},{32,36},... | collective-permute-start | bytes 393224 | tf_op jit(solution)/shard_map/ppermute | solution.py:18
  45.3 9.2 %collective-permute-start.14 = (f32[128,256]{1,0:T(8,128)S(1)}, f32[128,256]{1,0:T(8,128)S(1)}, u32[]{:S(2)}, u32[]{:S(2)}) collective-permute-start(f32[128,256]{1,0:T(8,128)S(1)} %add.38.q0), channel_id=1, source_target_pairs={{0,16},{4,20},{8,24},{12,28},{16,0},{20,4},{24,8},{28,12},{32,48},... | collective-permute-start | bytes 393224 | tf_op jit(solution)/shard_map/ppermute | solution.py:18
  47.0 5.8 %collective-permute-start.16 = (f32[64,256]{1,0:T(8,128)S(1)}, f32[64,256]{1,0:T(8,128)S(1)}, u32[]{:S(2)}, u32[]{:S(2)}) collective-permute-start(f32[64,256]{1,0:T(8,128)S(1)} %slice.28), channel_id=1, source_target_pairs={{0,32},{4,36},{8,40},{12,44},{16,48},{20,52},{24,56},{28,60},{32,0... | collective-permute-start | bytes 196616 | tf_op jit(solution)/shard_map/ppermute | solution.py:18
  49.0 5.5 %collective-permute-start.15 = (f32[64,256]{1,0:T(8,128)S(1)}, f32[64,256]{1,0:T(8,128)S(1)}, u32[]{:S(2)}, u32[]{:S(2)}) collective-permute-start(f32[64,256]{1,0:T(8,128)S(1)} %slice.28), channel_id=1, source_target_pairs={{0,48},{4,52},{8,56},{12,60},{16,32},{20,36},{24,40},{28,44},{32,1... | collective-permute-start | bytes 196616 | tf_op jit(solution)/shard_map/ppermute | solution.py:18
  56.3 2.7 %collective-permute-start.17 = (f32[1024,256]{1,0:T(8,128)S(1)}, f32[1024,256]{1,0:T(8,128)S(1)}, u32[]{:S(2)}, u32[]{:S(2)}) collective-permute-start(f32[1024,256]{1,0:T(8,128)S(1)} %get-tuple-element.84.refs_0_), channel_id=1, source_target_pairs={{0,1},{1,0},{2,3},{3,2},{4,5},{5,4},{6,7},{7,6},{8,9},{9,8},{10,11... | collective-permute-start | bytes 3145736 | tf_op jit(solution)/shard_map/ppermute | solution.py:18
  56.4 14.8 %collective-permute-start.18 = (f32[1024,128]{1,0:T(8,128)S(1)}, f32[1024,128]{1,0:T(8,128)S(1)}, u32[]{:S(2)}, u32[]{:S(2)}) collective-permute-start(f32[1024,128]{1,0:T(8,128)S(1)} %get-tuple-element.86), channel_id=1, source_target_pairs={{0,2},{1,3},{2,0},{3,1},{4,6},{5,7},{6,4},{7,5},{8,10},{9,11},{10,... | collective-permute-start | bytes 1572872 | tf_op jit(solution)/shard_map/ppermute | solution.py:18
  56.5 25.5 %collective-permute-start.22 = (f32[1024,128]{1,0:T(8,128)S(1)}, f32[1024,128]{1,0:T(8,128)S(1)}, u32[]{:S(2)}, u32[]{:S(2)}) collective-permute-start(f32[1024,128]{1,0:T(8,128)S(1)} %get-tuple-element.95), channel_id=1, source_target_pairs={{0,2},{1,3},{2,0},{3,1},{4,6},{5,7},{6,4},{7,5},{8,10},{9,11},{10,... | collective-permute-start | bytes 1572872 | tf_op jit(solution)/shard_map/ppermute | solution.py:18
  61.1 10.2 %collective-permute-start.19 = (f32[2,64,256]{2,1,0:T(8,128)S(1)}, f32[2,64,256]{2,1,0:T(8,128)S(1)}, u32[]{:S(2)}, u32[]{:S(2)}) collective-permute-start(f32[2,64,256]{2,1,0:T(8,128)S(1)} %get-tuple-element.88), channel_id=1, source_target_pairs={{0,32},{4,36},{8,40},{12,44},{16,48},{20,52},{24,56},{28,60},{32,0... | collective-permute-start | bytes 393224 | tf_op jit(solution)/shard_map/ppermute | solution.py:18
  62.0 9.2 %collective-permute-start.20 = (f32[2,64,256]{2,1,0:T(8,128)S(1)}, f32[2,64,256]{2,1,0:T(8,128)S(1)}, u32[]{:S(2)}, u32[]{:S(2)}) collective-permute-start(f32[2,64,256]{2,1,0:T(8,128)S(1)} %get-tuple-element.89), channel_id=1, source_target_pairs={{0,16},{4,20},{8,24},{12,28},{16,0},{20,4},{24,8},{28,12},{32,48},... | collective-permute-start | bytes 393224 | tf_op jit(solution)/shard_map/ppermute | solution.py:18
  63.0 8.3 %collective-permute-start.21 = (f32[2,64,256]{2,1,0:T(8,128)S(1)}, f32[2,64,256]{2,1,0:T(8,128)S(1)}, u32[]{:S(2)}, u32[]{:S(2)}) collective-permute-start(f32[2,64,256]{2,1,0:T(8,128)S(1)} %get-tuple-element.90), channel_id=1, source_target_pairs={{0,48},{4,52},{8,56},{12,60},{16,32},{20,36},{24,40},{28,44},{32,1... | collective-permute-start | bytes 393224 | tf_op jit(solution)/shard_map/ppermute | solution.py:18
  71.9 10.0 %collective-permute-start.23 = (f32[2,32,256]{2,1,0:T(8,128)S(1)}, f32[2,32,256]{2,1,0:T(8,128)S(1)}, u32[]{:S(2)}, u32[]{:S(2)}) collective-permute-start(f32[2,32,256]{2,1,0:T(8,128)S(1)} %get-tuple-element.98), channel_id=1, source_target_pairs={{0,32},{4,36},{8,40},{12,44},{16,48},{20,52},{24,56},{28,60},{32,0... | collective-permute-start | bytes 196616 | tf_op jit(solution)/shard_map/ppermute | solution.py:18
  73.0 9.0 %collective-permute-start.24 = (f32[2,32,256]{2,1,0:T(8,128)S(1)}, f32[2,32,256]{2,1,0:T(8,128)S(1)}, u32[]{:S(2)}, u32[]{:S(2)}) collective-permute-start(f32[2,32,256]{2,1,0:T(8,128)S(1)} %get-tuple-element.99), channel_id=1, source_target_pairs={{0,16},{4,20},{8,24},{12,28},{16,0},{20,4},{24,8},{28,12},{32,48},... | collective-permute-start | bytes 196616 | tf_op jit(solution)/shard_map/ppermute | solution.py:18
  73.9 8.1 %collective-permute-start.25 = (f32[2,32,256]{2,1,0:T(8,128)S(1)}, f32[2,32,256]{2,1,0:T(8,128)S(1)}, u32[]{:S(2)}, u32[]{:S(2)}) collective-permute-start(f32[2,32,256]{2,1,0:T(8,128)S(1)} %get-tuple-element.100), channel_id=1, source_target_pairs={{0,48},{4,52},{8,56},{12,60},{16,32},{20,36},{24,40},{28,44},{32,1... | collective-permute-start | bytes 196616 | tf_op jit(solution)/shard_map/ppermute | solution.py:18
  82.7 6.3 %collective-permute-start.26 = (f32[2,32,256]{2,1,0:T(8,128)S(1)}, f32[2,32,256]{2,1,0:T(8,128)S(1)}, u32[]{:S(2)}, u32[]{:S(2)}) collective-permute-start(f32[2,32,256]{2,1,0:T(8,128)S(1)} %get-tuple-element.107), channel_id=1, source_target_pairs={{0,32},{4,36},{8,40},{12,44},{16,48},{20,52},{24,56},{28,60},{32,0... | collective-permute-start | bytes 196616 | tf_op jit(solution)/shard_map/ppermute | solution.py:18
  84.0 5.0 %collective-permute-start.27 = (f32[2,32,256]{2,1,0:T(8,128)S(1)}, f32[2,32,256]{2,1,0:T(8,128)S(1)}, u32[]{:S(2)}, u32[]{:S(2)}) collective-permute-start(f32[2,32,256]{2,1,0:T(8,128)S(1)} %get-tuple-element.108), channel_id=1, source_target_pairs={{0,16},{4,20},{8,24},{12,28},{16,0},{20,4},{24,8},{28,12},{32,48},... | collective-permute-start | bytes 196616 | tf_op jit(solution)/shard_map/ppermute | solution.py:18
  84.9 5.5 %collective-permute-start.28 = (f32[2,32,256]{2,1,0:T(8,128)S(1)}, f32[2,32,256]{2,1,0:T(8,128)S(1)}, u32[]{:S(2)}, u32[]{:S(2)}) collective-permute-start(f32[2,32,256]{2,1,0:T(8,128)S(1)} %get-tuple-element.109), channel_id=1, source_target_pairs={{0,48},{4,52},{8,56},{12,60},{16,32},{20,36},{24,40},{28,44},{32,1... | collective-permute-start | bytes 196616 | tf_op jit(solution)/shard_map/ppermute | solution.py:18
  90.4 1.3 %collective-permute-start.29 = (f32[64,256]{1,0:T(8,128)S(1)}, f32[64,256]{1,0:T(8,128)S(1)}, u32[]{:S(2)}, u32[]{:S(2)}) collective-permute-start(f32[64,256]{1,0:T(8,128)S(1)} %get-tuple-element.111), channel_id=1, source_target_pairs={{0,1},{1,0},{2,3},{3,2},{4,5},{5,4},{6,7},{7,6},{8,9},{9,8},{10,11... | collective-permute-start | bytes 196616 | tf_op jit(solution)/shard_map/ppermute | solution.py:18
  91.8 5.9 %collective-permute-start.30 = (f32[64,256]{1,0:T(8,128)S(1)}, f32[64,256]{1,0:T(8,128)S(1)}, u32[]{:S(2)}, u32[]{:S(2)}) collective-permute-start(f32[64,256]{1,0:T(8,128)S(1)} %get-tuple-element.113), channel_id=1, source_target_pairs={{0,128},{4,132},{8,136},{12,140},{16,144},{20,148},{24,152},{28,15... | collective-permute-start | bytes 196616 | tf_op jit(solution)/shard_map/ppermute | solution.py:18
  94.7 4.3 %collective-permute-start.31 = (f32[64,256]{1,0:T(8,128)S(1)}, f32[64,256]{1,0:T(8,128)S(1)}, u32[]{:S(2)}, u32[]{:S(2)}) collective-permute-start(f32[64,256]{1,0:T(8,128)S(1)} %get-tuple-element.114), channel_id=1, source_target_pairs={{0,64},{4,68},{8,72},{12,76},{16,80},{20,84},{24,88},{28,92},{32,9... | collective-permute-start | bytes 196616 | tf_op jit(solution)/shard_map/ppermute | solution.py:18
  95.4 5.5 %collective-permute-start.32 = (f32[64,256]{1,0:T(8,128)S(1)}, f32[64,256]{1,0:T(8,128)S(1)}, u32[]{:S(2)}, u32[]{:S(2)}) collective-permute-start(f32[64,256]{1,0:T(8,128)S(1)} %get-tuple-element.115), channel_id=1, source_target_pairs={{0,192},{4,196},{8,200},{12,204},{16,208},{20,212},{24,216},{28,22... | collective-permute-start | bytes 196616 | tf_op jit(solution)/shard_map/ppermute | solution.py:18
  100.9 7.2 %collective-permute-start.33 = (f32[32,256]{1,0:T(8,128)S(1)}, f32[32,256]{1,0:T(8,128)S(1)}, u32[]{:S(2)}, u32[]{:S(2)}) collective-permute-start(f32[32,256]{1,0:T(8,128)S(1)} %get-tuple-element.117), channel_id=1, source_target_pairs={{0,12},{4,8},{8,4},{12,0},{16,28},{20,24},{24,20},{28,16},{32,44},... | collective-permute-start | bytes 98312 | tf_op jit(solution)/shard_map/ppermute | solution.py:18
  108.1 4.7 %collective-permute-start.34 = (f32[16,256]{1,0:T(8,128)S(1)}, f32[16,256]{1,0:T(8,128)S(1)}, u32[]{:S(2)}, u32[]{:S(2)}) collective-permute-start(f32[16,256]{1,0:T(8,128)S(1)} %get-tuple-element.119), channel_id=1, source_target_pairs={{0,4},{4,0},{8,12},{12,8},{16,20},{20,16},{24,28},{28,24},{32,36},... | collective-permute-start | bytes 49160 | tf_op jit(solution)/shard_map/ppermute | solution.py:18
